TPU v7x, 32 devices: a whole 2x2x4 slice. The times are simulated.
32 devices in a mesh: gx: 8 (over z, y), gy: 4 (over x, core).
Axes of the slice: x: 2, y: 2, z: 4, core: 2. Of those that a mesh axis runs over, the one named last changes fastest.
Arguments:
- dual_ops: bfloat16 [8, 4, 1200, 1200], P('gx', 'gy'), as said below
- mode_traces: float32 [8, 4, 4, 6, 300], P('gx', 'gy')
- primal_trace: float32 [8, 4, 16, 1200], P('gx', 'gy')
- mode_loads: float32 [8, 4, 6, 16], P('gx', 'gy'), may hold values from -6 to 6
- face_maps: int32 [8, 4, 4, 300], P('gx', 'gy'), may hold values from 0 to 299, each once within a row
- face_live: int32 [8, 4, 4], P('gx', 'gy'), may hold values from 150 to 300, as said below
Outputs:
- multipliers: float32 [8, 4, 4, 16, 300], P('gx', 'gy')
- residual: float32 [8, 4, 4, 16, 300], P('gx', 'gy')
Inputs may be any that keep to these rules, and one draw needn't show every extreme that they name: `dual_ops`: each subdomain's matrix is symmetric. `face_maps`: each face's map is a permutation of the 300 slots. `face_live`: the two faces that meet at an interface carry the same count; faces on the outer boundary of the subdomain grid are fully coupled.
All inputs are finite; a program needn't handle non-finite values.
Results may differ from a plain program's by a relative error of at most 0.019.
Values sent between devices are 32-bit elements; how exact they have to be, the bound alone decides.
No kernel may reach another device: no remote copies, remote signals or barrier semaphores. Data moves between devices by JAX's collectives and lax.ppermute only.
A program may use at most 64 MiB of HBM per device.

v0:
```python
import jax
import jax.numpy as jnp
from jax import lax
from jax.sharding import PartitionSpec as P

SWEEPS = 2
ITERS = 2


SIGNS = (-1.0, 1.0, -1.0, 1.0)
HIGHEST = lax.Precision.HIGHEST


def extended(block, sides, width):
    for axis, dim in sides:
        count = lax.axis_size(axis)
        forward = [(i, i + 1) for i in range(count - 1)]
        backward = [(target, source) for source, target in forward]
        low = lax.ppermute(
            lax.slice_in_dim(block, block.shape[dim] - width, None, axis=dim), axis, forward
        )
        high = lax.ppermute(lax.slice_in_dim(block, 0, width, axis=dim), axis, backward)
        block = jnp.concatenate([low, block, high], axis=dim)
    return block


def sign_column():
    return jnp.array(SIGNS, jnp.float32)[:, None, None]


def invert_blocks(matrix):
    block_order = matrix.shape[-1]
    inverse = jnp.broadcast_to(jnp.eye(block_order, dtype=jnp.float32), matrix.shape)
    reduced = matrix
    for pivot_index in range(block_order):
        unit_column = (jnp.arange(block_order) == pivot_index).astype(jnp.float32)[:, None]
        pivot_value = reduced[..., pivot_index : pivot_index + 1, pivot_index : pivot_index + 1]
        scaled_row = reduced[..., pivot_index : pivot_index + 1, :] / pivot_value
        scaled_inverse = inverse[..., pivot_index : pivot_index + 1, :] / pivot_value
        column = reduced[..., :, pivot_index : pivot_index + 1] - unit_column
        reduced = reduced - column * scaled_row
        inverse = inverse - column * scaled_inverse
    return inverse


def live_mask(face_live, face_size):
    slots = lax.broadcasted_iota(jnp.int32, face_live.shape + (1, face_size), 4)
    return (slots < face_live[..., None, None]).astype(jnp.float32)


def face_weights(sub_count):
    shape_three = (sub_count, 1, 4)
    column = lax.axis_index("gx") * sub_count + lax.broadcasted_iota(jnp.int32, shape_three, 0)
    row_index = lax.axis_index("gy") + jnp.zeros(shape_three, jnp.int32)
    facet = lax.broadcasted_iota(jnp.int32, shape_three, 2)
    last_column = lax.axis_size("gx") * sub_count - 1
    last_row = lax.axis_size("gy") - 1
    on_boundary = (
        (facet == 0) & (column == 0)
        | (facet == 1) & (column == last_column)
        | (facet == 2) & (row_index == 0)
        | (facet == 3) & (row_index == last_row)
    )
    return jnp.where(on_boundary, 1.0, 0.5).astype(jnp.float32)[..., None, None]


def slot_table(face_maps):
    face_size = face_maps.shape[-1]
    slots = lax.broadcasted_iota(jnp.int32, face_maps.shape + (face_size,), 4)
    return (face_maps[..., None] == slots).astype(jnp.float32)


def neighbours(canonical):
    sub_count = canonical.shape[0]
    along_x = canonical[:, 0, 0:2].reshape((2 * sub_count,) + canonical.shape[3:])
    padded_x = extended(along_x, (("gx", 0),), 1)
    below_x = padded_x[0 : 2 * sub_count : 2]
    above_x = padded_x[3::2]
    along_y = canonical[:, 0, 2:4]
    padded_y = extended(along_y, (("gy", 1),), 1)
    below_y = padded_y[:, 0]
    above_y = padded_y[:, 3]
    return jnp.stack([below_x, above_x, below_y, above_y], axis=1)[:, None]


def jump_of(canonical, live):
    return live * sign_column() * (canonical - neighbours(canonical))


def to_local(field, table):
    signed = field * sign_column()
    picked = jnp.einsum("abfkc,abflc->ablfk", table, signed, precision=HIGHEST)
    return picked.reshape(picked.shape[:3] + (picked.shape[3] * picked.shape[4],))


def to_canonical(local, table):
    split = local.reshape(local.shape[:-1] + (4, local.shape[-1] // 4))
    return jnp.einsum("abfkc,ablfk->abflc", table, split, precision=HIGHEST)


def apply_operators(local, dual_ops):
    rounded = local.astype(jnp.bfloat16)
    return jnp.einsum("aylm,aymn->ayln", rounded, dual_ops, preferred_element_type=jnp.float32)


def coarse_of(field, mode_traces):
    return jnp.einsum("abfjc,abflc->abjl", mode_traces * sign_column(), field, precision=HIGHEST)


def trace_of(coarse_field, mode_traces):
    return jnp.einsum("abfjc,abjl->abflc", mode_traces, coarse_field, precision=HIGHEST)


def blocks_apply(matrices, coarse_field):
    return jnp.einsum("abjk,abkl->abjl", matrices, coarse_field, precision=HIGHEST)


def global_dot(first, second, weights):
    return lax.psum(jnp.sum(weights * first * second), ("gx", "gy"))


def body(dual_ops, mode_traces, primal_trace, mode_loads, face_maps, face_live):
    sub_count = dual_ops.shape[0]
    face_size = face_maps.shape[-1]
    live = live_mask(face_live, face_size)
    weights = face_weights(sub_count)
    table = slot_table(face_maps)
    diagonal = jnp.einsum("abfjc,abfkc->abjk", mode_traces * live, mode_traces, precision=HIGHEST)
    block_inverse = invert_blocks(diagonal)

    def lift_faces(coarse_field):
        return jump_of(trace_of(coarse_field, mode_traces), live)

    def coarse_operator(coarse_field):
        return coarse_of(lift_faces(coarse_field), mode_traces)

    def coarse_solve(loads):
        coarse_field = blocks_apply(block_inverse, loads)
        for sweep_index in range(SWEEPS):
            coarse_field = coarse_field + blocks_apply(
                block_inverse, loads - coarse_operator(coarse_field)
            )
        return coarse_field

    def project(field):
        return field - lift_faces(coarse_solve(coarse_of(field, mode_traces)))

    multipliers = lift_faces(coarse_solve(mode_loads))
    local_rest = primal_trace - apply_operators(to_local(multipliers, table), dual_ops)
    residual = jump_of(to_canonical(local_rest, table), live)
    projected = project(residual)
    gamma_now = global_dot(residual, projected, weights)
    direction = projected
    for iteration in range(ITERS):
        image_field = jump_of(
            to_canonical(apply_operators(to_local(direction, table), dual_ops), table), live
        )
        step_size = gamma_now / global_dot(direction, image_field, weights)
        multipliers = multipliers + step_size * direction
        residual = residual - step_size * image_field
        if iteration + 1 < ITERS:
            projected = project(residual)
            gamma_fresh = global_dot(residual, projected, weights)
            direction = projected + gamma_fresh / gamma_now * direction
            gamma_now = gamma_fresh
    return (multipliers, residual)


def solution(mesh):
    in_specs = (
        P("gx", "gy", None, None),
        P("gx", "gy", None, None, None),
        P("gx", "gy", None, None),
        P("gx", "gy", None, None),
        P("gx", "gy", None, None),
        P("gx", "gy", None),
    )
    out_specs = (P("gx", "gy", None, None, None), P("gx", "gy", None, None, None))
    return jax.shard_map(body, mesh=mesh, in_specs=in_specs, out_specs=out_specs, check_vma=False)
```

profile of v0, /device:TPU:5, one launch (start us, length us, event | category | flops | bytes accessed | tf_op | source)
XLA Modules:
  0.0 361.8 jit_solution(12085105665511287655)
XLA Ops:
  17.8 3.7 %collective-permute-start.2 = (f32[1,1,16,300]{3,2,1,0:T(8,128)S(1)}, f32[1,1,16,300]{3,2,1,0:T(8,128)S(1)}, u32[]{:S(2)}, u32[]{:S(2)}) collective-permute-start(f32[1,1,16,300]{3,2,1,0:T(8,128)S(1)} %get-tuple-element.54), channel_id=1, source_target_pairs={{0,1},{1,2},{2,3},{4,5},{5,6},{6,7},{8,9},{9,10},{10,11},{12,13},{... | collective-permute-start | bytes 57608 | tf_op jit(solution)/shard_map/ppermute | solution.py:19
  23.4 3.1 collective-permute-start
  34.3 5.1 %collective-permute-start.6 = (f32[1,1,16,300]{3,2,1,0:T(8,128)S(1)}, f32[1,1,16,300]{3,2,1,0:T(8,128)S(1)}, u32[]{:S(2)}, u32[]{:S(2)}) collective-permute-start(f32[1,1,16,300]{3,2,1,0:T(8,128)S(1)} %get-tuple-element.52), channel_id=1, source_target_pairs={{0,1},{1,2},{2,3},{4,5},{5,6},{6,7},{8,9},{9,10},{10,11},{12,13},{... | collective-permute-start | bytes 57608 | tf_op jit(solution)/shard_map/ppermute | solution.py:19
  43.6 3.0 collective-permute-start.5
  51.4 5.1 %collective-permute-start.10 = (f32[1,1,16,300]{3,2,1,0:T(8,128)S(1)}, f32[1,1,16,300]{3,2,1,0:T(8,128)S(1)}, u32[]{:S(2)}, u32[]{:S(2)}) collective-permute-start(f32[1,1,16,300]{3,2,1,0:T(8,128)S(1)} %get-tuple-element.50), channel_id=1, source_target_pairs={{0,1},{1,2},{2,3},{4,5},{5,6},{6,7},{8,9},{9,10},{10,11},{12,13},{... | collective-permute-start | bytes 57608 | tf_op jit(solution)/shard_map/ppermute | solution.py:19
  58.4 3.1 collective-permute-start.8
  63.7 3.3 collective-permute-done.9
  69.8 5.1 %collective-permute-start.14 = (f32[1,1,16,300]{3,2,1,0:T(8,128)S(1)}, f32[1,1,16,300]{3,2,1,0:T(8,128)S(1)}, u32[]{:S(2)}, u32[]{:S(2)}) collective-permute-start(f32[1,1,16,300]{3,2,1,0:T(8,128)S(1)} %get-tuple-element.48), channel_id=1, source_target_pairs={{0,1},{1,2},{2,3},{4,5},{5,6},{6,7},{8,9},{9,10},{10,11},{12,13},{... | collective-permute-start | bytes 57608 | tf_op jit(solution)/shard_map/ppermute | solution.py:19
  79.0 3.0 collective-permute-start.13
  85.3 5.1 %collective-permute-start.18 = (f32[1,1,16,300]{3,2,1,0:T(8,128)S(1)}, f32[1,1,16,300]{3,2,1,0:T(8,128)S(1)}, u32[]{:S(2)}, u32[]{:S(2)}) collective-permute-start(f32[1,1,16,300]{3,2,1,0:T(8,128)S(1)} %get-tuple-element.46), channel_id=1, source_target_pairs={{0,1},{1,2},{2,3},{4,5},{5,6},{6,7},{8,9},{9,10},{10,11},{12,13},{... | collective-permute-start | bytes 57608 | tf_op jit(solution)/shard_map/ppermute | solution.py:19
  92.3 3.1 collective-permute-start.16
  97.6 3.3 collective-permute-done.17
  101.7 5.1 %collective-permute-start.22 = (f32[1,1,16,300]{3,2,1,0:T(8,128)S(1)}, f32[1,1,16,300]{3,2,1,0:T(8,128)S(1)}, u32[]{:S(2)}, u32[]{:S(2)}) collective-permute-start(f32[1,1,16,300]{3,2,1,0:T(8,128)S(1)} %get-tuple-element.44), channel_id=1, source_target_pairs={{0,1},{1,2},{2,3},{4,5},{5,6},{6,7},{8,9},{9,10},{10,11},{12,13},{... | collective-permute-start | bytes 57608 | tf_op jit(solution)/shard_map/ppermute | solution.py:19
  111.0 3.0 collective-permute-start.21
  118.5 5.1 %collective-permute-start.26 = (f32[1,1,16,300]{3,2,1,0:T(8,128)}, f32[1,1,16,300]{3,2,1,0:T(8,128)S(1)}, u32[]{:S(2)}, u32[]{:S(2)}) collective-permute-start(f32[1,1,16,300]{3,2,1,0:T(8,128)} %get-tuple-element.42), channel_id=1, source_target_pairs={{0,1},{1,2},{2,3},{4,5},{5,6},{6,7},{8,9},{9,10},{10,11},{12,13},{... | collective-permute-start | bytes 57608 | tf_op jit(solution)/shard_map/ppermute | solution.py:19
  127.4 3.4 collective-permute-start.25
  130.8 4.9 %reshape.3128 = bf16[4,300,1200]{1,0,2:T(4,128)(2,1)} reshape(bf16[1200,1200]{0,1:T(8,128)(2,1)S(1)} %bitcast.474) | data formatting | bytes 5760000 | tf_op jit(solution)/shard_map/aylm,aymn->ayln/dot_general | solution.py:103
  135.6 7.3 %copy.83 = bf16[4,300,1200]{2,1,0:T(8,128)(2,1)S(1)} copy(bf16[4,300,1200]{1,0,2:T(4,128)(2,1)} %reshape.3128) | data formatting | bytes 5760000 | tf_op jit(solution)/shard_map/aylm,aymn->ayln/dot_general | solution.py:103
  147.5 4.2 %collective-permute-start.30 = (f32[1,1,16,300]{3,2,1,0:T(8,128)S(1)}, f32[1,1,16,300]{3,2,1,0:T(8,128)S(1)}, u32[]{:S(2)}, u32[]{:S(2)}) collective-permute-start(f32[1,1,16,300]{3,2,1,0:T(8,128)S(1)} %get-tuple-element.40), channel_id=1, source_target_pairs={{0,1},{1,2},{2,3},{4,5},{5,6},{6,7},{8,9},{9,10},{10,11},{12,13},{... | collective-permute-start | bytes 57608 | tf_op jit(solution)/shard_map/ppermute | solution.py:19
  163.3 39.4 %all-reduce = (f32[]{:T(128)}, f32[]{:T(128)}) all-reduce(f32[]{:T(128)} %get-tuple-element.3, f32[]{:T(128)} %get-tuple-element.2), channel_id=1, replica_groups=mesh['gx'=8,'gy'=4] {'gx','gy'}, use_global_device_ids=true, to_apply=%region_1.2 | all-reduce | flops 2 | bytes 16 | tf_op jit(solution)/shard_map/psum | solution.py:119
  205.7 4.5 %collective-permute-start.34 = (f32[1,1,16,300]{3,2,1,0:T(8,128)S(1)}, f32[1,1,16,300]{3,2,1,0:T(8,128)S(1)}, u32[]{:S(2)}, u32[]{:S(2)}) collective-permute-start(f32[1,1,16,300]{3,2,1,0:T(8,128)S(1)} %get-tuple-element.38), channel_id=1, source_target_pairs={{0,1},{1,2},{2,3},{4,5},{5,6},{6,7},{8,9},{9,10},{10,11},{12,13},{... | collective-permute-start | bytes 57608 | tf_op jit(solution)/shard_map/ppermute | solution.py:19
  212.1 4.6 %collective-permute-start.32 = (f32[1,16,300]{2,1,0:T(8,128)S(1)}, f32[1,16,300]{2,1,0:T(8,128)S(1)}, u32[]{:S(2)}, u32[]{:S(2)}) collective-permute-start(f32[1,16,300]{2,1,0:T(8,128)S(1)} %get-tuple-element.14), channel_id=1, source_target_pairs={{0,4},{4,8},{8,12},{12,16},{16,20},{20,24},{24,28},{1,5},{5,9},{9,... | collective-permute-start | bytes 57608 | tf_op jit(solution)/shard_map/ppermute | solution.py:19
  218.6 3.5 collective-permute-done.33
  222.9 5.1 %collective-permute-start.38 = (f32[1,1,16,300]{3,2,1,0:T(8,128)S(1)}, f32[1,1,16,300]{3,2,1,0:T(8,128)S(1)}, u32[]{:S(2)}, u32[]{:S(2)}) collective-permute-start(f32[1,1,16,300]{3,2,1,0:T(8,128)S(1)} %get-tuple-element.36), channel_id=1, source_target_pairs={{0,1},{1,2},{2,3},{4,5},{5,6},{6,7},{8,9},{9,10},{10,11},{12,13},{... | collective-permute-start | bytes 57608 | tf_op jit(solution)/shard_map/ppermute | solution.py:19
  231.9 3.4 collective-permute-start.37
  238.1 4.8 %collective-permute-start.42 = (f32[1,1,16,300]{3,2,1,0:T(8,128)S(1)}, f32[1,1,16,300]{3,2,1,0:T(8,128)S(1)}, u32[]{:S(2)}, u32[]{:S(2)}) collective-permute-start(f32[1,1,16,300]{3,2,1,0:T(8,128)S(1)} %get-tuple-element.34), channel_id=1, source_target_pairs={{0,1},{1,2},{2,3},{4,5},{5,6},{6,7},{8,9},{9,10},{10,11},{12,13},{... | collective-permute-start | bytes 57608 | tf_op jit(solution)/shard_map/ppermute | solution.py:19
  250.5 3.0 collective-permute-done.41
  255.4 39.5 %psum.30 = f32[]{:T(128)} all-reduce(f32[]{:T(128)} %get-tuple-element.6), channel_id=1, replica_groups=mesh['gx'=8,'gy'=4] {'gx','gy'}, use_global_device_ids=true, to_apply=%region_5.6 | all-reduce | flops 1 | bytes 8 | tf_op jit(solution)/shard_map/psum | solution.py:119
  300.9 4.5 %collective-permute-start.46 = (f32[1,1,16,300]{3,2,1,0:T(8,128)S(1)}, f32[1,1,16,300]{3,2,1,0:T(8,128)S(1)}, u32[]{:S(2)}, u32[]{:S(2)}) collective-permute-start(f32[1,1,16,300]{3,2,1,0:T(8,128)S(1)} %get-tuple-element.32), channel_id=1, source_target_pairs={{0,1},{1,2},{2,3},{4,5},{5,6},{6,7},{8,9},{9,10},{10,11},{12,13},{... | collective-permute-start | bytes 57608 | tf_op jit(solution)/shard_map/ppermute | solution.py:19
  307.3 4.3 %collective-permute-start.44 = (f32[1,16,300]{2,1,0:T(8,128)S(1)}, f32[1,16,300]{2,1,0:T(8,128)S(1)}, u32[]{:S(2)}, u32[]{:S(2)}) collective-permute-start(f32[1,16,300]{2,1,0:T(8,128)S(1)} %get-tuple-element.8), channel_id=1, source_target_pairs={{0,4},{4,8},{8,12},{12,16},{16,20},{20,24},{24,28},{1,5},{5,9},{9,... | collective-permute-start | bytes 57608 | tf_op jit(solution)/shard_map/ppermute | solution.py:19
  313.6 3.5 collective-permute-done.45
  318.5 39.7 %psum.31 = f32[]{:T(128)} all-reduce(f32[]{:T(128)} %fusion.111), channel_id=1, replica_groups=mesh['gx'=8,'gy'=4] {'gx','gy'}, use_global_device_ids=true, to_apply=%region_7.8 | all-reduce | flops 1 | bytes 8 | tf_op jit(solution)/shard_map/psum | solution.py:119
  (263 shorter events, 117.2 us)
Async XLA Ops:
  17.8 11.7 %collective-permute-start.2 = (f32[1,1,16,300]{3,2,1,0:T(8,128)S(1)}, f32[1,1,16,300]{3,2,1,0:T(8,128)S(1)}, u32[]{:S(2)}, u32[]{:S(2)}) collective-permute-start(f32[1,1,16,300]{3,2,1,0:T(8,128)S(1)} %get-tuple-element.54), channel_id=1, source_target_pairs={{0,1},{1,2},{2,3},{4,5},{5,6},{6,7},{8,9},{9,10},{10,11},{12,13},{... | collective-permute-start | bytes 57608 | tf_op jit(solution)/shard_map/ppermute | solution.py:19
  21.5 8.0 %collective-permute-start.3 = (f32[1,1,16,300]{3,2,1,0:T(8,128)S(1)}, f32[1,1,16,300]{3,2,1,0:T(8,128)S(1)}, u32[]{:S(2)}, u32[]{:S(2)}) collective-permute-start(f32[1,1,16,300]{3,2,1,0:T(8,128)S(1)} %get-tuple-element.55), channel_id=1, source_target_pairs={{1,0},{2,1},{3,2},{5,4},{6,5},{7,6},{9,8},{10,9},{11,10},{13,12},{... | collective-permute-start | bytes 57608 | tf_op jit(solution)/shard_map/ppermute | solution.py:22
  23.4 6.1 %collective-permute-start = (f32[1,16,300]{2,1,0:T(8,128)S(1)}, f32[1,16,300]{2,1,0:T(8,128)S(1)}, u32[]{:S(2)}, u32[]{:S(2)}) collective-permute-start(f32[1,16,300]{2,1,0:T(8,128)S(1)} %get-tuple-element.30), channel_id=1, source_target_pairs={{0,4},{4,8},{8,12},{12,16},{16,20},{20,24},{24,28},{1,5},{5,9},{9,... | collective-permute-start | bytes 57608 | tf_op jit(solution)/shard_map/ppermute | solution.py:19
  26.6 5.5 %collective-permute-start.1 = (f32[1,16,300]{2,1,0:T(8,128)S(1)}, f32[1,16,300]{2,1,0:T(8,128)S(1)}, u32[]{:S(2)}, u32[]{:S(2)}) collective-permute-start(f32[1,16,300]{2,1,0:T(8,128)S(1)} %get-tuple-element.31), channel_id=1, source_target_pairs={{4,0},{8,4},{12,8},{16,12},{20,16},{24,20},{28,24},{5,1},{9,5},{13... | collective-permute-start | bytes 57608 | tf_op jit(solution)/shard_map/ppermute | solution.py:22
  34.3 12.3 %collective-permute-start.6 = (f32[1,1,16,300]{3,2,1,0:T(8,128)S(1)}, f32[1,1,16,300]{3,2,1,0:T(8,128)S(1)}, u32[]{:S(2)}, u32[]{:S(2)}) collective-permute-start(f32[1,1,16,300]{3,2,1,0:T(8,128)S(1)} %get-tuple-element.52), channel_id=1, source_target_pairs={{0,1},{1,2},{2,3},{4,5},{5,6},{6,7},{8,9},{9,10},{10,11},{12,13},{... | collective-permute-start | bytes 57608 | tf_op jit(solution)/shard_map/ppermute | solution.py:19
  39.4 7.2 %collective-permute-start.7 = (f32[1,1,16,300]{3,2,1,0:T(8,128)S(1)}, f32[1,1,16,300]{3,2,1,0:T(8,128)S(1)}, u32[]{:S(2)}, u32[]{:S(2)}) collective-permute-start(f32[1,1,16,300]{3,2,1,0:T(8,128)S(1)} %get-tuple-element.53), channel_id=1, source_target_pairs={{1,0},{2,1},{3,2},{5,4},{6,5},{7,6},{9,8},{10,9},{11,10},{13,12},{... | collective-permute-start | bytes 57608 | tf_op jit(solution)/shard_map/ppermute | solution.py:22
  43.6 5.5 %collective-permute-start.5 = (f32[1,16,300]{2,1,0:T(8,128)S(1)}, f32[1,16,300]{2,1,0:T(8,128)S(1)}, u32[]{:S(2)}, u32[]{:S(2)}) collective-permute-start(f32[1,16,300]{2,1,0:T(8,128)S(1)} %get-tuple-element.29), channel_id=1, source_target_pairs={{4,0},{8,4},{12,8},{16,12},{20,16},{24,20},{28,24},{5,1},{9,5},{13... | collective-permute-start | bytes 57608 | tf_op jit(solution)/shard_map/ppermute | solution.py:22
  51.4 12.3 %collective-permute-start.10 = (f32[1,1,16,300]{3,2,1,0:T(8,128)S(1)}, f32[1,1,16,300]{3,2,1,0:T(8,128)S(1)}, u32[]{:S(2)}, u32[]{:S(2)}) collective-permute-start(f32[1,1,16,300]{3,2,1,0:T(8,128)S(1)} %get-tuple-element.50), channel_id=1, source_target_pairs={{0,1},{1,2},{2,3},{4,5},{5,6},{6,7},{8,9},{9,10},{10,11},{12,13},{... | collective-permute-start | bytes 57608 | tf_op jit(solution)/shard_map/ppermute | solution.py:19
  56.5 7.2 %collective-permute-start.11 = (f32[1,1,16,300]{3,2,1,0:T(8,128)S(1)}, f32[1,1,16,300]{3,2,1,0:T(8,128)S(1)}, u32[]{:S(2)}, u32[]{:S(2)}) collective-permute-start(f32[1,1,16,300]{3,2,1,0:T(8,128)S(1)} %get-tuple-element.51), channel_id=1, source_target_pairs={{1,0},{2,1},{3,2},{5,4},{6,5},{7,6},{9,8},{10,9},{11,10},{13,12},{... | collective-permute-start | bytes 57608 | tf_op jit(solution)/shard_map/ppermute | solution.py:22
  69.8 13.1 %collective-permute-start.14 = (f32[1,1,16,300]{3,2,1,0:T(8,128)S(1)}, f32[1,1,16,300]{3,2,1,0:T(8,128)S(1)}, u32[]{:S(2)}, u32[]{:S(2)}) collective-permute-start(f32[1,1,16,300]{3,2,1,0:T(8,128)S(1)} %get-tuple-element.48), channel_id=1, source_target_pairs={{0,1},{1,2},{2,3},{4,5},{5,6},{6,7},{8,9},{9,10},{10,11},{12,13},{... | collective-permute-start | bytes 57608 | tf_op jit(solution)/shard_map/ppermute | solution.py:19
  74.8 8.0 %collective-permute-start.15 = (f32[1,1,16,300]{3,2,1,0:T(8,128)S(1)}, f32[1,1,16,300]{3,2,1,0:T(8,128)S(1)}, u32[]{:S(2)}, u32[]{:S(2)}) collective-permute-start(f32[1,1,16,300]{3,2,1,0:T(8,128)S(1)} %get-tuple-element.49), channel_id=1, source_target_pairs={{1,0},{2,1},{3,2},{5,4},{6,5},{7,6},{9,8},{10,9},{11,10},{13,12},{... | collective-permute-start | bytes 57608 | tf_op jit(solution)/shard_map/ppermute | solution.py:22
  76.8 6.1 %collective-permute-start.12 = (f32[1,16,300]{2,1,0:T(8,128)S(1)}, f32[1,16,300]{2,1,0:T(8,128)S(1)}, u32[]{:S(2)}, u32[]{:S(2)}) collective-permute-start(f32[1,16,300]{2,1,0:T(8,128)S(1)} %get-tuple-element.24), channel_id=1, source_target_pairs={{0,4},{4,8},{8,12},{12,16},{16,20},{20,24},{24,28},{1,5},{5,9},{9,... | collective-permute-start | bytes 57608 | tf_op jit(solution)/shard_map/ppermute | solution.py:19
  85.3 12.3 %collective-permute-start.18 = (f32[1,1,16,300]{3,2,1,0:T(8,128)S(1)}, f32[1,1,16,300]{3,2,1,0:T(8,128)S(1)}, u32[]{:S(2)}, u32[]{:S(2)}) collective-permute-start(f32[1,1,16,300]{3,2,1,0:T(8,128)S(1)} %get-tuple-element.46), channel_id=1, source_target_pairs={{0,1},{1,2},{2,3},{4,5},{5,6},{6,7},{8,9},{9,10},{10,11},{12,13},{... | collective-permute-start | bytes 57608 | tf_op jit(solution)/shard_map/ppermute | solution.py:19
  90.4 7.2 %collective-permute-start.19 = (f32[1,1,16,300]{3,2,1,0:T(8,128)S(1)}, f32[1,1,16,300]{3,2,1,0:T(8,128)S(1)}, u32[]{:S(2)}, u32[]{:S(2)}) collective-permute-start(f32[1,1,16,300]{3,2,1,0:T(8,128)S(1)} %get-tuple-element.47), channel_id=1, source_target_pairs={{1,0},{2,1},{3,2},{5,4},{6,5},{7,6},{9,8},{10,9},{11,10},{13,12},{... | collective-permute-start | bytes 57608 | tf_op jit(solution)/shard_map/ppermute | solution.py:22
  101.7 12.3 %collective-permute-start.22 = (f32[1,1,16,300]{3,2,1,0:T(8,128)S(1)}, f32[1,1,16,300]{3,2,1,0:T(8,128)S(1)}, u32[]{:S(2)}, u32[]{:S(2)}) collective-permute-start(f32[1,1,16,300]{3,2,1,0:T(8,128)S(1)} %get-tuple-element.44), channel_id=1, source_target_pairs={{0,1},{1,2},{2,3},{4,5},{5,6},{6,7},{8,9},{9,10},{10,11},{12,13},{... | collective-permute-start | bytes 57608 | tf_op jit(solution)/shard_map/ppermute | solution.py:19
  106.8 7.2 %collective-permute-start.23 = (f32[1,1,16,300]{3,2,1,0:T(8,128)S(1)}, f32[1,1,16,300]{3,2,1,0:T(8,128)S(1)}, u32[]{:S(2)}, u32[]{:S(2)}) collective-permute-start(f32[1,1,16,300]{3,2,1,0:T(8,128)S(1)} %get-tuple-element.45), channel_id=1, source_target_pairs={{1,0},{2,1},{3,2},{5,4},{6,5},{7,6},{9,8},{10,9},{11,10},{13,12},{... | collective-permute-start | bytes 57608 | tf_op jit(solution)/shard_map/ppermute | solution.py:22
  118.5 24.5 %collective-permute-start.26 = (f32[1,1,16,300]{3,2,1,0:T(8,128)}, f32[1,1,16,300]{3,2,1,0:T(8,128)S(1)}, u32[]{:S(2)}, u32[]{:S(2)}) collective-permute-start(f32[1,1,16,300]{3,2,1,0:T(8,128)} %get-tuple-element.42), channel_id=1, source_target_pairs={{0,1},{1,2},{2,3},{4,5},{5,6},{6,7},{8,9},{9,10},{10,11},{12,13},{... | collective-permute-start | bytes 57608 | tf_op jit(solution)/shard_map/ppermute | solution.py:19
  123.5 19.4 %collective-permute-start.27 = (f32[1,1,16,300]{3,2,1,0:T(8,128)}, f32[1,1,16,300]{3,2,1,0:T(8,128)S(1)}, u32[]{:S(2)}, u32[]{:S(2)}) collective-permute-start(f32[1,1,16,300]{3,2,1,0:T(8,128)} %get-tuple-element.43), channel_id=1, source_target_pairs={{1,0},{2,1},{3,2},{5,4},{6,5},{7,6},{9,8},{10,9},{11,10},{13,12},{... | collective-permute-start | bytes 57608 | tf_op jit(solution)/shard_map/ppermute | solution.py:22
  125.4 17.5 %collective-permute-start.24 = (f32[1,16,300]{2,1,0:T(8,128)}, f32[1,16,300]{2,1,0:T(8,128)S(1)}, u32[]{:S(2)}, u32[]{:S(2)}) collective-permute-start(f32[1,16,300]{2,1,0:T(8,128)} %get-tuple-element.18), channel_id=1, source_target_pairs={{0,4},{4,8},{8,12},{12,16},{16,20},{20,24},{24,28},{1,5},{5,9},{9,... | collective-permute-start | bytes 57608 | tf_op jit(solution)/shard_map/ppermute | solution.py:19
  127.4 15.6 %collective-permute-start.25 = (f32[1,16,300]{2,1,0:T(8,128)}, f32[1,16,300]{2,1,0:T(8,128)S(1)}, u32[]{:S(2)}, u32[]{:S(2)}) collective-permute-start(f32[1,16,300]{2,1,0:T(8,128)} %get-tuple-element.19), channel_id=1, source_target_pairs={{4,0},{8,4},{12,8},{16,12},{20,16},{24,20},{28,24},{5,1},{9,5},{13... | collective-permute-start | bytes 57608 | tf_op jit(solution)/shard_map/ppermute | solution.py:22
  147.5 11.5 %collective-permute-start.30 = (f32[1,1,16,300]{3,2,1,0:T(8,128)S(1)}, f32[1,1,16,300]{3,2,1,0:T(8,128)S(1)}, u32[]{:S(2)}, u32[]{:S(2)}) collective-permute-start(f32[1,1,16,300]{3,2,1,0:T(8,128)S(1)} %get-tuple-element.40), channel_id=1, source_target_pairs={{0,1},{1,2},{2,3},{4,5},{5,6},{6,7},{8,9},{9,10},{10,11},{12,13},{... | collective-permute-start | bytes 57608 | tf_op jit(solution)/shard_map/ppermute | solution.py:19
  151.7 7.3 %collective-permute-start.31 = (f32[1,1,16,300]{3,2,1,0:T(8,128)S(1)}, f32[1,1,16,300]{3,2,1,0:T(8,128)S(1)}, u32[]{:S(2)}, u32[]{:S(2)}) collective-permute-start(f32[1,1,16,300]{3,2,1,0:T(8,128)S(1)} %get-tuple-element.41), channel_id=1, source_target_pairs={{1,0},{2,1},{3,2},{5,4},{6,5},{7,6},{9,8},{10,9},{11,10},{13,12},{... | collective-permute-start | bytes 57608 | tf_op jit(solution)/shard_map/ppermute | solution.py:22
  205.7 12.9 %collective-permute-start.34 = (f32[1,1,16,300]{3,2,1,0:T(8,128)S(1)}, f32[1,1,16,300]{3,2,1,0:T(8,128)S(1)}, u32[]{:S(2)}, u32[]{:S(2)}) collective-permute-start(f32[1,1,16,300]{3,2,1,0:T(8,128)S(1)} %get-tuple-element.38), channel_id=1, source_target_pairs={{0,1},{1,2},{2,3},{4,5},{5,6},{6,7},{8,9},{9,10},{10,11},{12,13},{... | collective-permute-start | bytes 57608 | tf_op jit(solution)/shard_map/ppermute | solution.py:19
  210.1 8.5 %collective-permute-start.35 = (f32[1,1,16,300]{3,2,1,0:T(8,128)S(1)}, f32[1,1,16,300]{3,2,1,0:T(8,128)S(1)}, u32[]{:S(2)}, u32[]{:S(2)}) collective-permute-start(f32[1,1,16,300]{3,2,1,0:T(8,128)S(1)} %get-tuple-element.39), channel_id=1, source_target_pairs={{1,0},{2,1},{3,2},{5,4},{6,5},{7,6},{9,8},{10,9},{11,10},{13,12},{... | collective-permute-start | bytes 57608 | tf_op jit(solution)/shard_map/ppermute | solution.py:22
  212.1 6.6 %collective-permute-start.32 = (f32[1,16,300]{2,1,0:T(8,128)S(1)}, f32[1,16,300]{2,1,0:T(8,128)S(1)}, u32[]{:S(2)}, u32[]{:S(2)}) collective-permute-start(f32[1,16,300]{2,1,0:T(8,128)S(1)} %get-tuple-element.14), channel_id=1, source_target_pairs={{0,4},{4,8},{8,12},{12,16},{16,20},{20,24},{24,28},{1,5},{5,9},{9,... | collective-permute-start | bytes 57608 | tf_op jit(solution)/shard_map/ppermute | solution.py:19
  222.9 12.3 %collective-permute-start.38 = (f32[1,1,16,300]{3,2,1,0:T(8,128)S(1)}, f32[1,1,16,300]{3,2,1,0:T(8,128)S(1)}, u32[]{:S(2)}, u32[]{:S(2)}) collective-permute-start(f32[1,1,16,300]{3,2,1,0:T(8,128)S(1)} %get-tuple-element.36), channel_id=1, source_target_pairs={{0,1},{1,2},{2,3},{4,5},{5,6},{6,7},{8,9},{9,10},{10,11},{12,13},{... | collective-permute-start | bytes 57608 | tf_op jit(solution)/shard_map/ppermute | solution.py:19
  228.0 7.2 %collective-permute-start.39 = (f32[1,1,16,300]{3,2,1,0:T(8,128)S(1)}, f32[1,1,16,300]{3,2,1,0:T(8,128)S(1)}, u32[]{:S(2)}, u32[]{:S(2)}) collective-permute-start(f32[1,1,16,300]{3,2,1,0:T(8,128)S(1)} %get-tuple-element.37), channel_id=1, source_target_pairs={{1,0},{2,1},{3,2},{5,4},{6,5},{7,6},{9,8},{10,9},{11,10},{13,12},{... | collective-permute-start | bytes 57608 | tf_op jit(solution)/shard_map/ppermute | solution.py:22
  238.1 12.4 %collective-permute-start.42 = (f32[1,1,16,300]{3,2,1,0:T(8,128)S(1)}, f32[1,1,16,300]{3,2,1,0:T(8,128)S(1)}, u32[]{:S(2)}, u32[]{:S(2)}) collective-permute-start(f32[1,1,16,300]{3,2,1,0:T(8,128)S(1)} %get-tuple-element.34), channel_id=1, source_target_pairs={{0,1},{1,2},{2,3},{4,5},{5,6},{6,7},{8,9},{9,10},{10,11},{12,13},{... | collective-permute-start | bytes 57608 | tf_op jit(solution)/shard_map/ppermute | solution.py:19
  242.9 7.6 %collective-permute-start.43 = (f32[1,1,16,300]{3,2,1,0:T(8,128)S(1)}, f32[1,1,16,300]{3,2,1,0:T(8,128)S(1)}, u32[]{:S(2)}, u32[]{:S(2)}) collective-permute-start(f32[1,1,16,300]{3,2,1,0:T(8,128)S(1)} %get-tuple-element.35), channel_id=1, source_target_pairs={{1,0},{2,1},{3,2},{5,4},{6,5},{7,6},{9,8},{10,9},{11,10},{13,12},{... | collective-permute-start | bytes 57608 | tf_op jit(solution)/shard_map/ppermute | solution.py:22
  300.9 12.7 %collective-permute-start.46 = (f32[1,1,16,300]{3,2,1,0:T(8,128)S(1)}, f32[1,1,16,300]{3,2,1,0:T(8,128)S(1)}, u32[]{:S(2)}, u32[]{:S(2)}) collective-permute-start(f32[1,1,16,300]{3,2,1,0:T(8,128)S(1)} %get-tuple-element.32), channel_id=1, source_target_pairs={{0,1},{1,2},{2,3},{4,5},{5,6},{6,7},{8,9},{9,10},{10,11},{12,13},{... | collective-permute-start | bytes 57608 | tf_op jit(solution)/shard_map/ppermute | solution.py:19
  305.3 8.2 %collective-permute-start.47 = (f32[1,1,16,300]{3,2,1,0:T(8,128)S(1)}, f32[1,1,16,300]{3,2,1,0:T(8,128)S(1)}, u32[]{:S(2)}, u32[]{:S(2)}) collective-permute-start(f32[1,1,16,300]{3,2,1,0:T(8,128)S(1)} %get-tuple-element.33), channel_id=1, source_target_pairs={{1,0},{2,1},{3,2},{5,4},{6,5},{7,6},{9,8},{10,9},{11,10},{13,12},{... | collective-permute-start | bytes 57608 | tf_op jit(solution)/shard_map/ppermute | solution.py:22
  307.3 6.3 %collective-permute-start.44 = (f32[1,16,300]{2,1,0:T(8,128)S(1)}, f32[1,16,300]{2,1,0:T(8,128)S(1)}, u32[]{:S(2)}, u32[]{:S(2)}) collective-permute-start(f32[1,16,300]{2,1,0:T(8,128)S(1)} %get-tuple-element.8), channel_id=1, source_target_pairs={{0,4},{4,8},{8,12},{12,16},{16,20},{20,24},{24,28},{1,5},{5,9},{9,... | collective-permute-start | bytes 57608 | tf_op jit(solution)/shard_map/ppermute | solution.py:19
  (48 other events, 1095.6 us)
where the time goes:
time: 367 us; the launch traced here: 362 us
  starting transfers between devices  146 us (40%)
  blocking collectives  119 us (32%)
  waiting for transfers between devices  30.4 us (8%)
  matrix products  21.4 us (6%)
  other arithmetic  20.5 us (6%)
  local copies, waits for them, and re-layouts  19 us (5%)
  between operations  5.94 us (2%)
    psum x3, blocking collectives, global_dot(): return lax.psum(jnp.sum(weights * first * second), ('gx', 'gy'))  119 us
    ppermute x24, starting transfers between devices, extended(): lax.ppermute(lax.slice_in_dim(block, block.shape[dim] - width, None, axis...  91.6 us
    ppermute x24, starting transfers between devices, extended(): lax.ppermute(lax.slice_in_dim(block, 0, width, axis=dim), axis, backward)  54.5 us
    ppermute x24, waiting for transfers between devices, extended(): lax.ppermute(lax.slice_in_dim(block, 0, width, axis=dim), axis, backward)  30.3 us
    dot_general x2, local copies, waits for them, and re-layouts, apply_operators(): jnp.einsum('aylm,aymn->ayln', rounded, dual_ops, preferred_element_type=j...  12.1 us
  transfers between devices with their start and end apart: 48, of which 11 were waited for; matrix products, arithmetic and copies ran while one was open for 4% of the time, Pallas kernels for 0%

commit v1 on v0

v1 whole, which is shorter than its diff:
```python
import jax
import jax.numpy as jnp
from jax import lax
from jax.sharding import PartitionSpec as P

SIGNS = (-1.0, 1.0, -1.0, 1.0)
HIGHEST = lax.Precision.HIGHEST
AXES = ("gx", "gy")
SWEEPS = 2


def exchange(faces):
    parts = []
    for axis, low, high in (("gx", 0, 1), ("gy", 2, 3)):
        count = lax.axis_size(axis)
        forward = [(i, i + 1) for i in range(count - 1)]
        backward = [(i + 1, i) for i in range(count - 1)]
        parts.append(lax.ppermute(faces[high], axis, forward))
        parts.append(lax.ppermute(faces[low], axis, backward))
    return jnp.stack(parts)


def gather(values):
    count = lax.axis_size("gx") * lax.axis_size("gy")
    copies = jnp.broadcast_to(values, (count,) + values.shape)
    return lax.all_to_all(copies, AXES, 0, 0, tiled=True)


def doubling_gather(values):
    rows = values[None]
    for axis in ("gy", "gx"):
        count, unit = lax.axis_size(axis), rows.shape[0]
        held = 1
        while held < count:
            step = min(held, count - held)
            pairs = [(i, (i - held) % count) for i in range(count)]
            rows = jnp.concatenate([rows, lax.ppermute(rows[: step * unit], axis, pairs)])
            held += step
    return rows


def invert(matrix):
    order = matrix.shape[-1]
    inverse = jnp.eye(order, dtype=jnp.float32)
    reduced = matrix
    for pivot in range(order):
        unit = (jnp.arange(order) == pivot).astype(jnp.float32)[:, None]
        value = reduced[pivot : pivot + 1, pivot : pivot + 1]
        row = reduced[pivot : pivot + 1, :] / value
        inverse_row = inverse[pivot : pivot + 1, :] / value
        column = reduced[:, pivot : pivot + 1] - unit
        reduced = reduced - column * row
        inverse = inverse - column * inverse_row
    return inverse


def shifted(field, face, row):
    return jnp.roll(field, (row, -row, 1, -1)[face], axis=-1)


def body(dual_ops, mode_traces, primal_trace, mode_loads, face_maps, face_live):
    nx, ny = lax.axis_size("gx"), lax.axis_size("gy")
    ix, iy = lax.axis_index("gx"), lax.axis_index("gy")
    ops, traces, primal, loads = dual_ops[0, 0], mode_traces[0, 0], primal_trace[0, 0], mode_loads[0, 0]
    maps, counts = face_maps[0, 0], face_live[0, 0]
    modes, size = traces.shape[1:]
    cases = loads.shape[1]
    signs = jnp.array(SIGNS, jnp.float32)[:, None, None]
    slots = lax.broadcasted_iota(jnp.int32, (4, 1, size), 2)
    live = (slots < counts[:, None, None]).astype(jnp.float32)
    signed_live = live * signs
    table = (maps[..., None] == lax.broadcasted_iota(jnp.int32, (4, size, size), 2)).astype(jnp.float32)
    boundary = jnp.stack([ix == 0, ix == nx - 1, iy == 0, iy == ny - 1])
    weights = jnp.where(boundary, 1.0, 0.5).astype(jnp.float32)[:, None, None]

    def to_local(field):
        picked = jnp.einsum("fkc,flc->lfk", table, field * signs, precision=HIGHEST)
        return picked.reshape(cases, 4 * size)

    def to_canonical(local):
        return jnp.einsum("fkc,lfk->flc", table, local.reshape(cases, 4, size), precision=HIGHEST)

    def apply(local):
        return jnp.einsum("lm,mn->ln", local.astype(jnp.bfloat16), ops, preferred_element_type=jnp.float32)

    live_traces = traces * live
    next_traces = exchange(traces)
    inverse = invert(jnp.einsum("fjc,fkc->jk", live_traces, traces, precision=HIGHEST))
    coupling = jnp.einsum("fjc,fkc->fjk", live_traces, next_traces, precision=HIGHEST)
    coupling = jnp.einsum("ij,fjk->fik", inverse, coupling, precision=HIGHEST)
    first = jnp.einsum("jk,kl->jl", inverse, loads, precision=HIGHEST)
    everyone = gather(jnp.concatenate([inverse.reshape(-1), coupling.reshape(-1), first.reshape(-1)])).T
    square = modes * modes
    all_inverse = everyone[:square].reshape(modes, modes, -1)
    all_coupling = everyone[square : 5 * square].reshape(4, modes, modes, 1, -1)
    all_first = everyone[5 * square :].reshape(modes, cases, -1)
    spot = ix * ny + iy

    def pick(field, face):
        moved = shifted(field, face, ny) if face >= 0 else field
        return lax.dynamic_slice_in_dim(moved, spot, 1, axis=2)[..., 0]

    near_inverse = jnp.stack([pick(all_inverse, face) for face in range(4)])
    own_rows = jnp.einsum("ij,fjc->fic", inverse, live_traces, precision=HIGHEST)
    next_rows = jnp.einsum("fij,fjc->fic", near_inverse, next_traces * live, precision=HIGHEST)
    rows = jnp.concatenate([own_rows, next_rows], axis=1)
    lift_rows = jnp.concatenate([traces * signed_live, -next_traces * signed_live], axis=1)

    def coarse_lift(start):
        field = start
        for sweep in range(SWEEPS):
            update = start
            for face in range(4):
                near = shifted(field, face, ny)
                for k in range(modes):
                    update = update + all_coupling[face, :, k] * near[k][None]
            field = update
        own = jnp.broadcast_to(pick(field, -1), (4, modes, cases))
        near = jnp.stack([pick(field, face) for face in range(4)])
        return jnp.einsum("fjc,fjl->flc", lift_rows, jnp.concatenate([own, near], axis=1), precision=HIGHEST)

    def jump_and_lift(canonical, scalars):
        parts = jnp.einsum("fjc,flc->fjl", rows, canonical, precision=HIGHEST)
        mine = jnp.sum(parts[:, :modes], axis=0)
        sent = jnp.concatenate([mine.reshape(-1), parts[:, modes:].reshape(-1)] + [s.reshape(1) for s in scalars])
        received = gather(sent).T
        field = signed_live * (canonical - exchange(canonical))
        block = modes * cases
        start = received[:block]
        for face in range(4):
            across = received[(1 + (face ^ 1)) * block : (2 + (face ^ 1)) * block]
            start = start - shifted(across, face, ny)
        lifted = coarse_lift(start.reshape(modes, cases, -1))
        sums = jnp.sum(received[5 * block :], axis=1)
        return field, lifted, sums

    multipliers = coarse_lift(all_first)
    residual, lifted, _ = jump_and_lift(to_canonical(primal - apply(to_local(multipliers))), [])
    direction = residual - lifted
    local_direction = to_local(direction)
    image_local = apply(local_direction)
    image, lifted, sums = jump_and_lift(
        to_canonical(image_local),
        [jnp.sum(weights * residual * direction), jnp.sum(local_direction * image_local)],
    )
    gamma, curvature = sums[0], sums[1]
    alpha = gamma / curvature
    multipliers = multipliers + alpha * direction
    residual = residual - alpha * image
    projected = direction - alpha * (image - lifted)
    local_projected = to_local(projected)
    fresh_local = apply(local_projected)
    fresh_canonical = to_canonical(fresh_local)
    sums = doubling_gather(jnp.stack([
        jnp.sum(weights * residual * projected),
        jnp.sum(local_projected * fresh_local),
        jnp.sum(weights * projected * image) + jnp.sum(local_direction * fresh_local),
    ])).sum(axis=0)
    fresh_image = signed_live * (fresh_canonical - exchange(fresh_canonical))
    beta = sums[0] / gamma
    alpha = sums[0] / (sums[1] + beta * sums[2] + beta * beta * curvature)
    multipliers = multipliers + alpha * (projected + beta * direction)
    residual = residual - alpha * (fresh_image + beta * image)
    return multipliers[None, None], residual[None, None]


def solution(mesh):
    in_specs = (
        P("gx", "gy", None, None),
        P("gx", "gy", None, None, None),
        P("gx", "gy", None, None),
        P("gx", "gy", None, None),
        P("gx", "gy", None, None),
        P("gx", "gy", None),
    )
    out_specs = (P("gx", "gy", None, None, None), P("gx", "gy", None, None, None))
    return jax.shard_map(body, mesh=mesh, in_specs=in_specs, out_specs=out_specs, check_vma=False)
```

time: 367 us -> 188 us (0.51)
  the two profiles are of different devices: /device:TPU:5 before, /device:TPU:30 now
where the time goes in v1:
time: 188 us; the launch traced here: 186 us
  starting transfers between devices  68.5 us (36%)
  local copies, waits for them, and re-layouts  32.9 us (18%)
  other arithmetic  32.1 us (17%)
  matrix products  24.4 us (13%)
  waiting for transfers between devices  19.1 us (10%)
  between operations  8.91 us (5%)
    ppermute x8, starting transfers between devices, exchange(): parts.append(lax.ppermute(faces[low], axis, backward))  34.2 us
    all_to_all x3, starting transfers between devices, gather(): return lax.all_to_all(copies, AXES, 0, 0, tiled=True)  19.6 us
    ppermute x5, waiting for transfers between devices, doubling_gather(): lax.ppermute(rows[:step * unit], axis, pairs)  17.3 us
    ppermute x8, starting transfers between devices, exchange(): parts.append(lax.ppermute(faces[high], axis, forward))  12.8 us
    slice x45, local copies, waits for them, and re-layouts, shifted(): return jnp.roll(field, (row, -row, 1, -1)[face], axis=-1)  8.42 us
    dynamic_slice x14, other arithmetic, pick(): return lax.dynamic_slice_in_dim(moved, spot, 1, axis=2)[..., 0]  5.52 us
    mul x24, other arithmetic, coarse_lift(): update = update + all_coupling[face, :, k] * near[k][None]  5.3 us
    dot_general x3, matrix products, to_local(): picked = jnp.einsum('fkc,flc->lfk', table, field * signs, precision=HIGHEST)  5.23 us
  transfers between devices with their start and end apart: 24, of which 5 were waited for; matrix products, arithmetic and copies ran while one was open for 22% of the time, Pallas kernels for 0%

profile of v1, /device:TPU:30, one launch (start us, length us, event | category | flops | bytes accessed | tf_op | source)
XLA Modules:
  0.0 186.0 jit_solution(8560147679000972118)
XLA Ops:
  2.9 4.5 %collective-permute-start.1 = (f32[6,300]{1,0:T(8,128)S(1)}, f32[6,300]{1,0:T(8,128)S(1)}, u32[]{:S(2)}, u32[]{:S(2)}) collective-permute-start(f32[6,300]{1,0:T(8,128)S(1)} %get-tuple-element.279), channel_id=1, source_target_pairs={{4,0},{8,4},{12,8},{16,12},{20,16},{24,20},{28,24},{5,1},{9,5},{13... | collective-permute-start | bytes 21608 | tf_op jit(solution)/shard_map/ppermute | solution.py:19
  7.4 1.9 %collective-permute-start.2 = (f32[6,300]{1,0:T(8,128)S(1)}, f32[6,300]{1,0:T(8,128)S(1)}, u32[]{:S(2)}, u32[]{:S(2)}) collective-permute-start(f32[6,300]{1,0:T(8,128)S(1)} %get-tuple-element.278), channel_id=1, source_target_pairs={{0,1},{1,2},{2,3},{4,5},{5,6},{6,7},{8,9},{9,10},{10,11},{12,13},{... | collective-permute-start | bytes 21608 | tf_op jit(solution)/shard_map/ppermute | solution.py:18
  9.4 3.6 %collective-permute-start.3 = (f32[6,300]{1,0:T(8,128)S(1)}, f32[6,300]{1,0:T(8,128)S(1)}, u32[]{:S(2)}, u32[]{:S(2)}) collective-permute-start(f32[6,300]{1,0:T(8,128)S(1)} %get-tuple-element.280), channel_id=1, source_target_pairs={{1,0},{2,1},{3,2},{5,4},{6,5},{7,6},{9,8},{10,9},{11,10},{13,12},{... | collective-permute-start | bytes 21608 | tf_op jit(solution)/shard_map/ppermute | solution.py:19
  33.5 5.8 %all-to-all-start = ((f32[32,1,276]{2,1,0:T(1,128)}), f32[32,1,276]{2,1,0:T(1,128)S(1)}, u32[]{:S(2)}, u32[]{:S(2)}) async-start(f32[32,1,276]{2,1,0:T(1,128)} %broadcast_in_dim.43), calls=%async_computation | async-start | bytes 98304 | tf_op jit(solution)/shard_map/all_to_all | solution.py:26
  40.1 1.8 all-to-all-done
  57.5 1.4 fusion.6
  59.7 1.7 fusion.13
  67.8 7.9 %all-to-all-start.1 = ((f32[32,1,480]{2,1,0:T(1,128)}), f32[32,1,480]{2,1,0:T(1,128)}, u32[]{:S(2)}, u32[]{:S(2)}) async-start(f32[32,1,480]{2,1,0:T(1,128)} %broadcast_in_dim.45), calls=%async_computation.1 | async-start | bytes 131072 | tf_op jit(solution)/shard_map/all_to_all | solution.py:26
  77.7 5.1 %collective-permute-start.5 = (f32[16,300]{1,0:T(8,128)}, f32[16,300]{1,0:T(8,128)}, u32[]{:S(2)}, u32[]{:S(2)}) collective-permute-start(f32[16,300]{1,0:T(8,128)} %get-tuple-element.129), channel_id=1, source_target_pairs={{4,0},{8,4},{12,8},{16,12},{20,16},{24,20},{28,24},{5,1},{9,5},{13... | collective-permute-start | bytes 57608 | tf_op jit(solution)/shard_map/ppermute | solution.py:19
  82.8 1.9 %collective-permute-start.6 = (f32[16,300]{1,0:T(8,128)}, f32[16,300]{1,0:T(8,128)}, u32[]{:S(2)}, u32[]{:S(2)}) collective-permute-start(f32[16,300]{1,0:T(8,128)} %get-tuple-element.128), channel_id=1, source_target_pairs={{0,1},{1,2},{2,3},{4,5},{5,6},{6,7},{8,9},{9,10},{10,11},{12,13},{... | collective-permute-start | bytes 57608 | tf_op jit(solution)/shard_map/ppermute | solution.py:18
  84.7 3.6 %collective-permute-start.7 = (f32[16,300]{1,0:T(8,128)}, f32[16,300]{1,0:T(8,128)}, u32[]{:S(2)}, u32[]{:S(2)}) collective-permute-start(f32[16,300]{1,0:T(8,128)} %get-tuple-element.127), channel_id=1, source_target_pairs={{1,0},{2,1},{3,2},{5,4},{6,5},{7,6},{9,8},{10,9},{11,10},{13,12},{... | collective-permute-start | bytes 57608 | tf_op jit(solution)/shard_map/ppermute | solution.py:19
  93.3 1.7 multiply_reduce_fusion.2
  95.1 2.4 %fusion.444 = (bf16[16,4,300]{2,0,1:T(8,128)(2,1)}, f32[16,4,300]{2,0,1:T(8,128)S(1)}) fusion(s32[4,300]{1,0:T(4,128)} %bitcast.734, f32[4,16,300]{2,1,0:T(8,128)S(1)} %get-tuple-element.315, f32[4]{0:T(128)} %constant.37.clone), kind=kOutput, calls=%fused_computation.840 | convolution fusion | flops 69518400 | bytes 196816 | tf_op jit(solution)/shard_map/fkc,flc->lfk/dot_general | solution.py:77
  100.6 1.7 fusion.11
  104.7 5.9 %all-to-all-start.2 = ((f32[32,1,482]{2,1,0:T(1,128)}), f32[32,1,482]{2,1,0:T(1,128)}, u32[]{:S(2)}, u32[]{:S(2)}) async-start(f32[32,1,482]{2,1,0:T(1,128)} %broadcast_in_dim.49), calls=%async_computation.2 | async-start | bytes 131072 | tf_op jit(solution)/shard_map/all_to_all | solution.py:26
  112.5 5.2 %collective-permute-start.9 = (f32[16,300]{1,0:T(8,128)}, f32[16,300]{1,0:T(8,128)}, u32[]{:S(2)}, u32[]{:S(2)}) collective-permute-start(f32[16,300]{1,0:T(8,128)} %get-tuple-element.77), channel_id=1, source_target_pairs={{4,0},{8,4},{12,8},{16,12},{20,16},{24,20},{28,24},{5,1},{9,5},{13... | collective-permute-start | bytes 57608 | tf_op jit(solution)/shard_map/ppermute | solution.py:19
  117.7 1.9 %collective-permute-start.10 = (f32[16,300]{1,0:T(8,128)}, f32[16,300]{1,0:T(8,128)}, u32[]{:S(2)}, u32[]{:S(2)}) collective-permute-start(f32[16,300]{1,0:T(8,128)} %get-tuple-element.76), channel_id=1, source_target_pairs={{0,1},{1,2},{2,3},{4,5},{5,6},{6,7},{8,9},{9,10},{10,11},{12,13},{... | collective-permute-start | bytes 57608 | tf_op jit(solution)/shard_map/ppermute | solution.py:18
  119.6 3.8 %collective-permute-start.11 = (f32[16,300]{1,0:T(8,128)}, f32[16,300]{1,0:T(8,128)}, u32[]{:S(2)}, u32[]{:S(2)}) collective-permute-start(f32[16,300]{1,0:T(8,128)} %get-tuple-element.75), channel_id=1, source_target_pairs={{1,0},{2,1},{3,2},{5,4},{6,5},{7,6},{9,8},{10,9},{11,10},{13,12},{... | collective-permute-start | bytes 57608 | tf_op jit(solution)/shard_map/ppermute | solution.py:19
  131.6 1.9 %multiply_reduce_fusion.1 = (f32[]{:T(128)}, f32[]{:T(128)}, f32[4,16,300]{2,1,0:T(8,128)S(1)}) fusion(f32[]{:T(128)S(6)} %div.122, f32[4]{0:T(128)} %add_select_fusion, f32[4,16,300]{2,1,0:T(8,128)} %copy-done.5, f32[4,6,300]{2,1,0:T(8,128)} %copy-done.3, f32[4,6,300]{2,1,0:T(8,128)} %copy-done.2, f32[4,6,16]{1,2,0:T(8,128)S(1)} %copy.199, ...), kind=kOutput, calls=%fused_computation.49 | convolution fusion | flops 3183166 | bytes 526300 | tf_op jit(solution)/shard_map/fjc,fjl->flc/dot_general | solution.py:120
  133.5 1.8 fusion.445
  136.2 2.1 %multiply_reduce_fusion.4 = (f32[]{:T(128)}, f32[]{:T(128)}, f32[16,1200]{1,0:T(8,128)S(1)}) fusion(f32[16,1200]{1,0:T(8,128)S(1)} %reshape.309, f32[16,1200]{1,0:T(8,128)} %copy-done.1, bf16[16,1200]{1,0:T(8,128)(2,1)} %convert_element_type.111, bf16[1,1,1200,1200]{3,2,1,0:T(8,128)(2,1)S(1)} %copy-done), kind=kOutput, calls=%fused_computation.55 | convolution fusion | flops 46156800 | bytes 3148808 | tf_op jit(solution)/shard_map/lm,mn->ln/dot_general | solution.py:84
  141.7 1.7 fusion.9
  145.3 4.5 %collective-permute-start.18 = (f32[16,300]{1,0:T(8,128)}, f32[16,300]{1,0:T(8,128)S(1)}, u32[]{:S(2)}, u32[]{:S(2)}) collective-permute-start(f32[16,300]{1,0:T(8,128)} %get-tuple-element.25), channel_id=1, source_target_pairs={{4,0},{8,4},{12,8},{16,12},{20,16},{24,20},{28,24},{5,1},{9,5},{13... | collective-permute-start | bytes 57608 | tf_op jit(solution)/shard_map/ppermute | solution.py:19
  149.9 1.9 %collective-permute-start.19 = (f32[16,300]{1,0:T(8,128)}, f32[16,300]{1,0:T(8,128)}, u32[]{:S(2)}, u32[]{:S(2)}) collective-permute-start(f32[16,300]{1,0:T(8,128)} %get-tuple-element.24), channel_id=1, source_target_pairs={{0,1},{1,2},{2,3},{4,5},{5,6},{6,7},{8,9},{9,10},{10,11},{12,13},{... | collective-permute-start | bytes 57608 | tf_op jit(solution)/shard_map/ppermute | solution.py:18
  151.8 3.6 %collective-permute-start.20 = (f32[16,300]{1,0:T(8,128)}, f32[16,300]{1,0:T(8,128)}, u32[]{:S(2)}, u32[]{:S(2)}) collective-permute-start(f32[16,300]{1,0:T(8,128)} %get-tuple-element.23), channel_id=1, source_target_pairs={{1,0},{2,1},{3,2},{5,4},{6,5},{7,6},{9,8},{10,9},{11,10},{13,12},{... | collective-permute-start | bytes 57608 | tf_op jit(solution)/shard_map/ppermute | solution.py:19
  155.7 3.5 %collective-permute-done.13 = f32[2,3]{1,0:T(2,128)S(1)} collective-permute-done((f32[2,3]{1,0:T(2,128)S(1)}, f32[2,3]{1,0:T(2,128)S(1)}, u32[]{:S(2)}, u32[]{:S(2)}) %collective-permute-start.13) | collective-permute-done | bytes 56 | tf_op jit(solution)/shard_map/ppermute | solution.py:37
  159.1 1.8 collective-permute-start.14
  161.0 4.5 %collective-permute-done.14 = f32[4,3]{1,0:T(4,128)S(1)} collective-permute-done((f32[4,3]{1,0:T(4,128)S(1)}, f32[4,3]{1,0:T(4,128)S(1)}, u32[]{:S(2)}, u32[]{:S(2)}) %collective-permute-start.14) | collective-permute-done | bytes 80 | tf_op jit(solution)/shard_map/ppermute | solution.py:37
  166.2 4.7 %collective-permute-done.15 = f32[8,3]{1,0:T(8,128)S(1)} collective-permute-done((f32[8,3]{1,0:T(8,128)S(1)}, f32[8,3]{1,0:T(8,128)S(1)}, u32[]{:S(2)}, u32[]{:S(2)}) %collective-permute-start.15) | collective-permute-done | bytes 128 | tf_op jit(solution)/shard_map/ppermute | solution.py:37
  172.4 4.6 %collective-permute-done.16 = f32[16,3]{0,1:T(4,128)S(1)} collective-permute-done((f32[16,3]{0,1:T(4,128)}, f32[16,3]{0,1:T(4,128)S(1)}, u32[]{:S(2)}, u32[]{:S(2)}) %collective-permute-start.16) | collective-permute-done | bytes 224 | tf_op jit(solution)/shard_map/ppermute | solution.py:37
  182.7 1.6 add_bitcast_fusion
  184.4 1.6 fusion.33
  (417 shorter events, 75.1 us)
Async XLA Ops:
  0.6 56.8 %copy-start = (bf16[1,1,1200,1200]{3,2,1,0:T(8,128)(2,1)S(1)}, bf16[1,1,1200,1200]{3,2,1,0:T(8,128)(2,1)}, u32[]{:S(2)}) copy-start(bf16[1,1,1200,1200]{3,2,1,0:T(8,128)(2,1)} %param.7) | copy-start | bytes 8640004
  1.6 29.7 %collective-permute-start = (f32[6,300]{1,0:T(8,128)S(1)}, f32[6,300]{1,0:T(8,128)S(1)}, u32[]{:S(2)}, u32[]{:S(2)}) collective-permute-start(f32[6,300]{1,0:T(8,128)S(1)} %get-tuple-element.277), channel_id=1, source_target_pairs={{0,4},{4,8},{8,12},{12,16},{16,20},{20,24},{24,28},{1,5},{5,9},{9,... | collective-permute-start | bytes 21608 | tf_op jit(solution)/shard_map/ppermute | solution.py:18
  2.9 28.4 %collective-permute-start.1 = (f32[6,300]{1,0:T(8,128)S(1)}, f32[6,300]{1,0:T(8,128)S(1)}, u32[]{:S(2)}, u32[]{:S(2)}) collective-permute-start(f32[6,300]{1,0:T(8,128)S(1)} %get-tuple-element.279), channel_id=1, source_target_pairs={{4,0},{8,4},{12,8},{16,12},{20,16},{24,20},{28,24},{5,1},{9,5},{13... | collective-permute-start | bytes 21608 | tf_op jit(solution)/shard_map/ppermute | solution.py:19
  7.4 23.9 %collective-permute-start.2 = (f32[6,300]{1,0:T(8,128)S(1)}, f32[6,300]{1,0:T(8,128)S(1)}, u32[]{:S(2)}, u32[]{:S(2)}) collective-permute-start(f32[6,300]{1,0:T(8,128)S(1)} %get-tuple-element.278), channel_id=1, source_target_pairs={{0,1},{1,2},{2,3},{4,5},{5,6},{6,7},{8,9},{9,10},{10,11},{12,13},{... | collective-permute-start | bytes 21608 | tf_op jit(solution)/shard_map/ppermute | solution.py:18
  9.4 22.0 %collective-permute-start.3 = (f32[6,300]{1,0:T(8,128)S(1)}, f32[6,300]{1,0:T(8,128)S(1)}, u32[]{:S(2)}, u32[]{:S(2)}) collective-permute-start(f32[6,300]{1,0:T(8,128)S(1)} %get-tuple-element.280), channel_id=1, source_target_pairs={{1,0},{2,1},{3,2},{5,4},{6,5},{7,6},{9,8},{10,9},{11,10},{13,12},{... | collective-permute-start | bytes 21608 | tf_op jit(solution)/shard_map/ppermute | solution.py:19
  13.8 17.6 %copy-start.59 = (f32[4,300]{1,0:T(4,128)}, f32[4,300]{1,0:T(4,128)S(1)}, u32[]{:S(2)}) copy-start(f32[4,300]{1,0:T(4,128)S(1)} %fusion.365) | copy-start | bytes 14404
  31.3 14.2 %copy-start.63 = (f32[6,300]{1,0:T(8,128)}, f32[6,300]{1,0:T(8,128)S(1)}, u32[]{:S(2)}) copy-start(f32[6,300]{1,0:T(8,128)S(1)} %collective-permute-done.1) | copy-start | bytes 21604
  33.5 8.5 %all-to-all-start = ((f32[32,1,276]{2,1,0:T(1,128)}), f32[32,1,276]{2,1,0:T(1,128)S(1)}, u32[]{:S(2)}, u32[]{:S(2)}) async-start(f32[32,1,276]{2,1,0:T(1,128)} %broadcast_in_dim.43), calls=%async_computation | async-start | bytes 98304 | tf_op jit(solution)/shard_map/all_to_all | solution.py:26
  40.1 21.3 %copy-start.3 = (f32[4,6,300]{2,1,0:T(8,128)}, f32[4,6,300]{2,1,0:T(8,128)S(1)}, u32[]{:S(2)}) copy-start(f32[4,6,300]{2,1,0:T(8,128)S(1)} %get-tuple-element.294) | copy-start | bytes 86404
  40.1 53.2 %copy-start.2 = (f32[4,6,300]{2,1,0:T(8,128)}, f32[4,6,300]{2,1,0:T(8,128)S(1)}, u32[]{:S(2)}) copy-start(f32[4,6,300]{2,1,0:T(8,128)S(1)} %get-tuple-element.293) | copy-start | bytes 86404
  49.3 42.3 %copy-start.8 = (f32[1,6,1,1,32]{4,1,2,0,3:T(8,128)}, f32[1,6,1,1,32]{4,1,2,0,3:T(8,128)S(1)}, u32[]{:S(2)}) copy-start(f32[1,6,1,1,32]{4,1,2,0,3:T(8,128)S(1)} %copy.299) | copy-start | bytes 2308
  67.8 20.6 %all-to-all-start.1 = ((f32[32,1,480]{2,1,0:T(1,128)}), f32[32,1,480]{2,1,0:T(1,128)}, u32[]{:S(2)}, u32[]{:S(2)}) async-start(f32[32,1,480]{2,1,0:T(1,128)} %broadcast_in_dim.45), calls=%async_computation.1 | async-start | bytes 131072 | tf_op jit(solution)/shard_map/all_to_all | solution.py:26
  76.4 16.9 %collective-permute-start.4 = (f32[16,300]{1,0:T(8,128)}, f32[16,300]{1,0:T(8,128)}, u32[]{:S(2)}, u32[]{:S(2)}) collective-permute-start(f32[16,300]{1,0:T(8,128)} %get-tuple-element.126), channel_id=1, source_target_pairs={{0,4},{4,8},{8,12},{12,16},{16,20},{20,24},{24,28},{1,5},{5,9},{9,... | collective-permute-start | bytes 57608 | tf_op jit(solution)/shard_map/ppermute | solution.py:18
  77.7 15.6 %collective-permute-start.5 = (f32[16,300]{1,0:T(8,128)}, f32[16,300]{1,0:T(8,128)}, u32[]{:S(2)}, u32[]{:S(2)}) collective-permute-start(f32[16,300]{1,0:T(8,128)} %get-tuple-element.129), channel_id=1, source_target_pairs={{4,0},{8,4},{12,8},{16,12},{20,16},{24,20},{28,24},{5,1},{9,5},{13... | collective-permute-start | bytes 57608 | tf_op jit(solution)/shard_map/ppermute | solution.py:19
  82.8 10.5 %collective-permute-start.6 = (f32[16,300]{1,0:T(8,128)}, f32[16,300]{1,0:T(8,128)}, u32[]{:S(2)}, u32[]{:S(2)}) collective-permute-start(f32[16,300]{1,0:T(8,128)} %get-tuple-element.128), channel_id=1, source_target_pairs={{0,1},{1,2},{2,3},{4,5},{5,6},{6,7},{8,9},{9,10},{10,11},{12,13},{... | collective-permute-start | bytes 57608 | tf_op jit(solution)/shard_map/ppermute | solution.py:18
  84.7 8.6 %collective-permute-start.7 = (f32[16,300]{1,0:T(8,128)}, f32[16,300]{1,0:T(8,128)}, u32[]{:S(2)}, u32[]{:S(2)}) collective-permute-start(f32[16,300]{1,0:T(8,128)} %get-tuple-element.127), channel_id=1, source_target_pairs={{1,0},{2,1},{3,2},{5,4},{6,5},{7,6},{9,8},{10,9},{11,10},{13,12},{... | collective-permute-start | bytes 57608 | tf_op jit(solution)/shard_map/ppermute | solution.py:19
  104.7 18.7 %all-to-all-start.2 = ((f32[32,1,482]{2,1,0:T(1,128)}), f32[32,1,482]{2,1,0:T(1,128)}, u32[]{:S(2)}, u32[]{:S(2)}) async-start(f32[32,1,482]{2,1,0:T(1,128)} %broadcast_in_dim.49), calls=%async_computation.2 | async-start | bytes 131072 | tf_op jit(solution)/shard_map/all_to_all | solution.py:26
  111.3 20.2 %collective-permute-start.8 = (f32[16,300]{1,0:T(8,128)}, f32[16,300]{1,0:T(8,128)}, u32[]{:S(2)}, u32[]{:S(2)}) collective-permute-start(f32[16,300]{1,0:T(8,128)} %get-tuple-element.74), channel_id=1, source_target_pairs={{0,4},{4,8},{8,12},{12,16},{16,20},{20,24},{24,28},{1,5},{5,9},{9,... | collective-permute-start | bytes 57608 | tf_op jit(solution)/shard_map/ppermute | solution.py:18
  112.5 19.0 %collective-permute-start.9 = (f32[16,300]{1,0:T(8,128)}, f32[16,300]{1,0:T(8,128)}, u32[]{:S(2)}, u32[]{:S(2)}) collective-permute-start(f32[16,300]{1,0:T(8,128)} %get-tuple-element.77), channel_id=1, source_target_pairs={{4,0},{8,4},{12,8},{16,12},{20,16},{24,20},{28,24},{5,1},{9,5},{13... | collective-permute-start | bytes 57608 | tf_op jit(solution)/shard_map/ppermute | solution.py:19
  117.7 13.8 %collective-permute-start.10 = (f32[16,300]{1,0:T(8,128)}, f32[16,300]{1,0:T(8,128)}, u32[]{:S(2)}, u32[]{:S(2)}) collective-permute-start(f32[16,300]{1,0:T(8,128)} %get-tuple-element.76), channel_id=1, source_target_pairs={{0,1},{1,2},{2,3},{4,5},{5,6},{6,7},{8,9},{9,10},{10,11},{12,13},{... | collective-permute-start | bytes 57608 | tf_op jit(solution)/shard_map/ppermute | solution.py:18
  119.6 11.9 %collective-permute-start.11 = (f32[16,300]{1,0:T(8,128)}, f32[16,300]{1,0:T(8,128)}, u32[]{:S(2)}, u32[]{:S(2)}) collective-permute-start(f32[16,300]{1,0:T(8,128)} %get-tuple-element.75), channel_id=1, source_target_pairs={{1,0},{2,1},{3,2},{5,4},{6,5},{7,6},{9,8},{10,9},{11,10},{13,12},{... | collective-permute-start | bytes 57608 | tf_op jit(solution)/shard_map/ppermute | solution.py:19
  136.2 46.5 %copy-start.6 = (f32[4,16,300]{2,1,0:T(8,128)S(1)}, f32[4,16,300]{2,1,0:T(8,128)}, u32[]{:S(2)}) copy-start(f32[4,16,300]{2,1,0:T(8,128)} %copy-done.5) | copy-start | bytes 230404
  136.2 48.1 %copy-start.55 = (f32[4,300]{1,0:T(4,128)S(1)}, f32[4,300]{1,0:T(4,128)}, u32[]{:S(2)}) copy-start(f32[4,300]{1,0:T(4,128)} %copy-done.54) | copy-start | bytes 14404
  140.8 14.6 %collective-permute-start.12 = (f32[1,3]{1,0:T(1,128)S(1)}, f32[1,3]{1,0:T(1,128)S(1)}, u32[]{:S(2)}, u32[]{:S(2)}) collective-permute-start(f32[1,3]{1,0:T(1,128)S(1)} %fusion.453), channel_id=1, source_target_pairs={{0,3},{1,0},{2,1},{3,2},{4,7},{5,4},{6,5},{7,6},{8,11},{9,8},{10,9... | collective-permute-start | bytes 44 | tf_op jit(solution)/shard_map/ppermute | solution.py:37
  144.0 40.3 %collective-permute-start.17 = (f32[16,300]{1,0:T(8,128)}, f32[16,300]{1,0:T(8,128)S(1)}, u32[]{:S(2)}, u32[]{:S(2)}) collective-permute-start(f32[16,300]{1,0:T(8,128)} %get-tuple-element.22), channel_id=1, source_target_pairs={{0,4},{4,8},{8,12},{12,16},{16,20},{20,24},{24,28},{1,5},{5,9},{9,... | collective-permute-start | bytes 57608 | tf_op jit(solution)/shard_map/ppermute | solution.py:18
  145.3 39.0 %collective-permute-start.18 = (f32[16,300]{1,0:T(8,128)}, f32[16,300]{1,0:T(8,128)S(1)}, u32[]{:S(2)}, u32[]{:S(2)}) collective-permute-start(f32[16,300]{1,0:T(8,128)} %get-tuple-element.25), channel_id=1, source_target_pairs={{4,0},{8,4},{12,8},{16,12},{20,16},{24,20},{28,24},{5,1},{9,5},{13... | collective-permute-start | bytes 57608 | tf_op jit(solution)/shard_map/ppermute | solution.py:19
  149.9 34.5 %collective-permute-start.19 = (f32[16,300]{1,0:T(8,128)}, f32[16,300]{1,0:T(8,128)}, u32[]{:S(2)}, u32[]{:S(2)}) collective-permute-start(f32[16,300]{1,0:T(8,128)} %get-tuple-element.24), channel_id=1, source_target_pairs={{0,1},{1,2},{2,3},{4,5},{5,6},{6,7},{8,9},{9,10},{10,11},{12,13},{... | collective-permute-start | bytes 57608 | tf_op jit(solution)/shard_map/ppermute | solution.py:18
  151.8 32.5 %collective-permute-start.20 = (f32[16,300]{1,0:T(8,128)}, f32[16,300]{1,0:T(8,128)}, u32[]{:S(2)}, u32[]{:S(2)}) collective-permute-start(f32[16,300]{1,0:T(8,128)} %get-tuple-element.23), channel_id=1, source_target_pairs={{1,0},{2,1},{3,2},{5,4},{6,5},{7,6},{9,8},{10,9},{11,10},{13,12},{... | collective-permute-start | bytes 57608 | tf_op jit(solution)/shard_map/ppermute | solution.py:19
  155.5 3.6 %collective-permute-start.13 = (f32[2,3]{1,0:T(2,128)S(1)}, f32[2,3]{1,0:T(2,128)S(1)}, u32[]{:S(2)}, u32[]{:S(2)}) collective-permute-start(f32[2,3]{1,0:T(2,128)S(1)} %pad_maximum_fusion.42), channel_id=1, source_target_pairs={{0,2},{1,3},{2,0},{3,1},{4,6},{5,7},{6,4},{7,5},{8,10},{9,11},{10,... | collective-permute-start | bytes 80 | tf_op jit(solution)/shard_map/ppermute | solution.py:37
  159.1 6.3 %collective-permute-start.14 = (f32[4,3]{1,0:T(4,128)S(1)}, f32[4,3]{1,0:T(4,128)S(1)}, u32[]{:S(2)}, u32[]{:S(2)}) collective-permute-start(f32[4,3]{1,0:T(4,128)S(1)} %pad_maximum_fusion.41), channel_id=1, source_target_pairs={{0,28},{4,0},{8,4},{12,8},{16,12},{20,16},{24,20},{28,24},{1,29},{... | collective-permute-start | bytes 152 | tf_op jit(solution)/shard_map/ppermute | solution.py:37
  165.5 5.5 %collective-permute-start.15 = (f32[8,3]{1,0:T(8,128)S(1)}, f32[8,3]{1,0:T(8,128)S(1)}, u32[]{:S(2)}, u32[]{:S(2)}) collective-permute-start(f32[8,3]{1,0:T(8,128)S(1)} %pad_maximum_fusion.37), channel_id=1, source_target_pairs={{0,24},{4,28},{8,0},{12,4},{16,8},{20,12},{24,16},{28,20},{1,25},{... | collective-permute-start | bytes 296 | tf_op jit(solution)/shard_map/ppermute | solution.py:37
  172.3 4.7 %collective-permute-start.16 = (f32[16,3]{0,1:T(4,128)}, f32[16,3]{0,1:T(4,128)S(1)}, u32[]{:S(2)}, u32[]{:S(2)}) collective-permute-start(f32[16,3]{0,1:T(4,128)} %concatenate.260), channel_id=1, source_target_pairs={{0,16},{4,20},{8,24},{12,28},{16,0},{20,4},{24,8},{28,12},{1,17},{... | collective-permute-start | bytes 584 | tf_op jit(solution)/shard_map/ppermute | solution.py:37
  (62 other events, 220.8 us)

commit v2 on v0

v2 whole, which is shorter than its diff:
```python
import functools

import jax
import jax.numpy as jnp
from jax import lax
from jax.experimental import pallas as pl
from jax.experimental.pallas import tpu as pltpu
from jax.sharding import PartitionSpec as P

SIGNS = (-1.0, 1.0, -1.0, 1.0)
HIGHEST = lax.Precision.HIGHEST
AXES = ("gx", "gy")
F32 = jnp.float32
BF16 = jnp.bfloat16
VMEM = pltpu.VMEM
SMEM = pltpu.SMEM
FIRST_LANE = 32
INVERSE_LANE = 48
SCALAR_LANE = 96


class Sizes:
    def __init__(self, nx, ny, traces, loads):
        self.nx, self.ny = nx, ny
        self.count = nx * ny
        self.modes, self.face = traces.shape[-2:]
        self.cases = loads.shape[-1]
        self.order = 4 * self.face
        self.lanes = -(-self.face // 128) * 128
        self.starts = [f * self.face // 128 * 128 for f in range(4)]
        ends = [-(-(f + 1) * self.face // 128) * 128 for f in range(4)]
        self.width = max(e - s for s, e in zip(self.starts, ends))
        self.padded = max(s + self.width for s in self.starts)
        self.wide = min(nx, 9)
        self.rows = self.wide * ny * 8
        self.steps = (-ny, ny, -1, 1)


def dot(a, b, contract=(1, 0), precision=HIGHEST):
    dims = (((contract[0],), (contract[1],)), ((), ()))
    return lax.dot_general(a, b, dims, precision=precision, preferred_element_type=F32)


def iota(shape, dim):
    return lax.broadcasted_iota(jnp.int32, shape, dim)


def place():
    return lax.axis_index("gx"), lax.axis_index("gy")


def window_start(z, ix):
    return jnp.clip(ix - 4, 0, z.nx - z.wide) if z.wide < z.nx else 0


def spots(z, ix, iy):
    own = (ix - window_start(z, ix)) * z.ny + iy
    return [own] + [jnp.clip(own + step, 0, z.wide * z.ny - 1) for step in z.steps]


def live_row(z, counts, face):
    return (iota((1, z.lanes), 1) < counts[0, 0, face]).astype(F32)


def send_faces(z, faces, to_x, to_y):
    ix, iy = place()
    for ref, at, size, low, high in ((to_x, ix, z.nx, 0, 1), (to_y, iy, z.ny, 2, 3)):
        up = jnp.where(at + 1 < size, at + 1, at)
        down = jnp.where(at > 0, at - 1, at)
        ref[pl.ds(up, 1)] = faces[high][None]
        ref[pl.ds(down, 1)] = faces[low][None]


def faces_across(z, from_x, from_y):
    ix, iy = place()
    found = []
    for ref, at, size in ((from_x, ix, z.nx), (from_y, iy, z.ny)):
        for there, valid in ((at - 1, at > 0), (at + 1, at + 1 < size)):
            values = ref[pl.ds(jnp.clip(there, 0, size - 1), 1)][0]
            found.append(jnp.where(valid, values, jnp.zeros_like(values)))
    return found


def pack_traces(z, traces, padded, to_x, to_y):
    padded[...] = jnp.zeros_like(padded)
    for f in range(4):
        padded[f, 0 : z.modes, 0 : z.face] = traces[0, 0, f]
    send_faces(z, [padded[f] for f in range(4)], to_x, to_y)


def set_up(z, padded, counts, maps, loads, forward, backward, local_tile, flat, aug, small):
    flat[...] = jnp.zeros_like(flat)
    flat[0:4, 0 : z.face] = maps[0, 0]
    lane = iota((1, z.padded), 1)
    line = jnp.full((1, z.padded), -1, jnp.int32)
    for f in range(4):
        moved = pltpu.roll(flat[...], f * z.face, 1)[f : f + 1] if f else flat[0:1]
        line = jnp.where((lane >= f * z.face) & (lane < (f + 1) * z.face), moved, line)
    column = jnp.transpose(jnp.broadcast_to(line, (8, z.padded)))[:, 0:1]
    place_of = iota((z.padded, 1), 0)
    for f in range(4):
        low, high = f * z.face, (f + 1) * z.face
        window = slice(z.starts[f], z.starts[f] + z.width)
        here = jnp.where((lane >= low) & (lane < high), line, -1)[:, window]
        forward[f] = (iota((z.lanes, z.width), 0) == here).astype(F32).astype(BF16)
        there = jnp.where((place_of >= low) & (place_of < high), column, -1)[window]
        backward[f] = (iota((z.width, z.lanes), 1) == there).astype(F32).astype(BF16)
    diagonal = sum(dot(padded[f] * live_row(z, counts, f), padded[f], (1, 1)) for f in range(4))
    row, col = iota((8, 128), 0), iota((8, 128), 1)
    aug[...] = jnp.where((col == row + 8) & (row < z.modes), 1.0, 0.0).astype(F32)
    aug[:, 0:8] = diagonal
    matrix = aug[...]
    for p in range(z.modes):
        scaled = matrix[p : p + 1, :] / matrix[p : p + 1, p : p + 1]
        taken = matrix[:, p : p + 1] - (row[:, 0:1] == p).astype(F32)
        matrix = matrix - taken * scaled
    inverse = matrix[:, 8:16]
    small[...] = jnp.zeros_like(small)
    small[0 : z.modes, :] = loads[0, 0]
    local_tile[...] = jnp.zeros_like(local_tile)
    local_tile[:, FIRST_LANE : FIRST_LANE + z.cases] = dot(inverse, small[...])
    local_tile[:, INVERSE_LANE : INVERSE_LANE + 8] = inverse


def couple(z, padded, counts, from_x, from_y, local_tile, across, sent, tile):
    near = faces_across(z, from_x, from_y)
    inverse = local_tile[:, INVERSE_LANE : INVERSE_LANE + 8]
    tile[...] = local_tile[...]
    for f in range(4):
        across[f] = near[f]
        coupling = dot(padded[f] * live_row(z, counts, f), near[f], (1, 1))
        tile[:, 8 * f : 8 * f + 8] = dot(inverse, coupling)
    sent[...] = jnp.broadcast_to(tile[...][None], sent.shape)


def lifted(z, amplitudes, lift_rows, f):
    pair = jnp.concatenate([amplitudes[0:8], amplitudes[8 * f + 8 : 8 * f + 16]], axis=0)
    return dot(pair, lift_rows[f], (0, 0))


def apply(z, faces, ops, forward, backward, local, product):
    local[...] = jnp.zeros_like(local)
    for f in range(4):
        window = slice(z.starts[f], z.starts[f] + z.width)
        signed = (faces[f] * SIGNS[f]).astype(BF16)
        local[:, window] += dot(signed, forward[f], precision=None)
    operand = local[:, 0 : z.order].astype(BF16)
    return dot(operand, ops[0, 0], precision=None)


def canonical(z, values, backward, product):
    product[...] = jnp.zeros_like(product)
    product[:, 0 : z.order] = values
    found = []
    for f in range(4):
        part = product[:, z.starts[f] : z.starts[f] + z.width]
        high = part.astype(BF16)
        low = (part - high.astype(F32)).astype(BF16)
        both = dot(jnp.concatenate([high, low], axis=0), backward[f], precision=None)
        found.append(both[0 : z.cases] + both[z.cases :])
    return found


def send_coarse(z, faces, rows, scalars, sent, tile):
    tile[...] = jnp.zeros_like(tile)
    mine = jnp.zeros((8, z.cases), F32)
    for f in range(4):
        both = dot(rows[f], faces[f], (1, 1))
        mine = mine + both[0:8]
        tile[:, (1 + f) * z.cases : (2 + f) * z.cases] = both[8:16]
    tile[:, 0 : z.cases] = mine
    send_tile(tile[...], scalars, sent)


def send_tile(values, scalars, sent):
    row, col = iota((8, 128), 0), iota((8, 128), 1)
    for i, scalar in enumerate(scalars):
        values = jnp.where((row == 0) & (col == SCALAR_LANE + i), scalar, values)
    sent[...] = jnp.broadcast_to(values[None], sent.shape)


def scalar_of(total, i):
    row, col = iota((8, 128), 0), iota((8, 128), 1)
    return jnp.sum(jnp.where((row == 0) & (col == SCALAR_LANE + i), total, 0.0), keepdims=True)


def received_window(z, received):
    ix, _ = place()
    start = window_start(z, ix) * z.ny
    return received[pl.ds(start, z.wide * z.ny)].reshape(z.rows, 128)


def coarse_amplitudes(z, received, solve_rows):
    values = received_window(z, received)
    start = values
    for f in range(4):
        across = pltpu.roll(values, 128 - (1 + (f ^ 1)) * z.cases, 1)
        step = 8 * z.steps[f]
        empty = jnp.zeros((abs(step), 128), F32)
        if step > 0:
            moved = jnp.concatenate([across[step:], empty], axis=0)
        else:
            moved = jnp.concatenate([empty, across[: z.rows + step]], axis=0)
        start = start - moved
    return dot(solve_rows[...], start)[:, 0 : z.cases]


def total(values):
    return jnp.sum(values, keepdims=True)


def face_weights(z):
    ix, iy = place()
    edges = (ix == 0, ix == z.nx - 1, iy == 0, iy == z.ny - 1)
    return [jnp.where(edge, 1.0, 0.5).astype(F32) for edge in edges]


def begin(
    z, received, padded, across, counts, primal, ops, forward, backward, local_tile,
    solve_rows, rows, lift_rows, multipliers, faces, sent, to_x, to_y,
    matrix, local, product, tile,
):
    ix, iy = place()
    near_spots = spots(z, ix, iy)
    values = received_window(z, received)
    lane = iota((z.rows, 128), 1)
    row = iota((z.rows, 128), 0)
    tiled = []
    for f in range(4):
        part = jnp.where(lane // 8 == f, values, 0.0)
        for shift in (64, 32, 16, 8):
            part = part + pltpu.roll(part, shift, 1)
        tiled.append(part)
    for block in range(-(-z.rows // 128)):
        target = (lane + 128 * block) // 8 - row // 8
        part = jnp.zeros((z.rows, 128), F32)
        for f in range(4):
            part = part + jnp.where(target == z.steps[f], tiled[f], 0.0)
        matrix[:, 128 * block : 128 * block + 128] = part
    once = jnp.concatenate([matrix[pl.ds(pl.multiple_of(s * 8, 8), 8), 0 : z.rows] for s in near_spots], axis=0)
    twice = dot(once, matrix[:, 0 : z.rows])
    cols = z.rows
    unit = jnp.concatenate([
        (iota((8, cols), 1) == iota((8, cols), 0) + s * 8).astype(F32) for s in near_spots
    ], axis=0)
    solve = unit + once + twice
    solve_rows[...] = solve
    amplitudes = dot(solve, values)[:, FIRST_LANE : FIRST_LANE + z.cases]
    inverse = local_tile[:, INVERSE_LANE : INVERSE_LANE + 8]
    start = window_start(z, ix) * z.ny
    fields = []
    for f in range(4):
        live = live_row(z, counts, f)
        near_inverse = received[pl.ds(start + near_spots[1 + f], 1)][0][:, INVERSE_LANE : INVERSE_LANE + 8]
        own, near = padded[f] * live, across[f] * live
        rows[f] = jnp.concatenate([dot(inverse, own), dot(near_inverse, near)], axis=0)
        lift_rows[f] = jnp.concatenate([own * SIGNS[f], near * -SIGNS[f]], axis=0)
        fields.append(lifted(z, amplitudes, lift_rows, f))
        multipliers[f] = fields[f]
    image = primal[0, 0] - apply(z, fields, ops, forward, backward, local, product)
    image = canonical(z, image, backward, product)
    for f in range(4):
        faces[f] = image[f]
    send_faces(z, image, to_x, to_y)
    send_coarse(z, image, rows, [], sent, tile)


def jumped(z, counts, faces, from_x, from_y):
    near = faces_across(z, from_x, from_y)
    return [live_row(z, counts, f) * SIGNS[f] * (faces[f] - near[f]) for f in range(4)]


def first_direction(
    z, received, from_x, from_y, faces, counts, ops, forward, backward, solve_rows, rows, lift_rows,
    residual, direction, image, sent, to_x, to_y,
    local, product, tile,
):
    amplitudes = coarse_amplitudes(z, received, solve_rows)
    field = jumped(z, counts, faces, from_x, from_y)
    weights = face_weights(z)
    moved = [field[f] - lifted(z, amplitudes, lift_rows, f) for f in range(4)]
    found = canonical(z, apply(z, moved, ops, forward, backward, local, product), backward, product)
    for f in range(4):
        residual[f] = field[f]
        direction[f] = moved[f]
        image[f] = found[f]
    gamma = sum(weights[f] * total(field[f] * moved[f]) for f in range(4))
    curvature = sum(SIGNS[f] * total(moved[f] * found[f]) for f in range(4))
    send_faces(z, found, to_x, to_y)
    send_coarse(z, found, rows, [gamma, curvature], sent, tile)


def second_direction(
    z, received, from_x, from_y, faces, counts, ops, forward, backward, solve_rows, lift_rows,
    multipliers, residual, direction,
    next_multipliers, next_residual, projected, image, fresh, sums, sent, to_x, to_y,
    local, product,
):
    amplitudes = coarse_amplitudes(z, received, solve_rows)
    summed = jnp.sum(received[...], axis=0)
    sums[...] = summed
    alpha = scalar_of(summed, 0) / scalar_of(summed, 1)
    field = jumped(z, counts, faces, from_x, from_y)
    weights = face_weights(z)
    left, moved = [], []
    for f in range(4):
        image[f] = field[f]
        next_multipliers[f] = multipliers[f] + alpha * direction[f]
        left.append(residual[f] - alpha * field[f])
        moved.append(direction[f] - alpha * (field[f] - lifted(z, amplitudes, lift_rows, f)))
        next_residual[f] = left[f]
        projected[f] = moved[f]
    found = canonical(z, apply(z, moved, ops, forward, backward, local, product), backward, product)
    for f in range(4):
        fresh[f] = found[f]
    send_faces(z, found, to_x, to_y)
    gamma = sum(weights[f] * total(left[f] * moved[f]) for f in range(4))
    straight = sum(SIGNS[f] * total(moved[f] * found[f]) for f in range(4))
    crossed = sum(
        weights[f] * total(moved[f] * field[f]) + SIGNS[f] * total(direction[f] * found[f]) for f in range(4)
    )
    send_tile(jnp.zeros((8, 128), F32), [gamma, straight, crossed], sent)


def finish(
    z, received, from_x, from_y, faces, counts, sums, multipliers, residual, direction, projected, image,
    out_multipliers, out_residual,
):
    summed = jnp.sum(received[...], axis=0)
    field = jumped(z, counts, faces, from_x, from_y)
    gamma, curvature = scalar_of(sums[...], 0), scalar_of(sums[...], 1)
    fresh, straight, crossed = (scalar_of(summed, i) for i in range(3))
    beta = fresh / gamma
    alpha = fresh / (straight + beta * crossed + beta * beta * curvature)
    for f in range(4):
        step = projected[f] + beta * direction[f]
        out_multipliers[0, 0, f] = (multipliers[f] + alpha * step)[:, 0 : z.face]
        out_residual[0, 0, f] = (residual[f] - alpha * (field[f] + beta * image[f]))[:, 0 : z.face]


def call(z, kernel, outs, args, scratch=(), flops=0):
    shapes = [jax.ShapeDtypeStruct(shape, dtype) for shape, dtype in outs]
    moved = sum(a.size * a.dtype.itemsize for a in args) + sum(s.size * s.dtype.itemsize for s in shapes)
    return pl.pallas_call(
        functools.partial(kernel, z),
        out_shape=shapes,
        in_specs=[pl.BlockSpec(memory_space=SMEM if a.ndim == 3 and a.size == 4 else VMEM) for a in args],
        out_specs=[pl.BlockSpec(memory_space=VMEM) for _ in shapes],
        scratch_shapes=[VMEM(shape, dtype) for shape, dtype in scratch],
        compiler_params=pltpu.CompilerParams(vmem_limit_bytes=40 * 2**20),
        cost_estimate=pl.CostEstimate(flops=flops, bytes_accessed=moved, transcendentals=0),
        name=kernel.__name__,
    )(*args)


def swap(values, axis):
    return lax.all_to_all(values, axis, 0, 0, tiled=True)


def body(ops, traces, primal, loads, maps, counts):
    z = Sizes(lax.axis_size("gx"), lax.axis_size("gy"), traces, loads)
    field = ((4, z.cases, z.lanes), F32)
    mode_rows = ((4, 8, z.lanes), F32)
    pair_rows = ((4, 16, z.lanes), F32)
    tile = ((8, 128), F32)
    sent = ((z.count, 8, 128), F32)
    to_x, to_y = ((z.nx, z.cases, z.lanes), F32), ((z.ny, z.cases, z.lanes), F32)
    padded_rows = ((z.cases, z.padded), F32)
    columns = -(-z.rows // 128) * 128
    product_flops = 2 * z.cases * z.order * z.order

    padded, trace_x, trace_y = call(
        z, pack_traces,
        [mode_rows, ((z.nx, 8, z.lanes), F32), ((z.ny, 8, z.lanes), F32)], [traces],
    )
    trace_x, trace_y = swap(trace_x, "gx"), swap(trace_y, "gy")
    forward, backward, local_tile = call(
        z, set_up,
        [((4, z.lanes, z.width), BF16), ((4, z.width, z.lanes), BF16), tile], [padded, counts, maps, loads],
        [((8, z.padded), jnp.int32), tile, ((8, z.cases), F32)], product_flops,
    )
    across, blocks = call(z, couple, [mode_rows, sent], [padded, counts, trace_x, trace_y, local_tile], [tile])
    blocks = swap(blocks, AXES)
    solve_rows, rows, lift_rows, multipliers, faces, coarse, face_x, face_y = call(
        z, begin,
        [((40, z.rows), F32), pair_rows, pair_rows, field, field, sent, to_x, to_y],
        [blocks, padded, across, counts, primal, ops, forward, backward, local_tile],
        [((z.rows, columns), F32), padded_rows, padded_rows, tile], product_flops,
    )
    coarse, face_x, face_y = swap(coarse, AXES), swap(face_x, "gx"), swap(face_y, "gy")
    residual, direction, faces, coarse, face_x, face_y = call(
        z, first_direction,
        [field, field, field, sent, to_x, to_y],
        [coarse, face_x, face_y, faces, counts, ops, forward, backward, solve_rows, rows, lift_rows],
        [padded_rows, padded_rows, tile], product_flops,
    )
    coarse, face_x, face_y = swap(coarse, AXES), swap(face_x, "gx"), swap(face_y, "gy")
    multipliers, residual, projected, image, faces, sums, coarse, face_x, face_y = call(
        z, second_direction,
        [field, field, field, field, field, tile, sent, to_x, to_y],
        [coarse, face_x, face_y, faces, counts, ops, forward, backward, solve_rows, lift_rows,
         multipliers, residual, direction],
        [padded_rows, padded_rows], product_flops,
    )
    coarse, face_x, face_y = swap(coarse, AXES), swap(face_x, "gx"), swap(face_y, "gy")
    whole = ((1, 1, 4, z.cases, z.face), F32)
    multipliers, residual = call(
        z, finish, [whole, whole],
        [coarse, face_x, face_y, faces, counts, sums, multipliers, residual, direction, projected, image],
    )
    return multipliers, residual


def solution(mesh):
    in_specs = (
        P("gx", "gy", None, None),
        P("gx", "gy", None, None, None),
        P("gx", "gy", None, None),
        P("gx", "gy", None, None),
        P("gx", "gy", None, None),
        P("gx", "gy", None),
    )
    out_specs = (P("gx", "gy", None, None, None), P("gx", "gy", None, None, None))
    return jax.shard_map(body, mesh=mesh, in_specs=in_specs, out_specs=out_specs, check_vma=False)
```

time: 367 us -> 132 us (0.36)
  the two profiles are of different devices: /device:TPU:5 before, /device:TPU:0 now
where the time goes in v2:
time: 132 us; the launch traced here: 131 us
  blocking collectives  102 us (77%)
  Pallas kernels  13.6 us (10%)
  local copies, waits for them, and re-layouts  6.22 us (5%)
  starting transfers between devices  5.83 us (4%)
  waiting for transfers between devices  3.08 us (2%)
    all_to_all x11, blocking collectives, swap(): return lax.all_to_all(values, axis, 0, 0, tiled=True)  102 us
    pallas_call x7, Pallas kernels, call(): pl.pallas_call(functools.partial(kernel, z), out_shape=shapes, in_specs=[...  13.6 us
    unnamed x14, local copies, waits for them, and re-layouts  6.22 us
    all_to_all x1, starting transfers between devices, swap(): return lax.all_to_all(values, axis, 0, 0, tiled=True)  5.83 us
    all_to_all x1, waiting for transfers between devices, swap(): return lax.all_to_all(values, axis, 0, 0, tiled=True)  3.08 us
  transfers between devices with their start and end apart: 1, of which 1 were waited for; matrix products, arithmetic and copies ran while one was open for 1% of the time, Pallas kernels for 2%

profile of v2, /device:TPU:0, one launch (start us, length us, event | category | flops | bytes accessed | tf_op | source)
XLA Modules:
  0.0 130.9 jit_solution(13445359761907123647)
XLA Ops:
  0.6 0.8 copy.8.traces
  1.4 0.7 pack_traces.1
  2.1 8.0 %all_to_all.60.from_y = f32[4,8,384]{2,1,0:T(8,128)S(1)} all-to-all(f32[4,8,384]{2,1,0:T(8,128)S(1)} %get-tuple-element.35), channel_id=1, replica_groups=mesh['gx'=8,'gy'=4] {'gy'}, dimensions={0} | all-to-all | bytes 98304 | tf_op jit(solution)/shard_map/all_to_all | solution.py:357
  10.1 5.8 %all-to-all-start = ((f32[8,8,384]{2,1,0:T(8,128)}), f32[8,8,384]{2,1,0:T(8,128)S(1)}, u32[]{:S(2)}, u32[]{:S(2)}) async-start(f32[8,8,384]{2,1,0:T(8,128)} %get-tuple-element.34), calls=%async_computation | async-start | bytes 196608 | tf_op jit(solution)/shard_map/all_to_all | solution.py:357
  15.9 0.7 copy.9.loads
  16.6 0.7 copy-done.3
  17.3 0.0 copy-start.5
  17.3 0.7 copy-done.5
  18.0 2.0 %set_up.1 = (bf16[4,384,512]{2,1,0:T(8,128)(2,1)S(1)}, bf16[4,512,384]{2,1,0:T(8,128)(2,1)S(1)}, f32[8,128]{1,0:T(8,128)S(1)}) custom-call(f32[4,8,384]{2,1,0:T(8,128)S(1)} %get-tuple-element.33.padded, s32[1,1,4]{2,1,0:T(1,128)S(1)} %copy-done.3, s32[1,1,4,300]{3,2,1,0:T(4,128)S(1)} %copy-done.5, f32[1,1,6,16]{3,2,1,0:T(8,128)S(1)} %copy.9.loads), custom_call_target="tpu_custom_call" | custom-call | flops 46080000 | bytes 3204176 | tf_op jit(solution)/shard_map/set_up/pallas_call | solution.py:344
  20.0 3.1 %all-to-all-done.from_x = f32[8,8,384]{2,1,0:T(8,128)S(1)} async-done(((f32[8,8,384]{2,1,0:T(8,128)}), f32[8,8,384]{2,1,0:T(8,128)S(1)}, u32[]{:S(2)}, u32[]{:S(2)}) %all-to-all-start) | async-done | bytes 98336 | tf_op jit(solution)/shard_map/all_to_all | solution.py:357
  23.1 0.0 copy-start.4
  23.1 0.7 copy-done.4
  23.7 1.4 %couple.1 = (f32[4,8,384]{2,1,0:T(8,128)S(1)}, f32[32,8,128]{2,1,0:T(8,128)S(1)}) custom-call(f32[4,8,384]{2,1,0:T(8,128)S(1)} %get-tuple-element.33.padded, s32[1,1,4]{2,1,0:T(1,128)S(1)} %copy-done.4, f32[8,8,384]{2,1,0:T(8,128)S(1)} %all-to-all-done.from_x, f32[4,8,384]{2,1,0:T(8,128)S(1)} %all_to_all.60.from_y, f32[8,128]{1,0:T(8,128)S(1)} %get-tuple-element.36.local_tile), custom_call_target="tpu_custom_call" | custom-call | bytes 380944 | tf_op jit(solution)/shard_map/couple/pallas_call | solution.py:344
  25.1 10.1 %all_to_all.61.received = f32[32,8,128]{2,1,0:T(8,128)S(1)} all-to-all(f32[32,8,128]{2,1,0:T(8,128)S(1)} %get-tuple-element.37), channel_id=1, replica_groups=mesh['gx'=8,'gy'=4] {'gx','gy'}, dimensions={0} | all-to-all | bytes 262144 | tf_op jit(solution)/shard_map/all_to_all | solution.py:357
  35.1 0.0 copy-start
  35.1 1.9 %copy-done = bf16[1,1,1200,1200]{3,2,1,0:T(8,128)(2,1)S(1)} copy-done((bf16[1,1,1200,1200]{3,2,1,0:T(8,128)(2,1)S(1)}, bf16[1,1,1200,1200]{3,2,1,0:T(8,128)(2,1)}, u32[]{:S(2)}) %copy-start) | copy-done | bytes 2880024
  37.0 0.0 copy-start.2
  37.0 0.9 copy-done.2
  37.9 3.5 %begin.1 = (f32[40,256]{1,0:T(8,128)S(1)}, f32[4,16,384]{2,1,0:T(8,128)S(1)}, f32[4,16,384]{2,1,0:T(8,128)S(1)}, f32[4,16,384]{2,1,0:T(8,128)S(1)}, f32[4,16,384...) custom-call(f32[32,8,128]{2,1,0:T(8,128)S(1)} %all_to_all.61.received, ...), custom_call_target="tpu_custom_call" | custom-call | flops 46080000 | bytes 7196176 | tf_op jit(solution)/shard_map/begin/pallas_call | solution.py:344
  41.4 6.7 %all_to_all.62.from_y = f32[4,16,384]{2,1,0:T(8,128)S(1)} all-to-all(f32[4,16,384]{2,1,0:T(8,128)S(1)} %get-tuple-element.43), channel_id=1, replica_groups=mesh['gx'=8,'gy'=4] {'gy'}, dimensions={0} | all-to-all | bytes 196608 | tf_op jit(solution)/shard_map/all_to_all | solution.py:357
  48.0 9.9 %all_to_all.63.received = f32[32,8,128]{2,1,0:T(8,128)S(1)} all-to-all(f32[32,8,128]{2,1,0:T(8,128)S(1)} %get-tuple-element.41), channel_id=1, replica_groups=mesh['gx'=8,'gy'=4] {'gx','gy'}, dimensions={0} | all-to-all | bytes 262144 | tf_op jit(solution)/shard_map/all_to_all | solution.py:357
  58.0 11.0 %all_to_all.64.from_x = f32[8,16,384]{2,1,0:T(8,128)S(1)} all-to-all(f32[8,16,384]{2,1,0:T(8,128)S(1)} %get-tuple-element.42), channel_id=1, replica_groups=mesh['gx'=8,'gy'=4] {'gx'}, dimensions={0} | all-to-all | bytes 393216 | tf_op jit(solution)/shard_map/all_to_all | solution.py:357
  69.0 0.0 copy-done.1
  69.0 2.4 %first_direction.1 = (f32[4,16,384]{2,1,0:T(8,128)S(1)}, f32[4,16,384]{2,1,0:T(8,128)S(1)}, f32[4,16,384]{2,1,0:T(8,128)S(1)}, f32[32,8,128]{2,1,0:T(8,128)S(1)}...) custom-call(f32[32,8,128]{2,1,0:T(8,128)S(1)} %all_to_all.63.received, f32[8,16,384]{2,1,0:T(8,128)S(1)} %all_to_all.64.from_x, ...), custom_call_target="tpu_custom_call" | custom-call | flops 46080000 | bytes 7508496 | tf_op jit(solution)/shard_map/first_direction/pallas_call | solution.py:344
  71.4 6.7 %all_to_all.65.from_y = f32[4,16,384]{2,1,0:T(8,128)S(1)} all-to-all(f32[4,16,384]{2,1,0:T(8,128)S(1)} %get-tuple-element.50), channel_id=1, replica_groups=mesh['gx'=8,'gy'=4] {'gy'}, dimensions={0} | all-to-all | bytes 196608 | tf_op jit(solution)/shard_map/all_to_all | solution.py:357
  78.0 10.2 %all_to_all.66.received = f32[32,8,128]{2,1,0:T(8,128)S(1)} all-to-all(f32[32,8,128]{2,1,0:T(8,128)S(1)} %get-tuple-element.48), channel_id=1, replica_groups=mesh['gx'=8,'gy'=4] {'gx','gy'}, dimensions={0} | all-to-all | bytes 262144 | tf_op jit(solution)/shard_map/all_to_all | solution.py:357
  88.3 11.0 %all_to_all.67.from_x = f32[8,16,384]{2,1,0:T(8,128)S(1)} all-to-all(f32[8,16,384]{2,1,0:T(8,128)S(1)} %get-tuple-element.49), channel_id=1, replica_groups=mesh['gx'=8,'gy'=4] {'gx'}, dimensions={0} | all-to-all | bytes 393216 | tf_op jit(solution)/shard_map/all_to_all | solution.py:357
  99.3 2.3 %second_direction.1 = (f32[4,16,384]{2,1,0:T(8,128)S(1)}, f32[4,16,384]{2,1,0:T(8,128)S(1)}, f32[4,16,384]{2,1,0:T(8,128)S(1)}, f32[4,16,384]{2,1,0:T(8,128)S(1)...) custom-call(f32[32,8,128]{2,1,0:T(8,128)S(1)} %all_to_all.66.receive, ...), custom_call_target="tpu_custom_call" | custom-call | flops 46080000 | bytes 7905808 | tf_op jit(solution)/shard_map/second_direction/pallas_call | solution.py:344
  101.6 6.7 %all_to_all.68.from_y = f32[4,16,384]{2,1,0:T(8,128)S(1)} all-to-all(f32[4,16,384]{2,1,0:T(8,128)S(1)} %get-tuple-element.57), channel_id=1, replica_groups=mesh['gx'=8,'gy'=4] {'gy'}, dimensions={0} | all-to-all | bytes 196608 | tf_op jit(solution)/shard_map/all_to_all | solution.py:357
  108.2 10.2 %all_to_all.69.received = f32[32,8,128]{2,1,0:T(8,128)S(1)} all-to-all(f32[32,8,128]{2,1,0:T(8,128)S(1)} %get-tuple-element.55), channel_id=1, replica_groups=mesh['gx'=8,'gy'=4] {'gx','gy'}, dimensions={0} | all-to-all | bytes 262144 | tf_op jit(solution)/shard_map/all_to_all | solution.py:357
  118.5 11.0 %all_to_all.70.from_x = f32[8,16,384]{2,1,0:T(8,128)S(1)} all-to-all(f32[8,16,384]{2,1,0:T(8,128)S(1)} %get-tuple-element.56), channel_id=1, replica_groups=mesh['gx'=8,'gy'=4] {'gx'}, dimensions={0} | all-to-all | bytes 393216 | tf_op jit(solution)/shard_map/all_to_all | solution.py:357
  129.5 1.4 %finish.1 = (f32[1,1,4,16,300]{4,3,2,1,0:T(8,128)}, f32[1,1,4,16,300]{4,3,2,1,0:T(8,128)}) custom-call(f32[32,8,128]{2,1,0:T(8,128)S(1)} %all_to_all.69.received, f32[8,16,384]{2,1,0:T(8,128)S(1)} %all_to_all.70.from_x, f32[4,16,384]{2,1,0:T(8,128)S(1)} %all_to_all.68.from_y, f32[4,16,384]{2,1,0:T(8,128)S(1)} %get-tuple-element.58.faces, ...), custom_call_target="tpu_custom_call" | custom-call | bytes 1173520 | tf_op jit(solution)/shard_map/finish/pallas_call | solution.py:344
  (2 shorter events, 0.0 us)
Async XLA Ops:
  10.1 13.0 %all-to-all-start = ((f32[8,8,384]{2,1,0:T(8,128)}), f32[8,8,384]{2,1,0:T(8,128)S(1)}, u32[]{:S(2)}, u32[]{:S(2)}) async-start(f32[8,8,384]{2,1,0:T(8,128)} %get-tuple-element.34), calls=%async_computation | async-start | bytes 196608 | tf_op jit(solution)/shard_map/all_to_all | solution.py:357
  16.6 0.7 copy-start.3
  17.3 0.7 copy-start.5
  23.1 0.7 copy-start.4
  35.1 1.9 %copy-start = (bf16[1,1,1200,1200]{3,2,1,0:T(8,128)(2,1)S(1)}, bf16[1,1,1200,1200]{3,2,1,0:T(8,128)(2,1)}, u32[]{:S(2)}) copy-start(bf16[1,1,1200,1200]{3,2,1,0:T(8,128)(2,1)} %ops.5) | copy-start | bytes 8640004
  37.0 0.9 copy-start.2
  37.9 31.1 %copy-start.1 = (bf16[1,1,1200,1200]{3,2,1,0:T(8,128)(2,1)S(1)}, bf16[1,1,1200,1200]{3,2,1,0:T(8,128)(2,1)}, u32[]{:S(2)}) copy-start(bf16[1,1,1200,1200]{3,2,1,0:T(8,128)(2,1)} %ops.5) | copy-start | bytes 8640004

commit v3 on v2

--- a/solution.py
+++ b/solution.py
@@ -58,37 +58,45 @@
     return [own] + [jnp.clip(own + step, 0, z.wide * z.ny - 1) for step in z.steps]
 
 
-def live_row(z, counts, face):
-    return (iota((1, z.lanes), 1) < counts[0, 0, face]).astype(F32)
-
-
-def send_faces(z, faces, to_x, to_y):
-    ix, iy = place()
-    for ref, at, size, low, high in ((to_x, ix, z.nx, 0, 1), (to_y, iy, z.ny, 2, 3)):
-        up = jnp.where(at + 1 < size, at + 1, at)
-        down = jnp.where(at > 0, at - 1, at)
-        ref[pl.ds(up, 1)] = faces[high][None]
-        ref[pl.ds(down, 1)] = faces[low][None]
-
-
-def faces_across(z, from_x, from_y):
-    ix, iy = place()
+def send_faces(z, faces, sent):
+    for i, at in enumerate(place()):
+        even = at % 2 == 0
+        low, high = faces[2 * i], faces[2 * i + 1]
+        sent[2 * i][...] = jnp.where(even, high, low)
+        sent[2 * i + 1][...] = jnp.where(even, low, high)
+
+
+def across_faces(z, got):
     found = []
-    for ref, at, size in ((from_x, ix, z.nx), (from_y, iy, z.ny)):
-        for there, valid in ((at - 1, at > 0), (at + 1, at + 1 < size)):
-            values = ref[pl.ds(jnp.clip(there, 0, size - 1), 1)][0]
-            found.append(jnp.where(valid, values, jnp.zeros_like(values)))
+    for i, at in enumerate(place()):
+        even = at % 2 == 0
+        first, second = got[2 * i][...], got[2 * i + 1][...]
+        found += [jnp.where(even, second, first), jnp.where(even, first, second)]
     return found
 
 
-def pack_traces(z, traces, padded, to_x, to_y):
+def exchange(sent):
+    got = []
+    for i, values in enumerate(sent):
+        axis = AXES[i // 2]
+        pairs = []
+        for low in range(i % 2, lax.axis_size(axis) - 1, 2):
+            pairs += [(low, low + 1), (low + 1, low)]
+        got.append(lax.ppermute(values, axis, pairs))
+    return got
+
+
+def prepare(z, traces, counts, padded, masks, *sent):
     padded[...] = jnp.zeros_like(padded)
     for f in range(4):
-        padded[f, 0 : z.modes, 0 : z.face] = traces[0, 0, f]
-    send_faces(z, [padded[f] for f in range(4)], to_x, to_y)
-
-
-def set_up(z, padded, counts, maps, loads, forward, backward, local_tile, flat, aug, small):
+        for j in range(z.modes):
+            padded[f, j : j + 1, 0 : z.face] = traces[0, 0, j, f : f + 1]
+        live = (iota((8, z.lanes), 1) < counts[0, 0, f]).astype(F32)
+        masks[f] = live
+    send_faces(z, [padded[f] for f in range(4)], sent)
+
+
+def tables(z, maps, forward, backward, flat):
     flat[...] = jnp.zeros_like(flat)
     flat[0:4, 0 : z.face] = maps[0, 0]
     lane = iota((1, z.padded), 1)
@@ -105,7 +113,12 @@
         forward[f] = (iota((z.lanes, z.width), 0) == here).astype(F32).astype(BF16)
         there = jnp.where((place_of >= low) & (place_of < high), column, -1)[window]
         backward[f] = (iota((z.width, z.lanes), 1) == there).astype(F32).astype(BF16)
-    diagonal = sum(dot(padded[f] * live_row(z, counts, f), padded[f], (1, 1)) for f in range(4))
+
+
+def couple(z, padded, masks, loads, got0, got1, got2, got3, across, local_tile, sent, aug, small):
+    near = across_faces(z, (got0, got1, got2, got3))
+    live = [padded[f] * masks[f] for f in range(4)]
+    diagonal = sum(dot(live[f], padded[f], (1, 1)) for f in range(4))
     row, col = iota((8, 128), 0), iota((8, 128), 1)
     aug[...] = jnp.where((col == row + 8) & (row < z.modes), 1.0, 0.0).astype(F32)
     aug[:, 0:8] = diagonal
@@ -116,21 +129,16 @@
         matrix = matrix - taken * scaled
     inverse = matrix[:, 8:16]
     small[...] = jnp.zeros_like(small)
-    small[0 : z.modes, :] = loads[0, 0]
+    for j in range(z.modes):
+        small[j : j + 1, :] = loads[0, j]
     local_tile[...] = jnp.zeros_like(local_tile)
     local_tile[:, FIRST_LANE : FIRST_LANE + z.cases] = dot(inverse, small[...])
     local_tile[:, INVERSE_LANE : INVERSE_LANE + 8] = inverse
-
-
-def couple(z, padded, counts, from_x, from_y, local_tile, across, sent, tile):
-    near = faces_across(z, from_x, from_y)
-    inverse = local_tile[:, INVERSE_LANE : INVERSE_LANE + 8]
-    tile[...] = local_tile[...]
     for f in range(4):
         across[f] = near[f]
-        coupling = dot(padded[f] * live_row(z, counts, f), near[f], (1, 1))
-        tile[:, 8 * f : 8 * f + 8] = dot(inverse, coupling)
-    sent[...] = jnp.broadcast_to(tile[...][None], sent.shape)
+        coupling = dot(live[f], near[f], (1, 1))
+        local_tile[:, 8 * f : 8 * f + 8] = dot(inverse, coupling)
+    sent[...] = jnp.broadcast_to(local_tile[...][None], sent.shape)
 
 
 def lifted(z, amplitudes, lift_rows, f):
@@ -138,7 +146,7 @@
     return dot(pair, lift_rows[f], (0, 0))
 
 
-def apply(z, faces, ops, forward, backward, local, product):
+def apply(z, faces, ops, forward, local):
     local[...] = jnp.zeros_like(local)
     for f in range(4):
         window = slice(z.starts[f], z.starts[f] + z.width)
@@ -216,8 +224,8 @@
 
 
 def begin(
-    z, received, padded, across, counts, primal, ops, forward, backward, local_tile,
-    solve_rows, rows, lift_rows, multipliers, faces, sent, to_x, to_y,
+    z, received, padded, across, masks, primal, ops, forward, backward, local_tile,
+    solve_rows, rows, lift_rows, multipliers, faces, sent, to0, to1, to2, to3,
     matrix, local, product, tile,
 ):
     ix, iy = place()
@@ -250,57 +258,57 @@
     start = window_start(z, ix) * z.ny
     fields = []
     for f in range(4):
-        live = live_row(z, counts, f)
+        live = masks[f]
         near_inverse = received[pl.ds(start + near_spots[1 + f], 1)][0][:, INVERSE_LANE : INVERSE_LANE + 8]
         own, near = padded[f] * live, across[f] * live
         rows[f] = jnp.concatenate([dot(inverse, own), dot(near_inverse, near)], axis=0)
         lift_rows[f] = jnp.concatenate([own * SIGNS[f], near * -SIGNS[f]], axis=0)
         fields.append(lifted(z, amplitudes, lift_rows, f))
         multipliers[f] = fields[f]
-    image = primal[0, 0] - apply(z, fields, ops, forward, backward, local, product)
+    image = primal[0, 0] - apply(z, fields, ops, forward, local)
     image = canonical(z, image, backward, product)
     for f in range(4):
         faces[f] = image[f]
-    send_faces(z, image, to_x, to_y)
+    send_faces(z, image, (to0, to1, to2, to3))
     send_coarse(z, image, rows, [], sent, tile)
 
 
-def jumped(z, counts, faces, from_x, from_y):
-    near = faces_across(z, from_x, from_y)
-    return [live_row(z, counts, f) * SIGNS[f] * (faces[f] - near[f]) for f in range(4)]
+def jumped(z, masks, faces, got):
+    near = across_faces(z, got)
+    return [masks[f, 0:1] * SIGNS[f] * (faces[f] - near[f]) for f in range(4)]
 
 
 def first_direction(
-    z, received, from_x, from_y, faces, counts, ops, forward, backward, solve_rows, rows, lift_rows,
-    residual, direction, image, sent, to_x, to_y,
+    z, received, got0, got1, got2, got3, faces, masks, ops, forward, backward, solve_rows, rows, lift_rows,
+    residual, direction, image, sent, to0, to1, to2, to3,
     local, product, tile,
 ):
     amplitudes = coarse_amplitudes(z, received, solve_rows)
-    field = jumped(z, counts, faces, from_x, from_y)
+    field = jumped(z, masks, faces, (got0, got1, got2, got3))
     weights = face_weights(z)
     moved = [field[f] - lifted(z, amplitudes, lift_rows, f) for f in range(4)]
-    found = canonical(z, apply(z, moved, ops, forward, backward, local, product), backward, product)
+    found = canonical(z, apply(z, moved, ops, forward, local), backward, product)
     for f in range(4):
         residual[f] = field[f]
         direction[f] = moved[f]
         image[f] = found[f]
     gamma = sum(weights[f] * total(field[f] * moved[f]) for f in range(4))
     curvature = sum(SIGNS[f] * total(moved[f] * found[f]) for f in range(4))
-    send_faces(z, found, to_x, to_y)
+    send_faces(z, found, (to0, to1, to2, to3))
     send_coarse(z, found, rows, [gamma, curvature], sent, tile)
 
 
 def second_direction(
-    z, received, from_x, from_y, faces, counts, ops, forward, backward, solve_rows, lift_rows,
+    z, received, got0, got1, got2, got3, faces, masks, ops, forward, backward, solve_rows, lift_rows,
     multipliers, residual, direction,
-    next_multipliers, next_residual, projected, image, fresh, sums, sent, to_x, to_y,
+    next_multipliers, next_residual, projected, image, fresh, sums, sent, to0, to1, to2, to3,
     local, product,
 ):
     amplitudes = coarse_amplitudes(z, received, solve_rows)
     summed = jnp.sum(received[...], axis=0)
     sums[...] = summed
     alpha = scalar_of(summed, 0) / scalar_of(summed, 1)
-    field = jumped(z, counts, faces, from_x, from_y)
+    field = jumped(z, masks, faces, (got0, got1, got2, got3))
     weights = face_weights(z)
     left, moved = [], []
     for f in range(4):
@@ -310,10 +318,10 @@
         moved.append(direction[f] - alpha * (field[f] - lifted(z, amplitudes, lift_rows, f)))
         next_residual[f] = left[f]
         projected[f] = moved[f]
-    found = canonical(z, apply(z, moved, ops, forward, backward, local, product), backward, product)
+    found = canonical(z, apply(z, moved, ops, forward, local), backward, product)
     for f in range(4):
         fresh[f] = found[f]
-    send_faces(z, found, to_x, to_y)
+    send_faces(z, found, (to0, to1, to2, to3))
     gamma = sum(weights[f] * total(left[f] * moved[f]) for f in range(4))
     straight = sum(SIGNS[f] * total(moved[f] * found[f]) for f in range(4))
     crossed = sum(
@@ -323,11 +331,11 @@
 
 
 def finish(
-    z, received, from_x, from_y, faces, counts, sums, multipliers, residual, direction, projected, image,
+    z, received, got0, got1, got2, got3, faces, masks, sums, multipliers, residual, direction, projected, image,
     out_multipliers, out_residual,
 ):
     summed = jnp.sum(received[...], axis=0)
-    field = jumped(z, counts, faces, from_x, from_y)
+    field = jumped(z, masks, faces, (got0, got1, got2, got3))
     gamma, curvature = scalar_of(sums[...], 0), scalar_of(sums[...], 1)
     fresh, straight, crossed = (scalar_of(summed, i) for i in range(3))
     beta = fresh / gamma
@@ -353,8 +361,8 @@
     )(*args)
 
 
-def swap(values, axis):
-    return lax.all_to_all(values, axis, 0, 0, tiled=True)
+def gather(values):
+    return lax.all_to_all(values, AXES, 0, 0, tiled=True)
 
 
 def body(ops, traces, primal, loads, maps, counts):
@@ -364,49 +372,52 @@
     pair_rows = ((4, 16, z.lanes), F32)
     tile = ((8, 128), F32)
     sent = ((z.count, 8, 128), F32)
-    to_x, to_y = ((z.nx, z.cases, z.lanes), F32), ((z.ny, z.cases, z.lanes), F32)
+    to_faces = [((z.cases, z.lanes), F32)] * 4
     padded_rows = ((z.cases, z.padded), F32)
     columns = -(-z.rows // 128) * 128
     product_flops = 2 * z.cases * z.order * z.order
 
-    padded, trace_x, trace_y = call(
-        z, pack_traces,
-        [mode_rows, ((z.nx, 8, z.lanes), F32), ((z.ny, 8, z.lanes), F32)], [traces],
-    )
-    trace_x, trace_y = swap(trace_x, "gx"), swap(trace_y, "gy")
-    forward, backward, local_tile = call(
-        z, set_up,
-        [((4, z.lanes, z.width), BF16), ((4, z.width, z.lanes), BF16), tile], [padded, counts, maps, loads],
-        [((8, z.padded), jnp.int32), tile, ((8, z.cases), F32)], product_flops,
-    )
-    across, blocks = call(z, couple, [mode_rows, sent], [padded, counts, trace_x, trace_y, local_tile], [tile])
-    blocks = swap(blocks, AXES)
-    solve_rows, rows, lift_rows, multipliers, faces, coarse, face_x, face_y = call(
+    padded, masks, *trace_faces = call(
+        z, prepare, [mode_rows, mode_rows] + [((8, z.lanes), F32)] * 4,
+        [jnp.transpose(traces, (0, 1, 3, 2, 4)), counts],
+    )
+    got = exchange(trace_faces)
+    across, local_tile, blocks = call(
+        z, couple, [mode_rows, tile, sent],
+        [padded, masks, jnp.transpose(loads, (0, 2, 1, 3)), *got],
+        [tile, ((8, z.cases), F32)],
+    )
+    blocks = gather(blocks)
+    forward, backward = call(
+        z, tables, [((4, z.lanes, z.width), BF16), ((4, z.width, z.lanes), BF16)], [maps],
+        [((8, z.padded), jnp.int32)], product_flops,
+    )
+    solve_rows, rows, lift_rows, multipliers, faces, coarse, *sent_faces = call(
         z, begin,
-        [((40, z.rows), F32), pair_rows, pair_rows, field, field, sent, to_x, to_y],
-        [blocks, padded, across, counts, primal, ops, forward, backward, local_tile],
+        [((40, z.rows), F32), pair_rows, pair_rows, field, field, sent] + to_faces,
+        [blocks, padded, across, masks, primal, ops, forward, backward, local_tile],
         [((z.rows, columns), F32), padded_rows, padded_rows, tile], product_flops,
     )
-    coarse, face_x, face_y = swap(coarse, AXES), swap(face_x, "gx"), swap(face_y, "gy")
-    residual, direction, faces, coarse, face_x, face_y = call(
+    coarse, got = gather(coarse), exchange(sent_faces)
+    residual, direction, faces, coarse, *sent_faces = call(
         z, first_direction,
-        [field, field, field, sent, to_x, to_y],
-        [coarse, face_x, face_y, faces, counts, ops, forward, backward, solve_rows, rows, lift_rows],
+        [field, field, field, sent] + to_faces,
+        [coarse, *got, faces, masks, ops, forward, backward, solve_rows, rows, lift_rows],
         [padded_rows, padded_rows, tile], product_flops,
     )
-    coarse, face_x, face_y = swap(coarse, AXES), swap(face_x, "gx"), swap(face_y, "gy")
-    multipliers, residual, projected, image, faces, sums, coarse, face_x, face_y = call(
+    coarse, got = gather(coarse), exchange(sent_faces)
+    multipliers, residual, projected, image, faces, sums, coarse, *sent_faces = call(
         z, second_direction,
-        [field, field, field, field, field, tile, sent, to_x, to_y],
-        [coarse, face_x, face_y, faces, counts, ops, forward, backward, solve_rows, lift_rows,
+        [field, field, field, field, field, tile, sent] + to_faces,
+        [coarse, *got, faces, masks, ops, forward, backward, solve_rows, lift_rows,
          multipliers, residual, direction],
         [padded_rows, padded_rows], product_flops,
     )
-    coarse, face_x, face_y = swap(coarse, AXES), swap(face_x, "gx"), swap(face_y, "gy")
+    coarse, got = gather(coarse), exchange(sent_faces)
     whole = ((1, 1, 4, z.cases, z.face), F32)
     multipliers, residual = call(
         z, finish, [whole, whole],
-        [coarse, face_x, face_y, faces, counts, sums, multipliers, residual, direction, projected, image],
+        [coarse, *got, faces, masks, sums, multipliers, residual, direction, projected, image],
     )
     return multipliers, residual
 

time: 132 us -> 122 us (0.924)
  the two profiles are of different devices: /device:TPU:0 before, /device:TPU:5 now
where the time goes in v3:
time: 122 us; the launch traced here: 120 us
  starting transfers between devices  51.6 us (42%)
  local copies, waits for them, and re-layouts  45.6 us (37%)
  Pallas kernels  11.5 us (9%)
  waiting for transfers between devices  10.5 us (9%)
    unnamed x114, local copies, waits for them, and re-layouts  45.6 us
    ppermute x16, starting transfers between devices, exchange(): got.append(lax.ppermute(values, axis, pairs))  33.7 us
    all_to_all x4, starting transfers between devices, gather(): return lax.all_to_all(values, AXES, 0, 0, tiled=True)  17.8 us
    pallas_call x7, Pallas kernels, call(): pl.pallas_call(functools.partial(kernel, z), out_shape=shapes, in_specs=[...  11.5 us
    ppermute x16, waiting for transfers between devices, exchange(): got.append(lax.ppermute(values, axis, pairs))  7.68 us
    all_to_all x4, waiting for transfers between devices, gather(): return lax.all_to_all(values, AXES, 0, 0, tiled=True)  2.82 us
  transfers between devices with their start and end apart: 20, of which 5 were waited for; matrix products, arithmetic and copies ran while one was open for 0% of the time, Pallas kernels for 1%

profile of v3, /device:TPU:5, one launch (start us, length us, event | category | flops | bytes accessed | tf_op | source)
XLA Modules:
  0.0 120.1 jit_solution(5163725962277981264)
XLA Ops:
  2.7 4.4 %collective-permute-start.1 = (f32[8,384]{1,0:T(8,128)S(1)}, f32[8,384]{1,0:T(8,128)S(1)}, u32[]{:S(2)}, u32[]{:S(2)}) collective-permute-start(f32[8,384]{1,0:T(8,128)S(1)} %get-tuple-element.45), channel_id=1, source_target_pairs={{4,8},{8,4},{12,16},{16,12},{20,24},{24,20},{5,9},{9,5},{13,17},{1... | collective-permute-start | bytes 36872 | tf_op jit(solution)/shard_map/ppermute | solution.py:85
  7.1 1.3 %collective-permute-start.2 = (f32[8,384]{1,0:T(8,128)S(1)}, f32[8,384]{1,0:T(8,128)S(1)}, u32[]{:S(2)}, u32[]{:S(2)}) collective-permute-start(f32[8,384]{1,0:T(8,128)S(1)} %get-tuple-element.46), channel_id=1, source_target_pairs={{0,1},{1,0},{2,3},{3,2},{4,5},{5,4},{6,7},{7,6},{8,9},{9,8},{10,11... | collective-permute-start | bytes 36872 | tf_op jit(solution)/shard_map/ppermute | solution.py:85
  8.4 3.0 %collective-permute-start.3 = (f32[8,384]{1,0:T(8,128)S(1)}, f32[8,384]{1,0:T(8,128)S(1)}, u32[]{:S(2)}, u32[]{:S(2)}) collective-permute-start(f32[8,384]{1,0:T(8,128)S(1)} %get-tuple-element.47), channel_id=1, source_target_pairs={{1,2},{2,1},{5,6},{6,5},{9,10},{10,9},{13,14},{14,13},{17,18},{18,... | collective-permute-start | bytes 36872 | tf_op jit(solution)/shard_map/ppermute | solution.py:85
  11.4 1.9 %collective-permute-done.3.got3 = f32[8,384]{1,0:T(8,128)S(1)} collective-permute-done((f32[8,384]{1,0:T(8,128)S(1)}, f32[8,384]{1,0:T(8,128)S(1)}, u32[]{:S(2)}, u32[]{:S(2)}) %collective-permute-start.3) | collective-permute-done | bytes 12320 | tf_op jit(solution)/shard_map/ppermute | solution.py:85
  14.1 2.3 %couple.1 = (f32[4,8,384]{2,1,0:T(8,128)S(1)}, f32[8,128]{1,0:T(8,128)S(1)}, f32[32,8,128]{2,1,0:T(8,128)}) custom-call(f32[4,8,384]{2,1,0:T(8,128)S(1)} %get-tuple-element.42.padded, f32[4,8,384]{2,1,0:T(8,128)S(1)} %get-tuple-element.43.masks, f32[1,6,1,16]{3,2,1,0:T(1,128)S(1)} %bitcast.3, f32[8,384]{1,0:T(8,128)S(1)} %collective-permute-done.got0, ...), custom_call_target="tpu_custom_call" | custom-call | bytes 332160 | tf_op jit(solution)/shard_map/couple/pallas_call | solution.py:352
  16.4 4.8 %all-to-all-start = ((f32[32,8,128]{2,1,0:T(8,128)}), f32[32,8,128]{2,1,0:T(8,128)S(1)}, u32[]{:S(2)}, u32[]{:S(2)}) async-start(f32[32,8,128]{2,1,0:T(8,128)} %get-tuple-element.48), calls=%async_computation | async-start | bytes 262144 | tf_op jit(solution)/shard_map/all_to_all | solution.py:365
  21.9 1.1 tables.1
  22.9 1.1 copy-done.2
  24.1 1.1 copy-done.6
  25.2 2.8 %all-to-all-done.received = f32[32,8,128]{2,1,0:T(8,128)S(1)} async-done(((f32[32,8,128]{2,1,0:T(8,128)}), f32[32,8,128]{2,1,0:T(8,128)S(1)}, u32[]{:S(2)}, u32[]{:S(2)}) %all-to-all-start) | async-done | bytes 131104 | tf_op jit(solution)/shard_map/all_to_all | solution.py:365
  28.0 1.9 %copy-done = bf16[1,1,1200,1200]{3,2,1,0:T(8,128)(2,1)S(1)} copy-done((bf16[1,1,1200,1200]{3,2,1,0:T(8,128)(2,1)S(1)}, bf16[1,1,1200,1200]{3,2,1,0:T(8,128)(2,1)}, u32[]{:S(2)}) %copy-start) | copy-done | bytes 2880024
  29.9 1.4 %copy-done.3 = bf16[4,384,512]{2,1,0:T(8,128)(2,1)S(1)} copy-done((bf16[4,384,512]{2,1,0:T(8,128)(2,1)S(1)}, bf16[4,384,512]{2,1,0:T(8,128)(2,1)}, u32[]{:S(2)}) %copy-start.3) | copy-done | bytes 1572888
  31.3 1.4 %copy-done.7 = bf16[4,512,384]{2,1,0:T(8,128)(2,1)S(1)} copy-done((bf16[4,512,384]{2,1,0:T(8,128)(2,1)S(1)}, bf16[4,512,384]{2,1,0:T(8,128)(2,1)}, u32[]{:S(2)}) %copy-start.7) | copy-done | bytes 1572888
  33.6 3.1 %begin.1 = (f32[40,256]{1,0:T(8,128)S(1)}, f32[4,16,384]{2,1,0:T(8,128)S(1)}, f32[4,16,384]{2,1,0:T(8,128)S(1)}, f32[4,16,384]{2,1,0:T(8,128)S(1)}, f32[4,16,384...) custom-call(f32[32,8,128]{2,1,0:T(8,128)S(1)} %all-to-all-done.recei, ...), custom_call_target="tpu_custom_call" | custom-call | flops 46080000 | bytes 7048704 | tf_op jit(solution)/shard_map/begin/pallas_call | solution.py:352
  41.1 3.8 %all-to-all-start.1 = ((f32[32,8,128]{2,1,0:T(8,128)}), f32[32,8,128]{2,1,0:T(8,128)S(1)}, u32[]{:S(2)}, u32[]{:S(2)}) async-start(f32[32,8,128]{2,1,0:T(8,128)} %copy-done.12), calls=%async_computation.1 | async-start | bytes 262144 | tf_op jit(solution)/shard_map/all_to_all | solution.py:365
  45.1 4.3 %collective-permute-start.5 = (f32[16,384]{1,0:T(8,128)}, f32[16,384]{1,0:T(8,128)S(1)}, u32[]{:S(2)}, u32[]{:S(2)}) collective-permute-start(f32[16,384]{1,0:T(8,128)} %copy-done.54), channel_id=1, source_target_pairs={{4,8},{8,4},{12,16},{16,12},{20,24},{24,20},{5,9},{9,5},{13,17},{1... | collective-permute-start | bytes 73736 | tf_op jit(solution)/shard_map/ppermute | solution.py:85
  50.4 3.0 %collective-permute-start.7 = (f32[16,384]{1,0:T(8,128)}, f32[16,384]{1,0:T(8,128)S(1)}, u32[]{:S(2)}, u32[]{:S(2)}) collective-permute-start(f32[16,384]{1,0:T(8,128)} %copy-done.49), channel_id=1, source_target_pairs={{1,2},{2,1},{5,6},{6,5},{9,10},{10,9},{13,14},{14,13},{17,18},{18,... | collective-permute-start | bytes 73736 | tf_op jit(solution)/shard_map/ppermute | solution.py:85
  54.0 1.7 %collective-permute-done.7.got3 = f32[16,384]{1,0:T(8,128)S(1)} collective-permute-done((f32[16,384]{1,0:T(8,128)}, f32[16,384]{1,0:T(8,128)S(1)}, u32[]{:S(2)}, u32[]{:S(2)}) %collective-permute-start.7) | collective-permute-done | bytes 24608 | tf_op jit(solution)/shard_map/ppermute | solution.py:85
  56.3 1.4 %copy-done.4 = bf16[4,384,512]{2,1,0:T(8,128)(2,1)S(1)} copy-done((bf16[4,384,512]{2,1,0:T(8,128)(2,1)S(1)}, bf16[4,384,512]{2,1,0:T(8,128)(2,1)}, u32[]{:S(2)}) %copy-start.4) | copy-done | bytes 1572888
  57.7 1.4 %copy-done.8 = bf16[4,512,384]{2,1,0:T(8,128)(2,1)S(1)} copy-done((bf16[4,512,384]{2,1,0:T(8,128)(2,1)S(1)}, bf16[4,512,384]{2,1,0:T(8,128)(2,1)}, u32[]{:S(2)}) %copy-start.8) | copy-done | bytes 1572888
  62.4 1.8 %first_direction.1 = (f32[4,16,384]{2,1,0:T(8,128)S(1)}, f32[4,16,384]{2,1,0:T(8,128)S(1)}, f32[4,16,384]{2,1,0:T(8,128)S(1)}, f32[32,8,128]{2,1,0:T(8,128)S(1)}...) custom-call(f32[32,8,128]{2,1,0:T(8,128)S(1)} %all-to-all-done.1.received, ...), custom_call_target="tpu_custom_call" | custom-call | flops 46080000 | bytes 7164416 | tf_op jit(solution)/shard_map/first_direction/pallas_call | solution.py:352
  68.6 4.6 %all-to-all-start.2 = ((f32[32,8,128]{2,1,0:T(8,128)}), f32[32,8,128]{2,1,0:T(8,128)S(1)}, u32[]{:S(2)}, u32[]{:S(2)}) async-start(f32[32,8,128]{2,1,0:T(8,128)} %copy-done.11), calls=%async_computation.2 | async-start | bytes 262144 | tf_op jit(solution)/shard_map/all_to_all | solution.py:365
  73.4 4.2 %collective-permute-start.9 = (f32[16,384]{1,0:T(8,128)}, f32[16,384]{1,0:T(8,128)S(1)}, u32[]{:S(2)}, u32[]{:S(2)}) collective-permute-start(f32[16,384]{1,0:T(8,128)} %copy-done.53), channel_id=1, source_target_pairs={{4,8},{8,4},{12,16},{16,12},{20,24},{24,20},{5,9},{9,5},{13,17},{1... | collective-permute-start | bytes 73736 | tf_op jit(solution)/shard_map/ppermute | solution.py:85
  78.6 3.0 %collective-permute-start.11 = (f32[16,384]{1,0:T(8,128)}, f32[16,384]{1,0:T(8,128)S(1)}, u32[]{:S(2)}, u32[]{:S(2)}) collective-permute-start(f32[16,384]{1,0:T(8,128)} %copy-done.48), channel_id=1, source_target_pairs={{1,2},{2,1},{5,6},{6,5},{9,10},{10,9},{13,14},{14,13},{17,18},{18,... | collective-permute-start | bytes 73736 | tf_op jit(solution)/shard_map/ppermute | solution.py:85
  82.2 1.7 %collective-permute-done.11.got3 = f32[16,384]{1,0:T(8,128)S(1)} collective-permute-done((f32[16,384]{1,0:T(8,128)}, f32[16,384]{1,0:T(8,128)S(1)}, u32[]{:S(2)}, u32[]{:S(2)}) %collective-permute-start.11) | collective-permute-done | bytes 24608 | tf_op jit(solution)/shard_map/ppermute | solution.py:85
  84.6 1.4 %copy-done.5 = bf16[4,384,512]{2,1,0:T(8,128)(2,1)S(1)} copy-done((bf16[4,384,512]{2,1,0:T(8,128)(2,1)S(1)}, bf16[4,384,512]{2,1,0:T(8,128)(2,1)}, u32[]{:S(2)}) %copy-start.5) | copy-done | bytes 1572888
  86.0 1.4 %copy-done.9 = bf16[4,512,384]{2,1,0:T(8,128)(2,1)S(1)} copy-done((bf16[4,512,384]{2,1,0:T(8,128)(2,1)S(1)}, bf16[4,512,384]{2,1,0:T(8,128)(2,1)}, u32[]{:S(2)}) %copy-start.9) | copy-done | bytes 1572888
  91.5 1.7 %second_direction.1 = (f32[4,16,384]{2,1,0:T(8,128)S(1)}, f32[4,16,384]{2,1,0:T(8,128)S(1)}, f32[4,16,384]{2,1,0:T(8,128)S(1)}, f32[4,16,384]{2,1,0:T(8,128)S(1)...) custom-call(f32[32,8,128]{2,1,0:T(8,128)S(1)} %all-to-all-done.2.rec, ...), custom_call_target="tpu_custom_call" | custom-call | flops 46080000 | bytes 7561728 | tf_op jit(solution)/shard_map/second_direction/pallas_call | solution.py:352
  99.5 4.6 %all-to-all-start.3 = ((f32[32,8,128]{2,1,0:T(8,128)}), f32[32,8,128]{2,1,0:T(8,128)S(1)}, u32[]{:S(2)}, u32[]{:S(2)}) async-start(f32[32,8,128]{2,1,0:T(8,128)} %copy-done.10), calls=%async_computation.3 | async-start | bytes 262144 | tf_op jit(solution)/shard_map/all_to_all | solution.py:365
  104.3 4.2 %collective-permute-start.13 = (f32[16,384]{1,0:T(8,128)}, f32[16,384]{1,0:T(8,128)S(1)}, u32[]{:S(2)}, u32[]{:S(2)}) collective-permute-start(f32[16,384]{1,0:T(8,128)} %copy-done.47), channel_id=1, source_target_pairs={{4,8},{8,4},{12,16},{16,12},{20,24},{24,20},{5,9},{9,5},{13,17},{1... | collective-permute-start | bytes 73736 | tf_op jit(solution)/shard_map/ppermute | solution.py:85
  109.5 3.0 %collective-permute-start.15 = (f32[16,384]{1,0:T(8,128)}, f32[16,384]{1,0:T(8,128)S(1)}, u32[]{:S(2)}, u32[]{:S(2)}) collective-permute-start(f32[16,384]{1,0:T(8,128)} %copy-done.45), channel_id=1, source_target_pairs={{1,2},{2,1},{5,6},{6,5},{9,10},{10,9},{13,14},{14,13},{17,18},{18,... | collective-permute-start | bytes 73736 | tf_op jit(solution)/shard_map/ppermute | solution.py:85
  112.5 2.3 %collective-permute-done.15.got3 = f32[16,384]{1,0:T(8,128)S(1)} collective-permute-done((f32[16,384]{1,0:T(8,128)}, f32[16,384]{1,0:T(8,128)S(1)}, u32[]{:S(2)}, u32[]{:S(2)}) %collective-permute-start.15) | collective-permute-done | bytes 24608 | tf_op jit(solution)/shard_map/ppermute | solution.py:85
  (129 shorter events, 37.9 us)
Async XLA Ops:
  2.6 8.8 %collective-permute-start = (f32[8,384]{1,0:T(8,128)S(1)}, f32[8,384]{1,0:T(8,128)S(1)}, u32[]{:S(2)}, u32[]{:S(2)}) collective-permute-start(f32[8,384]{1,0:T(8,128)S(1)} %get-tuple-element.44), channel_id=1, source_target_pairs={{0,4},{4,0},{8,12},{12,8},{16,20},{20,16},{24,28},{28,24},{1,5},{5... | collective-permute-start | bytes 36872 | tf_op jit(solution)/shard_map/ppermute | solution.py:85
  2.7 8.7 %collective-permute-start.1 = (f32[8,384]{1,0:T(8,128)S(1)}, f32[8,384]{1,0:T(8,128)S(1)}, u32[]{:S(2)}, u32[]{:S(2)}) collective-permute-start(f32[8,384]{1,0:T(8,128)S(1)} %get-tuple-element.45), channel_id=1, source_target_pairs={{4,8},{8,4},{12,16},{16,12},{20,24},{24,20},{5,9},{9,5},{13,17},{1... | collective-permute-start | bytes 36872 | tf_op jit(solution)/shard_map/ppermute | solution.py:85
  7.1 4.4 %collective-permute-start.2 = (f32[8,384]{1,0:T(8,128)S(1)}, f32[8,384]{1,0:T(8,128)S(1)}, u32[]{:S(2)}, u32[]{:S(2)}) collective-permute-start(f32[8,384]{1,0:T(8,128)S(1)} %get-tuple-element.46), channel_id=1, source_target_pairs={{0,1},{1,0},{2,3},{3,2},{4,5},{5,4},{6,7},{7,6},{8,9},{9,8},{10,11... | collective-permute-start | bytes 36872 | tf_op jit(solution)/shard_map/ppermute | solution.py:85
  8.4 5.0 %collective-permute-start.3 = (f32[8,384]{1,0:T(8,128)S(1)}, f32[8,384]{1,0:T(8,128)S(1)}, u32[]{:S(2)}, u32[]{:S(2)}) collective-permute-start(f32[8,384]{1,0:T(8,128)S(1)} %get-tuple-element.47), channel_id=1, source_target_pairs={{1,2},{2,1},{5,6},{6,5},{9,10},{10,9},{13,14},{14,13},{17,18},{18,... | collective-permute-start | bytes 36872 | tf_op jit(solution)/shard_map/ppermute | solution.py:85
  16.4 11.6 %all-to-all-start = ((f32[32,8,128]{2,1,0:T(8,128)}), f32[32,8,128]{2,1,0:T(8,128)S(1)}, u32[]{:S(2)}, u32[]{:S(2)}) async-start(f32[32,8,128]{2,1,0:T(8,128)} %get-tuple-element.48), calls=%async_computation | async-start | bytes 262144 | tf_op jit(solution)/shard_map/all_to_all | solution.py:365
  22.9 1.1 copy-start.2
  24.1 1.1 copy-start.6
  28.0 1.9 %copy-start = (bf16[1,1,1200,1200]{3,2,1,0:T(8,128)(2,1)S(1)}, bf16[1,1,1200,1200]{3,2,1,0:T(8,128)(2,1)}, u32[]{:S(2)}) copy-start(bf16[1,1,1200,1200]{3,2,1,0:T(8,128)(2,1)} %ops.5) | copy-start | bytes 8640004
  29.9 1.4 %copy-start.3 = (bf16[4,384,512]{2,1,0:T(8,128)(2,1)S(1)}, bf16[4,384,512]{2,1,0:T(8,128)(2,1)}, u32[]{:S(2)}) copy-start(bf16[4,384,512]{2,1,0:T(8,128)(2,1)} %copy-done.2) | copy-start | bytes 4718596
  31.3 1.4 %copy-start.7 = (bf16[4,512,384]{2,1,0:T(8,128)(2,1)S(1)}, bf16[4,512,384]{2,1,0:T(8,128)(2,1)}, u32[]{:S(2)}) copy-start(bf16[4,512,384]{2,1,0:T(8,128)(2,1)} %copy-done.6) | copy-start | bytes 4718596
  33.6 22.7 %copy-start.1 = (bf16[1,1,1200,1200]{3,2,1,0:T(8,128)(2,1)S(1)}, bf16[1,1,1200,1200]{3,2,1,0:T(8,128)(2,1)}, u32[]{:S(2)}) copy-start(bf16[1,1,1200,1200]{3,2,1,0:T(8,128)(2,1)} %ops.5) | copy-start | bytes 8640004
  41.1 15.2 %all-to-all-start.1 = ((f32[32,8,128]{2,1,0:T(8,128)}), f32[32,8,128]{2,1,0:T(8,128)S(1)}, u32[]{:S(2)}, u32[]{:S(2)}) async-start(f32[32,8,128]{2,1,0:T(8,128)} %copy-done.12), calls=%async_computation.1 | async-start | bytes 262144 | tf_op jit(solution)/shard_map/all_to_all | solution.py:365
  45.0 8.4 %collective-permute-start.4 = (f32[16,384]{1,0:T(8,128)}, f32[16,384]{1,0:T(8,128)S(1)}, u32[]{:S(2)}, u32[]{:S(2)}) collective-permute-start(f32[16,384]{1,0:T(8,128)} %get-tuple-element.54), channel_id=1, source_target_pairs={{0,4},{4,0},{8,12},{12,8},{16,20},{20,16},{24,28},{28,24},{1,5},{5... | collective-permute-start | bytes 73736 | tf_op jit(solution)/shard_map/ppermute | solution.py:85
  45.1 8.3 %collective-permute-start.5 = (f32[16,384]{1,0:T(8,128)}, f32[16,384]{1,0:T(8,128)S(1)}, u32[]{:S(2)}, u32[]{:S(2)}) collective-permute-start(f32[16,384]{1,0:T(8,128)} %copy-done.54), channel_id=1, source_target_pairs={{4,8},{8,4},{12,16},{16,12},{20,24},{24,20},{5,9},{9,5},{13,17},{1... | collective-permute-start | bytes 73736 | tf_op jit(solution)/shard_map/ppermute | solution.py:85
  49.4 4.0 %collective-permute-start.6 = (f32[16,384]{1,0:T(8,128)}, f32[16,384]{1,0:T(8,128)S(1)}, u32[]{:S(2)}, u32[]{:S(2)}) collective-permute-start(f32[16,384]{1,0:T(8,128)} %copy-done.52), channel_id=1, source_target_pairs={{0,1},{1,0},{2,3},{3,2},{4,5},{5,4},{6,7},{7,6},{8,9},{9,8},{10,11... | collective-permute-start | bytes 73736 | tf_op jit(solution)/shard_map/ppermute | solution.py:85
  50.4 5.3 %collective-permute-start.7 = (f32[16,384]{1,0:T(8,128)}, f32[16,384]{1,0:T(8,128)S(1)}, u32[]{:S(2)}, u32[]{:S(2)}) collective-permute-start(f32[16,384]{1,0:T(8,128)} %copy-done.49), channel_id=1, source_target_pairs={{1,2},{2,1},{5,6},{6,5},{9,10},{10,9},{13,14},{14,13},{17,18},{18,... | collective-permute-start | bytes 73736 | tf_op jit(solution)/shard_map/ppermute | solution.py:85
  56.3 1.4 %copy-start.4 = (bf16[4,384,512]{2,1,0:T(8,128)(2,1)S(1)}, bf16[4,384,512]{2,1,0:T(8,128)(2,1)}, u32[]{:S(2)}) copy-start(bf16[4,384,512]{2,1,0:T(8,128)(2,1)} %copy-done.2) | copy-start | bytes 4718596
  57.7 1.4 %copy-start.8 = (bf16[4,512,384]{2,1,0:T(8,128)(2,1)S(1)}, bf16[4,512,384]{2,1,0:T(8,128)(2,1)}, u32[]{:S(2)}) copy-start(bf16[4,512,384]{2,1,0:T(8,128)(2,1)} %copy-done.6) | copy-start | bytes 4718596
  59.1 0.9 copy-start.30
  68.6 15.9 %all-to-all-start.2 = ((f32[32,8,128]{2,1,0:T(8,128)}), f32[32,8,128]{2,1,0:T(8,128)S(1)}, u32[]{:S(2)}, u32[]{:S(2)}) async-start(f32[32,8,128]{2,1,0:T(8,128)} %copy-done.11), calls=%async_computation.2 | async-start | bytes 262144 | tf_op jit(solution)/shard_map/all_to_all | solution.py:365
  73.3 8.3 %collective-permute-start.8 = (f32[16,384]{1,0:T(8,128)}, f32[16,384]{1,0:T(8,128)S(1)}, u32[]{:S(2)}, u32[]{:S(2)}) collective-permute-start(f32[16,384]{1,0:T(8,128)} %copy-done.55), channel_id=1, source_target_pairs={{0,4},{4,0},{8,12},{12,8},{16,20},{20,16},{24,28},{28,24},{1,5},{5... | collective-permute-start | bytes 73736 | tf_op jit(solution)/shard_map/ppermute | solution.py:85
  73.4 8.2 %collective-permute-start.9 = (f32[16,384]{1,0:T(8,128)}, f32[16,384]{1,0:T(8,128)S(1)}, u32[]{:S(2)}, u32[]{:S(2)}) collective-permute-start(f32[16,384]{1,0:T(8,128)} %copy-done.53), channel_id=1, source_target_pairs={{4,8},{8,4},{12,16},{16,12},{20,24},{24,20},{5,9},{9,5},{13,17},{1... | collective-permute-start | bytes 73736 | tf_op jit(solution)/shard_map/ppermute | solution.py:85
  77.6 4.0 %collective-permute-start.10 = (f32[16,384]{1,0:T(8,128)}, f32[16,384]{1,0:T(8,128)S(1)}, u32[]{:S(2)}, u32[]{:S(2)}) collective-permute-start(f32[16,384]{1,0:T(8,128)} %copy-done.51), channel_id=1, source_target_pairs={{0,1},{1,0},{2,3},{3,2},{4,5},{5,4},{6,7},{7,6},{8,9},{9,8},{10,11... | collective-permute-start | bytes 73736 | tf_op jit(solution)/shard_map/ppermute | solution.py:85
  78.6 5.3 %collective-permute-start.11 = (f32[16,384]{1,0:T(8,128)}, f32[16,384]{1,0:T(8,128)S(1)}, u32[]{:S(2)}, u32[]{:S(2)}) collective-permute-start(f32[16,384]{1,0:T(8,128)} %copy-done.48), channel_id=1, source_target_pairs={{1,2},{2,1},{5,6},{6,5},{9,10},{10,9},{13,14},{14,13},{17,18},{18,... | collective-permute-start | bytes 73736 | tf_op jit(solution)/shard_map/ppermute | solution.py:85
  84.5 1.4 %copy-start.5 = (bf16[4,384,512]{2,1,0:T(8,128)(2,1)S(1)}, bf16[4,384,512]{2,1,0:T(8,128)(2,1)}, u32[]{:S(2)}) copy-start(bf16[4,384,512]{2,1,0:T(8,128)(2,1)} %copy-done.2) | copy-start | bytes 4718596
  86.0 1.4 %copy-start.9 = (bf16[4,512,384]{2,1,0:T(8,128)(2,1)S(1)}, bf16[4,512,384]{2,1,0:T(8,128)(2,1)}, u32[]{:S(2)}) copy-start(bf16[4,512,384]{2,1,0:T(8,128)(2,1)} %copy-done.6) | copy-start | bytes 4718596
  99.5 15.3 %all-to-all-start.3 = ((f32[32,8,128]{2,1,0:T(8,128)}), f32[32,8,128]{2,1,0:T(8,128)S(1)}, u32[]{:S(2)}, u32[]{:S(2)}) async-start(f32[32,8,128]{2,1,0:T(8,128)} %copy-done.10), calls=%async_computation.3 | async-start | bytes 262144 | tf_op jit(solution)/shard_map/all_to_all | solution.py:365
  104.2 8.3 %collective-permute-start.12 = (f32[16,384]{1,0:T(8,128)}, f32[16,384]{1,0:T(8,128)S(1)}, u32[]{:S(2)}, u32[]{:S(2)}) collective-permute-start(f32[16,384]{1,0:T(8,128)} %copy-done.50), channel_id=1, source_target_pairs={{0,4},{4,0},{8,12},{12,8},{16,20},{20,16},{24,28},{28,24},{1,5},{5... | collective-permute-start | bytes 73736 | tf_op jit(solution)/shard_map/ppermute | solution.py:85
  104.3 8.2 %collective-permute-start.13 = (f32[16,384]{1,0:T(8,128)}, f32[16,384]{1,0:T(8,128)S(1)}, u32[]{:S(2)}, u32[]{:S(2)}) collective-permute-start(f32[16,384]{1,0:T(8,128)} %copy-done.47), channel_id=1, source_target_pairs={{4,8},{8,4},{12,16},{16,12},{20,24},{24,20},{5,9},{9,5},{13,17},{1... | collective-permute-start | bytes 73736 | tf_op jit(solution)/shard_map/ppermute | solution.py:85
  108.5 4.0 %collective-permute-start.14 = (f32[16,384]{1,0:T(8,128)}, f32[16,384]{1,0:T(8,128)S(1)}, u32[]{:S(2)}, u32[]{:S(2)}) collective-permute-start(f32[16,384]{1,0:T(8,128)} %copy-done.46), channel_id=1, source_target_pairs={{0,1},{1,0},{2,3},{3,2},{4,5},{5,4},{6,7},{7,6},{8,9},{9,8},{10,11... | collective-permute-start | bytes 73736 | tf_op jit(solution)/shard_map/ppermute | solution.py:85
  109.5 5.3 %collective-permute-start.15 = (f32[16,384]{1,0:T(8,128)}, f32[16,384]{1,0:T(8,128)S(1)}, u32[]{:S(2)}, u32[]{:S(2)}) collective-permute-start(f32[16,384]{1,0:T(8,128)} %copy-done.45), channel_id=1, source_target_pairs={{1,2},{2,1},{5,6},{6,5},{9,10},{10,9},{13,14},{14,13},{17,18},{18,... | collective-permute-start | bytes 73736 | tf_op jit(solution)/shard_map/ppermute | solution.py:85
  114.8 0.9 copy-start.14
  (45 other events, 31.3 us)

commit v4 on v3

--- a/solution.py
+++ b/solution.py
@@ -64,6 +64,8 @@
         low, high = faces[2 * i], faces[2 * i + 1]
         sent[2 * i][...] = jnp.where(even, high, low)
         sent[2 * i + 1][...] = jnp.where(even, low, high)
+        sent[2 * i].push()
+        sent[2 * i + 1].push()
 
 
 def across_faces(z, got):
@@ -87,7 +89,7 @@
 
 
 def prepare(z, traces, counts, padded, masks, *sent):
-    padded[...] = jnp.zeros_like(padded)
+    padded[...] = jnp.zeros(padded.shape, F32)
     for f in range(4):
         for j in range(z.modes):
             padded[f, j : j + 1, 0 : z.face] = traces[0, 0, j, f : f + 1]
@@ -115,7 +117,7 @@
         backward[f] = (iota((z.width, z.lanes), 1) == there).astype(F32).astype(BF16)
 
 
-def couple(z, padded, masks, loads, got0, got1, got2, got3, across, local_tile, sent, aug, small):
+def couple(z, padded, masks, got0, got1, got2, got3, loads, across, local_tile, sent, aug, small):
     near = across_faces(z, (got0, got1, got2, got3))
     live = [padded[f] * masks[f] for f in range(4)]
     diagonal = sum(dot(live[f], padded[f], (1, 1)) for f in range(4))
@@ -131,7 +133,7 @@
     small[...] = jnp.zeros_like(small)
     for j in range(z.modes):
         small[j : j + 1, :] = loads[0, j]
-    local_tile[...] = jnp.zeros_like(local_tile)
+    local_tile[...] = jnp.zeros(local_tile.shape, F32)
     local_tile[:, FIRST_LANE : FIRST_LANE + z.cases] = dot(inverse, small[...])
     local_tile[:, INVERSE_LANE : INVERSE_LANE + 8] = inverse
     for f in range(4):
@@ -139,6 +141,7 @@
         coupling = dot(live[f], near[f], (1, 1))
         local_tile[:, 8 * f : 8 * f + 8] = dot(inverse, coupling)
     sent[...] = jnp.broadcast_to(local_tile[...][None], sent.shape)
+    sent.push()
 
 
 def lifted(z, amplitudes, lift_rows, f):
@@ -185,6 +188,7 @@
     for i, scalar in enumerate(scalars):
         values = jnp.where((row == 0) & (col == SCALAR_LANE + i), scalar, values)
     sent[...] = jnp.broadcast_to(values[None], sent.shape)
+    sent.push()
 
 
 def scalar_of(total, i):
@@ -224,7 +228,7 @@
 
 
 def begin(
-    z, received, padded, across, masks, primal, ops, forward, backward, local_tile,
+    z, received, padded, across, masks, local_tile, forward, ops, primal, backward,
     solve_rows, rows, lift_rows, multipliers, faces, sent, to0, to1, to2, to3,
     matrix, local, product, tile,
 ):
@@ -265,10 +269,13 @@
         lift_rows[f] = jnp.concatenate([own * SIGNS[f], near * -SIGNS[f]], axis=0)
         fields.append(lifted(z, amplitudes, lift_rows, f))
         multipliers[f] = fields[f]
+    for item in (solve_rows, rows, lift_rows, multipliers):
+        item.push()
     image = primal[0, 0] - apply(z, fields, ops, forward, local)
     image = canonical(z, image, backward, product)
     for f in range(4):
         faces[f] = image[f]
+    faces.push()
     send_faces(z, image, (to0, to1, to2, to3))
     send_coarse(z, image, rows, [], sent, tile)
 
@@ -279,7 +286,7 @@
 
 
 def first_direction(
-    z, received, got0, got1, got2, got3, faces, masks, ops, forward, backward, solve_rows, rows, lift_rows,
+    z, received, got0, got1, got2, got3, faces, masks, solve_rows, lift_rows, forward, ops, backward, rows,
     residual, direction, image, sent, to0, to1, to2, to3,
     local, product, tile,
 ):
@@ -287,11 +294,15 @@
     field = jumped(z, masks, faces, (got0, got1, got2, got3))
     weights = face_weights(z)
     moved = [field[f] - lifted(z, amplitudes, lift_rows, f) for f in range(4)]
-    found = canonical(z, apply(z, moved, ops, forward, local), backward, product)
     for f in range(4):
         residual[f] = field[f]
         direction[f] = moved[f]
+    residual.push()
+    direction.push()
+    found = canonical(z, apply(z, moved, ops, forward, local), backward, product)
+    for f in range(4):
         image[f] = found[f]
+    image.push()
     gamma = sum(weights[f] * total(field[f] * moved[f]) for f in range(4))
     curvature = sum(SIGNS[f] * total(moved[f] * found[f]) for f in range(4))
     send_faces(z, found, (to0, to1, to2, to3))
@@ -299,8 +310,8 @@
 
 
 def second_direction(
-    z, received, got0, got1, got2, got3, faces, masks, ops, forward, backward, solve_rows, lift_rows,
-    multipliers, residual, direction,
+    z, received, got0, got1, got2, got3, faces, masks, solve_rows, lift_rows,
+    multipliers, residual, direction, forward, ops, backward,
     next_multipliers, next_residual, projected, image, fresh, sums, sent, to0, to1, to2, to3,
     local, product,
 ):
@@ -318,9 +329,12 @@
         moved.append(direction[f] - alpha * (field[f] - lifted(z, amplitudes, lift_rows, f)))
         next_residual[f] = left[f]
         projected[f] = moved[f]
+    for item in (sums, image, next_multipliers, next_residual, projected):
+        item.push()
     found = canonical(z, apply(z, moved, ops, forward, local), backward, product)
     for f in range(4):
         fresh[f] = found[f]
+    fresh.push()
     send_faces(z, found, (to0, to1, to2, to3))
     gamma = sum(weights[f] * total(left[f] * moved[f]) for f in range(4))
     straight = sum(SIGNS[f] * total(moved[f] * found[f]) for f in range(4))
@@ -346,16 +360,73 @@
         out_residual[0, 0, f] = (residual[f] - alpha * (field[f] + beta * image[f]))[:, 0 : z.face]
 
 
-def call(z, kernel, outs, args, scratch=(), flops=0):
+class Coming:
+    def __init__(self, source, held, semaphore):
+        self.held = held
+        self.copy = pltpu.make_async_copy(source, held, semaphore)
+        self.copy.start()
+
+    def ready(self):
+        if self.copy is not None:
+            self.copy.wait()
+            self.copy = None
+        return self.held
+
+    def __getitem__(self, index):
+        return self.ready()[index]
+
+
+class Going:
+    def __init__(self, held, target, semaphore):
+        self.held = held
+        self.copy = pltpu.make_async_copy(held, target, semaphore)
+        self.shape, self.dtype = held.shape, held.dtype
+        self.started = False
+
+    def __getitem__(self, index):
+        return self.held[index]
+
+    def __setitem__(self, index, values):
+        self.held[index] = values
+
+    def push(self):
+        if not self.started:
+            self.copy.start()
+            self.started = True
+
+
+def call(z, kernel, outs, args, scratch=(), flops=0, near=0):
     shapes = [jax.ShapeDtypeStruct(shape, dtype) for shape, dtype in outs]
     moved = sum(a.size * a.dtype.itemsize for a in args) + sum(s.size * s.dtype.itemsize for s in shapes)
+    far = len(args) - near
+
+    def run(*refs):
+        refs = list(refs)
+        take = lambda n: [refs.pop(0) for _ in range(n)]
+        sources, others, targets = take(far), take(near), take(len(outs))
+        held, made, work, semaphores = take(far), take(len(outs)), take(len(scratch)), refs[0]
+        coming = [Coming(a, b, semaphores.at[i]) for i, (a, b) in enumerate(zip(sources, held))]
+        going = [Going(a, b, semaphores.at[far + i]) for i, (a, b) in enumerate(zip(made, targets))]
+        kernel(z, *coming, *others, *going, *work)
+        for item in going:
+            item.push()
+        for item in coming:
+            item.ready()
+        for item in going:
+            item.copy.wait()
+
+    specs = [pl.BlockSpec(memory_space=pltpu.HBM)] * far
+    specs += [pl.BlockSpec(memory_space=SMEM if a.ndim == 3 and a.size == 4 else VMEM) for a in args[far:]]
+    buffers = [VMEM(a.shape, a.dtype) for a in args[:far]] + [VMEM(shape, dtype) for shape, dtype in outs]
     return pl.pallas_call(
-        functools.partial(kernel, z),
+        run,
         out_shape=shapes,
-        in_specs=[pl.BlockSpec(memory_space=SMEM if a.ndim == 3 and a.size == 4 else VMEM) for a in args],
-        out_specs=[pl.BlockSpec(memory_space=VMEM) for _ in shapes],
-        scratch_shapes=[VMEM(shape, dtype) for shape, dtype in scratch],
-        compiler_params=pltpu.CompilerParams(vmem_limit_bytes=40 * 2**20),
+        in_specs=specs,
+        out_specs=[pl.BlockSpec(memory_space=pltpu.HBM) for _ in shapes],
+        scratch_shapes=buffers
+        + [VMEM(shape, dtype) for shape, dtype in scratch]
+        + [pltpu.SemaphoreType.DMA((far + len(outs),))],
+        compiler_params=pltpu.CompilerParams(vmem_limit_bytes=32 * 2**20),
         cost_estimate=pl.CostEstimate(flops=flops, bytes_accessed=moved, transcendentals=0),
         name=kernel.__name__,
     )(*args)
@@ -379,38 +450,38 @@
 
     padded, masks, *trace_faces = call(
         z, prepare, [mode_rows, mode_rows] + [((8, z.lanes), F32)] * 4,
-        [jnp.transpose(traces, (0, 1, 3, 2, 4)), counts],
+        [jnp.transpose(traces, (0, 1, 3, 2, 4)), counts], near=2,
     )
     got = exchange(trace_faces)
     across, local_tile, blocks = call(
         z, couple, [mode_rows, tile, sent],
-        [padded, masks, jnp.transpose(loads, (0, 2, 1, 3)), *got],
-        [tile, ((8, z.cases), F32)],
+        [padded, masks, *got, jnp.transpose(loads, (0, 2, 1, 3))],
+        [tile, ((8, z.cases), F32)], near=1,
     )
     blocks = gather(blocks)
     forward, backward = call(
         z, tables, [((4, z.lanes, z.width), BF16), ((4, z.width, z.lanes), BF16)], [maps],
-        [((8, z.padded), jnp.int32)], product_flops,
+        [((8, z.padded), jnp.int32)], product_flops, near=1,
     )
     solve_rows, rows, lift_rows, multipliers, faces, coarse, *sent_faces = call(
         z, begin,
         [((40, z.rows), F32), pair_rows, pair_rows, field, field, sent] + to_faces,
-        [blocks, padded, across, masks, primal, ops, forward, backward, local_tile],
+        [blocks, padded, across, masks, local_tile, forward, ops, primal, backward],
         [((z.rows, columns), F32), padded_rows, padded_rows, tile], product_flops,
     )
     coarse, got = gather(coarse), exchange(sent_faces)
     residual, direction, faces, coarse, *sent_faces = call(
         z, first_direction,
         [field, field, field, sent] + to_faces,
-        [coarse, *got, faces, masks, ops, forward, backward, solve_rows, rows, lift_rows],
+        [coarse, *got, faces, masks, solve_rows, lift_rows, forward, ops, backward, rows],
         [padded_rows, padded_rows, tile], product_flops,
     )
     coarse, got = gather(coarse), exchange(sent_faces)
     multipliers, residual, projected, image, faces, sums, coarse, *sent_faces = call(
         z, second_direction,
         [field, field, field, field, field, tile, sent] + to_faces,
-        [coarse, *got, faces, masks, ops, forward, backward, solve_rows, lift_rows,
-         multipliers, residual, direction],
+        [coarse, *got, faces, masks, solve_rows, lift_rows,
+         multipliers, residual, direction, forward, ops, backward],
         [padded_rows, padded_rows], product_flops,
     )
     coarse, got = gather(coarse), exchange(sent_faces)

time: 122 us -> 133 us (1.090)
  Pallas kernels: 11.5 us -> 22.7 us
    pallas_call x7, Pallas kernels: 11.5 us -> 22.7 us  [call(): pl.pallas_call(run, out_shape=shapes, in_specs=specs, out_specs=[pl.Block...]
where the time goes in v4:
time: 133 us; the launch traced here: 131 us
  starting transfers between devices  51.6 us (39%)
  local copies, waits for them, and re-layouts  45.6 us (34%)
  Pallas kernels  22.7 us (17%)
  waiting for transfers between devices  10.3 us (8%)
    unnamed x114, local copies, waits for them, and re-layouts  45.6 us
    ppermute x16, starting transfers between devices, exchange(): got.append(lax.ppermute(values, axis, pairs))  33.7 us
    pallas_call x7, Pallas kernels, call(): pl.pallas_call(run, out_shape=shapes, in_specs=specs, out_specs=[pl.Block...  22.7 us
    all_to_all x4, starting transfers between devices, gather(): return lax.all_to_all(values, AXES, 0, 0, tiled=True)  17.8 us
    ppermute x16, waiting for transfers between devices, exchange(): got.append(lax.ppermute(values, axis, pairs))  7.68 us
  transfers between devices with their start and end apart: 20, of which 5 were waited for; matrix products, arithmetic and copies ran while one was open for 0% of the time, Pallas kernels for 1%

profile of v4, /device:TPU:5, one launch (start us, length us, event | category | flops | bytes accessed | tf_op | source)
XLA Modules:
  0.0 131.1 jit_solution(13834356125592959607)
XLA Ops:
  3.0 4.4 %collective-permute-start.1 = (f32[8,384]{1,0:T(8,128)S(1)}, f32[8,384]{1,0:T(8,128)S(1)}, u32[]{:S(2)}, u32[]{:S(2)}) collective-permute-start(f32[8,384]{1,0:T(8,128)S(1)} %get-tuple-element.45), channel_id=1, source_target_pairs={{4,8},{8,4},{12,16},{16,12},{20,24},{24,20},{5,9},{9,5},{13,17},{1... | collective-permute-start | bytes 36872 | tf_op jit(solution)/shard_map/ppermute | solution.py:87
  7.3 1.3 collective-permute-start.2
  8.6 3.0 %collective-permute-start.3 = (f32[8,384]{1,0:T(8,128)S(1)}, f32[8,384]{1,0:T(8,128)S(1)}, u32[]{:S(2)}, u32[]{:S(2)}) collective-permute-start(f32[8,384]{1,0:T(8,128)S(1)} %get-tuple-element.47), channel_id=1, source_target_pairs={{1,2},{2,1},{5,6},{6,5},{9,10},{10,9},{13,14},{14,13},{17,18},{18,... | collective-permute-start | bytes 36872 | tf_op jit(solution)/shard_map/ppermute | solution.py:87
  11.7 1.9 %collective-permute-done.3.refs_5_ = f32[8,384]{1,0:T(8,128)S(1)} collective-permute-done((f32[8,384]{1,0:T(8,128)S(1)}, f32[8,384]{1,0:T(8,128)S(1)}, u32[]{:S(2)}, u32[]{:S(2)}) %collective-permute-start.3) | collective-permute-done | bytes 12320 | tf_op jit(solution)/shard_map/ppermute | solution.py:87
  14.3 2.6 %couple.1 = (f32[4,8,384]{2,1,0:T(8,128)S(1)}, f32[8,128]{1,0:T(8,128)S(1)}, f32[32,8,128]{2,1,0:T(8,128)}) custom-call(f32[4,8,384]{2,1,0:T(8,128)S(1)} %get-tuple-element.42.refs_0_.refs_1_, f32[4,8,384]{2,1,0:T(8,128)S(1)} %get-tuple-element.43.refs_1_.refs_3_.refs_6_, f32[8,384]{1,0:T(8,128)S(1)} %collective-permute-done.refs_2_, ...), custom_call_target="tpu_custom_call" | custom-call | bytes 332160 | tf_op jit(solution)/shard_map/couple/pallas_call | solution.py:421
  16.9 4.8 %all-to-all-start = ((f32[32,8,128]{2,1,0:T(8,128)}), f32[32,8,128]{2,1,0:T(8,128)S(1)}, u32[]{:S(2)}, u32[]{:S(2)}) async-start(f32[32,8,128]{2,1,0:T(8,128)} %get-tuple-element.48), calls=%async_computation | async-start | bytes 262144 | tf_op jit(solution)/shard_map/all_to_all | solution.py:436
  22.4 1.3 tables.1
  24.8 1.1 copy-done.6
  26.0 2.6 %all-to-all-done.refs_0_ = f32[32,8,128]{2,1,0:T(8,128)S(1)} async-done(((f32[32,8,128]{2,1,0:T(8,128)}), f32[32,8,128]{2,1,0:T(8,128)S(1)}, u32[]{:S(2)}, u32[]{:S(2)}) %all-to-all-start) | async-done | bytes 131104 | tf_op jit(solution)/shard_map/all_to_all | solution.py:436
  28.6 1.9 %copy-done = bf16[1,1,1200,1200]{3,2,1,0:T(8,128)(2,1)S(1)} copy-done((bf16[1,1,1200,1200]{3,2,1,0:T(8,128)(2,1)S(1)}, bf16[1,1,1200,1200]{3,2,1,0:T(8,128)(2,1)}, u32[]{:S(2)}) %copy-start) | copy-done | bytes 2880024
  30.4 1.4 %copy-done.3 = bf16[4,384,512]{2,1,0:T(8,128)(2,1)S(1)} copy-done((bf16[4,384,512]{2,1,0:T(8,128)(2,1)S(1)}, bf16[4,384,512]{2,1,0:T(8,128)(2,1)}, u32[]{:S(2)}) %copy-start.3) | copy-done | bytes 1572888
  31.8 1.4 %copy-done.7 = bf16[4,512,384]{2,1,0:T(8,128)(2,1)S(1)} copy-done((bf16[4,512,384]{2,1,0:T(8,128)(2,1)S(1)}, bf16[4,512,384]{2,1,0:T(8,128)(2,1)}, u32[]{:S(2)}) %copy-start.7) | copy-done | bytes 1572888
  34.1 5.7 %begin.1 = (f32[40,256]{1,0:T(8,128)S(1)}, f32[4,16,384]{2,1,0:T(8,128)S(1)}, f32[4,16,384]{2,1,0:T(8,128)S(1)}, f32[4,16,384]{2,1,0:T(8,128)S(1)}, f32[4,16,384...) custom-call(f32[32,8,128]{2,1,0:T(8,128)S(1)} %all-to-all-done.refs_, ...), custom_call_target="tpu_custom_call" | custom-call | flops 46080000 | bytes 7048704 | tf_op jit(solution)/shard_map/begin/pallas_call | solution.py:421
  44.2 3.8 %all-to-all-start.1 = ((f32[32,8,128]{2,1,0:T(8,128)}), f32[32,8,128]{2,1,0:T(8,128)S(1)}, u32[]{:S(2)}, u32[]{:S(2)}) async-start(f32[32,8,128]{2,1,0:T(8,128)} %copy-done.12), calls=%async_computation.1 | async-start | bytes 262144 | tf_op jit(solution)/shard_map/all_to_all | solution.py:436
  48.2 4.3 %collective-permute-start.5 = (f32[16,384]{1,0:T(8,128)}, f32[16,384]{1,0:T(8,128)S(1)}, u32[]{:S(2)}, u32[]{:S(2)}) collective-permute-start(f32[16,384]{1,0:T(8,128)} %copy-done.54), channel_id=1, source_target_pairs={{4,8},{8,4},{12,16},{16,12},{20,24},{24,20},{5,9},{9,5},{13,17},{1... | collective-permute-start | bytes 73736 | tf_op jit(solution)/shard_map/ppermute | solution.py:87
  53.5 3.0 %collective-permute-start.7 = (f32[16,384]{1,0:T(8,128)}, f32[16,384]{1,0:T(8,128)S(1)}, u32[]{:S(2)}, u32[]{:S(2)}) collective-permute-start(f32[16,384]{1,0:T(8,128)} %copy-done.49), channel_id=1, source_target_pairs={{1,2},{2,1},{5,6},{6,5},{9,10},{10,9},{13,14},{14,13},{17,18},{18,... | collective-permute-start | bytes 73736 | tf_op jit(solution)/shard_map/ppermute | solution.py:87
  57.1 1.7 %collective-permute-done.7.refs_4_ = f32[16,384]{1,0:T(8,128)S(1)} collective-permute-done((f32[16,384]{1,0:T(8,128)}, f32[16,384]{1,0:T(8,128)S(1)}, u32[]{:S(2)}, u32[]{:S(2)}) %collective-permute-start.7) | collective-permute-done | bytes 24608 | tf_op jit(solution)/shard_map/ppermute | solution.py:87
  59.4 1.4 %copy-done.4 = bf16[4,384,512]{2,1,0:T(8,128)(2,1)S(1)} copy-done((bf16[4,384,512]{2,1,0:T(8,128)(2,1)S(1)}, bf16[4,384,512]{2,1,0:T(8,128)(2,1)}, u32[]{:S(2)}) %copy-start.4) | copy-done | bytes 1572888
  60.8 1.4 %copy-done.8 = bf16[4,512,384]{2,1,0:T(8,128)(2,1)S(1)} copy-done((bf16[4,512,384]{2,1,0:T(8,128)(2,1)S(1)}, bf16[4,512,384]{2,1,0:T(8,128)(2,1)}, u32[]{:S(2)}) %copy-start.8) | copy-done | bytes 1572888
  65.5 4.9 %first_direction.1 = (f32[4,16,384]{2,1,0:T(8,128)S(1)}, f32[4,16,384]{2,1,0:T(8,128)S(1)}, f32[4,16,384]{2,1,0:T(8,128)S(1)}, f32[32,8,128]{2,1,0:T(8,128)S(1)}...) custom-call(f32[32,8,128]{2,1,0:T(8,128)S(1)} %all-to-all-done.1.refs_0_, ...), custom_call_target="tpu_custom_call" | custom-call | flops 46080000 | bytes 7164416 | tf_op jit(solution)/shard_map/first_direction/pallas_call | solution.py:421
  74.8 4.6 %all-to-all-start.2 = ((f32[32,8,128]{2,1,0:T(8,128)}), f32[32,8,128]{2,1,0:T(8,128)S(1)}, u32[]{:S(2)}, u32[]{:S(2)}) async-start(f32[32,8,128]{2,1,0:T(8,128)} %copy-done.11), calls=%async_computation.2 | async-start | bytes 262144 | tf_op jit(solution)/shard_map/all_to_all | solution.py:436
  79.6 4.2 %collective-permute-start.9 = (f32[16,384]{1,0:T(8,128)}, f32[16,384]{1,0:T(8,128)S(1)}, u32[]{:S(2)}, u32[]{:S(2)}) collective-permute-start(f32[16,384]{1,0:T(8,128)} %copy-done.53), channel_id=1, source_target_pairs={{4,8},{8,4},{12,16},{16,12},{20,24},{24,20},{5,9},{9,5},{13,17},{1... | collective-permute-start | bytes 73736 | tf_op jit(solution)/shard_map/ppermute | solution.py:87
  84.8 3.0 %collective-permute-start.11 = (f32[16,384]{1,0:T(8,128)}, f32[16,384]{1,0:T(8,128)S(1)}, u32[]{:S(2)}, u32[]{:S(2)}) collective-permute-start(f32[16,384]{1,0:T(8,128)} %copy-done.48), channel_id=1, source_target_pairs={{1,2},{2,1},{5,6},{6,5},{9,10},{10,9},{13,14},{14,13},{17,18},{18,... | collective-permute-start | bytes 73736 | tf_op jit(solution)/shard_map/ppermute | solution.py:87
  88.4 1.7 %collective-permute-done.11.refs_4_ = f32[16,384]{1,0:T(8,128)S(1)} collective-permute-done((f32[16,384]{1,0:T(8,128)}, f32[16,384]{1,0:T(8,128)S(1)}, u32[]{:S(2)}, u32[]{:S(2)}) %collective-permute-start.11) | collective-permute-done | bytes 24608 | tf_op jit(solution)/shard_map/ppermute | solution.py:87
  90.7 1.4 %copy-done.5 = bf16[4,384,512]{2,1,0:T(8,128)(2,1)S(1)} copy-done((bf16[4,384,512]{2,1,0:T(8,128)(2,1)S(1)}, bf16[4,384,512]{2,1,0:T(8,128)(2,1)}, u32[]{:S(2)}) %copy-start.5) | copy-done | bytes 1572888
  92.1 1.4 %copy-done.9 = bf16[4,512,384]{2,1,0:T(8,128)(2,1)S(1)} copy-done((bf16[4,512,384]{2,1,0:T(8,128)(2,1)S(1)}, bf16[4,512,384]{2,1,0:T(8,128)(2,1)}, u32[]{:S(2)}) %copy-start.9) | copy-done | bytes 1572888
  97.7 5.3 %second_direction.1 = (f32[4,16,384]{2,1,0:T(8,128)S(1)}, f32[4,16,384]{2,1,0:T(8,128)S(1)}, f32[4,16,384]{2,1,0:T(8,128)S(1)}, f32[4,16,384]{2,1,0:T(8,128)S(1)...) custom-call(f32[32,8,128]{2,1,0:T(8,128)S(1)} %all-to-all-done.2.ref, ...), custom_call_target="tpu_custom_call" | custom-call | flops 46080000 | bytes 7561728 | tf_op jit(solution)/shard_map/second_direction/pallas_call | solution.py:421
  109.3 4.6 %all-to-all-start.3 = ((f32[32,8,128]{2,1,0:T(8,128)}), f32[32,8,128]{2,1,0:T(8,128)S(1)}, u32[]{:S(2)}, u32[]{:S(2)}) async-start(f32[32,8,128]{2,1,0:T(8,128)} %copy-done.10), calls=%async_computation.3 | async-start | bytes 262144 | tf_op jit(solution)/shard_map/all_to_all | solution.py:436
  114.0 4.2 %collective-permute-start.13 = (f32[16,384]{1,0:T(8,128)}, f32[16,384]{1,0:T(8,128)S(1)}, u32[]{:S(2)}, u32[]{:S(2)}) collective-permute-start(f32[16,384]{1,0:T(8,128)} %copy-done.47), channel_id=1, source_target_pairs={{4,8},{8,4},{12,16},{16,12},{20,24},{24,20},{5,9},{9,5},{13,17},{1... | collective-permute-start | bytes 73736 | tf_op jit(solution)/shard_map/ppermute | solution.py:87
  119.2 3.0 %collective-permute-start.15 = (f32[16,384]{1,0:T(8,128)}, f32[16,384]{1,0:T(8,128)S(1)}, u32[]{:S(2)}, u32[]{:S(2)}) collective-permute-start(f32[16,384]{1,0:T(8,128)} %copy-done.45), channel_id=1, source_target_pairs={{1,2},{2,1},{5,6},{6,5},{9,10},{10,9},{13,14},{14,13},{17,18},{18,... | collective-permute-start | bytes 73736 | tf_op jit(solution)/shard_map/ppermute | solution.py:87
  122.2 2.3 %collective-permute-done.15.refs_4_ = f32[16,384]{1,0:T(8,128)S(1)} collective-permute-done((f32[16,384]{1,0:T(8,128)}, f32[16,384]{1,0:T(8,128)S(1)}, u32[]{:S(2)}, u32[]{:S(2)}) %collective-permute-start.15) | collective-permute-done | bytes 24608 | tf_op jit(solution)/shard_map/ppermute | solution.py:87
  129.0 2.1 %finish.1 = (f32[1,1,4,16,300]{4,3,2,1,0:T(8,128)}, f32[1,1,4,16,300]{4,3,2,1,0:T(8,128)}) custom-call(f32[32,8,128]{2,1,0:T(8,128)S(1)} %all-to-all-done.3.refs_0_, f32[16,384]{1,0:T(8,128)S(1)} %collective-permute-done.12.refs_1_, f32[16,384]{1,0:T(8,128)S(1)} %collective-permute-done.13.refs_2_, f32[16,384]{1,0:T(8,128)S(1)} %collective-permute-done.14.refs_3_, ...), custom_call_target="tpu_custom_call" | custom-call | bytes 1026048 | tf_op jit(solution)/shard_map/finish/pallas_call | solution.py:421
  (129 shorter events, 38.4 us)
Async XLA Ops:
  2.9 8.8 %collective-permute-start = (f32[8,384]{1,0:T(8,128)S(1)}, f32[8,384]{1,0:T(8,128)S(1)}, u32[]{:S(2)}, u32[]{:S(2)}) collective-permute-start(f32[8,384]{1,0:T(8,128)S(1)} %get-tuple-element.44), channel_id=1, source_target_pairs={{0,4},{4,0},{8,12},{12,8},{16,20},{20,16},{24,28},{28,24},{1,5},{5... | collective-permute-start | bytes 36872 | tf_op jit(solution)/shard_map/ppermute | solution.py:87
  3.0 8.7 %collective-permute-start.1 = (f32[8,384]{1,0:T(8,128)S(1)}, f32[8,384]{1,0:T(8,128)S(1)}, u32[]{:S(2)}, u32[]{:S(2)}) collective-permute-start(f32[8,384]{1,0:T(8,128)S(1)} %get-tuple-element.45), channel_id=1, source_target_pairs={{4,8},{8,4},{12,16},{16,12},{20,24},{24,20},{5,9},{9,5},{13,17},{1... | collective-permute-start | bytes 36872 | tf_op jit(solution)/shard_map/ppermute | solution.py:87
  7.3 4.4 %collective-permute-start.2 = (f32[8,384]{1,0:T(8,128)S(1)}, f32[8,384]{1,0:T(8,128)S(1)}, u32[]{:S(2)}, u32[]{:S(2)}) collective-permute-start(f32[8,384]{1,0:T(8,128)S(1)} %get-tuple-element.46), channel_id=1, source_target_pairs={{0,1},{1,0},{2,3},{3,2},{4,5},{5,4},{6,7},{7,6},{8,9},{9,8},{10,11... | collective-permute-start | bytes 36872 | tf_op jit(solution)/shard_map/ppermute | solution.py:87
  8.6 5.0 %collective-permute-start.3 = (f32[8,384]{1,0:T(8,128)S(1)}, f32[8,384]{1,0:T(8,128)S(1)}, u32[]{:S(2)}, u32[]{:S(2)}) collective-permute-start(f32[8,384]{1,0:T(8,128)S(1)} %get-tuple-element.47), channel_id=1, source_target_pairs={{1,2},{2,1},{5,6},{6,5},{9,10},{10,9},{13,14},{14,13},{17,18},{18,... | collective-permute-start | bytes 36872 | tf_op jit(solution)/shard_map/ppermute | solution.py:87
  16.9 11.6 %all-to-all-start = ((f32[32,8,128]{2,1,0:T(8,128)}), f32[32,8,128]{2,1,0:T(8,128)S(1)}, u32[]{:S(2)}, u32[]{:S(2)}) async-start(f32[32,8,128]{2,1,0:T(8,128)} %get-tuple-element.48), calls=%async_computation | async-start | bytes 262144 | tf_op jit(solution)/shard_map/all_to_all | solution.py:436
  23.7 1.1 copy-start.2
  24.8 1.1 copy-start.6
  28.6 1.9 %copy-start = (bf16[1,1,1200,1200]{3,2,1,0:T(8,128)(2,1)S(1)}, bf16[1,1,1200,1200]{3,2,1,0:T(8,128)(2,1)}, u32[]{:S(2)}) copy-start(bf16[1,1,1200,1200]{3,2,1,0:T(8,128)(2,1)} %refs_13_.1) | copy-start | bytes 8640004
  30.4 1.4 %copy-start.3 = (bf16[4,384,512]{2,1,0:T(8,128)(2,1)S(1)}, bf16[4,384,512]{2,1,0:T(8,128)(2,1)}, u32[]{:S(2)}) copy-start(bf16[4,384,512]{2,1,0:T(8,128)(2,1)} %copy-done.2) | copy-start | bytes 4718596
  31.8 1.4 %copy-start.7 = (bf16[4,512,384]{2,1,0:T(8,128)(2,1)S(1)}, bf16[4,512,384]{2,1,0:T(8,128)(2,1)}, u32[]{:S(2)}) copy-start(bf16[4,512,384]{2,1,0:T(8,128)(2,1)} %copy-done.6) | copy-start | bytes 4718596
  34.1 25.3 %copy-start.1 = (bf16[1,1,1200,1200]{3,2,1,0:T(8,128)(2,1)S(1)}, bf16[1,1,1200,1200]{3,2,1,0:T(8,128)(2,1)}, u32[]{:S(2)}) copy-start(bf16[1,1,1200,1200]{3,2,1,0:T(8,128)(2,1)} %refs_13_.1) | copy-start | bytes 8640004
  44.2 15.2 %all-to-all-start.1 = ((f32[32,8,128]{2,1,0:T(8,128)}), f32[32,8,128]{2,1,0:T(8,128)S(1)}, u32[]{:S(2)}, u32[]{:S(2)}) async-start(f32[32,8,128]{2,1,0:T(8,128)} %copy-done.12), calls=%async_computation.1 | async-start | bytes 262144 | tf_op jit(solution)/shard_map/all_to_all | solution.py:436
  48.1 8.4 %collective-permute-start.4 = (f32[16,384]{1,0:T(8,128)}, f32[16,384]{1,0:T(8,128)S(1)}, u32[]{:S(2)}, u32[]{:S(2)}) collective-permute-start(f32[16,384]{1,0:T(8,128)} %get-tuple-element.54), channel_id=1, source_target_pairs={{0,4},{4,0},{8,12},{12,8},{16,20},{20,16},{24,28},{28,24},{1,5},{5... | collective-permute-start | bytes 73736 | tf_op jit(solution)/shard_map/ppermute | solution.py:87
  48.2 8.3 %collective-permute-start.5 = (f32[16,384]{1,0:T(8,128)}, f32[16,384]{1,0:T(8,128)S(1)}, u32[]{:S(2)}, u32[]{:S(2)}) collective-permute-start(f32[16,384]{1,0:T(8,128)} %copy-done.54), channel_id=1, source_target_pairs={{4,8},{8,4},{12,16},{16,12},{20,24},{24,20},{5,9},{9,5},{13,17},{1... | collective-permute-start | bytes 73736 | tf_op jit(solution)/shard_map/ppermute | solution.py:87
  52.5 4.0 %collective-permute-start.6 = (f32[16,384]{1,0:T(8,128)}, f32[16,384]{1,0:T(8,128)S(1)}, u32[]{:S(2)}, u32[]{:S(2)}) collective-permute-start(f32[16,384]{1,0:T(8,128)} %copy-done.52), channel_id=1, source_target_pairs={{0,1},{1,0},{2,3},{3,2},{4,5},{5,4},{6,7},{7,6},{8,9},{9,8},{10,11... | collective-permute-start | bytes 73736 | tf_op jit(solution)/shard_map/ppermute | solution.py:87
  53.5 5.3 %collective-permute-start.7 = (f32[16,384]{1,0:T(8,128)}, f32[16,384]{1,0:T(8,128)S(1)}, u32[]{:S(2)}, u32[]{:S(2)}) collective-permute-start(f32[16,384]{1,0:T(8,128)} %copy-done.49), channel_id=1, source_target_pairs={{1,2},{2,1},{5,6},{6,5},{9,10},{10,9},{13,14},{14,13},{17,18},{18,... | collective-permute-start | bytes 73736 | tf_op jit(solution)/shard_map/ppermute | solution.py:87
  59.4 1.4 %copy-start.4 = (bf16[4,384,512]{2,1,0:T(8,128)(2,1)S(1)}, bf16[4,384,512]{2,1,0:T(8,128)(2,1)}, u32[]{:S(2)}) copy-start(bf16[4,384,512]{2,1,0:T(8,128)(2,1)} %copy-done.2) | copy-start | bytes 4718596
  60.8 1.4 %copy-start.8 = (bf16[4,512,384]{2,1,0:T(8,128)(2,1)S(1)}, bf16[4,512,384]{2,1,0:T(8,128)(2,1)}, u32[]{:S(2)}) copy-start(bf16[4,512,384]{2,1,0:T(8,128)(2,1)} %copy-done.6) | copy-start | bytes 4718596
  62.2 0.9 copy-start.30
  74.8 15.9 %all-to-all-start.2 = ((f32[32,8,128]{2,1,0:T(8,128)}), f32[32,8,128]{2,1,0:T(8,128)S(1)}, u32[]{:S(2)}, u32[]{:S(2)}) async-start(f32[32,8,128]{2,1,0:T(8,128)} %copy-done.11), calls=%async_computation.2 | async-start | bytes 262144 | tf_op jit(solution)/shard_map/all_to_all | solution.py:436
  79.4 8.3 %collective-permute-start.8 = (f32[16,384]{1,0:T(8,128)}, f32[16,384]{1,0:T(8,128)S(1)}, u32[]{:S(2)}, u32[]{:S(2)}) collective-permute-start(f32[16,384]{1,0:T(8,128)} %copy-done.55), channel_id=1, source_target_pairs={{0,4},{4,0},{8,12},{12,8},{16,20},{20,16},{24,28},{28,24},{1,5},{5... | collective-permute-start | bytes 73736 | tf_op jit(solution)/shard_map/ppermute | solution.py:87
  79.6 8.2 %collective-permute-start.9 = (f32[16,384]{1,0:T(8,128)}, f32[16,384]{1,0:T(8,128)S(1)}, u32[]{:S(2)}, u32[]{:S(2)}) collective-permute-start(f32[16,384]{1,0:T(8,128)} %copy-done.53), channel_id=1, source_target_pairs={{4,8},{8,4},{12,16},{16,12},{20,24},{24,20},{5,9},{9,5},{13,17},{1... | collective-permute-start | bytes 73736 | tf_op jit(solution)/shard_map/ppermute | solution.py:87
  83.8 4.0 %collective-permute-start.10 = (f32[16,384]{1,0:T(8,128)}, f32[16,384]{1,0:T(8,128)S(1)}, u32[]{:S(2)}, u32[]{:S(2)}) collective-permute-start(f32[16,384]{1,0:T(8,128)} %copy-done.51), channel_id=1, source_target_pairs={{0,1},{1,0},{2,3},{3,2},{4,5},{5,4},{6,7},{7,6},{8,9},{9,8},{10,11... | collective-permute-start | bytes 73736 | tf_op jit(solution)/shard_map/ppermute | solution.py:87
  84.8 5.3 %collective-permute-start.11 = (f32[16,384]{1,0:T(8,128)}, f32[16,384]{1,0:T(8,128)S(1)}, u32[]{:S(2)}, u32[]{:S(2)}) collective-permute-start(f32[16,384]{1,0:T(8,128)} %copy-done.48), channel_id=1, source_target_pairs={{1,2},{2,1},{5,6},{6,5},{9,10},{10,9},{13,14},{14,13},{17,18},{18,... | collective-permute-start | bytes 73736 | tf_op jit(solution)/shard_map/ppermute | solution.py:87
  90.7 1.4 %copy-start.5 = (bf16[4,384,512]{2,1,0:T(8,128)(2,1)S(1)}, bf16[4,384,512]{2,1,0:T(8,128)(2,1)}, u32[]{:S(2)}) copy-start(bf16[4,384,512]{2,1,0:T(8,128)(2,1)} %copy-done.2) | copy-start | bytes 4718596
  92.1 1.4 %copy-start.9 = (bf16[4,512,384]{2,1,0:T(8,128)(2,1)S(1)}, bf16[4,512,384]{2,1,0:T(8,128)(2,1)}, u32[]{:S(2)}) copy-start(bf16[4,512,384]{2,1,0:T(8,128)(2,1)} %copy-done.6) | copy-start | bytes 4718596
  109.3 15.3 %all-to-all-start.3 = ((f32[32,8,128]{2,1,0:T(8,128)}), f32[32,8,128]{2,1,0:T(8,128)S(1)}, u32[]{:S(2)}, u32[]{:S(2)}) async-start(f32[32,8,128]{2,1,0:T(8,128)} %copy-done.10), calls=%async_computation.3 | async-start | bytes 262144 | tf_op jit(solution)/shard_map/all_to_all | solution.py:436
  113.9 8.3 %collective-permute-start.12 = (f32[16,384]{1,0:T(8,128)}, f32[16,384]{1,0:T(8,128)S(1)}, u32[]{:S(2)}, u32[]{:S(2)}) collective-permute-start(f32[16,384]{1,0:T(8,128)} %copy-done.50), channel_id=1, source_target_pairs={{0,4},{4,0},{8,12},{12,8},{16,20},{20,16},{24,28},{28,24},{1,5},{5... | collective-permute-start | bytes 73736 | tf_op jit(solution)/shard_map/ppermute | solution.py:87
  114.0 8.2 %collective-permute-start.13 = (f32[16,384]{1,0:T(8,128)}, f32[16,384]{1,0:T(8,128)S(1)}, u32[]{:S(2)}, u32[]{:S(2)}) collective-permute-start(f32[16,384]{1,0:T(8,128)} %copy-done.47), channel_id=1, source_target_pairs={{4,8},{8,4},{12,16},{16,12},{20,24},{24,20},{5,9},{9,5},{13,17},{1... | collective-permute-start | bytes 73736 | tf_op jit(solution)/shard_map/ppermute | solution.py:87
  118.2 4.0 %collective-permute-start.14 = (f32[16,384]{1,0:T(8,128)}, f32[16,384]{1,0:T(8,128)S(1)}, u32[]{:S(2)}, u32[]{:S(2)}) collective-permute-start(f32[16,384]{1,0:T(8,128)} %copy-done.46), channel_id=1, source_target_pairs={{0,1},{1,0},{2,3},{3,2},{4,5},{5,4},{6,7},{7,6},{8,9},{9,8},{10,11... | collective-permute-start | bytes 73736 | tf_op jit(solution)/shard_map/ppermute | solution.py:87
  119.2 5.3 %collective-permute-start.15 = (f32[16,384]{1,0:T(8,128)}, f32[16,384]{1,0:T(8,128)S(1)}, u32[]{:S(2)}, u32[]{:S(2)}) collective-permute-start(f32[16,384]{1,0:T(8,128)} %copy-done.45), channel_id=1, source_target_pairs={{1,2},{2,1},{5,6},{6,5},{9,10},{10,9},{13,14},{14,13},{17,18},{18,... | collective-permute-start | bytes 73736 | tf_op jit(solution)/shard_map/ppermute | solution.py:87
  124.6 0.9 copy-start.14
  (45 other events, 31.3 us)

commit v5 on v4

--- a/solution.py
+++ b/solution.py
@@ -98,7 +98,7 @@
     send_faces(z, [padded[f] for f in range(4)], sent)
 
 
-def tables(z, maps, forward, backward, flat):
+def arrange(z, ops, primal, maps, arranged, primal_faces, flat, half):
     flat[...] = jnp.zeros_like(flat)
     flat[0:4, 0 : z.face] = maps[0, 0]
     lane = iota((1, z.padded), 1)
@@ -108,13 +108,31 @@
         line = jnp.where((lane >= f * z.face) & (lane < (f + 1) * z.face), moved, line)
     column = jnp.transpose(jnp.broadcast_to(line, (8, z.padded)))[:, 0:1]
     place_of = iota((z.padded, 1), 0)
+    half[:, z.order :] = jnp.zeros((4 * z.lanes, z.padded - z.order), BF16)
     for f in range(4):
         low, high = f * z.face, (f + 1) * z.face
+        size = min(z.width, z.order - z.starts[f])
+        here = jnp.where((lane >= low) & (lane < high), line, -1)[:, z.starts[f] : z.starts[f] + size]
+        forward = jnp.where(iota((z.lanes, size), 0) == here, SIGNS[f], 0.0).astype(BF16)
+        rows = ops[0, 0, z.starts[f] : z.starts[f] + size, :]
+        half[f * z.lanes : (f + 1) * z.lanes, 0 : z.order] = dot(forward, rows, precision=None).astype(BF16)
+    values = primal[0, 0]
+    parts = []
+    for _ in range(3):
+        parts.append(values.astype(BF16))
+        values = values - parts[-1].astype(F32)
+    pieces = jnp.concatenate(parts, axis=0)
+    for f in range(4):
+        low, high = f * z.face, (f + 1) * z.face
+        size = min(z.width, z.order - z.starts[f])
         window = slice(z.starts[f], z.starts[f] + z.width)
-        here = jnp.where((lane >= low) & (lane < high), line, -1)[:, window]
-        forward[f] = (iota((z.lanes, z.width), 0) == here).astype(F32).astype(BF16)
         there = jnp.where((place_of >= low) & (place_of < high), column, -1)[window]
-        backward[f] = (iota((z.width, z.lanes), 1) == there).astype(F32).astype(BF16)
+        backward = (iota((z.width, z.lanes), 1) == there).astype(F32).astype(BF16)
+        block = slice(f * z.lanes, (f + 1) * z.lanes)
+        arranged[:, block] = dot(half[:, window], backward, precision=None).astype(BF16)
+        three = dot(pieces[:, z.starts[f] : z.starts[f] + size], backward[0:size], precision=None)
+        n = z.cases
+        primal_faces[f] = three[0:n] + (three[n : 2 * n] + three[2 * n :])
 
 
 def couple(z, padded, masks, got0, got1, got2, got3, loads, across, local_tile, sent, aug, small):
@@ -149,27 +167,10 @@
     return dot(pair, lift_rows[f], (0, 0))
 
 
-def apply(z, faces, ops, forward, local):
-    local[...] = jnp.zeros_like(local)
-    for f in range(4):
-        window = slice(z.starts[f], z.starts[f] + z.width)
-        signed = (faces[f] * SIGNS[f]).astype(BF16)
-        local[:, window] += dot(signed, forward[f], precision=None)
-    operand = local[:, 0 : z.order].astype(BF16)
-    return dot(operand, ops[0, 0], precision=None)
-
-
-def canonical(z, values, backward, product):
-    product[...] = jnp.zeros_like(product)
-    product[:, 0 : z.order] = values
-    found = []
-    for f in range(4):
-        part = product[:, z.starts[f] : z.starts[f] + z.width]
-        high = part.astype(BF16)
-        low = (part - high.astype(F32)).astype(BF16)
-        both = dot(jnp.concatenate([high, low], axis=0), backward[f], precision=None)
-        found.append(both[0 : z.cases] + both[z.cases :])
-    return found
+def apply(z, faces, arranged):
+    operand = jnp.concatenate([face.astype(BF16) for face in faces], axis=1)
+    image = dot(operand, arranged[...], precision=None)
+    return [image[:, f * z.lanes : (f + 1) * z.lanes] for f in range(4)]
 
 
 def send_coarse(z, faces, rows, scalars, sent, tile):
@@ -228,9 +229,9 @@
 
 
 def begin(
-    z, received, padded, across, masks, local_tile, forward, ops, primal, backward,
+    z, received, padded, across, masks, local_tile, arranged, primal,
     solve_rows, rows, lift_rows, multipliers, faces, sent, to0, to1, to2, to3,
-    matrix, local, product, tile,
+    matrix, tile,
 ):
     ix, iy = place()
     near_spots = spots(z, ix, iy)
@@ -271,8 +272,7 @@
         multipliers[f] = fields[f]
     for item in (solve_rows, rows, lift_rows, multipliers):
         item.push()
-    image = primal[0, 0] - apply(z, fields, ops, forward, local)
-    image = canonical(z, image, backward, product)
+    image = [primal[f] - part for f, part in enumerate(apply(z, fields, arranged))]
     for f in range(4):
         faces[f] = image[f]
     faces.push()
@@ -286,9 +286,9 @@
 
 
 def first_direction(
-    z, received, got0, got1, got2, got3, faces, masks, solve_rows, lift_rows, forward, ops, backward, rows,
+    z, received, got0, got1, got2, got3, faces, masks, solve_rows, lift_rows, arranged, rows,
     residual, direction, image, sent, to0, to1, to2, to3,
-    local, product, tile,
+    tile,
 ):
     amplitudes = coarse_amplitudes(z, received, solve_rows)
     field = jumped(z, masks, faces, (got0, got1, got2, got3))
@@ -299,7 +299,7 @@
         direction[f] = moved[f]
     residual.push()
     direction.push()
-    found = canonical(z, apply(z, moved, ops, forward, local), backward, product)
+    found = apply(z, moved, arranged)
     for f in range(4):
         image[f] = found[f]
     image.push()
@@ -311,9 +311,8 @@
 
 def second_direction(
     z, received, got0, got1, got2, got3, faces, masks, solve_rows, lift_rows,
-    multipliers, residual, direction, forward, ops, backward,
+    multipliers, residual, direction, arranged,
     next_multipliers, next_residual, projected, image, fresh, sums, sent, to0, to1, to2, to3,
-    local, product,
 ):
     amplitudes = coarse_amplitudes(z, received, solve_rows)
     summed = jnp.sum(received[...], axis=0)
@@ -331,7 +330,7 @@
         projected[f] = moved[f]
     for item in (sums, image, next_multipliers, next_residual, projected):
         item.push()
-    found = canonical(z, apply(z, moved, ops, forward, local), backward, product)
+    found = apply(z, moved, arranged)
     for f in range(4):
         fresh[f] = found[f]
     fresh.push()
@@ -426,7 +425,7 @@
         scratch_shapes=buffers
         + [VMEM(shape, dtype) for shape, dtype in scratch]
         + [pltpu.SemaphoreType.DMA((far + len(outs),))],
-        compiler_params=pltpu.CompilerParams(vmem_limit_bytes=32 * 2**20),
+        compiler_params=pltpu.CompilerParams(vmem_limit_bytes=60 * 2**20),
         cost_estimate=pl.CostEstimate(flops=flops, bytes_accessed=moved, transcendentals=0),
         name=kernel.__name__,
     )(*args)
@@ -444,9 +443,8 @@
     tile = ((8, 128), F32)
     sent = ((z.count, 8, 128), F32)
     to_faces = [((z.cases, z.lanes), F32)] * 4
-    padded_rows = ((z.cases, z.padded), F32)
     columns = -(-z.rows // 128) * 128
-    product_flops = 2 * z.cases * z.order * z.order
+    product_flops = 2 * z.cases * (4 * z.lanes) ** 2
 
     padded, masks, *trace_faces = call(
         z, prepare, [mode_rows, mode_rows] + [((8, z.lanes), F32)] * 4,
@@ -459,30 +457,31 @@
         [tile, ((8, z.cases), F32)], near=1,
     )
     blocks = gather(blocks)
-    forward, backward = call(
-        z, tables, [((4, z.lanes, z.width), BF16), ((4, z.width, z.lanes), BF16)], [maps],
-        [((8, z.padded), jnp.int32)], product_flops, near=1,
+    side = 4 * z.lanes
+    arranged, primal_faces = call(
+        z, arrange, [((side, side), BF16), field], [ops, primal, maps],
+        [((8, z.padded), jnp.int32), ((side, z.padded), BF16)], 2 * side * side * z.width, near=1,
     )
     solve_rows, rows, lift_rows, multipliers, faces, coarse, *sent_faces = call(
         z, begin,
         [((40, z.rows), F32), pair_rows, pair_rows, field, field, sent] + to_faces,
-        [blocks, padded, across, masks, local_tile, forward, ops, primal, backward],
-        [((z.rows, columns), F32), padded_rows, padded_rows, tile], product_flops,
+        [blocks, padded, across, masks, local_tile, arranged, primal_faces],
+        [((z.rows, columns), F32), tile], product_flops,
     )
     coarse, got = gather(coarse), exchange(sent_faces)
     residual, direction, faces, coarse, *sent_faces = call(
         z, first_direction,
         [field, field, field, sent] + to_faces,
-        [coarse, *got, faces, masks, solve_rows, lift_rows, forward, ops, backward, rows],
-        [padded_rows, padded_rows, tile], product_flops,
+        [coarse, *got, faces, masks, solve_rows, lift_rows, arranged, rows],
+        [tile], product_flops,
     )
     coarse, got = gather(coarse), exchange(sent_faces)
     multipliers, residual, projected, image, faces, sums, coarse, *sent_faces = call(
         z, second_direction,
         [field, field, field, field, field, tile, sent] + to_faces,
         [coarse, *got, faces, masks, solve_rows, lift_rows,
-         multipliers, residual, direction, forward, ops, backward],
-        [padded_rows, padded_rows], product_flops,
+         multipliers, residual, direction, arranged],
+        [], product_flops,
     )
     coarse, got = gather(coarse), exchange(sent_faces)
     whole = ((1, 1, 4, z.cases, z.face), F32)

time: 133 us -> 99.8 us (0.75)
  local copies, waits for them, and re-layouts: 45.6 us -> 3.2 us
  Pallas kernels: 22.7 us -> 32.3 us
  starting transfers between devices: 51.6 us -> 53.5 us
    unnamed x114 -> x40, local copies, waits for them, and re-layouts: 45.6 us -> 3.2 us
    pallas_call x7, Pallas kernels: 22.7 us -> 32.3 us  [call(): pl.pallas_call(run, out_shape=shapes, in_specs=specs, out_specs=[pl.Block...]
    all_to_all x4, waiting for transfers between devices: 2.59 us -> 0.01 us  [gather(): return lax.all_to_all(values, AXES, 0, 0, tiled=True)]
    all_to_all x4, starting transfers between devices: 17.8 us -> 19.8 us  [gather(): return lax.all_to_all(values, AXES, 0, 0, tiled=True)]
  transfers between devices with their start and end apart: 20 -> 20, of which waited for: 5 -> 4; matrix products, arithmetic and copies ran while one was open for 0% -> 0% of each run, Pallas kernels for 1% -> 11%
where the time goes in v5:
time: 99.8 us; the launch traced here: 99.1 us
  starting transfers between devices  53.5 us (54%)
  Pallas kernels  32.3 us (32%)
  waiting for transfers between devices  9.02 us (9%)
  local copies, waits for them, and re-layouts  3.2 us (3%)
  between operations  1.06 us (1%)
    ppermute x16, starting transfers between devices, exchange(): got.append(lax.ppermute(values, axis, pairs))  33.7 us
    pallas_call x7, Pallas kernels, call(): pl.pallas_call(run, out_shape=shapes, in_specs=specs, out_specs=[pl.Block...  32.3 us
    all_to_all x4, starting transfers between devices, gather(): return lax.all_to_all(values, AXES, 0, 0, tiled=True)  19.8 us
    ppermute x16, waiting for transfers between devices, exchange(): got.append(lax.ppermute(values, axis, pairs))  9.01 us
    unnamed x40, local copies, waits for them, and re-layouts  3.2 us
  transfers between devices with their start and end apart: 20, of which 4 were waited for; matrix products, arithmetic and copies ran while one was open for 0% of the time, Pallas kernels for 11%

profile of v5, /device:TPU:5, one launch (start us, length us, event | category | flops | bytes accessed | tf_op | source)
XLA Modules:
  0.0 99.1 jit_solution(1558944415654038261)
XLA Ops:
  0.6 1.5 %prepare.1 = (f32[4,8,384]{2,1,0:T(8,128)}, f32[4,8,384]{2,1,0:T(8,128)}, f32[8,384]{1,0:T(8,128)}, f32[8,384]{1,0:T(8,128)}, f32[8,384]{1,0:T(8,128)}, /*index=5*/f32[8,384]{1,0:T(8,128)}) custom-call(f32[1,1,6,4,300]{4,3,2,1,0:T(4,128)} %bitcast.2, s32[1,1,4]{2,1,0:T(1,128)} %refs_1_.2), custom_call_target="tpu_custom_call" | custom-call | bytes 176272 | tf_op jit(solution)/shard_map/prepare/pallas_call | solution.py:420
  2.2 4.4 %collective-permute-start.1 = (f32[8,384]{1,0:T(8,128)}, f32[8,384]{1,0:T(8,128)S(1)}, u32[]{:S(2)}, u32[]{:S(2)}) collective-permute-start(f32[8,384]{1,0:T(8,128)} %get-tuple-element.45), channel_id=1, source_target_pairs={{4,8},{8,4},{12,16},{16,12},{20,24},{24,20},{5,9},{9,5},{13,17},{1... | collective-permute-start | bytes 36872 | tf_op jit(solution)/shard_map/ppermute | solution.py:87
  6.6 1.3 %collective-permute-start.2 = (f32[8,384]{1,0:T(8,128)}, f32[8,384]{1,0:T(8,128)S(1)}, u32[]{:S(2)}, u32[]{:S(2)}) collective-permute-start(f32[8,384]{1,0:T(8,128)} %get-tuple-element.46), channel_id=1, source_target_pairs={{0,1},{1,0},{2,3},{3,2},{4,5},{5,4},{6,7},{7,6},{8,9},{9,8},{10,11... | collective-permute-start | bytes 36872 | tf_op jit(solution)/shard_map/ppermute | solution.py:87
  7.9 3.0 %collective-permute-start.3 = (f32[8,384]{1,0:T(8,128)}, f32[8,384]{1,0:T(8,128)S(1)}, u32[]{:S(2)}, u32[]{:S(2)}) collective-permute-start(f32[8,384]{1,0:T(8,128)} %get-tuple-element.47), channel_id=1, source_target_pairs={{1,2},{2,1},{5,6},{6,5},{9,10},{10,9},{13,14},{14,13},{17,18},{18,... | collective-permute-start | bytes 36872 | tf_op jit(solution)/shard_map/ppermute | solution.py:87
  11.0 2.1 %collective-permute-done.3.refs_5_ = f32[8,384]{1,0:T(8,128)S(1)} collective-permute-done((f32[8,384]{1,0:T(8,128)}, f32[8,384]{1,0:T(8,128)S(1)}, u32[]{:S(2)}, u32[]{:S(2)}) %collective-permute-start.3) | collective-permute-done | bytes 12320 | tf_op jit(solution)/shard_map/ppermute | solution.py:87
  13.1 0.6 copy-done.19
  13.7 4.0 %couple.1 = (f32[4,8,384]{2,1,0:T(8,128)}, f32[8,128]{1,0:T(8,128)}, f32[32,8,128]{2,1,0:T(8,128)}) custom-call(f32[4,8,384]{2,1,0:T(8,128)} %get-tuple-element.42.refs_0_.refs_1_, f32[4,8,384]{2,1,0:T(8,128)} %get-tuple-element.43.refs_1_.refs_3_.refs_6_, f32[8,384]{1,0:T(8,128)} %copy-done.16, f32[8,384]{1,0:T(8,128)} %copy-done.17, f32[8,384]{1,0:T(8,128)} %copy-done.18, ...), custom_call_target="tpu_custom_call" | custom-call | bytes 332160 | tf_op jit(solution)/shard_map/couple/pallas_call | solution.py:420
  17.7 4.8 %all-to-all-start = ((f32[32,8,128]{2,1,0:T(8,128)}), f32[32,8,128]{2,1,0:T(8,128)S(1)}, u32[]{:S(2)}, u32[]{:S(2)}) async-start(f32[32,8,128]{2,1,0:T(8,128)} %get-tuple-element.48), calls=%async_computation | async-start | bytes 262144 | tf_op jit(solution)/shard_map/all_to_all | solution.py:435
  22.5 10.8 %arrange.1 = (bf16[1536,1536]{1,0:T(8,128)(2,1)}, f32[4,16,384]{2,1,0:T(8,128)}) custom-call(bf16[1,1,1200,1200]{3,2,1,0:T(8,128)(2,1)} %refs_0_.1, f32[1,1,16,1200]{3,2,1,0:T(8,128)} %refs_1_.3, s32[1,1,4,300]{3,2,1,0:T(4,128)} %refs_2_.1), custom_call_target="tpu_custom_call" | custom-call | flops 2415919104 | bytes 7778496 | tf_op jit(solution)/shard_map/arrange/pallas_call | solution.py:420
  33.3 0.6 copy-done.1
  33.9 4.6 %begin.1 = (f32[40,256]{1,0:T(8,128)}, f32[4,16,384]{2,1,0:T(8,128)}, f32[4,16,384]{2,1,0:T(8,128)}, f32[4,16,384]{2,1,0:T(8,128)}, f32[4,16,384]{2,1,0:T(8,128)...) custom-call(f32[32,8,128]{2,1,0:T(8,128)} %copy-done.1, ...), custom_call_target="tpu_custom_call" | custom-call | flops 75497472 | bytes 5763072 | tf_op jit(solution)/shard_map/begin/pallas_call | solution.py:420
  38.6 5.8 %all-to-all-start.1 = ((f32[32,8,128]{2,1,0:T(8,128)}), f32[32,8,128]{2,1,0:T(8,128)S(1)}, u32[]{:S(2)}, u32[]{:S(2)}) async-start(f32[32,8,128]{2,1,0:T(8,128)} %get-tuple-element.53), calls=%async_computation.1 | async-start | bytes 262144 | tf_op jit(solution)/shard_map/all_to_all | solution.py:435
  44.6 4.2 %collective-permute-start.5 = (f32[16,384]{1,0:T(8,128)}, f32[16,384]{1,0:T(8,128)S(1)}, u32[]{:S(2)}, u32[]{:S(2)}) collective-permute-start(f32[16,384]{1,0:T(8,128)} %get-tuple-element.55), channel_id=1, source_target_pairs={{4,8},{8,4},{12,16},{16,12},{20,24},{24,20},{5,9},{9,5},{13,17},{1... | collective-permute-start | bytes 73736 | tf_op jit(solution)/shard_map/ppermute | solution.py:87
  48.8 1.0 collective-permute-start.6
  49.7 3.0 %collective-permute-start.7 = (f32[16,384]{1,0:T(8,128)}, f32[16,384]{1,0:T(8,128)S(1)}, u32[]{:S(2)}, u32[]{:S(2)}) collective-permute-start(f32[16,384]{1,0:T(8,128)} %get-tuple-element.57), channel_id=1, source_target_pairs={{1,2},{2,1},{5,6},{6,5},{9,10},{10,9},{13,14},{14,13},{17,18},{18,... | collective-permute-start | bytes 73736 | tf_op jit(solution)/shard_map/ppermute | solution.py:87
  52.8 2.3 %collective-permute-done.7.refs_4_ = f32[16,384]{1,0:T(8,128)S(1)} collective-permute-done((f32[16,384]{1,0:T(8,128)}, f32[16,384]{1,0:T(8,128)S(1)}, u32[]{:S(2)}, u32[]{:S(2)}) %collective-permute-start.7) | collective-permute-done | bytes 24608 | tf_op jit(solution)/shard_map/ppermute | solution.py:87
  55.1 0.6 copy-done.11
  55.8 4.7 %first_direction.1 = (f32[4,16,384]{2,1,0:T(8,128)}, f32[4,16,384]{2,1,0:T(8,128)}, f32[4,16,384]{2,1,0:T(8,128)}, f32[32,8,128]{2,1,0:T(8,128)}, f32[16,384]{1,...) custom-call(f32[32,8,128]{2,1,0:T(8,128)} %copy-done.3, f32[16,384]{1,0:T(8,128)} %copy-done.7, ...), custom_call_target="tpu_custom_call" | custom-call | flops 75497472 | bytes 5857280 | tf_op jit(solution)/shard_map/first_direction/pallas_call | solution.py:420
  60.5 4.6 %all-to-all-start.2 = ((f32[32,8,128]{2,1,0:T(8,128)}), f32[32,8,128]{2,1,0:T(8,128)S(1)}, u32[]{:S(2)}, u32[]{:S(2)}) async-start(f32[32,8,128]{2,1,0:T(8,128)} %get-tuple-element.62), calls=%async_computation.2 | async-start | bytes 262144 | tf_op jit(solution)/shard_map/all_to_all | solution.py:435
  65.2 4.2 %collective-permute-start.9 = (f32[16,384]{1,0:T(8,128)}, f32[16,384]{1,0:T(8,128)S(1)}, u32[]{:S(2)}, u32[]{:S(2)}) collective-permute-start(f32[16,384]{1,0:T(8,128)} %get-tuple-element.64), channel_id=1, source_target_pairs={{4,8},{8,4},{12,16},{16,12},{20,24},{24,20},{5,9},{9,5},{13,17},{1... | collective-permute-start | bytes 73736 | tf_op jit(solution)/shard_map/ppermute | solution.py:87
  69.4 1.0 collective-permute-start.10
  70.4 3.0 %collective-permute-start.11 = (f32[16,384]{1,0:T(8,128)}, f32[16,384]{1,0:T(8,128)S(1)}, u32[]{:S(2)}, u32[]{:S(2)}) collective-permute-start(f32[16,384]{1,0:T(8,128)} %get-tuple-element.66), channel_id=1, source_target_pairs={{1,2},{2,1},{5,6},{6,5},{9,10},{10,9},{13,14},{14,13},{17,18},{18,... | collective-permute-start | bytes 73736 | tf_op jit(solution)/shard_map/ppermute | solution.py:87
  73.5 2.3 %collective-permute-done.11.refs_4_ = f32[16,384]{1,0:T(8,128)S(1)} collective-permute-done((f32[16,384]{1,0:T(8,128)}, f32[16,384]{1,0:T(8,128)S(1)}, u32[]{:S(2)}, u32[]{:S(2)}) %collective-permute-start.11) | collective-permute-done | bytes 24608 | tf_op jit(solution)/shard_map/ppermute | solution.py:87
  75.8 0.6 copy-done.8
  76.4 4.6 %second_direction.1 = (f32[4,16,384]{2,1,0:T(8,128)}, f32[4,16,384]{2,1,0:T(8,128)}, f32[4,16,384]{2,1,0:T(8,128)}, f32[4,16,384]{2,1,0:T(8,128)}, f32[4,16,384]...) custom-call(f32[32,8,128]{2,1,0:T(8,128)} %copy-done, ...), custom_call_target="tpu_custom_call" | custom-call | flops 75497472 | bytes 6254592 | tf_op jit(solution)/shard_map/second_direction/pallas_call | solution.py:420
  81.1 4.6 %all-to-all-start.3 = ((f32[32,8,128]{2,1,0:T(8,128)}), f32[32,8,128]{2,1,0:T(8,128)S(1)}, u32[]{:S(2)}, u32[]{:S(2)}) async-start(f32[32,8,128]{2,1,0:T(8,128)} %get-tuple-element.71), calls=%async_computation.3 | async-start | bytes 262144 | tf_op jit(solution)/shard_map/all_to_all | solution.py:435
  85.8 4.2 %collective-permute-start.13 = (f32[16,384]{1,0:T(8,128)}, f32[16,384]{1,0:T(8,128)S(1)}, u32[]{:S(2)}, u32[]{:S(2)}) collective-permute-start(f32[16,384]{1,0:T(8,128)} %get-tuple-element.73), channel_id=1, source_target_pairs={{4,8},{8,4},{12,16},{16,12},{20,24},{24,20},{5,9},{9,5},{13,17},{1... | collective-permute-start | bytes 73736 | tf_op jit(solution)/shard_map/ppermute | solution.py:87
  90.0 1.0 collective-permute-start.14
  91.0 3.0 %collective-permute-start.15 = (f32[16,384]{1,0:T(8,128)}, f32[16,384]{1,0:T(8,128)S(1)}, u32[]{:S(2)}, u32[]{:S(2)}) collective-permute-start(f32[16,384]{1,0:T(8,128)} %get-tuple-element.75), channel_id=1, source_target_pairs={{1,2},{2,1},{5,6},{6,5},{9,10},{10,9},{13,14},{14,13},{17,18},{18,... | collective-permute-start | bytes 73736 | tf_op jit(solution)/shard_map/ppermute | solution.py:87
  94.1 2.3 %collective-permute-done.15.refs_4_ = f32[16,384]{1,0:T(8,128)S(1)} collective-permute-done((f32[16,384]{1,0:T(8,128)}, f32[16,384]{1,0:T(8,128)S(1)}, u32[]{:S(2)}, u32[]{:S(2)}) %collective-permute-start.15) | collective-permute-done | bytes 24608 | tf_op jit(solution)/shard_map/ppermute | solution.py:87
  96.4 0.6 copy-done.15
  97.0 2.1 %finish.1 = (f32[1,1,4,16,300]{4,3,2,1,0:T(8,128)}, f32[1,1,4,16,300]{4,3,2,1,0:T(8,128)}) custom-call(f32[32,8,128]{2,1,0:T(8,128)} %copy-done.2, f32[16,384]{1,0:T(8,128)} %copy-done.12, f32[16,384]{1,0:T(8,128)} %copy-done.13, f32[16,384]{1,0:T(8,128)} %copy-done.14, f32[16,384]{1,0:T(8,128)} %copy-done.15, f32[4,16,384]{2,1,0:T(8,128)} %get-tuple-element.76.refs_5_, ...), custom_call_target="tpu_custom_call" | custom-call | bytes 1026048 | tf_op jit(solution)/shard_map/finish/pallas_call | solution.py:420
  (55 shorter events, 0.8 us)
Async XLA Ops:
  2.2 8.8 %collective-permute-start = (f32[8,384]{1,0:T(8,128)}, f32[8,384]{1,0:T(8,128)S(1)}, u32[]{:S(2)}, u32[]{:S(2)}) collective-permute-start(f32[8,384]{1,0:T(8,128)} %get-tuple-element.44), channel_id=1, source_target_pairs={{0,4},{4,0},{8,12},{12,8},{16,20},{20,16},{24,28},{28,24},{1,5},{5... | collective-permute-start | bytes 36872 | tf_op jit(solution)/shard_map/ppermute | solution.py:87
  2.2 8.7 %collective-permute-start.1 = (f32[8,384]{1,0:T(8,128)}, f32[8,384]{1,0:T(8,128)S(1)}, u32[]{:S(2)}, u32[]{:S(2)}) collective-permute-start(f32[8,384]{1,0:T(8,128)} %get-tuple-element.45), channel_id=1, source_target_pairs={{4,8},{8,4},{12,16},{16,12},{20,24},{24,20},{5,9},{9,5},{13,17},{1... | collective-permute-start | bytes 36872 | tf_op jit(solution)/shard_map/ppermute | solution.py:87
  6.6 4.4 %collective-permute-start.2 = (f32[8,384]{1,0:T(8,128)}, f32[8,384]{1,0:T(8,128)S(1)}, u32[]{:S(2)}, u32[]{:S(2)}) collective-permute-start(f32[8,384]{1,0:T(8,128)} %get-tuple-element.46), channel_id=1, source_target_pairs={{0,1},{1,0},{2,3},{3,2},{4,5},{5,4},{6,7},{7,6},{8,9},{9,8},{10,11... | collective-permute-start | bytes 36872 | tf_op jit(solution)/shard_map/ppermute | solution.py:87
  7.9 5.2 %collective-permute-start.3 = (f32[8,384]{1,0:T(8,128)}, f32[8,384]{1,0:T(8,128)S(1)}, u32[]{:S(2)}, u32[]{:S(2)}) collective-permute-start(f32[8,384]{1,0:T(8,128)} %get-tuple-element.47), channel_id=1, source_target_pairs={{1,2},{2,1},{5,6},{6,5},{9,10},{10,9},{13,14},{14,13},{17,18},{18,... | collective-permute-start | bytes 36872 | tf_op jit(solution)/shard_map/ppermute | solution.py:87
  11.0 2.2 %copy-start.16 = (f32[8,384]{1,0:T(8,128)}, f32[8,384]{1,0:T(8,128)S(1)}, u32[]{:S(2)}) copy-start(f32[8,384]{1,0:T(8,128)S(1)} %collective-permute-done.refs_2_) | copy-start | bytes 36868
  11.0 2.2 %copy-start.17 = (f32[8,384]{1,0:T(8,128)}, f32[8,384]{1,0:T(8,128)S(1)}, u32[]{:S(2)}) copy-start(f32[8,384]{1,0:T(8,128)S(1)} %collective-permute-done.1.refs_3_) | copy-start | bytes 36868
  11.0 2.1 %copy-start.18 = (f32[8,384]{1,0:T(8,128)}, f32[8,384]{1,0:T(8,128)S(1)}, u32[]{:S(2)}) copy-start(f32[8,384]{1,0:T(8,128)S(1)} %collective-permute-done.2.refs_4_) | copy-start | bytes 36868
  17.7 15.6 %all-to-all-start = ((f32[32,8,128]{2,1,0:T(8,128)}), f32[32,8,128]{2,1,0:T(8,128)S(1)}, u32[]{:S(2)}, u32[]{:S(2)}) async-start(f32[32,8,128]{2,1,0:T(8,128)} %get-tuple-element.48), calls=%async_computation | async-start | bytes 262144 | tf_op jit(solution)/shard_map/all_to_all | solution.py:435
  38.6 16.5 %all-to-all-start.1 = ((f32[32,8,128]{2,1,0:T(8,128)}), f32[32,8,128]{2,1,0:T(8,128)S(1)}, u32[]{:S(2)}, u32[]{:S(2)}) async-start(f32[32,8,128]{2,1,0:T(8,128)} %get-tuple-element.53), calls=%async_computation.1 | async-start | bytes 262144 | tf_op jit(solution)/shard_map/all_to_all | solution.py:435
  44.4 8.3 %collective-permute-start.4 = (f32[16,384]{1,0:T(8,128)}, f32[16,384]{1,0:T(8,128)S(1)}, u32[]{:S(2)}, u32[]{:S(2)}) collective-permute-start(f32[16,384]{1,0:T(8,128)} %get-tuple-element.54), channel_id=1, source_target_pairs={{0,4},{4,0},{8,12},{12,8},{16,20},{20,16},{24,28},{28,24},{1,5},{5... | collective-permute-start | bytes 73736 | tf_op jit(solution)/shard_map/ppermute | solution.py:87
  44.6 8.2 %collective-permute-start.5 = (f32[16,384]{1,0:T(8,128)}, f32[16,384]{1,0:T(8,128)S(1)}, u32[]{:S(2)}, u32[]{:S(2)}) collective-permute-start(f32[16,384]{1,0:T(8,128)} %get-tuple-element.55), channel_id=1, source_target_pairs={{4,8},{8,4},{12,16},{16,12},{20,24},{24,20},{5,9},{9,5},{13,17},{1... | collective-permute-start | bytes 73736 | tf_op jit(solution)/shard_map/ppermute | solution.py:87
  48.8 4.0 %collective-permute-start.6 = (f32[16,384]{1,0:T(8,128)}, f32[16,384]{1,0:T(8,128)S(1)}, u32[]{:S(2)}, u32[]{:S(2)}) collective-permute-start(f32[16,384]{1,0:T(8,128)} %get-tuple-element.56), channel_id=1, source_target_pairs={{0,1},{1,0},{2,3},{3,2},{4,5},{5,4},{6,7},{7,6},{8,9},{9,8},{10,11... | collective-permute-start | bytes 73736 | tf_op jit(solution)/shard_map/ppermute | solution.py:87
  49.7 5.3 %collective-permute-start.7 = (f32[16,384]{1,0:T(8,128)}, f32[16,384]{1,0:T(8,128)S(1)}, u32[]{:S(2)}, u32[]{:S(2)}) collective-permute-start(f32[16,384]{1,0:T(8,128)} %get-tuple-element.57), channel_id=1, source_target_pairs={{1,2},{2,1},{5,6},{6,5},{9,10},{10,9},{13,14},{14,13},{17,18},{18,... | collective-permute-start | bytes 73736 | tf_op jit(solution)/shard_map/ppermute | solution.py:87
  52.7 2.3 %copy-start.7 = (f32[16,384]{1,0:T(8,128)}, f32[16,384]{1,0:T(8,128)S(1)}, u32[]{:S(2)}) copy-start(f32[16,384]{1,0:T(8,128)S(1)} %collective-permute-done.4.refs_1_) | copy-start | bytes 73732
  52.8 2.3 %copy-start.9 = (f32[16,384]{1,0:T(8,128)}, f32[16,384]{1,0:T(8,128)S(1)}, u32[]{:S(2)}) copy-start(f32[16,384]{1,0:T(8,128)S(1)} %collective-permute-done.5.refs_2_) | copy-start | bytes 73732
  52.8 2.3 %copy-start.10 = (f32[16,384]{1,0:T(8,128)}, f32[16,384]{1,0:T(8,128)S(1)}, u32[]{:S(2)}) copy-start(f32[16,384]{1,0:T(8,128)S(1)} %collective-permute-done.6.refs_3_) | copy-start | bytes 73732
  60.5 15.3 %all-to-all-start.2 = ((f32[32,8,128]{2,1,0:T(8,128)}), f32[32,8,128]{2,1,0:T(8,128)S(1)}, u32[]{:S(2)}, u32[]{:S(2)}) async-start(f32[32,8,128]{2,1,0:T(8,128)} %get-tuple-element.62), calls=%async_computation.2 | async-start | bytes 262144 | tf_op jit(solution)/shard_map/all_to_all | solution.py:435
  65.1 8.3 %collective-permute-start.8 = (f32[16,384]{1,0:T(8,128)}, f32[16,384]{1,0:T(8,128)S(1)}, u32[]{:S(2)}, u32[]{:S(2)}) collective-permute-start(f32[16,384]{1,0:T(8,128)} %get-tuple-element.63), channel_id=1, source_target_pairs={{0,4},{4,0},{8,12},{12,8},{16,20},{20,16},{24,28},{28,24},{1,5},{5... | collective-permute-start | bytes 73736 | tf_op jit(solution)/shard_map/ppermute | solution.py:87
  65.2 8.2 %collective-permute-start.9 = (f32[16,384]{1,0:T(8,128)}, f32[16,384]{1,0:T(8,128)S(1)}, u32[]{:S(2)}, u32[]{:S(2)}) collective-permute-start(f32[16,384]{1,0:T(8,128)} %get-tuple-element.64), channel_id=1, source_target_pairs={{4,8},{8,4},{12,16},{16,12},{20,24},{24,20},{5,9},{9,5},{13,17},{1... | collective-permute-start | bytes 73736 | tf_op jit(solution)/shard_map/ppermute | solution.py:87
  69.4 4.0 %collective-permute-start.10 = (f32[16,384]{1,0:T(8,128)}, f32[16,384]{1,0:T(8,128)S(1)}, u32[]{:S(2)}, u32[]{:S(2)}) collective-permute-start(f32[16,384]{1,0:T(8,128)} %get-tuple-element.65), channel_id=1, source_target_pairs={{0,1},{1,0},{2,3},{3,2},{4,5},{5,4},{6,7},{7,6},{8,9},{9,8},{10,11... | collective-permute-start | bytes 73736 | tf_op jit(solution)/shard_map/ppermute | solution.py:87
  70.4 5.3 %collective-permute-start.11 = (f32[16,384]{1,0:T(8,128)}, f32[16,384]{1,0:T(8,128)S(1)}, u32[]{:S(2)}, u32[]{:S(2)}) collective-permute-start(f32[16,384]{1,0:T(8,128)} %get-tuple-element.66), channel_id=1, source_target_pairs={{1,2},{2,1},{5,6},{6,5},{9,10},{10,9},{13,14},{14,13},{17,18},{18,... | collective-permute-start | bytes 73736 | tf_op jit(solution)/shard_map/ppermute | solution.py:87
  73.4 2.3 %copy-start.4 = (f32[16,384]{1,0:T(8,128)}, f32[16,384]{1,0:T(8,128)S(1)}, u32[]{:S(2)}) copy-start(f32[16,384]{1,0:T(8,128)S(1)} %collective-permute-done.8.refs_1_) | copy-start | bytes 73732
  73.4 2.3 %copy-start.5 = (f32[16,384]{1,0:T(8,128)}, f32[16,384]{1,0:T(8,128)S(1)}, u32[]{:S(2)}) copy-start(f32[16,384]{1,0:T(8,128)S(1)} %collective-permute-done.9.refs_2_) | copy-start | bytes 73732
  73.5 2.3 %copy-start.6 = (f32[16,384]{1,0:T(8,128)}, f32[16,384]{1,0:T(8,128)S(1)}, u32[]{:S(2)}) copy-start(f32[16,384]{1,0:T(8,128)S(1)} %collective-permute-done.10.refs_3_) | copy-start | bytes 73732
  81.1 15.3 %all-to-all-start.3 = ((f32[32,8,128]{2,1,0:T(8,128)}), f32[32,8,128]{2,1,0:T(8,128)S(1)}, u32[]{:S(2)}, u32[]{:S(2)}) async-start(f32[32,8,128]{2,1,0:T(8,128)} %get-tuple-element.71), calls=%async_computation.3 | async-start | bytes 262144 | tf_op jit(solution)/shard_map/all_to_all | solution.py:435
  85.7 8.3 %collective-permute-start.12 = (f32[16,384]{1,0:T(8,128)}, f32[16,384]{1,0:T(8,128)S(1)}, u32[]{:S(2)}, u32[]{:S(2)}) collective-permute-start(f32[16,384]{1,0:T(8,128)} %get-tuple-element.72), channel_id=1, source_target_pairs={{0,4},{4,0},{8,12},{12,8},{16,20},{20,16},{24,28},{28,24},{1,5},{5... | collective-permute-start | bytes 73736 | tf_op jit(solution)/shard_map/ppermute | solution.py:87
  85.8 8.2 %collective-permute-start.13 = (f32[16,384]{1,0:T(8,128)}, f32[16,384]{1,0:T(8,128)S(1)}, u32[]{:S(2)}, u32[]{:S(2)}) collective-permute-start(f32[16,384]{1,0:T(8,128)} %get-tuple-element.73), channel_id=1, source_target_pairs={{4,8},{8,4},{12,16},{16,12},{20,24},{24,20},{5,9},{9,5},{13,17},{1... | collective-permute-start | bytes 73736 | tf_op jit(solution)/shard_map/ppermute | solution.py:87
  90.0 4.0 %collective-permute-start.14 = (f32[16,384]{1,0:T(8,128)}, f32[16,384]{1,0:T(8,128)S(1)}, u32[]{:S(2)}, u32[]{:S(2)}) collective-permute-start(f32[16,384]{1,0:T(8,128)} %get-tuple-element.74), channel_id=1, source_target_pairs={{0,1},{1,0},{2,3},{3,2},{4,5},{5,4},{6,7},{7,6},{8,9},{9,8},{10,11... | collective-permute-start | bytes 73736 | tf_op jit(solution)/shard_map/ppermute | solution.py:87
  91.0 5.3 %collective-permute-start.15 = (f32[16,384]{1,0:T(8,128)}, f32[16,384]{1,0:T(8,128)S(1)}, u32[]{:S(2)}, u32[]{:S(2)}) collective-permute-start(f32[16,384]{1,0:T(8,128)} %get-tuple-element.75), channel_id=1, source_target_pairs={{1,2},{2,1},{5,6},{6,5},{9,10},{10,9},{13,14},{14,13},{17,18},{18,... | collective-permute-start | bytes 73736 | tf_op jit(solution)/shard_map/ppermute | solution.py:87
  94.0 2.3 %copy-start.12 = (f32[16,384]{1,0:T(8,128)}, f32[16,384]{1,0:T(8,128)S(1)}, u32[]{:S(2)}) copy-start(f32[16,384]{1,0:T(8,128)S(1)} %collective-permute-done.12.refs_1_) | copy-start | bytes 73732
  94.0 2.3 %copy-start.13 = (f32[16,384]{1,0:T(8,128)}, f32[16,384]{1,0:T(8,128)S(1)}, u32[]{:S(2)}) copy-start(f32[16,384]{1,0:T(8,128)S(1)} %collective-permute-done.13.refs_2_) | copy-start | bytes 73732
  94.0 2.3 %copy-start.14 = (f32[16,384]{1,0:T(8,128)}, f32[16,384]{1,0:T(8,128)S(1)}, u32[]{:S(2)}) copy-start(f32[16,384]{1,0:T(8,128)S(1)} %collective-permute-done.14.refs_3_) | copy-start | bytes 73732
  (8 other events, 5.1 us)

commit v6 on v5

--- a/solution.py
+++ b/solution.py
@@ -17,6 +17,7 @@
 FIRST_LANE = 32
 INVERSE_LANE = 48
 SCALAR_LANE = 96
+BLOCK = 512
 
 
 class Sizes:
@@ -78,13 +79,13 @@
 
 
 def exchange(sent):
-    got = []
-    for i, values in enumerate(sent):
+    got = [None] * 4
+    for i in (1, 3, 0, 2):
         axis = AXES[i // 2]
         pairs = []
         for low in range(i % 2, lax.axis_size(axis) - 1, 2):
             pairs += [(low, low + 1), (low + 1, low)]
-        got.append(lax.ppermute(values, axis, pairs))
+        got[i] = lax.ppermute(sent[i], axis, pairs)
     return got
 
 
@@ -93,9 +94,16 @@
     for f in range(4):
         for j in range(z.modes):
             padded[f, j : j + 1, 0 : z.face] = traces[0, 0, j, f : f + 1]
-        live = (iota((8, z.lanes), 1) < counts[0, 0, f]).astype(F32)
-        masks[f] = live
-    send_faces(z, [padded[f] for f in range(4)], sent)
+    for i, at in enumerate(place()):
+        even = at % 2 == 0
+        low, high = padded[2 * i], padded[2 * i + 1]
+        sent[2 * i][...] = jnp.where(even, high, low)
+        sent[2 * i + 1][...] = jnp.where(even, low, high)
+    row, lane = iota(masks.shape, 0), iota(masks.shape, 1)
+    live = jnp.zeros(masks.shape, F32)
+    for f in range(4):
+        live = jnp.where((row == f) & (lane < counts[0, 0, f]), 1.0, live)
+    masks[...] = live
 
 
 def arrange(z, ops, primal, maps, arranged, primal_faces, flat, half):
@@ -130,15 +138,14 @@
         backward = (iota((z.width, z.lanes), 1) == there).astype(F32).astype(BF16)
         block = slice(f * z.lanes, (f + 1) * z.lanes)
         arranged[:, block] = dot(half[:, window], backward, precision=None).astype(BF16)
+        arranged.push(f)
         three = dot(pieces[:, z.starts[f] : z.starts[f] + size], backward[0:size], precision=None)
         n = z.cases
         primal_faces[f] = three[0:n] + (three[n : 2 * n] + three[2 * n :])
 
 
-def couple(z, padded, masks, got0, got1, got2, got3, loads, across, local_tile, sent, aug, small):
-    near = across_faces(z, (got0, got1, got2, got3))
-    live = [padded[f] * masks[f] for f in range(4)]
-    diagonal = sum(dot(live[f], padded[f], (1, 1)) for f in range(4))
+def invert(z, padded, masks, loads, local_tile, aug, small):
+    diagonal = sum(dot(padded[f] * masks[f : f + 1], padded[f], (1, 1)) for f in range(4))
     row, col = iota((8, 128), 0), iota((8, 128), 1)
     aug[...] = jnp.where((col == row + 8) & (row < z.modes), 1.0, 0.0).astype(F32)
     aug[:, 0:8] = diagonal
@@ -148,18 +155,25 @@
         taken = matrix[:, p : p + 1] - (row[:, 0:1] == p).astype(F32)
         matrix = matrix - taken * scaled
     inverse = matrix[:, 8:16]
-    small[...] = jnp.zeros_like(small)
+    small[...] = jnp.zeros(small.shape, F32)
     for j in range(z.modes):
         small[j : j + 1, :] = loads[0, j]
     local_tile[...] = jnp.zeros(local_tile.shape, F32)
     local_tile[:, FIRST_LANE : FIRST_LANE + z.cases] = dot(inverse, small[...])
     local_tile[:, INVERSE_LANE : INVERSE_LANE + 8] = inverse
-    for f in range(4):
-        across[f] = near[f]
-        coupling = dot(live[f], near[f], (1, 1))
-        local_tile[:, 8 * f : 8 * f + 8] = dot(inverse, coupling)
-    sent[...] = jnp.broadcast_to(local_tile[...][None], sent.shape)
+
+
+def couple(z, padded, masks, local_tile, got0, got1, got2, got3, sent, live_rows, lift_rows, tile):
+    near = across_faces(z, (got0, got1, got2, got3))
+    inverse = local_tile[:, INVERSE_LANE : INVERSE_LANE + 8]
+    tile[...] = local_tile[...]
+    for f in range(4):
+        live = padded[f] * masks[f : f + 1]
+        lift_rows[f] = jnp.concatenate([live * SIGNS[f], near[f] * masks[f : f + 1] * -SIGNS[f]], axis=0)
+        tile[:, 8 * f : 8 * f + 8] = dot(inverse, dot(live, near[f], (1, 1)))
+    sent[...] = jnp.broadcast_to(tile[...][None], sent.shape)
     sent.push()
+    live_rows[...] = masks[...]
 
 
 def lifted(z, amplitudes, lift_rows, f):
@@ -169,7 +183,10 @@
 
 def apply(z, faces, arranged):
     operand = jnp.concatenate([face.astype(BF16) for face in faces], axis=1)
-    image = dot(operand, arranged[...], precision=None)
+    image = sum(
+        dot(operand[:, low : low + BLOCK], arranged[low : low + BLOCK, :], precision=None)
+        for low in range(0, 4 * z.lanes, BLOCK)
+    )
     return [image[:, f * z.lanes : (f + 1) * z.lanes] for f in range(4)]
 
 
@@ -229,8 +246,8 @@
 
 
 def begin(
-    z, received, padded, across, masks, local_tile, arranged, primal,
-    solve_rows, rows, lift_rows, multipliers, faces, sent, to0, to1, to2, to3,
+    z, received, lift_rows, primal, arranged,
+    solve_rows, rows, multipliers, faces, sent, to0, to1, to2, to3,
     matrix, tile,
 ):
     ix, iy = place()
@@ -259,18 +276,16 @@
     solve = unit + once + twice
     solve_rows[...] = solve
     amplitudes = dot(solve, values)[:, FIRST_LANE : FIRST_LANE + z.cases]
-    inverse = local_tile[:, INVERSE_LANE : INVERSE_LANE + 8]
     start = window_start(z, ix) * z.ny
+    inverses = [received[pl.ds(start + spot, 1)][0][:, INVERSE_LANE : INVERSE_LANE + 8] for spot in near_spots]
     fields = []
     for f in range(4):
-        live = masks[f]
-        near_inverse = received[pl.ds(start + near_spots[1 + f], 1)][0][:, INVERSE_LANE : INVERSE_LANE + 8]
-        own, near = padded[f] * live, across[f] * live
-        rows[f] = jnp.concatenate([dot(inverse, own), dot(near_inverse, near)], axis=0)
-        lift_rows[f] = jnp.concatenate([own * SIGNS[f], near * -SIGNS[f]], axis=0)
+        both = lift_rows[f]
+        own, near = both[0:8] * SIGNS[f], both[8:16] * -SIGNS[f]
+        rows[f] = jnp.concatenate([dot(inverses[0], own), dot(inverses[1 + f], near)], axis=0)
         fields.append(lifted(z, amplitudes, lift_rows, f))
         multipliers[f] = fields[f]
-    for item in (solve_rows, rows, lift_rows, multipliers):
+    for item in (solve_rows, rows, multipliers):
         item.push()
     image = [primal[f] - part for f, part in enumerate(apply(z, fields, arranged))]
     for f in range(4):
@@ -282,11 +297,11 @@
 
 def jumped(z, masks, faces, got):
     near = across_faces(z, got)
-    return [masks[f, 0:1] * SIGNS[f] * (faces[f] - near[f]) for f in range(4)]
+    return [masks[f : f + 1] * SIGNS[f] * (faces[f] - near[f]) for f in range(4)]
 
 
 def first_direction(
-    z, received, got0, got1, got2, got3, faces, masks, solve_rows, lift_rows, arranged, rows,
+    z, received, solve_rows, lift_rows, faces, masks, rows, arranged, got0, got1, got2, got3,
     residual, direction, image, sent, to0, to1, to2, to3,
     tile,
 ):
@@ -310,8 +325,8 @@
 
 
 def second_direction(
-    z, received, got0, got1, got2, got3, faces, masks, solve_rows, lift_rows,
-    multipliers, residual, direction, arranged,
+    z, received, solve_rows, lift_rows, faces, masks, residual, direction, multipliers, arranged,
+    got0, got1, got2, got3,
     next_multipliers, next_residual, projected, image, fresh, sums, sent, to0, to1, to2, to3,
 ):
     amplitudes = coarse_amplitudes(z, received, solve_rows)
@@ -344,7 +359,8 @@
 
 
 def finish(
-    z, received, got0, got1, got2, got3, faces, masks, sums, multipliers, residual, direction, projected, image,
+    z, received, sums, faces, masks, residual, image, multipliers, projected, direction,
+    got0, got1, got2, got3,
     out_multipliers, out_residual,
 ):
     summed = jnp.sum(received[...], axis=0)
@@ -360,27 +376,41 @@
 
 
 class Coming:
-    def __init__(self, source, held, semaphore):
+    def __init__(self, source, held, semaphores):
         self.held = held
-        self.copy = pltpu.make_async_copy(source, held, semaphore)
-        self.copy.start()
-
-    def ready(self):
-        if self.copy is not None:
-            self.copy.wait()
-            self.copy = None
+        size = len(semaphores)
+        step = -(-held.shape[0] // size) if size > 1 else 0
+        self.copies = []
+        for i, semaphore in enumerate(semaphores):
+            part = pl.ds(i * step, step)
+            pair = (source, held) if size == 1 else (source.at[part], held.at[part])
+            self.copies.append(pltpu.make_async_copy(*pair, semaphore))
+            self.copies[-1].start()
+        self.step = step
+
+    def ready(self, only=None):
+        for i, copy in enumerate(self.copies):
+            if copy is not None and only in (None, i):
+                copy.wait()
+                self.copies[i] = None
         return self.held
 
     def __getitem__(self, index):
-        return self.ready()[index]
+        return self.ready(index[0].start // self.step if self.step else None)[index]
 
 
 class Going:
-    def __init__(self, held, target, semaphore):
+    def __init__(self, held, target, semaphores):
         self.held = held
-        self.copy = pltpu.make_async_copy(held, target, semaphore)
         self.shape, self.dtype = held.shape, held.dtype
-        self.started = False
+        size = len(semaphores)
+        self.copies = []
+        for i, semaphore in enumerate(semaphores):
+            step = held.shape[-1] // size
+            part = (slice(None), pl.ds(i * step, step))
+            pair = (held, target) if size == 1 else (held.at[part], target.at[part])
+            self.copies.append(pltpu.make_async_copy(*pair, semaphore))
+        self.started = [False] * size
 
     def __getitem__(self, index):
         return self.held[index]
@@ -388,43 +418,49 @@
     def __setitem__(self, index, values):
         self.held[index] = values
 
-    def push(self):
-        if not self.started:
-            self.copy.start()
-            self.started = True
-
-
-def call(z, kernel, outs, args, scratch=(), flops=0, near=0):
+    def push(self, only=None):
+        for i, copy in enumerate(self.copies):
+            if not self.started[i] and only in (None, i):
+                copy.start()
+                self.started[i] = True
+
+
+def call(z, kernel, outs, args, scratch=(), flops=0, near=0, kept=0):
     shapes = [jax.ShapeDtypeStruct(shape, dtype) for shape, dtype in outs]
     moved = sum(a.size * a.dtype.itemsize for a in args) + sum(s.size * s.dtype.itemsize for s in shapes)
-    far = len(args) - near
+    far, sent = len(args) - near, len(outs) - kept
+    large = (4 * z.lanes, 4 * z.lanes)
+    parts_in = [large[0] // BLOCK if a.shape == large else 1 for a in args[:far]]
+    parts_out = [4 if a.shape == large else 1 for a in shapes[:sent]]
 
     def run(*refs):
         refs = list(refs)
         take = lambda n: [refs.pop(0) for _ in range(n)]
-        sources, others, targets = take(far), take(near), take(len(outs))
-        held, made, work, semaphores = take(far), take(len(outs)), take(len(scratch)), refs[0]
-        coming = [Coming(a, b, semaphores.at[i]) for i, (a, b) in enumerate(zip(sources, held))]
-        going = [Going(a, b, semaphores.at[far + i]) for i, (a, b) in enumerate(zip(made, targets))]
-        kernel(z, *coming, *others, *going, *work)
+        sources, others, targets, direct = take(far), take(near), take(sent), take(kept)
+        held, made, work = take(far), take(sent), take(len(scratch))
+        flags = [refs[0].at[i] for i in range(sum(parts_in) + sum(parts_out))] if refs else []
+        some = lambda n: [flags.pop(0) for _ in range(n)]
+        coming = [Coming(a, b, some(n)) for a, b, n in zip(sources, held, parts_in)]
+        going = [Going(a, b, some(n)) for a, b, n in zip(made, targets, parts_out)]
+        kernel(z, *coming, *others, *going, *direct, *work)
         for item in going:
             item.push()
         for item in coming:
             item.ready()
         for item in going:
-            item.copy.wait()
-
-    specs = [pl.BlockSpec(memory_space=pltpu.HBM)] * far
-    specs += [pl.BlockSpec(memory_space=SMEM if a.ndim == 3 and a.size == 4 else VMEM) for a in args[far:]]
-    buffers = [VMEM(a.shape, a.dtype) for a in args[:far]] + [VMEM(shape, dtype) for shape, dtype in outs]
+            for copy in item.copies:
+                copy.wait()
+
+    near_spec = lambda a: pl.BlockSpec(memory_space=SMEM if a.ndim == 3 and a.size == 4 else VMEM)
+    far_spec = pl.BlockSpec(memory_space=pltpu.HBM)
+    buffers = [VMEM(a.shape, a.dtype) for a in list(args[:far]) + shapes[:sent]]
+    semaphores = [pltpu.SemaphoreType.DMA((sum(parts_in) + sum(parts_out),))] if far + sent else []
     return pl.pallas_call(
         run,
         out_shape=shapes,
-        in_specs=specs,
-        out_specs=[pl.BlockSpec(memory_space=pltpu.HBM) for _ in shapes],
-        scratch_shapes=buffers
-        + [VMEM(shape, dtype) for shape, dtype in scratch]
-        + [pltpu.SemaphoreType.DMA((far + len(outs),))],
+        in_specs=[far_spec] * far + [near_spec(a) for a in args[far:]],
+        out_specs=[far_spec] * sent + [near_spec(a) for a in shapes[sent:]],
+        scratch_shapes=buffers + [VMEM(shape, dtype) for shape, dtype in scratch] + semaphores,
         compiler_params=pltpu.CompilerParams(vmem_limit_bytes=60 * 2**20),
         cost_estimate=pl.CostEstimate(flops=flops, bytes_accessed=moved, transcendentals=0),
         name=kernel.__name__,
@@ -440,6 +476,7 @@
     field = ((4, z.cases, z.lanes), F32)
     mode_rows = ((4, 8, z.lanes), F32)
     pair_rows = ((4, 16, z.lanes), F32)
+    live_rows = ((8, z.lanes), F32)
     tile = ((8, 128), F32)
     sent = ((z.count, 8, 128), F32)
     to_faces = [((z.cases, z.lanes), F32)] * 4
@@ -447,14 +484,16 @@
     product_flops = 2 * z.cases * (4 * z.lanes) ** 2
 
     padded, masks, *trace_faces = call(
-        z, prepare, [mode_rows, mode_rows] + [((8, z.lanes), F32)] * 4,
-        [jnp.transpose(traces, (0, 1, 3, 2, 4)), counts], near=2,
+        z, prepare, [mode_rows, live_rows] + [((8, z.lanes), F32)] * 4,
+        [jnp.transpose(traces, (0, 1, 3, 2, 4)), counts], near=2, kept=6,
     )
     got = exchange(trace_faces)
-    across, local_tile, blocks = call(
-        z, couple, [mode_rows, tile, sent],
-        [padded, masks, *got, jnp.transpose(loads, (0, 2, 1, 3))],
-        [tile, ((8, z.cases), F32)], near=1,
+    (local_tile,) = call(
+        z, invert, [tile], [padded, masks, jnp.transpose(loads, (0, 2, 1, 3))],
+        [tile, ((8, z.cases), F32)], product_flops, near=3, kept=1,
+    )
+    blocks, masks, lift_rows = call(
+        z, couple, [sent, live_rows, pair_rows], [padded, masks, local_tile, *got], [tile], near=7,
     )
     blocks = gather(blocks)
     side = 4 * z.lanes
@@ -462,32 +501,28 @@
         z, arrange, [((side, side), BF16), field], [ops, primal, maps],
         [((8, z.padded), jnp.int32), ((side, z.padded), BF16)], 2 * side * side * z.width, near=1,
     )
-    solve_rows, rows, lift_rows, multipliers, faces, coarse, *sent_faces = call(
-        z, begin,
-        [((40, z.rows), F32), pair_rows, pair_rows, field, field, sent] + to_faces,
-        [blocks, padded, across, masks, local_tile, arranged, primal_faces],
+    solve_rows, rows, multipliers, faces, coarse, *sent_faces = call(
+        z, begin, [((40, z.rows), F32), pair_rows, field, field, sent] + to_faces,
+        [blocks, lift_rows, primal_faces, arranged],
         [((z.rows, columns), F32), tile], product_flops,
     )
     coarse, got = gather(coarse), exchange(sent_faces)
     residual, direction, faces, coarse, *sent_faces = call(
-        z, first_direction,
-        [field, field, field, sent] + to_faces,
-        [coarse, *got, faces, masks, solve_rows, lift_rows, arranged, rows],
-        [tile], product_flops,
+        z, first_direction, [field, field, field, sent] + to_faces,
+        [coarse, solve_rows, lift_rows, faces, masks, rows, arranged, *got],
+        [tile], product_flops, near=4,
     )
     coarse, got = gather(coarse), exchange(sent_faces)
     multipliers, residual, projected, image, faces, sums, coarse, *sent_faces = call(
-        z, second_direction,
-        [field, field, field, field, field, tile, sent] + to_faces,
-        [coarse, *got, faces, masks, solve_rows, lift_rows,
-         multipliers, residual, direction, arranged],
-        [], product_flops,
+        z, second_direction, [field, field, field, field, field, tile, sent] + to_faces,
+        [coarse, solve_rows, lift_rows, faces, masks, residual, direction, multipliers, arranged, *got],
+        [], product_flops, near=4,
     )
     coarse, got = gather(coarse), exchange(sent_faces)
     whole = ((1, 1, 4, z.cases, z.face), F32)
     multipliers, residual = call(
         z, finish, [whole, whole],
-        [coarse, *got, faces, masks, sums, multipliers, residual, direction, projected, image],
+        [coarse, sums, faces, masks, residual, image, multipliers, projected, direction, *got], near=4,
     )
     return multipliers, residual
 

time: 99.8 us -> 99 us (level)
  waiting for transfers between devices: 9.02 us -> 6.9 us
  Pallas kernels: 32.3 us -> 33.5 us
    ppermute x16, waiting for transfers between devices: 9.01 us -> 6.89 us  [exchange(): got[i] = lax.ppermute(sent[i], axis, pairs)]
    pallas_call x7 -> x8, Pallas kernels: 32.3 us -> 33.5 us  [call(): pl.pallas_call(run, out_shape=shapes, in_specs=[far_spec] * far + [near_s...]
  transfers between devices with their start and end apart: 20 -> 20, of which waited for: 4 -> 3; matrix products, arithmetic and copies ran while one was open for 0% -> 0% of each run, Pallas kernels for 11% -> 12%
where the time goes in v6:
time: 99 us; the launch traced here: 98.1 us
  starting transfers between devices  52.9 us (53%)
  Pallas kernels  33.5 us (34%)
  waiting for transfers between devices  6.9 us (7%)
  local copies, waits for them, and re-layouts  3.77 us (4%)
  between operations  1.03 us (1%)
    ppermute x16, starting transfers between devices, exchange(): got[i] = lax.ppermute(sent[i], axis, pairs)  33.6 us
    pallas_call x8, Pallas kernels, call(): pl.pallas_call(run, out_shape=shapes, in_specs=[far_spec] * far + [near_s...  33.5 us
    all_to_all x4, starting transfers between devices, gather(): return lax.all_to_all(values, AXES, 0, 0, tiled=True)  19.3 us
    ppermute x16, waiting for transfers between devices, exchange(): got[i] = lax.ppermute(sent[i], axis, pairs)  6.89 us
    unnamed x40, local copies, waits for them, and re-layouts  3.77 us
  transfers between devices with their start and end apart: 20, of which 3 were waited for; matrix products, arithmetic and copies ran while one was open for 0% of the time, Pallas kernels for 12%

profile of v6, /device:TPU:5, one launch (start us, length us, event | category | flops | bytes accessed | tf_op | source)
XLA Modules:
  0.0 98.1 jit_solution(9892632899710668332)
XLA Ops:
  0.6 1.4 %prepare.1 = (f32[4,8,384]{2,1,0:T(8,128)}, f32[8,384]{1,0:T(8,128)}, f32[8,384]{1,0:T(8,128)}, f32[8,384]{1,0:T(8,128)}, f32[8,384]{1,0:T(8,128)}, /*index=5*/f32[8,384]{1,0:T(8,128)}) custom-call(f32[1,1,6,4,300]{4,3,2,1,0:T(4,128)} %bitcast.2, s32[1,1,4]{2,1,0:T(1,128)} %refs_1_.2), custom_call_target="tpu_custom_call" | custom-call | bytes 139408 | tf_op jit(solution)/shard_map/prepare/pallas_call | solution.py:458
  2.1 4.4 %collective-permute-start.1 = (f32[8,384]{1,0:T(8,128)}, f32[8,384]{1,0:T(8,128)S(1)}, u32[]{:S(2)}, u32[]{:S(2)}) collective-permute-start(f32[8,384]{1,0:T(8,128)} %get-tuple-element.44), channel_id=1, source_target_pairs={{4,8},{8,4},{12,16},{16,12},{20,24},{24,20},{5,9},{9,5},{13,17},{1... | collective-permute-start | bytes 36872 | tf_op jit(solution)/shard_map/ppermute | solution.py:88
  6.5 1.3 %collective-permute-start.2 = (f32[8,384]{1,0:T(8,128)}, f32[8,384]{1,0:T(8,128)S(1)}, u32[]{:S(2)}, u32[]{:S(2)}) collective-permute-start(f32[8,384]{1,0:T(8,128)} %get-tuple-element.45), channel_id=1, source_target_pairs={{0,1},{1,0},{2,3},{3,2},{4,5},{5,4},{6,7},{7,6},{8,9},{9,8},{10,11... | collective-permute-start | bytes 36872 | tf_op jit(solution)/shard_map/ppermute | solution.py:88
  7.8 3.0 %collective-permute-start.3 = (f32[8,384]{1,0:T(8,128)}, f32[8,384]{1,0:T(8,128)S(1)}, u32[]{:S(2)}, u32[]{:S(2)}) collective-permute-start(f32[8,384]{1,0:T(8,128)} %get-tuple-element.46), channel_id=1, source_target_pairs={{1,2},{2,1},{5,6},{6,5},{9,10},{10,9},{13,14},{14,13},{17,18},{18,... | collective-permute-start | bytes 36872 | tf_op jit(solution)/shard_map/ppermute | solution.py:88
  10.8 2.4 %invert.1.refs_2_ = f32[8,128]{1,0:T(8,128)} custom-call(f32[4,8,384]{2,1,0:T(8,128)} %get-tuple-element.41.refs_0_, f32[8,384]{1,0:T(8,128)} %get-tuple-element.42.refs_1_, f32[1,6,1,16]{3,2,1,0:T(1,128)} %bitcast.3), custom_call_target="tpu_custom_call" | custom-call | flops 75497472 | bytes 65920 | tf_op jit(solution)/shard_map/invert/pallas_call | solution.py:458
  13.8 0.6 copy-done.19
  14.4 2.4 %couple.1 = (f32[32,8,128]{2,1,0:T(8,128)}, f32[8,384]{1,0:T(8,128)}, f32[4,16,384]{2,1,0:T(8,128)}) custom-call(f32[4,8,384]{2,1,0:T(8,128)} %get-tuple-element.41.refs_0_, f32[8,384]{1,0:T(8,128)} %get-tuple-element.42.refs_1_, f32[8,128]{1,0:T(8,128)} %invert.1.refs_2_, f32[8,384]{1,0:T(8,128)} %copy-done.16, f32[8,384]{1,0:T(8,128)} %copy-done.17, ...), custom_call_target="tpu_custom_call" | custom-call | bytes 356352 | tf_op jit(solution)/shard_map/couple/pallas_call | solution.py:458
  16.8 4.3 %all-to-all-start = ((f32[32,8,128]{2,1,0:T(8,128)}), f32[32,8,128]{2,1,0:T(8,128)S(1)}, u32[]{:S(2)}, u32[]{:S(2)}) async-start(f32[32,8,128]{2,1,0:T(8,128)} %get-tuple-element.47), calls=%async_computation | async-start | bytes 262144 | tf_op jit(solution)/shard_map/all_to_all | solution.py:471
  21.1 9.7 %arrange.1 = (bf16[1536,1536]{1,0:T(8,128)(2,1)}, f32[4,16,384]{2,1,0:T(8,128)}) custom-call(bf16[1,1,1200,1200]{3,2,1,0:T(8,128)(2,1)} %refs_0_.1, f32[1,1,16,1200]{3,2,1,0:T(8,128)} %refs_1_.3, s32[1,1,4,300]{3,2,1,0:T(4,128)} %refs_2_.1), custom_call_target="tpu_custom_call" | custom-call | flops 2415919104 | bytes 7778496 | tf_op jit(solution)/shard_map/arrange/pallas_call | solution.py:458
  30.8 0.6 copy-done.3
  31.5 4.7 %begin.1 = (f32[40,256]{1,0:T(8,128)}, f32[4,16,384]{2,1,0:T(8,128)}, f32[4,16,384]{2,1,0:T(8,128)}, f32[4,16,384]{2,1,0:T(8,128)}, f32[32,8,128]{2,1,0:T(8,128)...) custom-call(f32[32,8,128]{2,1,0:T(8,128)} %copy-done.3, ...), custom_call_target="tpu_custom_call" | custom-call | flops 75497472 | bytes 5611520 | tf_op jit(solution)/shard_map/begin/pallas_call | solution.py:458
  36.2 5.8 %all-to-all-start.1 = ((f32[32,8,128]{2,1,0:T(8,128)}), f32[32,8,128]{2,1,0:T(8,128)S(1)}, u32[]{:S(2)}, u32[]{:S(2)}) async-start(f32[32,8,128]{2,1,0:T(8,128)} %get-tuple-element.51), calls=%async_computation.1 | async-start | bytes 262144 | tf_op jit(solution)/shard_map/all_to_all | solution.py:471
  42.2 4.2 %collective-permute-start.5 = (f32[16,384]{1,0:T(8,128)}, f32[16,384]{1,0:T(8,128)S(1)}, u32[]{:S(2)}, u32[]{:S(2)}) collective-permute-start(f32[16,384]{1,0:T(8,128)} %get-tuple-element.57), channel_id=1, source_target_pairs={{4,8},{8,4},{12,16},{16,12},{20,24},{24,20},{5,9},{9,5},{13,17},{1... | collective-permute-start | bytes 73736 | tf_op jit(solution)/shard_map/ppermute | solution.py:88
  46.4 1.0 %collective-permute-start.6 = (f32[16,384]{1,0:T(8,128)}, f32[16,384]{1,0:T(8,128)S(1)}, u32[]{:S(2)}, u32[]{:S(2)}) collective-permute-start(f32[16,384]{1,0:T(8,128)} %get-tuple-element.58), channel_id=1, source_target_pairs={{0,1},{1,0},{2,3},{3,2},{4,5},{5,4},{6,7},{7,6},{8,9},{9,8},{10,11... | collective-permute-start | bytes 73736 | tf_op jit(solution)/shard_map/ppermute | solution.py:88
  47.3 3.0 %collective-permute-start.7 = (f32[16,384]{1,0:T(8,128)}, f32[16,384]{1,0:T(8,128)S(1)}, u32[]{:S(2)}, u32[]{:S(2)}) collective-permute-start(f32[16,384]{1,0:T(8,128)} %get-tuple-element.59), channel_id=1, source_target_pairs={{1,2},{2,1},{5,6},{6,5},{9,10},{10,9},{13,14},{14,13},{17,18},{18,... | collective-permute-start | bytes 73736 | tf_op jit(solution)/shard_map/ppermute | solution.py:88
  50.4 2.3 %collective-permute-done.7.refs_10_ = f32[16,384]{1,0:T(8,128)S(1)} collective-permute-done((f32[16,384]{1,0:T(8,128)}, f32[16,384]{1,0:T(8,128)S(1)}, u32[]{:S(2)}, u32[]{:S(2)}) %collective-permute-start.7) | collective-permute-done | bytes 24608 | tf_op jit(solution)/shard_map/ppermute | solution.py:88
  52.7 0.6 copy-done.11
  53.4 5.1 %first_direction.1 = (f32[4,16,384]{2,1,0:T(8,128)}, f32[4,16,384]{2,1,0:T(8,128)}, f32[4,16,384]{2,1,0:T(8,128)}, f32[32,8,128]{2,1,0:T(8,128)}, f32[16,384]{1,...) custom-call(f32[32,8,128]{2,1,0:T(8,128)} %copy-done.1, ...), custom_call_target="tpu_custom_call" | custom-call | flops 75497472 | bytes 5820416 | tf_op jit(solution)/shard_map/first_direction/pallas_call | solution.py:458
  58.5 4.6 %all-to-all-start.2 = ((f32[32,8,128]{2,1,0:T(8,128)}), f32[32,8,128]{2,1,0:T(8,128)S(1)}, u32[]{:S(2)}, u32[]{:S(2)}) async-start(f32[32,8,128]{2,1,0:T(8,128)} %get-tuple-element.60), calls=%async_computation.2 | async-start | bytes 262144 | tf_op jit(solution)/shard_map/all_to_all | solution.py:471
  63.2 4.2 %collective-permute-start.9 = (f32[16,384]{1,0:T(8,128)}, f32[16,384]{1,0:T(8,128)S(1)}, u32[]{:S(2)}, u32[]{:S(2)}) collective-permute-start(f32[16,384]{1,0:T(8,128)} %get-tuple-element.66), channel_id=1, source_target_pairs={{4,8},{8,4},{12,16},{16,12},{20,24},{24,20},{5,9},{9,5},{13,17},{1... | collective-permute-start | bytes 73736 | tf_op jit(solution)/shard_map/ppermute | solution.py:88
  67.4 1.0 %collective-permute-start.10 = (f32[16,384]{1,0:T(8,128)}, f32[16,384]{1,0:T(8,128)S(1)}, u32[]{:S(2)}, u32[]{:S(2)}) collective-permute-start(f32[16,384]{1,0:T(8,128)} %get-tuple-element.67), channel_id=1, source_target_pairs={{0,1},{1,0},{2,3},{3,2},{4,5},{5,4},{6,7},{7,6},{8,9},{9,8},{10,11... | collective-permute-start | bytes 73736 | tf_op jit(solution)/shard_map/ppermute | solution.py:88
  68.4 3.0 %collective-permute-start.11 = (f32[16,384]{1,0:T(8,128)}, f32[16,384]{1,0:T(8,128)S(1)}, u32[]{:S(2)}, u32[]{:S(2)}) collective-permute-start(f32[16,384]{1,0:T(8,128)} %get-tuple-element.68), channel_id=1, source_target_pairs={{1,2},{2,1},{5,6},{6,5},{9,10},{10,9},{13,14},{14,13},{17,18},{18,... | collective-permute-start | bytes 73736 | tf_op jit(solution)/shard_map/ppermute | solution.py:88
  71.4 2.3 %collective-permute-done.11.refs_12_ = f32[16,384]{1,0:T(8,128)S(1)} collective-permute-done((f32[16,384]{1,0:T(8,128)}, f32[16,384]{1,0:T(8,128)S(1)}, u32[]{:S(2)}, u32[]{:S(2)}) %collective-permute-start.11) | collective-permute-done | bytes 24608 | tf_op jit(solution)/shard_map/ppermute | solution.py:88
  73.8 0.6 copy-done.8
  74.4 5.0 %second_direction.1 = (f32[4,16,384]{2,1,0:T(8,128)}, f32[4,16,384]{2,1,0:T(8,128)}, f32[4,16,384]{2,1,0:T(8,128)}, f32[4,16,384]{2,1,0:T(8,128)}, f32[4,16,384]...) custom-call(f32[32,8,128]{2,1,0:T(8,128)} %copy-done, ...), custom_call_target="tpu_custom_call" | custom-call | flops 75497472 | bytes 6217728 | tf_op jit(solution)/shard_map/second_direction/pallas_call | solution.py:458
  79.4 4.6 %all-to-all-start.3 = ((f32[32,8,128]{2,1,0:T(8,128)}), f32[32,8,128]{2,1,0:T(8,128)S(1)}, u32[]{:S(2)}, u32[]{:S(2)}) async-start(f32[32,8,128]{2,1,0:T(8,128)} %get-tuple-element.69), calls=%async_computation.3 | async-start | bytes 262144 | tf_op jit(solution)/shard_map/all_to_all | solution.py:471
  84.1 4.2 %collective-permute-start.13 = (f32[16,384]{1,0:T(8,128)}, f32[16,384]{1,0:T(8,128)S(1)}, u32[]{:S(2)}, u32[]{:S(2)}) collective-permute-start(f32[16,384]{1,0:T(8,128)} %get-tuple-element.77), channel_id=1, source_target_pairs={{4,8},{8,4},{12,16},{16,12},{20,24},{24,20},{5,9},{9,5},{13,17},{1... | collective-permute-start | bytes 73736 | tf_op jit(solution)/shard_map/ppermute | solution.py:88
  88.3 1.0 %collective-permute-start.14 = (f32[16,384]{1,0:T(8,128)}, f32[16,384]{1,0:T(8,128)S(1)}, u32[]{:S(2)}, u32[]{:S(2)}) collective-permute-start(f32[16,384]{1,0:T(8,128)} %get-tuple-element.78), channel_id=1, source_target_pairs={{0,1},{1,0},{2,3},{3,2},{4,5},{5,4},{6,7},{7,6},{8,9},{9,8},{10,11... | collective-permute-start | bytes 73736 | tf_op jit(solution)/shard_map/ppermute | solution.py:88
  89.3 3.0 %collective-permute-start.15 = (f32[16,384]{1,0:T(8,128)}, f32[16,384]{1,0:T(8,128)S(1)}, u32[]{:S(2)}, u32[]{:S(2)}) collective-permute-start(f32[16,384]{1,0:T(8,128)} %get-tuple-element.79), channel_id=1, source_target_pairs={{1,2},{2,1},{5,6},{6,5},{9,10},{10,9},{13,14},{14,13},{17,18},{18,... | collective-permute-start | bytes 73736 | tf_op jit(solution)/shard_map/ppermute | solution.py:88
  92.4 2.3 %collective-permute-done.15.refs_12_ = f32[16,384]{1,0:T(8,128)S(1)} collective-permute-done((f32[16,384]{1,0:T(8,128)}, f32[16,384]{1,0:T(8,128)S(1)}, u32[]{:S(2)}, u32[]{:S(2)}) %collective-permute-start.15) | collective-permute-done | bytes 24608 | tf_op jit(solution)/shard_map/ppermute | solution.py:88
  94.7 0.6 copy-done.15
  95.3 2.8 %finish.1 = (f32[1,1,4,16,300]{4,3,2,1,0:T(8,128)}, f32[1,1,4,16,300]{4,3,2,1,0:T(8,128)}) custom-call(f32[32,8,128]{2,1,0:T(8,128)} %copy-done.2, f32[8,128]{1,0:T(8,128)} %get-tuple-element.70.refs_1_, f32[4,16,384]{2,1,0:T(8,128)} %get-tuple-element.71.refs_2_, f32[8,384]{1,0:T(8,128)} %get-tuple-element.54.refs_4_.refs_3_, ...), custom_call_target="tpu_custom_call" | custom-call | bytes 989184 | tf_op jit(solution)/shard_map/finish/pallas_call | solution.py:458
  (56 shorter events, 1.3 us)
Async XLA Ops:
  2.1 11.1 %collective-permute-start = (f32[8,384]{1,0:T(8,128)}, f32[8,384]{1,0:T(8,128)S(1)}, u32[]{:S(2)}, u32[]{:S(2)}) collective-permute-start(f32[8,384]{1,0:T(8,128)} %get-tuple-element.43), channel_id=1, source_target_pairs={{0,4},{4,0},{8,12},{12,8},{16,20},{20,16},{24,28},{28,24},{1,5},{5... | collective-permute-start | bytes 36872 | tf_op jit(solution)/shard_map/ppermute | solution.py:88
  2.1 11.1 %collective-permute-start.1 = (f32[8,384]{1,0:T(8,128)}, f32[8,384]{1,0:T(8,128)S(1)}, u32[]{:S(2)}, u32[]{:S(2)}) collective-permute-start(f32[8,384]{1,0:T(8,128)} %get-tuple-element.44), channel_id=1, source_target_pairs={{4,8},{8,4},{12,16},{16,12},{20,24},{24,20},{5,9},{9,5},{13,17},{1... | collective-permute-start | bytes 36872 | tf_op jit(solution)/shard_map/ppermute | solution.py:88
  6.5 6.8 %collective-permute-start.2 = (f32[8,384]{1,0:T(8,128)}, f32[8,384]{1,0:T(8,128)S(1)}, u32[]{:S(2)}, u32[]{:S(2)}) collective-permute-start(f32[8,384]{1,0:T(8,128)} %get-tuple-element.45), channel_id=1, source_target_pairs={{0,1},{1,0},{2,3},{3,2},{4,5},{5,4},{6,7},{7,6},{8,9},{9,8},{10,11... | collective-permute-start | bytes 36872 | tf_op jit(solution)/shard_map/ppermute | solution.py:88
  7.8 5.5 %collective-permute-start.3 = (f32[8,384]{1,0:T(8,128)}, f32[8,384]{1,0:T(8,128)S(1)}, u32[]{:S(2)}, u32[]{:S(2)}) collective-permute-start(f32[8,384]{1,0:T(8,128)} %get-tuple-element.46), channel_id=1, source_target_pairs={{1,2},{2,1},{5,6},{6,5},{9,10},{10,9},{13,14},{14,13},{17,18},{18,... | collective-permute-start | bytes 36872 | tf_op jit(solution)/shard_map/ppermute | solution.py:88
  16.8 14.0 %all-to-all-start = ((f32[32,8,128]{2,1,0:T(8,128)}), f32[32,8,128]{2,1,0:T(8,128)S(1)}, u32[]{:S(2)}, u32[]{:S(2)}) async-start(f32[32,8,128]{2,1,0:T(8,128)} %get-tuple-element.47), calls=%async_computation | async-start | bytes 262144 | tf_op jit(solution)/shard_map/all_to_all | solution.py:471
  30.8 0.7 copy-start.3
  36.2 16.5 %all-to-all-start.1 = ((f32[32,8,128]{2,1,0:T(8,128)}), f32[32,8,128]{2,1,0:T(8,128)S(1)}, u32[]{:S(2)}, u32[]{:S(2)}) async-start(f32[32,8,128]{2,1,0:T(8,128)} %get-tuple-element.51), calls=%async_computation.1 | async-start | bytes 262144 | tf_op jit(solution)/shard_map/all_to_all | solution.py:471
  42.0 8.3 %collective-permute-start.4 = (f32[16,384]{1,0:T(8,128)}, f32[16,384]{1,0:T(8,128)S(1)}, u32[]{:S(2)}, u32[]{:S(2)}) collective-permute-start(f32[16,384]{1,0:T(8,128)} %get-tuple-element.56), channel_id=1, source_target_pairs={{0,4},{4,0},{8,12},{12,8},{16,20},{20,16},{24,28},{28,24},{1,5},{5... | collective-permute-start | bytes 73736 | tf_op jit(solution)/shard_map/ppermute | solution.py:88
  42.2 8.2 %collective-permute-start.5 = (f32[16,384]{1,0:T(8,128)}, f32[16,384]{1,0:T(8,128)S(1)}, u32[]{:S(2)}, u32[]{:S(2)}) collective-permute-start(f32[16,384]{1,0:T(8,128)} %get-tuple-element.57), channel_id=1, source_target_pairs={{4,8},{8,4},{12,16},{16,12},{20,24},{24,20},{5,9},{9,5},{13,17},{1... | collective-permute-start | bytes 73736 | tf_op jit(solution)/shard_map/ppermute | solution.py:88
  46.4 4.0 %collective-permute-start.6 = (f32[16,384]{1,0:T(8,128)}, f32[16,384]{1,0:T(8,128)S(1)}, u32[]{:S(2)}, u32[]{:S(2)}) collective-permute-start(f32[16,384]{1,0:T(8,128)} %get-tuple-element.58), channel_id=1, source_target_pairs={{0,1},{1,0},{2,3},{3,2},{4,5},{5,4},{6,7},{7,6},{8,9},{9,8},{10,11... | collective-permute-start | bytes 73736 | tf_op jit(solution)/shard_map/ppermute | solution.py:88
  47.3 5.3 %collective-permute-start.7 = (f32[16,384]{1,0:T(8,128)}, f32[16,384]{1,0:T(8,128)S(1)}, u32[]{:S(2)}, u32[]{:S(2)}) collective-permute-start(f32[16,384]{1,0:T(8,128)} %get-tuple-element.59), channel_id=1, source_target_pairs={{1,2},{2,1},{5,6},{6,5},{9,10},{10,9},{13,14},{14,13},{17,18},{18,... | collective-permute-start | bytes 73736 | tf_op jit(solution)/shard_map/ppermute | solution.py:88
  50.4 2.3 %copy-start.7 = (f32[16,384]{1,0:T(8,128)}, f32[16,384]{1,0:T(8,128)S(1)}, u32[]{:S(2)}) copy-start(f32[16,384]{1,0:T(8,128)S(1)} %collective-permute-done.4.refs_7_) | copy-start | bytes 73732
  50.4 2.3 %copy-start.9 = (f32[16,384]{1,0:T(8,128)}, f32[16,384]{1,0:T(8,128)S(1)}, u32[]{:S(2)}) copy-start(f32[16,384]{1,0:T(8,128)S(1)} %collective-permute-done.5.refs_8_) | copy-start | bytes 73732
  50.4 2.3 %copy-start.10 = (f32[16,384]{1,0:T(8,128)}, f32[16,384]{1,0:T(8,128)S(1)}, u32[]{:S(2)}) copy-start(f32[16,384]{1,0:T(8,128)S(1)} %collective-permute-done.6.refs_9_) | copy-start | bytes 73732
  52.7 0.7 copy-start.1
  58.5 15.3 %all-to-all-start.2 = ((f32[32,8,128]{2,1,0:T(8,128)}), f32[32,8,128]{2,1,0:T(8,128)S(1)}, u32[]{:S(2)}, u32[]{:S(2)}) async-start(f32[32,8,128]{2,1,0:T(8,128)} %get-tuple-element.60), calls=%async_computation.2 | async-start | bytes 262144 | tf_op jit(solution)/shard_map/all_to_all | solution.py:471
  63.1 8.3 %collective-permute-start.8 = (f32[16,384]{1,0:T(8,128)}, f32[16,384]{1,0:T(8,128)S(1)}, u32[]{:S(2)}, u32[]{:S(2)}) collective-permute-start(f32[16,384]{1,0:T(8,128)} %get-tuple-element.65), channel_id=1, source_target_pairs={{0,4},{4,0},{8,12},{12,8},{16,20},{20,16},{24,28},{28,24},{1,5},{5... | collective-permute-start | bytes 73736 | tf_op jit(solution)/shard_map/ppermute | solution.py:88
  63.2 8.2 %collective-permute-start.9 = (f32[16,384]{1,0:T(8,128)}, f32[16,384]{1,0:T(8,128)S(1)}, u32[]{:S(2)}, u32[]{:S(2)}) collective-permute-start(f32[16,384]{1,0:T(8,128)} %get-tuple-element.66), channel_id=1, source_target_pairs={{4,8},{8,4},{12,16},{16,12},{20,24},{24,20},{5,9},{9,5},{13,17},{1... | collective-permute-start | bytes 73736 | tf_op jit(solution)/shard_map/ppermute | solution.py:88
  67.4 4.0 %collective-permute-start.10 = (f32[16,384]{1,0:T(8,128)}, f32[16,384]{1,0:T(8,128)S(1)}, u32[]{:S(2)}, u32[]{:S(2)}) collective-permute-start(f32[16,384]{1,0:T(8,128)} %get-tuple-element.67), channel_id=1, source_target_pairs={{0,1},{1,0},{2,3},{3,2},{4,5},{5,4},{6,7},{7,6},{8,9},{9,8},{10,11... | collective-permute-start | bytes 73736 | tf_op jit(solution)/shard_map/ppermute | solution.py:88
  68.4 5.3 %collective-permute-start.11 = (f32[16,384]{1,0:T(8,128)}, f32[16,384]{1,0:T(8,128)S(1)}, u32[]{:S(2)}, u32[]{:S(2)}) collective-permute-start(f32[16,384]{1,0:T(8,128)} %get-tuple-element.68), channel_id=1, source_target_pairs={{1,2},{2,1},{5,6},{6,5},{9,10},{10,9},{13,14},{14,13},{17,18},{18,... | collective-permute-start | bytes 73736 | tf_op jit(solution)/shard_map/ppermute | solution.py:88
  71.4 2.3 %copy-start.4 = (f32[16,384]{1,0:T(8,128)}, f32[16,384]{1,0:T(8,128)S(1)}, u32[]{:S(2)}) copy-start(f32[16,384]{1,0:T(8,128)S(1)} %collective-permute-done.8.refs_9_) | copy-start | bytes 73732
  71.4 2.3 %copy-start.5 = (f32[16,384]{1,0:T(8,128)}, f32[16,384]{1,0:T(8,128)S(1)}, u32[]{:S(2)}) copy-start(f32[16,384]{1,0:T(8,128)S(1)} %collective-permute-done.9.refs_10_) | copy-start | bytes 73732
  71.4 2.3 %copy-start.6 = (f32[16,384]{1,0:T(8,128)}, f32[16,384]{1,0:T(8,128)S(1)}, u32[]{:S(2)}) copy-start(f32[16,384]{1,0:T(8,128)S(1)} %collective-permute-done.10.refs_11_) | copy-start | bytes 73732
  73.7 0.7 copy-start
  79.4 15.3 %all-to-all-start.3 = ((f32[32,8,128]{2,1,0:T(8,128)}), f32[32,8,128]{2,1,0:T(8,128)S(1)}, u32[]{:S(2)}, u32[]{:S(2)}) async-start(f32[32,8,128]{2,1,0:T(8,128)} %get-tuple-element.69), calls=%async_computation.3 | async-start | bytes 262144 | tf_op jit(solution)/shard_map/all_to_all | solution.py:471
  84.0 8.3 %collective-permute-start.12 = (f32[16,384]{1,0:T(8,128)}, f32[16,384]{1,0:T(8,128)S(1)}, u32[]{:S(2)}, u32[]{:S(2)}) collective-permute-start(f32[16,384]{1,0:T(8,128)} %get-tuple-element.76), channel_id=1, source_target_pairs={{0,4},{4,0},{8,12},{12,8},{16,20},{20,16},{24,28},{28,24},{1,5},{5... | collective-permute-start | bytes 73736 | tf_op jit(solution)/shard_map/ppermute | solution.py:88
  84.1 8.2 %collective-permute-start.13 = (f32[16,384]{1,0:T(8,128)}, f32[16,384]{1,0:T(8,128)S(1)}, u32[]{:S(2)}, u32[]{:S(2)}) collective-permute-start(f32[16,384]{1,0:T(8,128)} %get-tuple-element.77), channel_id=1, source_target_pairs={{4,8},{8,4},{12,16},{16,12},{20,24},{24,20},{5,9},{9,5},{13,17},{1... | collective-permute-start | bytes 73736 | tf_op jit(solution)/shard_map/ppermute | solution.py:88
  88.3 4.0 %collective-permute-start.14 = (f32[16,384]{1,0:T(8,128)}, f32[16,384]{1,0:T(8,128)S(1)}, u32[]{:S(2)}, u32[]{:S(2)}) collective-permute-start(f32[16,384]{1,0:T(8,128)} %get-tuple-element.78), channel_id=1, source_target_pairs={{0,1},{1,0},{2,3},{3,2},{4,5},{5,4},{6,7},{7,6},{8,9},{9,8},{10,11... | collective-permute-start | bytes 73736 | tf_op jit(solution)/shard_map/ppermute | solution.py:88
  89.3 5.3 %collective-permute-start.15 = (f32[16,384]{1,0:T(8,128)}, f32[16,384]{1,0:T(8,128)S(1)}, u32[]{:S(2)}, u32[]{:S(2)}) collective-permute-start(f32[16,384]{1,0:T(8,128)} %get-tuple-element.79), channel_id=1, source_target_pairs={{1,2},{2,1},{5,6},{6,5},{9,10},{10,9},{13,14},{14,13},{17,18},{18,... | collective-permute-start | bytes 73736 | tf_op jit(solution)/shard_map/ppermute | solution.py:88
  92.3 2.3 %copy-start.12 = (f32[16,384]{1,0:T(8,128)}, f32[16,384]{1,0:T(8,128)S(1)}, u32[]{:S(2)}) copy-start(f32[16,384]{1,0:T(8,128)S(1)} %collective-permute-done.12.refs_9_) | copy-start | bytes 73732
  92.3 2.3 %copy-start.13 = (f32[16,384]{1,0:T(8,128)}, f32[16,384]{1,0:T(8,128)S(1)}, u32[]{:S(2)}) copy-start(f32[16,384]{1,0:T(8,128)S(1)} %collective-permute-done.13.refs_10_) | copy-start | bytes 73732
  92.4 2.3 %copy-start.14 = (f32[16,384]{1,0:T(8,128)}, f32[16,384]{1,0:T(8,128)S(1)}, u32[]{:S(2)}) copy-start(f32[16,384]{1,0:T(8,128)S(1)} %collective-permute-done.14.refs_11_) | copy-start | bytes 73732
  (8 other events, 4.9 us)

commit v7 on v6

--- a/solution.py
+++ b/solution.py
@@ -17,7 +17,7 @@
 FIRST_LANE = 32
 INVERSE_LANE = 48
 SCALAR_LANE = 96
-BLOCK = 512
+BLOCK = 256
 
 
 class Sizes:
@@ -106,42 +106,48 @@
     masks[...] = live
 
 
-def arrange(z, ops, primal, maps, arranged, primal_faces, flat, half):
+def blocks_of(z):
+    found = []
+    for low in range(0, z.order, BLOCK):
+        high = min(low + BLOCK, z.order)
+        first, last = low // z.face, (high - 1) // z.face
+        found.append((low, high, first * z.face // 128 * 128, min(-(-(last + 1) * z.face // 128) * 128, z.order)))
+    return found
+
+
+def arrange(z, ops, primal, maps, primal_packed, arranged, flat, half):
     flat[...] = jnp.zeros_like(flat)
     flat[0:4, 0 : z.face] = maps[0, 0]
     lane = iota((1, z.padded), 1)
     line = jnp.full((1, z.padded), -1, jnp.int32)
+    signs = jnp.zeros((1, z.padded), F32)
     for f in range(4):
         moved = pltpu.roll(flat[...], f * z.face, 1)[f : f + 1] if f else flat[0:1]
-        line = jnp.where((lane >= f * z.face) & (lane < (f + 1) * z.face), moved, line)
+        here = (lane >= f * z.face) & (lane < (f + 1) * z.face)
+        line = jnp.where(here, moved + f * z.face, line)
+        signs = jnp.where(here, SIGNS[f], signs)
     column = jnp.transpose(jnp.broadcast_to(line, (8, z.padded)))[:, 0:1]
-    place_of = iota((z.padded, 1), 0)
-    half[:, z.order :] = jnp.zeros((4 * z.lanes, z.padded - z.order), BF16)
-    for f in range(4):
-        low, high = f * z.face, (f + 1) * z.face
-        size = min(z.width, z.order - z.starts[f])
-        here = jnp.where((lane >= low) & (lane < high), line, -1)[:, z.starts[f] : z.starts[f] + size]
-        forward = jnp.where(iota((z.lanes, size), 0) == here, SIGNS[f], 0.0).astype(BF16)
-        rows = ops[0, 0, z.starts[f] : z.starts[f] + size, :]
-        half[f * z.lanes : (f + 1) * z.lanes, 0 : z.order] = dot(forward, rows, precision=None).astype(BF16)
+    spread = []
+    for low, high, first, last in blocks_of(z):
+        hit = (iota((last - first, high - low), 1) + low) == column[first:last]
+        spread.append(hit.astype(F32).astype(BF16))
+    for low, high, first, last in blocks_of(z):
+        hit = (iota((high - low, last - first), 0) + low) == line[:, first:last]
+        collect = jnp.where(hit, signs[:, first:last], 0.0).astype(BF16)
+        half[low:high, :] = dot(collect, ops[0, 0, first:last, :], precision=None).astype(BF16)
     values = primal[0, 0]
     parts = []
     for _ in range(3):
         parts.append(values.astype(BF16))
         values = values - parts[-1].astype(F32)
     pieces = jnp.concatenate(parts, axis=0)
-    for f in range(4):
-        low, high = f * z.face, (f + 1) * z.face
-        size = min(z.width, z.order - z.starts[f])
-        window = slice(z.starts[f], z.starts[f] + z.width)
-        there = jnp.where((place_of >= low) & (place_of < high), column, -1)[window]
-        backward = (iota((z.width, z.lanes), 1) == there).astype(F32).astype(BF16)
-        block = slice(f * z.lanes, (f + 1) * z.lanes)
-        arranged[:, block] = dot(half[:, window], backward, precision=None).astype(BF16)
-        arranged.push(f)
-        three = dot(pieces[:, z.starts[f] : z.starts[f] + size], backward[0:size], precision=None)
-        n = z.cases
-        primal_faces[f] = three[0:n] + (three[n : 2 * n] + three[2 * n :])
+    n = z.cases
+    for (low, high, first, last), there in zip(blocks_of(z), spread):
+        three = dot(pieces[:, first:last], there, precision=None)
+        primal_packed[:, low:high] = three[0:n] + (three[n : 2 * n] + three[2 * n :])
+    primal_packed.push()
+    for (low, high, first, last), there in zip(blocks_of(z), spread):
+        arranged[:, low:high] = dot(half[:, first:last], there, precision=None).astype(BF16)
 
 
 def invert(z, padded, masks, loads, local_tile, aug, small):
@@ -181,13 +187,24 @@
     return dot(pair, lift_rows[f], (0, 0))
 
 
-def apply(z, faces, arranged):
-    operand = jnp.concatenate([face.astype(BF16) for face in faces], axis=1)
-    image = sum(
-        dot(operand[:, low : low + BLOCK], arranged[low : low + BLOCK, :], precision=None)
-        for low in range(0, 4 * z.lanes, BLOCK)
-    )
-    return [image[:, f * z.lanes : (f + 1) * z.lanes] for f in range(4)]
+def apply(z, faces, arranged, packed):
+    packed[...] = jnp.zeros(packed.shape, F32)
+    for f in range(4):
+        wide = jnp.concatenate([faces[f], jnp.zeros((z.cases, z.width - z.lanes), F32)], axis=1)
+        shift = f * z.face - z.starts[f]
+        packed[:, z.starts[f] : z.starts[f] + z.width] += pltpu.roll(wide, shift, 1) if shift else wide
+    return dot(packed[:, 0 : z.order].astype(BF16), arranged[...], precision=None)
+
+
+def unpacked(z, values, packed):
+    packed[:, 0 : z.order] = values
+    found = []
+    for f in range(4):
+        part = packed[:, z.starts[f] : z.starts[f] + z.width]
+        shift = f * z.face - z.starts[f]
+        part = (pltpu.roll(part, z.width - shift, 1) if shift else part)[:, 0 : z.lanes]
+        found.append(jnp.where(iota(part.shape, 1) < z.face, part, 0.0))
+    return found
 
 
 def send_coarse(z, faces, rows, scalars, sent, tile):
@@ -246,9 +263,9 @@
 
 
 def begin(
-    z, received, lift_rows, primal, arranged,
+    z, lift_rows, primal, received, arranged,
     solve_rows, rows, multipliers, faces, sent, to0, to1, to2, to3,
-    matrix, tile,
+    matrix, tile, packed,
 ):
     ix, iy = place()
     near_spots = spots(z, ix, iy)
@@ -287,7 +304,7 @@
         multipliers[f] = fields[f]
     for item in (solve_rows, rows, multipliers):
         item.push()
-    image = [primal[f] - part for f, part in enumerate(apply(z, fields, arranged))]
+    image = unpacked(z, primal[...] - apply(z, fields, arranged, packed), packed)
     for f in range(4):
         faces[f] = image[f]
     faces.push()
@@ -301,9 +318,9 @@
 
 
 def first_direction(
-    z, received, solve_rows, lift_rows, faces, masks, rows, arranged, got0, got1, got2, got3,
+    z, solve_rows, lift_rows, faces, masks, rows, got0, got1, got2, got3, received, arranged,
     residual, direction, image, sent, to0, to1, to2, to3,
-    tile,
+    tile, packed,
 ):
     amplitudes = coarse_amplitudes(z, received, solve_rows)
     field = jumped(z, masks, faces, (got0, got1, got2, got3))
@@ -314,7 +331,7 @@
         direction[f] = moved[f]
     residual.push()
     direction.push()
-    found = apply(z, moved, arranged)
+    found = unpacked(z, apply(z, moved, arranged, packed), packed)
     for f in range(4):
         image[f] = found[f]
     image.push()
@@ -325,9 +342,10 @@
 
 
 def second_direction(
-    z, received, solve_rows, lift_rows, faces, masks, residual, direction, multipliers, arranged,
-    got0, got1, got2, got3,
+    z, solve_rows, lift_rows, faces, masks, residual, direction, multipliers,
+    got0, got1, got2, got3, received, arranged,
     next_multipliers, next_residual, projected, image, fresh, sums, sent, to0, to1, to2, to3,
+    packed,
 ):
     amplitudes = coarse_amplitudes(z, received, solve_rows)
     summed = jnp.sum(received[...], axis=0)
@@ -345,7 +363,7 @@
         projected[f] = moved[f]
     for item in (sums, image, next_multipliers, next_residual, projected):
         item.push()
-    found = apply(z, moved, arranged)
+    found = unpacked(z, apply(z, moved, arranged, packed), packed)
     for f in range(4):
         fresh[f] = found[f]
     fresh.push()
@@ -359,8 +377,8 @@
 
 
 def finish(
-    z, received, sums, faces, masks, residual, image, multipliers, projected, direction,
-    got0, got1, got2, got3,
+    z, sums, faces, masks, residual, image, multipliers, projected, direction,
+    got0, got1, got2, got3, received,
     out_multipliers, out_residual,
 ):
     summed = jnp.sum(received[...], axis=0)
@@ -376,41 +394,27 @@
 
 
 class Coming:
-    def __init__(self, source, held, semaphores):
+    def __init__(self, source, held, semaphore):
         self.held = held
-        size = len(semaphores)
-        step = -(-held.shape[0] // size) if size > 1 else 0
-        self.copies = []
-        for i, semaphore in enumerate(semaphores):
-            part = pl.ds(i * step, step)
-            pair = (source, held) if size == 1 else (source.at[part], held.at[part])
-            self.copies.append(pltpu.make_async_copy(*pair, semaphore))
-            self.copies[-1].start()
-        self.step = step
-
-    def ready(self, only=None):
-        for i, copy in enumerate(self.copies):
-            if copy is not None and only in (None, i):
-                copy.wait()
-                self.copies[i] = None
+        self.copy = pltpu.make_async_copy(source, held, semaphore)
+        self.copy.start()
+
+    def ready(self):
+        if self.copy is not None:
+            self.copy.wait()
+            self.copy = None
         return self.held
 
     def __getitem__(self, index):
-        return self.ready(index[0].start // self.step if self.step else None)[index]
+        return self.ready()[index]
 
 
 class Going:
-    def __init__(self, held, target, semaphores):
+    def __init__(self, held, target, semaphore):
         self.held = held
+        self.copy = pltpu.make_async_copy(held, target, semaphore)
         self.shape, self.dtype = held.shape, held.dtype
-        size = len(semaphores)
-        self.copies = []
-        for i, semaphore in enumerate(semaphores):
-            step = held.shape[-1] // size
-            part = (slice(None), pl.ds(i * step, step))
-            pair = (held, target) if size == 1 else (held.at[part], target.at[part])
-            self.copies.append(pltpu.make_async_copy(*pair, semaphore))
-        self.started = [False] * size
+        self.started = False
 
     def __getitem__(self, index):
         return self.held[index]
@@ -418,53 +422,46 @@
     def __setitem__(self, index, values):
         self.held[index] = values
 
-    def push(self, only=None):
-        for i, copy in enumerate(self.copies):
-            if not self.started[i] and only in (None, i):
-                copy.start()
-                self.started[i] = True
+    def push(self):
+        if not self.started:
+            self.copy.start()
+            self.started = True
 
 
 def call(z, kernel, outs, args, scratch=(), flops=0, near=0, kept=0):
     shapes = [jax.ShapeDtypeStruct(shape, dtype) for shape, dtype in outs]
     moved = sum(a.size * a.dtype.itemsize for a in args) + sum(s.size * s.dtype.itemsize for s in shapes)
     far, sent = len(args) - near, len(outs) - kept
-    large = (4 * z.lanes, 4 * z.lanes)
-    parts_in = [large[0] // BLOCK if a.shape == large else 1 for a in args[:far]]
-    parts_out = [4 if a.shape == large else 1 for a in shapes[:sent]]
 
     def run(*refs):
         refs = list(refs)
         take = lambda n: [refs.pop(0) for _ in range(n)]
         sources, others, targets, direct = take(far), take(near), take(sent), take(kept)
         held, made, work = take(far), take(sent), take(len(scratch))
-        flags = [refs[0].at[i] for i in range(sum(parts_in) + sum(parts_out))] if refs else []
-        some = lambda n: [flags.pop(0) for _ in range(n)]
-        coming = [Coming(a, b, some(n)) for a, b, n in zip(sources, held, parts_in)]
-        going = [Going(a, b, some(n)) for a, b, n in zip(made, targets, parts_out)]
+        coming = [Coming(a, b, refs[0].at[i]) for i, (a, b) in enumerate(zip(sources, held))]
+        going = [Going(a, b, refs[0].at[far + i]) for i, (a, b) in enumerate(zip(made, targets))]
         kernel(z, *coming, *others, *going, *direct, *work)
         for item in going:
             item.push()
         for item in coming:
             item.ready()
         for item in going:
-            for copy in item.copies:
-                copy.wait()
+            item.copy.wait()
 
     near_spec = lambda a: pl.BlockSpec(memory_space=SMEM if a.ndim == 3 and a.size == 4 else VMEM)
     far_spec = pl.BlockSpec(memory_space=pltpu.HBM)
     buffers = [VMEM(a.shape, a.dtype) for a in list(args[:far]) + shapes[:sent]]
-    semaphores = [pltpu.SemaphoreType.DMA((sum(parts_in) + sum(parts_out),))] if far + sent else []
+    semaphores = [pltpu.SemaphoreType.DMA((far + sent,))] if far + sent else []
     return pl.pallas_call(
         run,
-        out_shape=shapes,
+        out_shape=[pltpu.HBM(a.shape, a.dtype) for a in shapes[:sent]] + shapes[sent:],
         in_specs=[far_spec] * far + [near_spec(a) for a in args[far:]],
         out_specs=[far_spec] * sent + [near_spec(a) for a in shapes[sent:]],
         scratch_shapes=buffers + [VMEM(shape, dtype) for shape, dtype in scratch] + semaphores,
-        compiler_params=pltpu.CompilerParams(vmem_limit_bytes=60 * 2**20),
+        compiler_params=pltpu.CompilerParams(vmem_limit_bytes=24 * 2**20),
         cost_estimate=pl.CostEstimate(flops=flops, bytes_accessed=moved, transcendentals=0),
         name=kernel.__name__,
-    )(*args)
+    )(*[pltpu.with_memory_space_constraint(a, pltpu.HBM) for a in args[:far]], *args[far:])
 
 
 def gather(values):
@@ -481,7 +478,7 @@
     sent = ((z.count, 8, 128), F32)
     to_faces = [((z.cases, z.lanes), F32)] * 4
     columns = -(-z.rows // 128) * 128
-    product_flops = 2 * z.cases * (4 * z.lanes) ** 2
+    product_flops = 2 * z.cases * z.order**2
 
     padded, masks, *trace_faces = call(
         z, prepare, [mode_rows, live_rows] + [((8, z.lanes), F32)] * 4,
@@ -496,33 +493,33 @@
         z, couple, [sent, live_rows, pair_rows], [padded, masks, local_tile, *got], [tile], near=7,
     )
     blocks = gather(blocks)
-    side = 4 * z.lanes
-    arranged, primal_faces = call(
-        z, arrange, [((side, side), BF16), field], [ops, primal, maps],
-        [((8, z.padded), jnp.int32), ((side, z.padded), BF16)], 2 * side * side * z.width, near=1,
+    packed = ((z.cases, z.padded), F32)
+    primal_packed, arranged = call(
+        z, arrange, [((z.cases, z.order), F32), ((z.order, z.order), BF16)], [ops, primal, maps],
+        [((8, z.padded), jnp.int32), ((z.order, z.order), BF16)], 4 * z.order**2 * z.width, near=1, kept=1,
     )
     solve_rows, rows, multipliers, faces, coarse, *sent_faces = call(
         z, begin, [((40, z.rows), F32), pair_rows, field, field, sent] + to_faces,
-        [blocks, lift_rows, primal_faces, arranged],
-        [((z.rows, columns), F32), tile], product_flops,
+        [lift_rows, primal_packed, blocks, arranged],
+        [((z.rows, columns), F32), tile, packed], product_flops, near=2,
     )
     coarse, got = gather(coarse), exchange(sent_faces)
     residual, direction, faces, coarse, *sent_faces = call(
         z, first_direction, [field, field, field, sent] + to_faces,
-        [coarse, solve_rows, lift_rows, faces, masks, rows, arranged, *got],
-        [tile], product_flops, near=4,
+        [solve_rows, lift_rows, faces, masks, rows, *got, coarse, arranged],
+        [tile, packed], product_flops, near=2,
     )
     coarse, got = gather(coarse), exchange(sent_faces)
     multipliers, residual, projected, image, faces, sums, coarse, *sent_faces = call(
         z, second_direction, [field, field, field, field, field, tile, sent] + to_faces,
-        [coarse, solve_rows, lift_rows, faces, masks, residual, direction, multipliers, arranged, *got],
-        [], product_flops, near=4,
+        [solve_rows, lift_rows, faces, masks, residual, direction, multipliers, *got, coarse, arranged],
+        [packed], product_flops, near=2,
     )
     coarse, got = gather(coarse), exchange(sent_faces)
     whole = ((1, 1, 4, z.cases, z.face), F32)
     multipliers, residual = call(
         z, finish, [whole, whole],
-        [coarse, sums, faces, masks, residual, image, multipliers, projected, direction, *got], near=4,
+        [sums, faces, masks, residual, image, multipliers, projected, direction, *got, coarse], near=1,
     )
     return multipliers, residual
 

time: 99 us -> 89.5 us (0.904)
  Pallas kernels: 33.5 us -> 22.5 us
    pallas_call x8, Pallas kernels: 33.5 us -> 22.5 us  [call(): pl.pallas_call(run, out_shape=[pltpu.HBM(a.shape, a.dtype) for a in shape...]
    unnamed x40 -> x32, local copies, waits for them, and re-layouts: 3.77 us -> 4.56 us
  transfers between devices with their start and end apart: 20 -> 20, of which waited for: 3 -> 4; matrix products, arithmetic and copies ran while one was open for 0% -> 0% of each run, Pallas kernels for 12% -> 9%
where the time goes in v7:
time: 89.5 us; the launch traced here: 88.7 us
  starting transfers between devices  53.5 us (60%)
  Pallas kernels  22.5 us (25%)
  waiting for transfers between devices  7.18 us (8%)
  local copies, waits for them, and re-layouts  4.56 us (5%)
  between operations  1.03 us (1%)
    ppermute x16, starting transfers between devices, exchange(): got[i] = lax.ppermute(sent[i], axis, pairs)  33.7 us
    pallas_call x8, Pallas kernels, call(): pl.pallas_call(run, out_shape=[pltpu.HBM(a.shape, a.dtype) for a in shape...  22.5 us
    all_to_all x4, starting transfers between devices, gather(): return lax.all_to_all(values, AXES, 0, 0, tiled=True)  19.8 us
    ppermute x16, waiting for transfers between devices, exchange(): got[i] = lax.ppermute(sent[i], axis, pairs)  7.17 us
    unnamed x32, local copies, waits for them, and re-layouts  4.56 us
  transfers between devices with their start and end apart: 20, of which 4 were waited for; matrix products, arithmetic and copies ran while one was open for 0% of the time, Pallas kernels for 9%

profile of v7, /device:TPU:5, one launch (start us, length us, event | category | flops | bytes accessed | tf_op | source)
XLA Modules:
  0.0 88.7 jit_solution(10612645935579731762)
XLA Ops:
  0.6 0.8 copy-done
  1.4 0.7 copy-done.1
  2.7 4.4 %collective-permute-start.1 = (f32[8,384]{1,0:T(8,128)S(1)}, f32[8,384]{1,0:T(8,128)S(1)}, u32[]{:S(2)}, u32[]{:S(2)}) collective-permute-start(f32[8,384]{1,0:T(8,128)S(1)} %get-tuple-element.44), channel_id=1, source_target_pairs={{4,8},{8,4},{12,16},{16,12},{20,24},{24,20},{5,9},{9,5},{13,17},{1... | collective-permute-start | bytes 36872 | tf_op jit(solution)/shard_map/ppermute | solution.py:88
  7.1 1.3 %collective-permute-start.2 = (f32[8,384]{1,0:T(8,128)S(1)}, f32[8,384]{1,0:T(8,128)S(1)}, u32[]{:S(2)}, u32[]{:S(2)}) collective-permute-start(f32[8,384]{1,0:T(8,128)S(1)} %get-tuple-element.45), channel_id=1, source_target_pairs={{0,1},{1,0},{2,3},{3,2},{4,5},{5,4},{6,7},{7,6},{8,9},{9,8},{10,11... | collective-permute-start | bytes 36872 | tf_op jit(solution)/shard_map/ppermute | solution.py:88
  8.4 3.0 %collective-permute-start.3 = (f32[8,384]{1,0:T(8,128)S(1)}, f32[8,384]{1,0:T(8,128)S(1)}, u32[]{:S(2)}, u32[]{:S(2)}) collective-permute-start(f32[8,384]{1,0:T(8,128)S(1)} %get-tuple-element.46), channel_id=1, source_target_pairs={{1,2},{2,1},{5,6},{6,5},{9,10},{10,9},{13,14},{14,13},{17,18},{18,... | collective-permute-start | bytes 36872 | tf_op jit(solution)/shard_map/ppermute | solution.py:88
  11.4 0.7 copy-done.3
  12.1 1.0 %invert.1.refs_2_ = f32[8,128]{1,0:T(8,128)S(1)} custom-call(f32[4,8,384]{2,1,0:T(8,128)S(1)} %get-tuple-element.41.refs_0_, f32[8,384]{1,0:T(8,128)S(1)} %get-tuple-element.42.refs_1_, f32[1,6,1,16]{3,2,1,0:T(1,128)S(1)} %bitcast.3), custom_call_target="tpu_custom_call" | custom-call | flops 46080000 | bytes 65920 | tf_op jit(solution)/shard_map/invert/pallas_call | solution.py:455
  13.4 1.5 %couple.1 = (f32[32,8,128]{2,1,0:T(8,128)}, f32[8,384]{1,0:T(8,128)}, f32[4,16,384]{2,1,0:T(8,128)}) custom-call(f32[4,8,384]{2,1,0:T(8,128)S(1)} %get-tuple-element.41.refs_0_, f32[8,384]{1,0:T(8,128)S(1)} %get-tuple-element.42.refs_1_, f32[8,128]{1,0:T(8,128)S(1)} %invert.1.refs_2_, f32[8,384]{1,0:T(8,128)S(1)} %collective-permute-done.refs_3_, ...), custom_call_target="tpu_custom_call" | custom-call | bytes 356352 | tf_op jit(solution)/shard_map/couple/pallas_call | solution.py:455
  14.9 4.8 %all-to-all-start = ((f32[32,8,128]{2,1,0:T(8,128)}), f32[32,8,128]{2,1,0:T(8,128)S(1)}, u32[]{:S(2)}, u32[]{:S(2)}) async-start(f32[32,8,128]{2,1,0:T(8,128)} %get-tuple-element.49), calls=%async_computation | async-start | bytes 262144 | tf_op jit(solution)/shard_map/all_to_all | solution.py:468
  19.7 0.7 copy-done.2
  20.4 6.6 %arrange.1 = (f32[16,1200]{1,0:T(8,128)}, bf16[1200,1200]{1,0:T(8,128)(2,1)S(1)}) custom-call(bf16[1,1,1200,1200]{3,2,1,0:T(8,128)(2,1)} %refs_0_.1, f32[1,1,16,1200]{3,2,1,0:T(8,128)} %refs_1_.3, s32[1,1,4,300]{3,2,1,0:T(4,128)S(1)} %copy-done.2), custom_call_target="tpu_custom_call" | custom-call | flops 2949120000 | bytes 5918400 | tf_op jit(solution)/shard_map/arrange/pallas_call | solution.py:455
  27.1 4.1 %begin.1 = (f32[40,256]{1,0:T(8,128)}, f32[4,16,384]{2,1,0:T(8,128)}, f32[4,16,384]{2,1,0:T(8,128)}, f32[4,16,384]{2,1,0:T(8,128)}, f32[32,8,128]{2,1,0:T(8,128)...) custom-call(f32[4,16,384]{2,1,0:T(8,128)} %get-tuple-element.47.refs_0_.refs_1_, ...), custom_call_target="tpu_custom_call" | custom-call | flops 46080000 | bytes 3751424 | tf_op jit(solution)/shard_map/begin/pallas_call | solution.py:455
  31.2 5.8 %all-to-all-start.1 = ((f32[32,8,128]{2,1,0:T(8,128)}), f32[32,8,128]{2,1,0:T(8,128)S(1)}, u32[]{:S(2)}, u32[]{:S(2)}) async-start(f32[32,8,128]{2,1,0:T(8,128)} %get-tuple-element.59), calls=%async_computation.1 | async-start | bytes 262144 | tf_op jit(solution)/shard_map/all_to_all | solution.py:468
  37.2 4.2 %collective-permute-start.5 = (f32[16,384]{1,0:T(8,128)}, f32[16,384]{1,0:T(8,128)S(1)}, u32[]{:S(2)}, u32[]{:S(2)}) collective-permute-start(f32[16,384]{1,0:T(8,128)} %get-tuple-element.56), channel_id=1, source_target_pairs={{4,8},{8,4},{12,16},{16,12},{20,24},{24,20},{5,9},{9,5},{13,17},{1... | collective-permute-start | bytes 73736 | tf_op jit(solution)/shard_map/ppermute | solution.py:88
  41.4 1.0 %collective-permute-start.6 = (f32[16,384]{1,0:T(8,128)}, f32[16,384]{1,0:T(8,128)S(1)}, u32[]{:S(2)}, u32[]{:S(2)}) collective-permute-start(f32[16,384]{1,0:T(8,128)} %get-tuple-element.57), channel_id=1, source_target_pairs={{0,1},{1,0},{2,3},{3,2},{4,5},{5,4},{6,7},{7,6},{8,9},{9,8},{10,11... | collective-permute-start | bytes 73736 | tf_op jit(solution)/shard_map/ppermute | solution.py:88
  42.4 3.0 %collective-permute-start.7 = (f32[16,384]{1,0:T(8,128)}, f32[16,384]{1,0:T(8,128)S(1)}, u32[]{:S(2)}, u32[]{:S(2)}) collective-permute-start(f32[16,384]{1,0:T(8,128)} %get-tuple-element.58), channel_id=1, source_target_pairs={{1,2},{2,1},{5,6},{6,5},{9,10},{10,9},{13,14},{14,13},{17,18},{18,... | collective-permute-start | bytes 73736 | tf_op jit(solution)/shard_map/ppermute | solution.py:88
  45.4 2.3 %collective-permute-done.7.refs_8_ = f32[16,384]{1,0:T(8,128)S(1)} collective-permute-done((f32[16,384]{1,0:T(8,128)}, f32[16,384]{1,0:T(8,128)S(1)}, u32[]{:S(2)}, u32[]{:S(2)}) %collective-permute-start.7) | collective-permute-done | bytes 24608 | tf_op jit(solution)/shard_map/ppermute | solution.py:88
  47.7 0.6 copy-done.11
  48.3 3.3 %first_direction.1 = (f32[4,16,384]{2,1,0:T(8,128)}, f32[4,16,384]{2,1,0:T(8,128)}, f32[4,16,384]{2,1,0:T(8,128)}, f32[32,8,128]{2,1,0:T(8,128)}, f32[16,384]{1,...) custom-call(f32[40,256]{1,0:T(8,128)} %get-tuple-element.51.refs_0_, ...), custom_call_target="tpu_custom_call" | custom-call | flops 46080000 | bytes 3981824 | tf_op jit(solution)/shard_map/first_direction/pallas_call | solution.py:455
  51.7 4.6 %all-to-all-start.2 = ((f32[32,8,128]{2,1,0:T(8,128)}), f32[32,8,128]{2,1,0:T(8,128)S(1)}, u32[]{:S(2)}, u32[]{:S(2)}) async-start(f32[32,8,128]{2,1,0:T(8,128)} %get-tuple-element.68), calls=%async_computation.2 | async-start | bytes 262144 | tf_op jit(solution)/shard_map/all_to_all | solution.py:468
  56.4 4.2 %collective-permute-start.9 = (f32[16,384]{1,0:T(8,128)}, f32[16,384]{1,0:T(8,128)S(1)}, u32[]{:S(2)}, u32[]{:S(2)}) collective-permute-start(f32[16,384]{1,0:T(8,128)} %get-tuple-element.65), channel_id=1, source_target_pairs={{4,8},{8,4},{12,16},{16,12},{20,24},{24,20},{5,9},{9,5},{13,17},{1... | collective-permute-start | bytes 73736 | tf_op jit(solution)/shard_map/ppermute | solution.py:88
  60.6 1.0 %collective-permute-start.10 = (f32[16,384]{1,0:T(8,128)}, f32[16,384]{1,0:T(8,128)S(1)}, u32[]{:S(2)}, u32[]{:S(2)}) collective-permute-start(f32[16,384]{1,0:T(8,128)} %get-tuple-element.66), channel_id=1, source_target_pairs={{0,1},{1,0},{2,3},{3,2},{4,5},{5,4},{6,7},{7,6},{8,9},{9,8},{10,11... | collective-permute-start | bytes 73736 | tf_op jit(solution)/shard_map/ppermute | solution.py:88
  61.6 3.0 %collective-permute-start.11 = (f32[16,384]{1,0:T(8,128)}, f32[16,384]{1,0:T(8,128)S(1)}, u32[]{:S(2)}, u32[]{:S(2)}) collective-permute-start(f32[16,384]{1,0:T(8,128)} %get-tuple-element.67), channel_id=1, source_target_pairs={{1,2},{2,1},{5,6},{6,5},{9,10},{10,9},{13,14},{14,13},{17,18},{18,... | collective-permute-start | bytes 73736 | tf_op jit(solution)/shard_map/ppermute | solution.py:88
  64.7 2.3 %collective-permute-done.11.refs_10_ = f32[16,384]{1,0:T(8,128)S(1)} collective-permute-done((f32[16,384]{1,0:T(8,128)}, f32[16,384]{1,0:T(8,128)S(1)}, u32[]{:S(2)}, u32[]{:S(2)}) %collective-permute-start.11) | collective-permute-done | bytes 24608 | tf_op jit(solution)/shard_map/ppermute | solution.py:88
  67.0 0.6 copy-done.8
  67.6 3.2 %second_direction.1 = (f32[4,16,384]{2,1,0:T(8,128)}, f32[4,16,384]{2,1,0:T(8,128)}, f32[4,16,384]{2,1,0:T(8,128)}, f32[4,16,384]{2,1,0:T(8,128)}, f32[4,16,384]...) custom-call(f32[40,256]{1,0:T(8,128)} %get-tuple-element.51.refs_0_,, ...), custom_call_target="tpu_custom_call" | custom-call | flops 46080000 | bytes 4379136 | tf_op jit(solution)/shard_map/second_direction/pallas_call | solution.py:455
  70.8 4.6 %all-to-all-start.3 = ((f32[32,8,128]{2,1,0:T(8,128)}), f32[32,8,128]{2,1,0:T(8,128)S(1)}, u32[]{:S(2)}, u32[]{:S(2)}) async-start(f32[32,8,128]{2,1,0:T(8,128)} %get-tuple-element.79), calls=%async_computation.3 | async-start | bytes 262144 | tf_op jit(solution)/shard_map/all_to_all | solution.py:468
  75.5 4.2 %collective-permute-start.13 = (f32[16,384]{1,0:T(8,128)}, f32[16,384]{1,0:T(8,128)S(1)}, u32[]{:S(2)}, u32[]{:S(2)}) collective-permute-start(f32[16,384]{1,0:T(8,128)} %get-tuple-element.76), channel_id=1, source_target_pairs={{4,8},{8,4},{12,16},{16,12},{20,24},{24,20},{5,9},{9,5},{13,17},{1... | collective-permute-start | bytes 73736 | tf_op jit(solution)/shard_map/ppermute | solution.py:88
  79.7 1.0 %collective-permute-start.14 = (f32[16,384]{1,0:T(8,128)}, f32[16,384]{1,0:T(8,128)S(1)}, u32[]{:S(2)}, u32[]{:S(2)}) collective-permute-start(f32[16,384]{1,0:T(8,128)} %get-tuple-element.77), channel_id=1, source_target_pairs={{0,1},{1,0},{2,3},{3,2},{4,5},{5,4},{6,7},{7,6},{8,9},{9,8},{10,11... | collective-permute-start | bytes 73736 | tf_op jit(solution)/shard_map/ppermute | solution.py:88
  80.7 3.0 %collective-permute-start.15 = (f32[16,384]{1,0:T(8,128)}, f32[16,384]{1,0:T(8,128)S(1)}, u32[]{:S(2)}, u32[]{:S(2)}) collective-permute-start(f32[16,384]{1,0:T(8,128)} %get-tuple-element.78), channel_id=1, source_target_pairs={{1,2},{2,1},{5,6},{6,5},{9,10},{10,9},{13,14},{14,13},{17,18},{18,... | collective-permute-start | bytes 73736 | tf_op jit(solution)/shard_map/ppermute | solution.py:88
  83.8 2.3 %collective-permute-done.15.refs_11_ = f32[16,384]{1,0:T(8,128)S(1)} collective-permute-done((f32[16,384]{1,0:T(8,128)}, f32[16,384]{1,0:T(8,128)S(1)}, u32[]{:S(2)}, u32[]{:S(2)}) %collective-permute-start.15) | collective-permute-done | bytes 24608 | tf_op jit(solution)/shard_map/ppermute | solution.py:88
  86.7 2.0 %finish.1 = (f32[1,1,4,16,300]{4,3,2,1,0:T(8,128)}, f32[1,1,4,16,300]{4,3,2,1,0:T(8,128)}) custom-call(f32[8,128]{1,0:T(8,128)} %get-tuple-element.69.refs_0_, f32[4,16,384]{2,1,0:T(8,128)} %get-tuple-element.70.refs_1_, f32[8,384]{1,0:T(8,128)} %get-tuple-element.53.refs_3_.refs_2_, f32[4,16,384]{2,1,0:T(8,128)} %get-tuple-element.71.refs_3_, ...), custom_call_target="tpu_custom_call" | custom-call | bytes 989184 | tf_op jit(solution)/shard_map/finish/pallas_call | solution.py:455
  (48 shorter events, 2.0 us)
Async XLA Ops:
  0.6 0.8 copy-start
  2.6 10.5 %collective-permute-start = (f32[8,384]{1,0:T(8,128)S(1)}, f32[8,384]{1,0:T(8,128)S(1)}, u32[]{:S(2)}, u32[]{:S(2)}) collective-permute-start(f32[8,384]{1,0:T(8,128)S(1)} %get-tuple-element.43), channel_id=1, source_target_pairs={{0,4},{4,0},{8,12},{12,8},{16,20},{20,16},{24,28},{28,24},{1,5},{5... | collective-permute-start | bytes 36872 | tf_op jit(solution)/shard_map/ppermute | solution.py:88
  2.7 10.4 %collective-permute-start.1 = (f32[8,384]{1,0:T(8,128)S(1)}, f32[8,384]{1,0:T(8,128)S(1)}, u32[]{:S(2)}, u32[]{:S(2)}) collective-permute-start(f32[8,384]{1,0:T(8,128)S(1)} %get-tuple-element.44), channel_id=1, source_target_pairs={{4,8},{8,4},{12,16},{16,12},{20,24},{24,20},{5,9},{9,5},{13,17},{1... | collective-permute-start | bytes 36872 | tf_op jit(solution)/shard_map/ppermute | solution.py:88
  7.1 6.0 %collective-permute-start.2 = (f32[8,384]{1,0:T(8,128)S(1)}, f32[8,384]{1,0:T(8,128)S(1)}, u32[]{:S(2)}, u32[]{:S(2)}) collective-permute-start(f32[8,384]{1,0:T(8,128)S(1)} %get-tuple-element.45), channel_id=1, source_target_pairs={{0,1},{1,0},{2,3},{3,2},{4,5},{5,4},{6,7},{7,6},{8,9},{9,8},{10,11... | collective-permute-start | bytes 36872 | tf_op jit(solution)/shard_map/ppermute | solution.py:88
  8.4 5.0 %collective-permute-start.3 = (f32[8,384]{1,0:T(8,128)S(1)}, f32[8,384]{1,0:T(8,128)S(1)}, u32[]{:S(2)}, u32[]{:S(2)}) collective-permute-start(f32[8,384]{1,0:T(8,128)S(1)} %get-tuple-element.46), channel_id=1, source_target_pairs={{1,2},{2,1},{5,6},{6,5},{9,10},{10,9},{13,14},{14,13},{17,18},{18,... | collective-permute-start | bytes 36872 | tf_op jit(solution)/shard_map/ppermute | solution.py:88
  11.4 0.7 copy-start.3
  14.9 12.1 %all-to-all-start = ((f32[32,8,128]{2,1,0:T(8,128)}), f32[32,8,128]{2,1,0:T(8,128)S(1)}, u32[]{:S(2)}, u32[]{:S(2)}) async-start(f32[32,8,128]{2,1,0:T(8,128)} %get-tuple-element.49), calls=%async_computation | async-start | bytes 262144 | tf_op jit(solution)/shard_map/all_to_all | solution.py:468
  19.7 0.7 copy-start.2
  31.2 16.5 %all-to-all-start.1 = ((f32[32,8,128]{2,1,0:T(8,128)}), f32[32,8,128]{2,1,0:T(8,128)S(1)}, u32[]{:S(2)}, u32[]{:S(2)}) async-start(f32[32,8,128]{2,1,0:T(8,128)} %get-tuple-element.59), calls=%async_computation.1 | async-start | bytes 262144 | tf_op jit(solution)/shard_map/all_to_all | solution.py:468
  37.0 8.3 %collective-permute-start.4 = (f32[16,384]{1,0:T(8,128)}, f32[16,384]{1,0:T(8,128)S(1)}, u32[]{:S(2)}, u32[]{:S(2)}) collective-permute-start(f32[16,384]{1,0:T(8,128)} %get-tuple-element.55), channel_id=1, source_target_pairs={{0,4},{4,0},{8,12},{12,8},{16,20},{20,16},{24,28},{28,24},{1,5},{5... | collective-permute-start | bytes 73736 | tf_op jit(solution)/shard_map/ppermute | solution.py:88
  37.2 8.2 %collective-permute-start.5 = (f32[16,384]{1,0:T(8,128)}, f32[16,384]{1,0:T(8,128)S(1)}, u32[]{:S(2)}, u32[]{:S(2)}) collective-permute-start(f32[16,384]{1,0:T(8,128)} %get-tuple-element.56), channel_id=1, source_target_pairs={{4,8},{8,4},{12,16},{16,12},{20,24},{24,20},{5,9},{9,5},{13,17},{1... | collective-permute-start | bytes 73736 | tf_op jit(solution)/shard_map/ppermute | solution.py:88
  41.4 4.0 %collective-permute-start.6 = (f32[16,384]{1,0:T(8,128)}, f32[16,384]{1,0:T(8,128)S(1)}, u32[]{:S(2)}, u32[]{:S(2)}) collective-permute-start(f32[16,384]{1,0:T(8,128)} %get-tuple-element.57), channel_id=1, source_target_pairs={{0,1},{1,0},{2,3},{3,2},{4,5},{5,4},{6,7},{7,6},{8,9},{9,8},{10,11... | collective-permute-start | bytes 73736 | tf_op jit(solution)/shard_map/ppermute | solution.py:88
  42.4 5.3 %collective-permute-start.7 = (f32[16,384]{1,0:T(8,128)}, f32[16,384]{1,0:T(8,128)S(1)}, u32[]{:S(2)}, u32[]{:S(2)}) collective-permute-start(f32[16,384]{1,0:T(8,128)} %get-tuple-element.58), channel_id=1, source_target_pairs={{1,2},{2,1},{5,6},{6,5},{9,10},{10,9},{13,14},{14,13},{17,18},{18,... | collective-permute-start | bytes 73736 | tf_op jit(solution)/shard_map/ppermute | solution.py:88
  45.4 2.3 %copy-start.7 = (f32[16,384]{1,0:T(8,128)}, f32[16,384]{1,0:T(8,128)S(1)}, u32[]{:S(2)}) copy-start(f32[16,384]{1,0:T(8,128)S(1)} %collective-permute-done.4.refs_5_) | copy-start | bytes 73732
  45.4 2.3 %copy-start.9 = (f32[16,384]{1,0:T(8,128)}, f32[16,384]{1,0:T(8,128)S(1)}, u32[]{:S(2)}) copy-start(f32[16,384]{1,0:T(8,128)S(1)} %collective-permute-done.5.refs_6_) | copy-start | bytes 73732
  45.4 2.3 %copy-start.10 = (f32[16,384]{1,0:T(8,128)}, f32[16,384]{1,0:T(8,128)S(1)}, u32[]{:S(2)}) copy-start(f32[16,384]{1,0:T(8,128)S(1)} %collective-permute-done.6.refs_7_) | copy-start | bytes 73732
  51.7 15.3 %all-to-all-start.2 = ((f32[32,8,128]{2,1,0:T(8,128)}), f32[32,8,128]{2,1,0:T(8,128)S(1)}, u32[]{:S(2)}, u32[]{:S(2)}) async-start(f32[32,8,128]{2,1,0:T(8,128)} %get-tuple-element.68), calls=%async_computation.2 | async-start | bytes 262144 | tf_op jit(solution)/shard_map/all_to_all | solution.py:468
  56.3 8.3 %collective-permute-start.8 = (f32[16,384]{1,0:T(8,128)}, f32[16,384]{1,0:T(8,128)S(1)}, u32[]{:S(2)}, u32[]{:S(2)}) collective-permute-start(f32[16,384]{1,0:T(8,128)} %get-tuple-element.64), channel_id=1, source_target_pairs={{0,4},{4,0},{8,12},{12,8},{16,20},{20,16},{24,28},{28,24},{1,5},{5... | collective-permute-start | bytes 73736 | tf_op jit(solution)/shard_map/ppermute | solution.py:88
  56.4 8.2 %collective-permute-start.9 = (f32[16,384]{1,0:T(8,128)}, f32[16,384]{1,0:T(8,128)S(1)}, u32[]{:S(2)}, u32[]{:S(2)}) collective-permute-start(f32[16,384]{1,0:T(8,128)} %get-tuple-element.65), channel_id=1, source_target_pairs={{4,8},{8,4},{12,16},{16,12},{20,24},{24,20},{5,9},{9,5},{13,17},{1... | collective-permute-start | bytes 73736 | tf_op jit(solution)/shard_map/ppermute | solution.py:88
  60.6 4.0 %collective-permute-start.10 = (f32[16,384]{1,0:T(8,128)}, f32[16,384]{1,0:T(8,128)S(1)}, u32[]{:S(2)}, u32[]{:S(2)}) collective-permute-start(f32[16,384]{1,0:T(8,128)} %get-tuple-element.66), channel_id=1, source_target_pairs={{0,1},{1,0},{2,3},{3,2},{4,5},{5,4},{6,7},{7,6},{8,9},{9,8},{10,11... | collective-permute-start | bytes 73736 | tf_op jit(solution)/shard_map/ppermute | solution.py:88
  61.6 5.3 %collective-permute-start.11 = (f32[16,384]{1,0:T(8,128)}, f32[16,384]{1,0:T(8,128)S(1)}, u32[]{:S(2)}, u32[]{:S(2)}) collective-permute-start(f32[16,384]{1,0:T(8,128)} %get-tuple-element.67), channel_id=1, source_target_pairs={{1,2},{2,1},{5,6},{6,5},{9,10},{10,9},{13,14},{14,13},{17,18},{18,... | collective-permute-start | bytes 73736 | tf_op jit(solution)/shard_map/ppermute | solution.py:88
  64.6 2.3 %copy-start.4 = (f32[16,384]{1,0:T(8,128)}, f32[16,384]{1,0:T(8,128)S(1)}, u32[]{:S(2)}) copy-start(f32[16,384]{1,0:T(8,128)S(1)} %collective-permute-done.8.refs_7_) | copy-start | bytes 73732
  64.6 2.3 %copy-start.5 = (f32[16,384]{1,0:T(8,128)}, f32[16,384]{1,0:T(8,128)S(1)}, u32[]{:S(2)}) copy-start(f32[16,384]{1,0:T(8,128)S(1)} %collective-permute-done.9.refs_8_) | copy-start | bytes 73732
  64.7 2.3 %copy-start.6 = (f32[16,384]{1,0:T(8,128)}, f32[16,384]{1,0:T(8,128)S(1)}, u32[]{:S(2)}) copy-start(f32[16,384]{1,0:T(8,128)S(1)} %collective-permute-done.10.refs_9_) | copy-start | bytes 73732
  70.8 15.3 %all-to-all-start.3 = ((f32[32,8,128]{2,1,0:T(8,128)}), f32[32,8,128]{2,1,0:T(8,128)S(1)}, u32[]{:S(2)}, u32[]{:S(2)}) async-start(f32[32,8,128]{2,1,0:T(8,128)} %get-tuple-element.79), calls=%async_computation.3 | async-start | bytes 262144 | tf_op jit(solution)/shard_map/all_to_all | solution.py:468
  75.4 8.3 %collective-permute-start.12 = (f32[16,384]{1,0:T(8,128)}, f32[16,384]{1,0:T(8,128)S(1)}, u32[]{:S(2)}, u32[]{:S(2)}) collective-permute-start(f32[16,384]{1,0:T(8,128)} %get-tuple-element.75), channel_id=1, source_target_pairs={{0,4},{4,0},{8,12},{12,8},{16,20},{20,16},{24,28},{28,24},{1,5},{5... | collective-permute-start | bytes 73736 | tf_op jit(solution)/shard_map/ppermute | solution.py:88
  75.5 8.2 %collective-permute-start.13 = (f32[16,384]{1,0:T(8,128)}, f32[16,384]{1,0:T(8,128)S(1)}, u32[]{:S(2)}, u32[]{:S(2)}) collective-permute-start(f32[16,384]{1,0:T(8,128)} %get-tuple-element.76), channel_id=1, source_target_pairs={{4,8},{8,4},{12,16},{16,12},{20,24},{24,20},{5,9},{9,5},{13,17},{1... | collective-permute-start | bytes 73736 | tf_op jit(solution)/shard_map/ppermute | solution.py:88
  79.7 4.0 %collective-permute-start.14 = (f32[16,384]{1,0:T(8,128)}, f32[16,384]{1,0:T(8,128)S(1)}, u32[]{:S(2)}, u32[]{:S(2)}) collective-permute-start(f32[16,384]{1,0:T(8,128)} %get-tuple-element.77), channel_id=1, source_target_pairs={{0,1},{1,0},{2,3},{3,2},{4,5},{5,4},{6,7},{7,6},{8,9},{9,8},{10,11... | collective-permute-start | bytes 73736 | tf_op jit(solution)/shard_map/ppermute | solution.py:88
  80.7 5.3 %collective-permute-start.15 = (f32[16,384]{1,0:T(8,128)}, f32[16,384]{1,0:T(8,128)S(1)}, u32[]{:S(2)}, u32[]{:S(2)}) collective-permute-start(f32[16,384]{1,0:T(8,128)} %get-tuple-element.78), channel_id=1, source_target_pairs={{1,2},{2,1},{5,6},{6,5},{9,10},{10,9},{13,14},{14,13},{17,18},{18,... | collective-permute-start | bytes 73736 | tf_op jit(solution)/shard_map/ppermute | solution.py:88
  83.7 2.3 %copy-start.12 = (f32[16,384]{1,0:T(8,128)}, f32[16,384]{1,0:T(8,128)S(1)}, u32[]{:S(2)}) copy-start(f32[16,384]{1,0:T(8,128)S(1)} %collective-permute-done.12.refs_8_) | copy-start | bytes 73732
  83.8 2.3 %copy-start.13 = (f32[16,384]{1,0:T(8,128)}, f32[16,384]{1,0:T(8,128)S(1)}, u32[]{:S(2)}) copy-start(f32[16,384]{1,0:T(8,128)S(1)} %collective-permute-done.13.refs_9_) | copy-start | bytes 73732
  83.8 2.3 %copy-start.14 = (f32[16,384]{1,0:T(8,128)}, f32[16,384]{1,0:T(8,128)S(1)}, u32[]{:S(2)}) copy-start(f32[16,384]{1,0:T(8,128)S(1)} %collective-permute-done.14.refs_10_) | copy-start | bytes 73732
  (4 other events, 2.5 us)

commit v8 on v7

--- a/solution.py
+++ b/solution.py
@@ -177,7 +177,7 @@
         live = padded[f] * masks[f : f + 1]
         lift_rows[f] = jnp.concatenate([live * SIGNS[f], near[f] * masks[f : f + 1] * -SIGNS[f]], axis=0)
         tile[:, 8 * f : 8 * f + 8] = dot(inverse, dot(live, near[f], (1, 1)))
-    sent[...] = jnp.broadcast_to(tile[...][None], sent.shape)
+    sent[...] = tile[...]
     sent.push()
     live_rows[...] = masks[...]
 
@@ -222,7 +222,7 @@
     row, col = iota((8, 128), 0), iota((8, 128), 1)
     for i, scalar in enumerate(scalars):
         values = jnp.where((row == 0) & (col == SCALAR_LANE + i), scalar, values)
-    sent[...] = jnp.broadcast_to(values[None], sent.shape)
+    sent[...] = values
     sent.push()
 
 
@@ -263,7 +263,7 @@
 
 
 def begin(
-    z, lift_rows, primal, received, arranged,
+    z, received, lift_rows, primal, arranged,
     solve_rows, rows, multipliers, faces, sent, to0, to1, to2, to3,
     matrix, tile, packed,
 ):
@@ -318,7 +318,7 @@
 
 
 def first_direction(
-    z, solve_rows, lift_rows, faces, masks, rows, got0, got1, got2, got3, received, arranged,
+    z, received, solve_rows, lift_rows, faces, masks, rows, got0, got1, got2, got3, arranged,
     residual, direction, image, sent, to0, to1, to2, to3,
     tile, packed,
 ):
@@ -342,8 +342,8 @@
 
 
 def second_direction(
-    z, solve_rows, lift_rows, faces, masks, residual, direction, multipliers,
-    got0, got1, got2, got3, received, arranged,
+    z, received, solve_rows, lift_rows, faces, masks, residual, direction, multipliers,
+    got0, got1, got2, got3, arranged,
     next_multipliers, next_residual, projected, image, fresh, sums, sent, to0, to1, to2, to3,
     packed,
 ):
@@ -377,8 +377,8 @@
 
 
 def finish(
-    z, sums, faces, masks, residual, image, multipliers, projected, direction,
-    got0, got1, got2, got3, received,
+    z, received, sums, faces, masks, residual, image, multipliers, projected, direction,
+    got0, got1, got2, got3,
     out_multipliers, out_residual,
 ):
     summed = jnp.sum(received[...], axis=0)
@@ -465,7 +465,7 @@
 
 
 def gather(values):
-    return lax.all_to_all(values, AXES, 0, 0, tiled=True)
+    return lax.all_gather(values, AXES)
 
 
 def body(ops, traces, primal, loads, maps, counts):
@@ -475,7 +475,7 @@
     pair_rows = ((4, 16, z.lanes), F32)
     live_rows = ((8, z.lanes), F32)
     tile = ((8, 128), F32)
-    sent = ((z.count, 8, 128), F32)
+    sent = ((8, 128), F32)
     to_faces = [((z.cases, z.lanes), F32)] * 4
     columns = -(-z.rows // 128) * 128
     product_flops = 2 * z.cases * z.order**2
@@ -500,26 +500,26 @@
     )
     solve_rows, rows, multipliers, faces, coarse, *sent_faces = call(
         z, begin, [((40, z.rows), F32), pair_rows, field, field, sent] + to_faces,
-        [lift_rows, primal_packed, blocks, arranged],
-        [((z.rows, columns), F32), tile, packed], product_flops, near=2,
+        [blocks, lift_rows, primal_packed, arranged],
+        [((z.rows, columns), F32), tile, packed], product_flops, near=1,
     )
     coarse, got = gather(coarse), exchange(sent_faces)
     residual, direction, faces, coarse, *sent_faces = call(
         z, first_direction, [field, field, field, sent] + to_faces,
-        [solve_rows, lift_rows, faces, masks, rows, *got, coarse, arranged],
-        [tile, packed], product_flops, near=2,
+        [coarse, solve_rows, lift_rows, faces, masks, rows, *got, arranged],
+        [tile, packed], product_flops, near=5,
     )
     coarse, got = gather(coarse), exchange(sent_faces)
     multipliers, residual, projected, image, faces, sums, coarse, *sent_faces = call(
         z, second_direction, [field, field, field, field, field, tile, sent] + to_faces,
-        [solve_rows, lift_rows, faces, masks, residual, direction, multipliers, *got, coarse, arranged],
-        [packed], product_flops, near=2,
+        [coarse, solve_rows, lift_rows, faces, masks, residual, direction, multipliers, *got, arranged],
+        [packed], product_flops, near=5,
     )
     coarse, got = gather(coarse), exchange(sent_faces)
     whole = ((1, 1, 4, z.cases, z.face), F32)
     multipliers, residual = call(
         z, finish, [whole, whole],
-        [sums, faces, masks, residual, image, multipliers, projected, direction, *got, coarse], near=1,
+        [coarse, sums, faces, masks, residual, image, multipliers, projected, direction, *got], near=4,
     )
     return multipliers, residual
 

time: 89.5 us -> 210 us (2.35)
  the two profiles are of different devices: /device:TPU:5 before, /device:TPU:0 now
where the time goes in v8:
time: 210 us
  blocking collectives  174 us (83%)
  Pallas kernels  23 us (11%)
  starting transfers between devices  9.79 us (5%)
  local copies, waits for them, and re-layouts  2.11 us (1%)
    all_gather x4, blocking collectives, gather(): return lax.all_gather(values, AXES)  174 us
    pallas_call x8, Pallas kernels, call(): pl.pallas_call(run, out_shape=[pltpu.HBM(a.shape, a.dtype) for a in shape...  23 us
    ppermute x16, starting transfers between devices, exchange(): got[i] = lax.ppermute(sent[i], axis, pairs)  9.79 us
  transfers between devices with their start and end apart: 16, of which 0 were waited for; matrix products, arithmetic and copies ran while one was open for 0% of the time, Pallas kernels for 4%

profile of v8, /device:TPU:0, one launch (start us, length us, event | category | flops | bytes accessed | tf_op | source)
XLA Modules:
  0.0 209.5 jit_solution(2141482068134972053)
XLA Ops:
  0.6 0.8 copy-done
  1.4 0.7 copy-done.1
  2.1 0.6 prepare.1
  2.6 3.0 %collective-permute-start = (f32[8,384]{1,0:T(8,128)S(1)}, f32[8,384]{1,0:T(8,128)S(1)}, u32[]{:S(2)}, u32[]{:S(2)}) collective-permute-start(f32[8,384]{1,0:T(8,128)S(1)} %get-tuple-element.43), channel_id=1, source_target_pairs={{0,4},{4,0},{8,12},{12,8},{16,20},{20,16},{24,28},{28,24},{1,5},{5... | collective-permute-start | bytes 36872 | tf_op jit(solution)/shard_map/ppermute | solution.py:88
  5.7 0.7 collective-permute-start.1
  6.3 0.1 collective-permute-start.2
  6.4 0.7 collective-permute-start.3
  7.1 0.7 copy-done.2
  7.8 6.7 %arrange.1 = (f32[16,1200]{1,0:T(8,128)}, bf16[1200,1200]{1,0:T(8,128)(2,1)S(1)}) custom-call(bf16[1,1,1200,1200]{3,2,1,0:T(8,128)(2,1)} %refs_0_.1, f32[1,1,16,1200]{3,2,1,0:T(8,128)} %refs_1_.3, s32[1,1,4,300]{3,2,1,0:T(4,128)S(1)} %copy-done.2), custom_call_target="tpu_custom_call" | custom-call | flops 2949120000 | bytes 5918400 | tf_op jit(solution)/shard_map/arrange/pallas_call | solution.py:455
  14.4 1.0 invert.1.refs_2_
  15.4 0.0 collective-permute-done.2.refs_5_
  15.5 1.5 couple.1
  17.0 45.9 %all-gather = f32[256,128]{1,0:T(8,128)} all-gather(f32[8,128]{1,0:T(8,128)} %get-tuple-element.47), channel_id=2, replica_groups=mesh['gx'=8,'gy'=4] {'gx','gy'}, dimensions={0}, use_global_device_ids=true | all-gather | bytes 135168 | tf_op jit(solution)/shard_map/all_gather | solution.py:468
  62.9 4.4 %begin.1 = (f32[40,256]{1,0:T(8,128)}, f32[4,16,384]{2,1,0:T(8,128)}, f32[4,16,384]{2,1,0:T(8,128)}, f32[4,16,384]{2,1,0:T(8,128)}, f32[8,128]{1,0:T(8,128)}, /*...) custom-call(f32[32,8,128]{2,1,0:T(8,128)} %bitcast.11, ...), custom_call_target="tpu_custom_call" | custom-call | flops 46080000 | bytes 3624448 | tf_op jit(solution)/shard_map/begin/pallas_call | solution.py:455
  67.3 0.1 collective-permute-start.4
  67.4 0.7 collective-permute-start.5
  68.0 0.4 collective-permute-start.6
  68.5 0.7 collective-permute-start.7
  69.1 42.6 %all-gather.1 = f32[256,128]{1,0:T(8,128)} all-gather(f32[8,128]{1,0:T(8,128)} %get-tuple-element.51), channel_id=3, replica_groups=mesh['gx'=8,'gy'=4] {'gx','gy'}, dimensions={0}, use_global_device_ids=true | all-gather | bytes 135168 | tf_op jit(solution)/shard_map/all_gather | solution.py:468
  111.7 3.6 %first_direction.1 = (f32[4,16,384]{2,1,0:T(8,128)}, f32[4,16,384]{2,1,0:T(8,128)}, f32[4,16,384]{2,1,0:T(8,128)}, f32[8,128]{1,0:T(8,128)}, f32[16,384]{1,0:T(8...) custom-call(f32[32,8,128]{2,1,0:T(8,128)} %bitcast.9, f32[40,256]{1,0:T(8,128)} %get-tuple-element.52.refs_1_, ...), custom_call_target="tpu_custom_call" | custom-call | flops 46080000 | bytes 3854848 | tf_op jit(solution)/shard_map/first_direction/pallas_call | solution.py:455
  115.3 0.1 collective-permute-start.8
  115.4 0.7 collective-permute-start.9
  116.1 0.4 collective-permute-start.10
  116.5 0.7 collective-permute-start.11
  117.1 42.6 %all-gather.2 = f32[256,128]{1,0:T(8,128)} all-gather(f32[8,128]{1,0:T(8,128)} %get-tuple-element.60), channel_id=4, replica_groups=mesh['gx'=8,'gy'=4] {'gx','gy'}, dimensions={0}, use_global_device_ids=true | all-gather | bytes 135168 | tf_op jit(solution)/shard_map/all_gather | solution.py:468
  159.8 3.3 %second_direction.1 = (f32[4,16,384]{2,1,0:T(8,128)}, f32[4,16,384]{2,1,0:T(8,128)}, f32[4,16,384]{2,1,0:T(8,128)}, f32[4,16,384]{2,1,0:T(8,128)}, f32[4,16,384]...) custom-call(f32[32,8,128]{2,1,0:T(8,128)} %bitcast.8, ...), custom_call_target="tpu_custom_call" | custom-call | flops 46080000 | bytes 4252160 | tf_op jit(solution)/shard_map/second_direction/pallas_call | solution.py:455
  163.1 0.1 collective-permute-start.12
  163.2 0.7 collective-permute-start.13
  163.8 0.4 collective-permute-start.14
  164.2 0.7 collective-permute-start.15
  164.9 42.6 %all-gather.3 = f32[256,128]{1,0:T(8,128)} all-gather(f32[8,128]{1,0:T(8,128)} %get-tuple-element.69), channel_id=5, replica_groups=mesh['gx'=8,'gy'=4] {'gx','gy'}, dimensions={0}, use_global_device_ids=true | all-gather | bytes 135168 | tf_op jit(solution)/shard_map/all_gather | solution.py:468
  207.5 2.0 finish.1
  (20 shorter events, 0.1 us)
Async XLA Ops:
  0.6 0.8 copy-start
  1.4 0.7 copy-start.1
  2.6 12.8 %collective-permute-start = (f32[8,384]{1,0:T(8,128)S(1)}, f32[8,384]{1,0:T(8,128)S(1)}, u32[]{:S(2)}, u32[]{:S(2)}) collective-permute-start(f32[8,384]{1,0:T(8,128)S(1)} %get-tuple-element.43), channel_id=1, source_target_pairs={{0,4},{4,0},{8,12},{12,8},{16,20},{20,16},{24,28},{28,24},{1,5},{5... | collective-permute-start | bytes 36872 | tf_op jit(solution)/shard_map/ppermute | solution.py:88
  5.7 9.8 %collective-permute-start.1 = (f32[8,384]{1,0:T(8,128)S(1)}, f32[8,384]{1,0:T(8,128)S(1)}, u32[]{:S(2)}, u32[]{:S(2)}) collective-permute-start(f32[8,384]{1,0:T(8,128)S(1)} %get-tuple-element.44), channel_id=1, source_target_pairs={{4,8},{8,4},{12,16},{16,12},{20,24},{24,20},{5,9},{9,5},{13,17},{1... | collective-permute-start | bytes 36872 | tf_op jit(solution)/shard_map/ppermute | solution.py:88
  6.3 9.1 %collective-permute-start.2 = (f32[8,384]{1,0:T(8,128)S(1)}, f32[8,384]{1,0:T(8,128)S(1)}, u32[]{:S(2)}, u32[]{:S(2)}) collective-permute-start(f32[8,384]{1,0:T(8,128)S(1)} %get-tuple-element.45), channel_id=1, source_target_pairs={{0,1},{1,0},{2,3},{3,2},{4,5},{5,4},{6,7},{7,6},{8,9},{9,8},{10,11... | collective-permute-start | bytes 36872 | tf_op jit(solution)/shard_map/ppermute | solution.py:88
  6.4 9.1 %collective-permute-start.3 = (f32[8,384]{1,0:T(8,128)S(1)}, f32[8,384]{1,0:T(8,128)S(1)}, u32[]{:S(2)}, u32[]{:S(2)}) collective-permute-start(f32[8,384]{1,0:T(8,128)S(1)} %get-tuple-element.46), channel_id=1, source_target_pairs={{1,2},{2,1},{5,6},{6,5},{9,10},{10,9},{13,14},{14,13},{17,18},{18,... | collective-permute-start | bytes 36872 | tf_op jit(solution)/shard_map/ppermute | solution.py:88
  7.1 0.7 copy-start.2
  7.8 6.7 %copy-start.3 = (f32[1,1,6,16]{3,1,2,0:T(1,128)S(1)}, f32[1,1,6,16]{3,1,2,0:T(1,128)}, u32[]{:S(2)}) copy-start(f32[1,1,6,16]{3,1,2,0:T(1,128)} %param.9) | copy-start | bytes 1156
  67.3 44.4 %collective-permute-start.4 = (f32[16,384]{1,0:T(8,128)}, f32[16,384]{1,0:T(8,128)S(1)}, u32[]{:S(2)}, u32[]{:S(2)}) collective-permute-start(f32[16,384]{1,0:T(8,128)} %get-tuple-element.56), channel_id=1, source_target_pairs={{0,4},{4,0},{8,12},{12,8},{16,20},{20,16},{24,28},{28,24},{1,5},{5... | collective-permute-start | bytes 73736 | tf_op jit(solution)/shard_map/ppermute | solution.py:88
  67.4 44.3 %collective-permute-start.5 = (f32[16,384]{1,0:T(8,128)}, f32[16,384]{1,0:T(8,128)S(1)}, u32[]{:S(2)}, u32[]{:S(2)}) collective-permute-start(f32[16,384]{1,0:T(8,128)} %get-tuple-element.57), channel_id=1, source_target_pairs={{4,8},{8,4},{12,16},{16,12},{20,24},{24,20},{5,9},{9,5},{13,17},{1... | collective-permute-start | bytes 73736 | tf_op jit(solution)/shard_map/ppermute | solution.py:88
  68.0 43.7 %collective-permute-start.6 = (f32[16,384]{1,0:T(8,128)}, f32[16,384]{1,0:T(8,128)S(1)}, u32[]{:S(2)}, u32[]{:S(2)}) collective-permute-start(f32[16,384]{1,0:T(8,128)} %get-tuple-element.58), channel_id=1, source_target_pairs={{0,1},{1,0},{2,3},{3,2},{4,5},{5,4},{6,7},{7,6},{8,9},{9,8},{10,11... | collective-permute-start | bytes 73736 | tf_op jit(solution)/shard_map/ppermute | solution.py:88
  68.5 43.3 %collective-permute-start.7 = (f32[16,384]{1,0:T(8,128)}, f32[16,384]{1,0:T(8,128)S(1)}, u32[]{:S(2)}, u32[]{:S(2)}) collective-permute-start(f32[16,384]{1,0:T(8,128)} %get-tuple-element.59), channel_id=1, source_target_pairs={{1,2},{2,1},{5,6},{6,5},{9,10},{10,9},{13,14},{14,13},{17,18},{18,... | collective-permute-start | bytes 73736 | tf_op jit(solution)/shard_map/ppermute | solution.py:88
  115.3 44.4 %collective-permute-start.8 = (f32[16,384]{1,0:T(8,128)}, f32[16,384]{1,0:T(8,128)S(1)}, u32[]{:S(2)}, u32[]{:S(2)}) collective-permute-start(f32[16,384]{1,0:T(8,128)} %get-tuple-element.65), channel_id=1, source_target_pairs={{0,4},{4,0},{8,12},{12,8},{16,20},{20,16},{24,28},{28,24},{1,5},{5... | collective-permute-start | bytes 73736 | tf_op jit(solution)/shard_map/ppermute | solution.py:88
  115.4 44.3 %collective-permute-start.9 = (f32[16,384]{1,0:T(8,128)}, f32[16,384]{1,0:T(8,128)S(1)}, u32[]{:S(2)}, u32[]{:S(2)}) collective-permute-start(f32[16,384]{1,0:T(8,128)} %get-tuple-element.66), channel_id=1, source_target_pairs={{4,8},{8,4},{12,16},{16,12},{20,24},{24,20},{5,9},{9,5},{13,17},{1... | collective-permute-start | bytes 73736 | tf_op jit(solution)/shard_map/ppermute | solution.py:88
  116.1 43.7 %collective-permute-start.10 = (f32[16,384]{1,0:T(8,128)}, f32[16,384]{1,0:T(8,128)S(1)}, u32[]{:S(2)}, u32[]{:S(2)}) collective-permute-start(f32[16,384]{1,0:T(8,128)} %get-tuple-element.67), channel_id=1, source_target_pairs={{0,1},{1,0},{2,3},{3,2},{4,5},{5,4},{6,7},{7,6},{8,9},{9,8},{10,11... | collective-permute-start | bytes 73736 | tf_op jit(solution)/shard_map/ppermute | solution.py:88
  116.5 43.3 %collective-permute-start.11 = (f32[16,384]{1,0:T(8,128)}, f32[16,384]{1,0:T(8,128)S(1)}, u32[]{:S(2)}, u32[]{:S(2)}) collective-permute-start(f32[16,384]{1,0:T(8,128)} %get-tuple-element.68), channel_id=1, source_target_pairs={{1,2},{2,1},{5,6},{6,5},{9,10},{10,9},{13,14},{14,13},{17,18},{18,... | collective-permute-start | bytes 73736 | tf_op jit(solution)/shard_map/ppermute | solution.py:88
  163.1 44.4 %collective-permute-start.12 = (f32[16,384]{1,0:T(8,128)}, f32[16,384]{1,0:T(8,128)S(1)}, u32[]{:S(2)}, u32[]{:S(2)}) collective-permute-start(f32[16,384]{1,0:T(8,128)} %get-tuple-element.76), channel_id=1, source_target_pairs={{0,4},{4,0},{8,12},{12,8},{16,20},{20,16},{24,28},{28,24},{1,5},{5... | collective-permute-start | bytes 73736 | tf_op jit(solution)/shard_map/ppermute | solution.py:88
  163.2 44.3 %collective-permute-start.13 = (f32[16,384]{1,0:T(8,128)}, f32[16,384]{1,0:T(8,128)S(1)}, u32[]{:S(2)}, u32[]{:S(2)}) collective-permute-start(f32[16,384]{1,0:T(8,128)} %get-tuple-element.77), channel_id=1, source_target_pairs={{4,8},{8,4},{12,16},{16,12},{20,24},{24,20},{5,9},{9,5},{13,17},{1... | collective-permute-start | bytes 73736 | tf_op jit(solution)/shard_map/ppermute | solution.py:88
  163.8 43.7 %collective-permute-start.14 = (f32[16,384]{1,0:T(8,128)}, f32[16,384]{1,0:T(8,128)S(1)}, u32[]{:S(2)}, u32[]{:S(2)}) collective-permute-start(f32[16,384]{1,0:T(8,128)} %get-tuple-element.78), channel_id=1, source_target_pairs={{0,1},{1,0},{2,3},{3,2},{4,5},{5,4},{6,7},{7,6},{8,9},{9,8},{10,11... | collective-permute-start | bytes 73736 | tf_op jit(solution)/shard_map/ppermute | solution.py:88
  164.2 43.3 %collective-permute-start.15 = (f32[16,384]{1,0:T(8,128)}, f32[16,384]{1,0:T(8,128)S(1)}, u32[]{:S(2)}, u32[]{:S(2)}) collective-permute-start(f32[16,384]{1,0:T(8,128)} %get-tuple-element.79), channel_id=1, source_target_pairs={{1,2},{2,1},{5,6},{6,5},{9,10},{10,9},{13,14},{14,13},{17,18},{18,... | collective-permute-start | bytes 73736 | tf_op jit(solution)/shard_map/ppermute | solution.py:88

commit v9 on v7

--- a/solution.py
+++ b/solution.py
@@ -18,6 +18,7 @@
 INVERSE_LANE = 48
 SCALAR_LANE = 96
 BLOCK = 256
+SWAPS = (1, 3, 0, 2)
 
 
 class Sizes:
@@ -79,13 +80,13 @@
 
 
 def exchange(sent):
-    got = [None] * 4
-    for i in (1, 3, 0, 2):
+    got = []
+    for i in SWAPS:
         axis = AXES[i // 2]
         pairs = []
         for low in range(i % 2, lax.axis_size(axis) - 1, 2):
             pairs += [(low, low + 1), (low + 1, low)]
-        got[i] = lax.ppermute(sent[i], axis, pairs)
+        got.append(lax.ppermute(sent[i], axis, pairs))
     return got
 
 
@@ -115,7 +116,7 @@
     return found
 
 
-def arrange(z, ops, primal, maps, primal_packed, arranged, flat, half):
+def arrange(z, maps, ops, primal, primal_packed, arranged, flat, half):
     flat[...] = jnp.zeros_like(flat)
     flat[0:4, 0 : z.face] = maps[0, 0]
     lane = iota((1, z.padded), 1)
@@ -150,7 +151,7 @@
         arranged[:, low:high] = dot(half[:, first:last], there, precision=None).astype(BF16)
 
 
-def invert(z, padded, masks, loads, local_tile, aug, small):
+def invert(z, loads, padded, masks, local_tile, aug, small):
     diagonal = sum(dot(padded[f] * masks[f : f + 1], padded[f], (1, 1)) for f in range(4))
     row, col = iota((8, 128), 0), iota((8, 128), 1)
     aug[...] = jnp.where((col == row + 8) & (row < z.modes), 1.0, 0.0).astype(F32)
@@ -169,7 +170,7 @@
     local_tile[:, INVERSE_LANE : INVERSE_LANE + 8] = inverse
 
 
-def couple(z, padded, masks, local_tile, got0, got1, got2, got3, sent, live_rows, lift_rows, tile):
+def couple(z, padded, masks, local_tile, got1, got3, got0, got2, sent, live_rows, lift_rows, tile):
     near = across_faces(z, (got0, got1, got2, got3))
     inverse = local_tile[:, INVERSE_LANE : INVERSE_LANE + 8]
     tile[...] = local_tile[...]
@@ -318,7 +319,7 @@
 
 
 def first_direction(
-    z, solve_rows, lift_rows, faces, masks, rows, got0, got1, got2, got3, received, arranged,
+    z, solve_rows, lift_rows, faces, masks, rows, got1, got3, got0, got2, received, arranged,
     residual, direction, image, sent, to0, to1, to2, to3,
     tile, packed,
 ):
@@ -343,7 +344,7 @@
 
 def second_direction(
     z, solve_rows, lift_rows, faces, masks, residual, direction, multipliers,
-    got0, got1, got2, got3, received, arranged,
+    got1, got3, got0, got2, received, arranged,
     next_multipliers, next_residual, projected, image, fresh, sums, sent, to0, to1, to2, to3,
     packed,
 ):
@@ -378,7 +379,7 @@
 
 def finish(
     z, sums, faces, masks, residual, image, multipliers, projected, direction,
-    got0, got1, got2, got3, received,
+    got1, got3, got0, got2, received,
     out_multipliers, out_residual,
 ):
     summed = jnp.sum(received[...], axis=0)
@@ -450,7 +451,7 @@
 
     near_spec = lambda a: pl.BlockSpec(memory_space=SMEM if a.ndim == 3 and a.size == 4 else VMEM)
     far_spec = pl.BlockSpec(memory_space=pltpu.HBM)
-    buffers = [VMEM(a.shape, a.dtype) for a in list(args[:far]) + shapes[:sent]]
+    buffers = [(SMEM if a.size == 4 else VMEM)(a.shape, a.dtype) for a in list(args[:far]) + shapes[:sent]]
     semaphores = [pltpu.SemaphoreType.DMA((far + sent,))] if far + sent else []
     return pl.pallas_call(
         run,
@@ -482,12 +483,12 @@
 
     padded, masks, *trace_faces = call(
         z, prepare, [mode_rows, live_rows] + [((8, z.lanes), F32)] * 4,
-        [jnp.transpose(traces, (0, 1, 3, 2, 4)), counts], near=2, kept=6,
+        [jnp.transpose(traces, (0, 1, 3, 2, 4)), counts], kept=6,
     )
     got = exchange(trace_faces)
     (local_tile,) = call(
-        z, invert, [tile], [padded, masks, jnp.transpose(loads, (0, 2, 1, 3))],
-        [tile, ((8, z.cases), F32)], product_flops, near=3, kept=1,
+        z, invert, [tile], [jnp.transpose(loads, (0, 2, 1, 3)), padded, masks],
+        [tile, ((8, z.cases), F32)], product_flops, near=2, kept=1,
     )
     blocks, masks, lift_rows = call(
         z, couple, [sent, live_rows, pair_rows], [padded, masks, local_tile, *got], [tile], near=7,
@@ -495,8 +496,8 @@
     blocks = gather(blocks)
     packed = ((z.cases, z.padded), F32)
     primal_packed, arranged = call(
-        z, arrange, [((z.cases, z.order), F32), ((z.order, z.order), BF16)], [ops, primal, maps],
-        [((8, z.padded), jnp.int32), ((z.order, z.order), BF16)], 4 * z.order**2 * z.width, near=1, kept=1,
+        z, arrange, [((z.cases, z.order), F32), ((z.order, z.order), BF16)], [maps, ops, primal],
+        [((8, z.padded), jnp.int32), ((z.order, z.order), BF16)], 4 * z.order**2 * z.width, kept=1,
     )
     solve_rows, rows, multipliers, faces, coarse, *sent_faces = call(
         z, begin, [((40, z.rows), F32), pair_rows, field, field, sent] + to_faces,

time: 89.5 us -> 84.5 us (0.944)
  starting transfers between devices: 53.5 us -> 47.6 us
  local copies, waits for them, and re-layouts: 4.56 us -> 1.78 us
  waiting for transfers between devices: 7.18 us -> 9.93 us
    ppermute x16, starting transfers between devices: 33.7 us -> 27.8 us  [exchange(): got.append(lax.ppermute(sent[i], axis, pairs))]
    unnamed x32 -> x24, local copies, waits for them, and re-layouts: 4.56 us -> 1.78 us
    ppermute x16, waiting for transfers between devices: 7.17 us -> 9.75 us  [exchange(): got.append(lax.ppermute(sent[i], axis, pairs))]
  transfers between devices with their start and end apart: 20 -> 20, of which waited for: 4 -> 9; matrix products, arithmetic and copies ran while one was open for 0% -> 0% of each run, Pallas kernels for 9% -> 9%
where the time goes in v9:
time: 84.5 us; the launch traced here: 83.1 us
  starting transfers between devices  47.6 us (56%)
  Pallas kernels  22.8 us (27%)
  waiting for transfers between devices  9.93 us (12%)
  local copies, waits for them, and re-layouts  1.78 us (2%)
  between operations  0.97 us (1%)
    ppermute x16, starting transfers between devices, exchange(): got.append(lax.ppermute(sent[i], axis, pairs))  27.8 us
    pallas_call x8, Pallas kernels, call(): pl.pallas_call(run, out_shape=[pltpu.HBM(a.shape, a.dtype) for a in shape...  22.8 us
    all_to_all x4, starting transfers between devices, gather(): return lax.all_to_all(values, AXES, 0, 0, tiled=True)  19.8 us
    ppermute x16, waiting for transfers between devices, exchange(): got.append(lax.ppermute(sent[i], axis, pairs))  9.75 us
    unnamed x24, local copies, waits for them, and re-layouts  1.78 us
  transfers between devices with their start and end apart: 20, of which 9 were waited for; matrix products, arithmetic and copies ran while one was open for 0% of the time, Pallas kernels for 9%

profile of v9, /device:TPU:5, one launch (start us, length us, event | category | flops | bytes accessed | tf_op | source)
XLA Modules:
  0.0 83.1 jit_solution(3653622550907242753)
XLA Ops:
  0.6 0.8 prepare.1
  1.5 3.1 %collective-permute-start = (f32[8,384]{1,0:T(8,128)S(1)}, f32[8,384]{1,0:T(8,128)S(1)}, u32[]{:S(2)}, u32[]{:S(2)}) collective-permute-start(f32[8,384]{1,0:T(8,128)S(1)} %get-tuple-element.43), channel_id=1, source_target_pairs={{4,8},{8,4},{12,16},{16,12},{20,24},{24,20},{5,9},{9,5},{13,17},{1... | collective-permute-start | bytes 36872 | tf_op jit(solution)/shard_map/ppermute | solution.py:89
  4.6 4.0 %collective-permute-start.1 = (f32[8,384]{1,0:T(8,128)S(1)}, f32[8,384]{1,0:T(8,128)S(1)}, u32[]{:S(2)}, u32[]{:S(2)}) collective-permute-start(f32[8,384]{1,0:T(8,128)S(1)} %get-tuple-element.44), channel_id=1, source_target_pairs={{1,2},{2,1},{5,6},{6,5},{9,10},{10,9},{13,14},{14,13},{17,18},{18,... | collective-permute-start | bytes 36872 | tf_op jit(solution)/shard_map/ppermute | solution.py:89
  8.7 1.0 %invert.1.refs_2_ = f32[8,128]{1,0:T(8,128)S(1)} custom-call(f32[1,6,1,16]{3,2,1,0:T(1,128)} %bitcast.3, f32[4,8,384]{2,1,0:T(8,128)S(1)} %get-tuple-element.41.refs_1_.refs_0_, f32[8,384]{1,0:T(8,128)S(1)} %get-tuple-element.42.refs_2_.refs_1_), custom_call_target="tpu_custom_call" | custom-call | flops 46080000 | bytes 65920 | tf_op jit(solution)/shard_map/invert/pallas_call | solution.py:456
  9.8 0.2 collective-permute-done.1.refs_4_
  10.0 1.2 %collective-permute-done.2.refs_5_ = f32[8,384]{1,0:T(8,128)S(1)} collective-permute-done((f32[8,384]{1,0:T(8,128)S(1)}, f32[8,384]{1,0:T(8,128)S(1)}, u32[]{:S(2)}, u32[]{:S(2)}) %collective-permute-start.2) | collective-permute-done | bytes 12320 | tf_op jit(solution)/shard_map/ppermute | solution.py:89
  11.2 1.5 %couple.1 = (f32[32,8,128]{2,1,0:T(8,128)}, f32[8,384]{1,0:T(8,128)}, f32[4,16,384]{2,1,0:T(8,128)}) custom-call(f32[4,8,384]{2,1,0:T(8,128)S(1)} %get-tuple-element.41.refs_1_.refs_0_, f32[8,384]{1,0:T(8,128)S(1)} %get-tuple-element.42.refs_2_.refs_1_, f32[8,128]{1,0:T(8,128)S(1)} %invert.1.refs_2_, f32[8,384]{1,0:T(8,128)S(1)} %collective-permute-done.refs_3_, ...), custom_call_target="tpu_custom_call" | custom-call | bytes 356352 | tf_op jit(solution)/shard_map/couple/pallas_call | solution.py:456
  12.8 4.8 %all-to-all-start = ((f32[32,8,128]{2,1,0:T(8,128)}), f32[32,8,128]{2,1,0:T(8,128)S(1)}, u32[]{:S(2)}, u32[]{:S(2)}) async-start(f32[32,8,128]{2,1,0:T(8,128)} %get-tuple-element.49), calls=%async_computation | async-start | bytes 262144 | tf_op jit(solution)/shard_map/all_to_all | solution.py:469
  17.6 6.7 %arrange.1 = (f32[16,1200]{1,0:T(8,128)}, bf16[1200,1200]{1,0:T(8,128)(2,1)S(1)}) custom-call(s32[1,1,4,300]{3,2,1,0:T(4,128)} %refs_0_.1, bf16[1,1,1200,1200]{3,2,1,0:T(8,128)(2,1)} %refs_1_.3, f32[1,1,16,1200]{3,2,1,0:T(8,128)} %refs_2_.1), custom_call_target="tpu_custom_call" | custom-call | flops 2949120000 | bytes 5918400 | tf_op jit(solution)/shard_map/arrange/pallas_call | solution.py:456
  24.2 0.2 all-to-all-done.refs_2_
  24.4 4.1 %begin.1 = (f32[40,256]{1,0:T(8,128)}, f32[4,16,384]{2,1,0:T(8,128)}, f32[4,16,384]{2,1,0:T(8,128)}, f32[4,16,384]{2,1,0:T(8,128)}, f32[32,8,128]{2,1,0:T(8,128)...) custom-call(f32[4,16,384]{2,1,0:T(8,128)} %get-tuple-element.47.refs_0_.refs_1_, ...), custom_call_target="tpu_custom_call" | custom-call | flops 46080000 | bytes 3751424 | tf_op jit(solution)/shard_map/begin/pallas_call | solution.py:456
  28.5 5.7 %all-to-all-start.1 = ((f32[32,8,128]{2,1,0:T(8,128)}), f32[32,8,128]{2,1,0:T(8,128)S(1)}, u32[]{:S(2)}, u32[]{:S(2)}) async-start(f32[32,8,128]{2,1,0:T(8,128)} %get-tuple-element.59), calls=%async_computation.1 | async-start | bytes 262144 | tf_op jit(solution)/shard_map/all_to_all | solution.py:469
  34.2 3.1 %collective-permute-start.4 = (f32[16,384]{1,0:T(8,128)}, f32[16,384]{1,0:T(8,128)S(1)}, u32[]{:S(2)}, u32[]{:S(2)}) collective-permute-start(f32[16,384]{1,0:T(8,128)} %get-tuple-element.55), channel_id=1, source_target_pairs={{4,8},{8,4},{12,16},{16,12},{20,24},{24,20},{5,9},{9,5},{13,17},{1... | collective-permute-start | bytes 73736 | tf_op jit(solution)/shard_map/ppermute | solution.py:89
  37.3 3.6 %collective-permute-start.5 = (f32[16,384]{1,0:T(8,128)}, f32[16,384]{1,0:T(8,128)S(1)}, u32[]{:S(2)}, u32[]{:S(2)}) collective-permute-start(f32[16,384]{1,0:T(8,128)} %get-tuple-element.56), channel_id=1, source_target_pairs={{1,2},{2,1},{5,6},{6,5},{9,10},{10,9},{13,14},{14,13},{17,18},{18,... | collective-permute-start | bytes 73736 | tf_op jit(solution)/shard_map/ppermute | solution.py:89
  41.1 1.6 %collective-permute-done.5.refs_6_ = f32[16,384]{1,0:T(8,128)S(1)} collective-permute-done((f32[16,384]{1,0:T(8,128)}, f32[16,384]{1,0:T(8,128)S(1)}, u32[]{:S(2)}, u32[]{:S(2)}) %collective-permute-start.5) | collective-permute-done | bytes 24608 | tf_op jit(solution)/shard_map/ppermute | solution.py:89
  42.7 1.2 %collective-permute-done.6.refs_7_ = f32[16,384]{1,0:T(8,128)S(1)} collective-permute-done((f32[16,384]{1,0:T(8,128)}, f32[16,384]{1,0:T(8,128)S(1)}, u32[]{:S(2)}, u32[]{:S(2)}) %collective-permute-start.6) | collective-permute-done | bytes 24608 | tf_op jit(solution)/shard_map/ppermute | solution.py:89
  43.9 0.6 copy-done.6
  44.5 3.4 %first_direction.1 = (f32[4,16,384]{2,1,0:T(8,128)}, f32[4,16,384]{2,1,0:T(8,128)}, f32[4,16,384]{2,1,0:T(8,128)}, f32[32,8,128]{2,1,0:T(8,128)}, f32[16,384]{1,...) custom-call(f32[40,256]{1,0:T(8,128)} %get-tuple-element.51.refs_0_, ...), custom_call_target="tpu_custom_call" | custom-call | flops 46080000 | bytes 3981824 | tf_op jit(solution)/shard_map/first_direction/pallas_call | solution.py:456
  47.9 4.6 %all-to-all-start.2 = ((f32[32,8,128]{2,1,0:T(8,128)}), f32[32,8,128]{2,1,0:T(8,128)S(1)}, u32[]{:S(2)}, u32[]{:S(2)}) async-start(f32[32,8,128]{2,1,0:T(8,128)} %get-tuple-element.68), calls=%async_computation.2 | async-start | bytes 262144 | tf_op jit(solution)/shard_map/all_to_all | solution.py:469
  52.5 3.1 %collective-permute-start.8 = (f32[16,384]{1,0:T(8,128)}, f32[16,384]{1,0:T(8,128)S(1)}, u32[]{:S(2)}, u32[]{:S(2)}) collective-permute-start(f32[16,384]{1,0:T(8,128)} %get-tuple-element.64), channel_id=1, source_target_pairs={{4,8},{8,4},{12,16},{16,12},{20,24},{24,20},{5,9},{9,5},{13,17},{1... | collective-permute-start | bytes 73736 | tf_op jit(solution)/shard_map/ppermute | solution.py:89
  55.6 3.6 %collective-permute-start.9 = (f32[16,384]{1,0:T(8,128)}, f32[16,384]{1,0:T(8,128)S(1)}, u32[]{:S(2)}, u32[]{:S(2)}) collective-permute-start(f32[16,384]{1,0:T(8,128)} %get-tuple-element.65), channel_id=1, source_target_pairs={{1,2},{2,1},{5,6},{6,5},{9,10},{10,9},{13,14},{14,13},{17,18},{18,... | collective-permute-start | bytes 73736 | tf_op jit(solution)/shard_map/ppermute | solution.py:89
  59.4 1.6 %collective-permute-done.9.refs_8_ = f32[16,384]{1,0:T(8,128)S(1)} collective-permute-done((f32[16,384]{1,0:T(8,128)}, f32[16,384]{1,0:T(8,128)S(1)}, u32[]{:S(2)}, u32[]{:S(2)}) %collective-permute-start.9) | collective-permute-done | bytes 24608 | tf_op jit(solution)/shard_map/ppermute | solution.py:89
  61.0 1.2 %collective-permute-done.10.refs_9_ = f32[16,384]{1,0:T(8,128)S(1)} collective-permute-done((f32[16,384]{1,0:T(8,128)}, f32[16,384]{1,0:T(8,128)S(1)}, u32[]{:S(2)}, u32[]{:S(2)}) %collective-permute-start.10) | collective-permute-done | bytes 24608 | tf_op jit(solution)/shard_map/ppermute | solution.py:89
  62.3 0.6 copy-done.2
  62.8 3.3 %second_direction.1 = (f32[4,16,384]{2,1,0:T(8,128)}, f32[4,16,384]{2,1,0:T(8,128)}, f32[4,16,384]{2,1,0:T(8,128)}, f32[4,16,384]{2,1,0:T(8,128)}, f32[4,16,384]...) custom-call(f32[40,256]{1,0:T(8,128)} %get-tuple-element.51.refs_0_,, ...), custom_call_target="tpu_custom_call" | custom-call | flops 46080000 | bytes 4379136 | tf_op jit(solution)/shard_map/second_direction/pallas_call | solution.py:456
  66.1 4.6 %all-to-all-start.3 = ((f32[32,8,128]{2,1,0:T(8,128)}), f32[32,8,128]{2,1,0:T(8,128)S(1)}, u32[]{:S(2)}, u32[]{:S(2)}) async-start(f32[32,8,128]{2,1,0:T(8,128)} %get-tuple-element.79), calls=%async_computation.3 | async-start | bytes 262144 | tf_op jit(solution)/shard_map/all_to_all | solution.py:469
  70.8 3.1 %collective-permute-start.12 = (f32[16,384]{1,0:T(8,128)}, f32[16,384]{1,0:T(8,128)S(1)}, u32[]{:S(2)}, u32[]{:S(2)}) collective-permute-start(f32[16,384]{1,0:T(8,128)} %get-tuple-element.75), channel_id=1, source_target_pairs={{4,8},{8,4},{12,16},{16,12},{20,24},{24,20},{5,9},{9,5},{13,17},{1... | collective-permute-start | bytes 73736 | tf_op jit(solution)/shard_map/ppermute | solution.py:89
  73.9 3.6 %collective-permute-start.13 = (f32[16,384]{1,0:T(8,128)}, f32[16,384]{1,0:T(8,128)S(1)}, u32[]{:S(2)}, u32[]{:S(2)}) collective-permute-start(f32[16,384]{1,0:T(8,128)} %get-tuple-element.76), channel_id=1, source_target_pairs={{1,2},{2,1},{5,6},{6,5},{9,10},{10,9},{13,14},{14,13},{17,18},{18,... | collective-permute-start | bytes 73736 | tf_op jit(solution)/shard_map/ppermute | solution.py:89
  77.7 1.6 %collective-permute-done.13.refs_9_ = f32[16,384]{1,0:T(8,128)S(1)} collective-permute-done((f32[16,384]{1,0:T(8,128)}, f32[16,384]{1,0:T(8,128)S(1)}, u32[]{:S(2)}, u32[]{:S(2)}) %collective-permute-start.13) | collective-permute-done | bytes 24608 | tf_op jit(solution)/shard_map/ppermute | solution.py:89
  79.2 1.2 %collective-permute-done.14.refs_10_ = f32[16,384]{1,0:T(8,128)S(1)} collective-permute-done((f32[16,384]{1,0:T(8,128)}, f32[16,384]{1,0:T(8,128)S(1)}, u32[]{:S(2)}, u32[]{:S(2)}) %collective-permute-start.14) | collective-permute-done | bytes 24608 | tf_op jit(solution)/shard_map/ppermute | solution.py:89
  80.5 0.6 copy-done.10
  81.0 2.1 %finish.1 = (f32[1,1,4,16,300]{4,3,2,1,0:T(8,128)}, f32[1,1,4,16,300]{4,3,2,1,0:T(8,128)}) custom-call(f32[8,128]{1,0:T(8,128)} %get-tuple-element.69.refs_0_, f32[4,16,384]{2,1,0:T(8,128)} %get-tuple-element.70.refs_1_, f32[8,384]{1,0:T(8,128)} %get-tuple-element.53.refs_3_.refs_2_, f32[4,16,384]{2,1,0:T(8,128)} %get-tuple-element.71.refs_3_, ...), custom_call_target="tpu_custom_call" | custom-call | bytes 989184 | tf_op jit(solution)/shard_map/finish/pallas_call | solution.py:456
  (40 shorter events, 0.7 us)
Async XLA Ops:
  1.5 8.3 %collective-permute-start = (f32[8,384]{1,0:T(8,128)S(1)}, f32[8,384]{1,0:T(8,128)S(1)}, u32[]{:S(2)}, u32[]{:S(2)}) collective-permute-start(f32[8,384]{1,0:T(8,128)S(1)} %get-tuple-element.43), channel_id=1, source_target_pairs={{4,8},{8,4},{12,16},{16,12},{20,24},{24,20},{5,9},{9,5},{13,17},{1... | collective-permute-start | bytes 36872 | tf_op jit(solution)/shard_map/ppermute | solution.py:89
  4.6 5.3 %collective-permute-start.1 = (f32[8,384]{1,0:T(8,128)S(1)}, f32[8,384]{1,0:T(8,128)S(1)}, u32[]{:S(2)}, u32[]{:S(2)}) collective-permute-start(f32[8,384]{1,0:T(8,128)S(1)} %get-tuple-element.44), channel_id=1, source_target_pairs={{1,2},{2,1},{5,6},{6,5},{9,10},{10,9},{13,14},{14,13},{17,18},{18,... | collective-permute-start | bytes 36872 | tf_op jit(solution)/shard_map/ppermute | solution.py:89
  8.6 2.6 %collective-permute-start.2 = (f32[8,384]{1,0:T(8,128)S(1)}, f32[8,384]{1,0:T(8,128)S(1)}, u32[]{:S(2)}, u32[]{:S(2)}) collective-permute-start(f32[8,384]{1,0:T(8,128)S(1)} %get-tuple-element.45), channel_id=1, source_target_pairs={{0,4},{4,0},{8,12},{12,8},{16,20},{20,16},{24,28},{28,24},{1,5},{5... | collective-permute-start | bytes 36872 | tf_op jit(solution)/shard_map/ppermute | solution.py:89
  8.7 2.5 %collective-permute-start.3 = (f32[8,384]{1,0:T(8,128)S(1)}, f32[8,384]{1,0:T(8,128)S(1)}, u32[]{:S(2)}, u32[]{:S(2)}) collective-permute-start(f32[8,384]{1,0:T(8,128)S(1)} %get-tuple-element.46), channel_id=1, source_target_pairs={{0,1},{1,0},{2,3},{3,2},{4,5},{5,4},{6,7},{7,6},{8,9},{9,8},{10,11... | collective-permute-start | bytes 36872 | tf_op jit(solution)/shard_map/ppermute | solution.py:89
  12.8 11.7 %all-to-all-start = ((f32[32,8,128]{2,1,0:T(8,128)}), f32[32,8,128]{2,1,0:T(8,128)S(1)}, u32[]{:S(2)}, u32[]{:S(2)}) async-start(f32[32,8,128]{2,1,0:T(8,128)} %get-tuple-element.49), calls=%async_computation | async-start | bytes 262144 | tf_op jit(solution)/shard_map/all_to_all | solution.py:469
  28.5 15.4 %all-to-all-start.1 = ((f32[32,8,128]{2,1,0:T(8,128)}), f32[32,8,128]{2,1,0:T(8,128)S(1)}, u32[]{:S(2)}, u32[]{:S(2)}) async-start(f32[32,8,128]{2,1,0:T(8,128)} %get-tuple-element.59), calls=%async_computation.1 | async-start | bytes 262144 | tf_op jit(solution)/shard_map/all_to_all | solution.py:469
  34.2 6.9 %collective-permute-start.4 = (f32[16,384]{1,0:T(8,128)}, f32[16,384]{1,0:T(8,128)S(1)}, u32[]{:S(2)}, u32[]{:S(2)}) collective-permute-start(f32[16,384]{1,0:T(8,128)} %get-tuple-element.55), channel_id=1, source_target_pairs={{4,8},{8,4},{12,16},{16,12},{20,24},{24,20},{5,9},{9,5},{13,17},{1... | collective-permute-start | bytes 73736 | tf_op jit(solution)/shard_map/ppermute | solution.py:89
  37.3 5.4 %collective-permute-start.5 = (f32[16,384]{1,0:T(8,128)}, f32[16,384]{1,0:T(8,128)S(1)}, u32[]{:S(2)}, u32[]{:S(2)}) collective-permute-start(f32[16,384]{1,0:T(8,128)} %get-tuple-element.56), channel_id=1, source_target_pairs={{1,2},{2,1},{5,6},{6,5},{9,10},{10,9},{13,14},{14,13},{17,18},{18,... | collective-permute-start | bytes 73736 | tf_op jit(solution)/shard_map/ppermute | solution.py:89
  40.9 3.0 %collective-permute-start.6 = (f32[16,384]{1,0:T(8,128)}, f32[16,384]{1,0:T(8,128)S(1)}, u32[]{:S(2)}, u32[]{:S(2)}) collective-permute-start(f32[16,384]{1,0:T(8,128)} %get-tuple-element.57), channel_id=1, source_target_pairs={{0,4},{4,0},{8,12},{12,8},{16,20},{20,16},{24,28},{28,24},{1,5},{5... | collective-permute-start | bytes 73736 | tf_op jit(solution)/shard_map/ppermute | solution.py:89
  41.0 2.9 %collective-permute-start.7 = (f32[16,384]{1,0:T(8,128)}, f32[16,384]{1,0:T(8,128)S(1)}, u32[]{:S(2)}, u32[]{:S(2)}) collective-permute-start(f32[16,384]{1,0:T(8,128)} %get-tuple-element.58), channel_id=1, source_target_pairs={{0,1},{1,0},{2,3},{3,2},{4,5},{5,4},{6,7},{7,6},{8,9},{9,8},{10,11... | collective-permute-start | bytes 73736 | tf_op jit(solution)/shard_map/ppermute | solution.py:89
  41.1 2.8 %copy-start.3 = (f32[16,384]{1,0:T(8,128)}, f32[16,384]{1,0:T(8,128)S(1)}, u32[]{:S(2)}) copy-start(f32[16,384]{1,0:T(8,128)S(1)} %collective-permute-done.4.refs_5_) | copy-start | bytes 73732
  42.7 1.2 %copy-start.5 = (f32[16,384]{1,0:T(8,128)}, f32[16,384]{1,0:T(8,128)S(1)}, u32[]{:S(2)}) copy-start(f32[16,384]{1,0:T(8,128)S(1)} %collective-permute-done.5.refs_6_) | copy-start | bytes 73732
  43.9 0.6 copy-start.6
  43.9 0.6 copy-start.7
  47.9 14.3 %all-to-all-start.2 = ((f32[32,8,128]{2,1,0:T(8,128)}), f32[32,8,128]{2,1,0:T(8,128)S(1)}, u32[]{:S(2)}, u32[]{:S(2)}) async-start(f32[32,8,128]{2,1,0:T(8,128)} %get-tuple-element.68), calls=%async_computation.2 | async-start | bytes 262144 | tf_op jit(solution)/shard_map/all_to_all | solution.py:469
  52.5 6.9 %collective-permute-start.8 = (f32[16,384]{1,0:T(8,128)}, f32[16,384]{1,0:T(8,128)S(1)}, u32[]{:S(2)}, u32[]{:S(2)}) collective-permute-start(f32[16,384]{1,0:T(8,128)} %get-tuple-element.64), channel_id=1, source_target_pairs={{4,8},{8,4},{12,16},{16,12},{20,24},{24,20},{5,9},{9,5},{13,17},{1... | collective-permute-start | bytes 73736 | tf_op jit(solution)/shard_map/ppermute | solution.py:89
  55.6 5.4 %collective-permute-start.9 = (f32[16,384]{1,0:T(8,128)}, f32[16,384]{1,0:T(8,128)S(1)}, u32[]{:S(2)}, u32[]{:S(2)}) collective-permute-start(f32[16,384]{1,0:T(8,128)} %get-tuple-element.65), channel_id=1, source_target_pairs={{1,2},{2,1},{5,6},{6,5},{9,10},{10,9},{13,14},{14,13},{17,18},{18,... | collective-permute-start | bytes 73736 | tf_op jit(solution)/shard_map/ppermute | solution.py:89
  59.3 3.0 %collective-permute-start.10 = (f32[16,384]{1,0:T(8,128)}, f32[16,384]{1,0:T(8,128)S(1)}, u32[]{:S(2)}, u32[]{:S(2)}) collective-permute-start(f32[16,384]{1,0:T(8,128)} %get-tuple-element.66), channel_id=1, source_target_pairs={{0,4},{4,0},{8,12},{12,8},{16,20},{20,16},{24,28},{28,24},{1,5},{5... | collective-permute-start | bytes 73736 | tf_op jit(solution)/shard_map/ppermute | solution.py:89
  59.3 2.9 %collective-permute-start.11 = (f32[16,384]{1,0:T(8,128)}, f32[16,384]{1,0:T(8,128)S(1)}, u32[]{:S(2)}, u32[]{:S(2)}) collective-permute-start(f32[16,384]{1,0:T(8,128)} %get-tuple-element.67), channel_id=1, source_target_pairs={{0,1},{1,0},{2,3},{3,2},{4,5},{5,4},{6,7},{7,6},{8,9},{9,8},{10,11... | collective-permute-start | bytes 73736 | tf_op jit(solution)/shard_map/ppermute | solution.py:89
  59.4 2.8 %copy-start = (f32[16,384]{1,0:T(8,128)}, f32[16,384]{1,0:T(8,128)S(1)}, u32[]{:S(2)}) copy-start(f32[16,384]{1,0:T(8,128)S(1)} %collective-permute-done.8.refs_7_) | copy-start | bytes 73732
  61.0 1.2 %copy-start.1 = (f32[16,384]{1,0:T(8,128)}, f32[16,384]{1,0:T(8,128)S(1)}, u32[]{:S(2)}) copy-start(f32[16,384]{1,0:T(8,128)S(1)} %collective-permute-done.9.refs_8_) | copy-start | bytes 73732
  62.2 0.6 copy-start.2
  62.2 0.6 copy-start.4
  66.1 14.3 %all-to-all-start.3 = ((f32[32,8,128]{2,1,0:T(8,128)}), f32[32,8,128]{2,1,0:T(8,128)S(1)}, u32[]{:S(2)}, u32[]{:S(2)}) async-start(f32[32,8,128]{2,1,0:T(8,128)} %get-tuple-element.79), calls=%async_computation.3 | async-start | bytes 262144 | tf_op jit(solution)/shard_map/all_to_all | solution.py:469
  70.8 6.9 %collective-permute-start.12 = (f32[16,384]{1,0:T(8,128)}, f32[16,384]{1,0:T(8,128)S(1)}, u32[]{:S(2)}, u32[]{:S(2)}) collective-permute-start(f32[16,384]{1,0:T(8,128)} %get-tuple-element.75), channel_id=1, source_target_pairs={{4,8},{8,4},{12,16},{16,12},{20,24},{24,20},{5,9},{9,5},{13,17},{1... | collective-permute-start | bytes 73736 | tf_op jit(solution)/shard_map/ppermute | solution.py:89
  73.9 5.4 %collective-permute-start.13 = (f32[16,384]{1,0:T(8,128)}, f32[16,384]{1,0:T(8,128)S(1)}, u32[]{:S(2)}, u32[]{:S(2)}) collective-permute-start(f32[16,384]{1,0:T(8,128)} %get-tuple-element.76), channel_id=1, source_target_pairs={{1,2},{2,1},{5,6},{6,5},{9,10},{10,9},{13,14},{14,13},{17,18},{18,... | collective-permute-start | bytes 73736 | tf_op jit(solution)/shard_map/ppermute | solution.py:89
  77.5 3.0 %collective-permute-start.14 = (f32[16,384]{1,0:T(8,128)}, f32[16,384]{1,0:T(8,128)S(1)}, u32[]{:S(2)}, u32[]{:S(2)}) collective-permute-start(f32[16,384]{1,0:T(8,128)} %get-tuple-element.77), channel_id=1, source_target_pairs={{0,4},{4,0},{8,12},{12,8},{16,20},{20,16},{24,28},{28,24},{1,5},{5... | collective-permute-start | bytes 73736 | tf_op jit(solution)/shard_map/ppermute | solution.py:89
  77.6 2.9 %collective-permute-start.15 = (f32[16,384]{1,0:T(8,128)}, f32[16,384]{1,0:T(8,128)S(1)}, u32[]{:S(2)}, u32[]{:S(2)}) collective-permute-start(f32[16,384]{1,0:T(8,128)} %get-tuple-element.78), channel_id=1, source_target_pairs={{0,1},{1,0},{2,3},{3,2},{4,5},{5,4},{6,7},{7,6},{8,9},{9,8},{10,11... | collective-permute-start | bytes 73736 | tf_op jit(solution)/shard_map/ppermute | solution.py:89
  77.7 2.8 %copy-start.8 = (f32[16,384]{1,0:T(8,128)}, f32[16,384]{1,0:T(8,128)S(1)}, u32[]{:S(2)}) copy-start(f32[16,384]{1,0:T(8,128)S(1)} %collective-permute-done.12.refs_8_) | copy-start | bytes 73732
  79.2 1.2 %copy-start.9 = (f32[16,384]{1,0:T(8,128)}, f32[16,384]{1,0:T(8,128)S(1)}, u32[]{:S(2)}) copy-start(f32[16,384]{1,0:T(8,128)S(1)} %collective-permute-done.13.refs_9_) | copy-start | bytes 73732
  80.4 0.6 copy-start.10
  80.4 0.6 copy-start.11

commit v10 on v9

--- a/solution.py
+++ b/solution.py
@@ -18,7 +18,7 @@
 INVERSE_LANE = 48
 SCALAR_LANE = 96
 BLOCK = 256
-SWAPS = (1, 3, 0, 2)
+SWAPS = (1, 0, 3, 2)
 
 
 class Sizes:
@@ -170,7 +170,7 @@
     local_tile[:, INVERSE_LANE : INVERSE_LANE + 8] = inverse
 
 
-def couple(z, padded, masks, local_tile, got1, got3, got0, got2, sent, live_rows, lift_rows, tile):
+def couple(z, padded, masks, local_tile, got1, got0, got3, got2, sent, live_rows, lift_rows, tile):
     near = across_faces(z, (got0, got1, got2, got3))
     inverse = local_tile[:, INVERSE_LANE : INVERSE_LANE + 8]
     tile[...] = local_tile[...]
@@ -319,7 +319,7 @@
 
 
 def first_direction(
-    z, solve_rows, lift_rows, faces, masks, rows, got1, got3, got0, got2, received, arranged,
+    z, solve_rows, lift_rows, faces, masks, rows, got1, got0, got3, got2, received, arranged,
     residual, direction, image, sent, to0, to1, to2, to3,
     tile, packed,
 ):
@@ -344,7 +344,7 @@
 
 def second_direction(
     z, solve_rows, lift_rows, faces, masks, residual, direction, multipliers,
-    got1, got3, got0, got2, received, arranged,
+    got1, got0, got3, got2, received, arranged,
     next_multipliers, next_residual, projected, image, fresh, sums, sent, to0, to1, to2, to3,
     packed,
 ):
@@ -379,7 +379,7 @@
 
 def finish(
     z, sums, faces, masks, residual, image, multipliers, projected, direction,
-    got1, got3, got0, got2, received,
+    got1, got0, got3, got2, received,
     out_multipliers, out_residual,
 ):
     summed = jnp.sum(received[...], axis=0)
@@ -508,19 +508,19 @@
     residual, direction, faces, coarse, *sent_faces = call(
         z, first_direction, [field, field, field, sent] + to_faces,
         [solve_rows, lift_rows, faces, masks, rows, *got, coarse, arranged],
-        [tile, packed], product_flops, near=2,
+        [tile, packed], product_flops, near=6,
     )
     coarse, got = gather(coarse), exchange(sent_faces)
     multipliers, residual, projected, image, faces, sums, coarse, *sent_faces = call(
         z, second_direction, [field, field, field, field, field, tile, sent] + to_faces,
         [solve_rows, lift_rows, faces, masks, residual, direction, multipliers, *got, coarse, arranged],
-        [packed], product_flops, near=2,
+        [packed], product_flops, near=6,
     )
     coarse, got = gather(coarse), exchange(sent_faces)
     whole = ((1, 1, 4, z.cases, z.face), F32)
     multipliers, residual = call(
         z, finish, [whole, whole],
-        [sums, faces, masks, residual, image, multipliers, projected, direction, *got, coarse], near=1,
+        [sums, faces, masks, residual, image, multipliers, projected, direction, *got, coarse], near=5,
     )
     return multipliers, residual
 

time: 84.5 us -> 85.3 us (level)
  the two profiles are of different devices: /device:TPU:5 before, /device:TPU:1 now
where the time goes in v10:
time: 85.3 us; the launch traced here: 84.6 us
  starting transfers between devices  54.5 us (64%)
  Pallas kernels  22.6 us (26%)
  waiting for transfers between devices  6.61 us (8%)
  between operations  0.88 us (1%)
    ppermute x16, starting transfers between devices, exchange(): got.append(lax.ppermute(sent[i], axis, pairs))  35.1 us
    pallas_call x8, Pallas kernels, call(): pl.pallas_call(run, out_shape=[pltpu.HBM(a.shape, a.dtype) for a in shape...  22.6 us
    all_to_all x4, starting transfers between devices, gather(): return lax.all_to_all(values, AXES, 0, 0, tiled=True)  19.4 us
    ppermute x16, waiting for transfers between devices, exchange(): got.append(lax.ppermute(sent[i], axis, pairs))  5.09 us
  transfers between devices with their start and end apart: 20, of which 5 were waited for; matrix products, arithmetic and copies ran while one was open for 0% of the time, Pallas kernels for 9%

profile of v10, /device:TPU:1, one launch (start us, length us, event | category | flops | bytes accessed | tf_op | source)
XLA Modules:
  0.0 84.6 jit_solution(6264449872216575470)
XLA Ops:
  0.6 0.8 prepare.1
  1.5 0.7 collective-permute-start
  2.1 4.6 %collective-permute-start.1 = (f32[8,384]{1,0:T(8,128)S(1)}, f32[8,384]{1,0:T(8,128)S(1)}, u32[]{:S(2)}, u32[]{:S(2)}) collective-permute-start(f32[8,384]{1,0:T(8,128)S(1)} %get-tuple-element.44), channel_id=1, source_target_pairs={{0,4},{4,0},{8,12},{12,8},{16,20},{20,16},{24,28},{28,24},{1,5},{5... | collective-permute-start | bytes 36872 | tf_op jit(solution)/shard_map/ppermute | solution.py:89
  6.8 4.2 %collective-permute-start.2 = (f32[8,384]{1,0:T(8,128)S(1)}, f32[8,384]{1,0:T(8,128)S(1)}, u32[]{:S(2)}, u32[]{:S(2)}) collective-permute-start(f32[8,384]{1,0:T(8,128)S(1)} %get-tuple-element.45), channel_id=1, source_target_pairs={{1,2},{2,1},{5,6},{6,5},{9,10},{10,9},{13,14},{14,13},{17,18},{18,... | collective-permute-start | bytes 36872 | tf_op jit(solution)/shard_map/ppermute | solution.py:89
  11.0 0.1 collective-permute-start.3
  11.1 1.0 %invert.1.refs_2_ = f32[8,128]{1,0:T(8,128)S(1)} custom-call(f32[1,6,1,16]{3,2,1,0:T(1,128)} %bitcast.3, f32[4,8,384]{2,1,0:T(8,128)S(1)} %get-tuple-element.41.refs_1_.refs_0_, f32[8,384]{1,0:T(8,128)S(1)} %get-tuple-element.42.refs_2_.refs_1_), custom_call_target="tpu_custom_call" | custom-call | flops 46080000 | bytes 65920 | tf_op jit(solution)/shard_map/invert/pallas_call | solution.py:456
  12.1 0.2 collective-permute-done.2.refs_5_
  12.4 1.5 %couple.1 = (f32[32,8,128]{2,1,0:T(8,128)}, f32[8,384]{1,0:T(8,128)}, f32[4,16,384]{2,1,0:T(8,128)}) custom-call(f32[4,8,384]{2,1,0:T(8,128)S(1)} %get-tuple-element.41.refs_1_.refs_0_, f32[8,384]{1,0:T(8,128)S(1)} %get-tuple-element.42.refs_2_.refs_1_, f32[8,128]{1,0:T(8,128)S(1)} %invert.1.refs_2_, f32[8,384]{1,0:T(8,128)S(1)} %collective-permute-done.refs_3_, ...), custom_call_target="tpu_custom_call" | custom-call | bytes 356352 | tf_op jit(solution)/shard_map/couple/pallas_call | solution.py:456
  13.9 5.1 %all-to-all-start = ((f32[32,8,128]{2,1,0:T(8,128)}), f32[32,8,128]{2,1,0:T(8,128)S(1)}, u32[]{:S(2)}, u32[]{:S(2)}) async-start(f32[32,8,128]{2,1,0:T(8,128)} %get-tuple-element.49), calls=%async_computation | async-start | bytes 262144 | tf_op jit(solution)/shard_map/all_to_all | solution.py:469
  19.0 6.7 %arrange.1 = (f32[16,1200]{1,0:T(8,128)}, bf16[1200,1200]{1,0:T(8,128)(2,1)S(1)}) custom-call(s32[1,1,4,300]{3,2,1,0:T(4,128)} %refs_0_.1, bf16[1,1,1200,1200]{3,2,1,0:T(8,128)(2,1)} %refs_1_.3, f32[1,1,16,1200]{3,2,1,0:T(8,128)} %refs_2_.1), custom_call_target="tpu_custom_call" | custom-call | flops 2949120000 | bytes 5918400 | tf_op jit(solution)/shard_map/arrange/pallas_call | solution.py:456
  25.7 1.5 %all-to-all-done.refs_2_ = f32[32,8,128]{2,1,0:T(8,128)S(1)} async-done(((f32[32,8,128]{2,1,0:T(8,128)}), f32[32,8,128]{2,1,0:T(8,128)S(1)}, u32[]{:S(2)}, u32[]{:S(2)}) %all-to-all-start) | async-done | bytes 131104 | tf_op jit(solution)/shard_map/all_to_all | solution.py:469
  27.2 4.1 %begin.1 = (f32[40,256]{1,0:T(8,128)}, f32[4,16,384]{2,1,0:T(8,128)}, f32[4,16,384]{2,1,0:T(8,128)}, f32[4,16,384]{2,1,0:T(8,128)}, f32[32,8,128]{2,1,0:T(8,128)...) custom-call(f32[4,16,384]{2,1,0:T(8,128)} %get-tuple-element.47.refs_0_.refs_1_, ...), custom_call_target="tpu_custom_call" | custom-call | flops 46080000 | bytes 3751424 | tf_op jit(solution)/shard_map/begin/pallas_call | solution.py:456
  31.3 4.3 %all-to-all-start.1 = ((f32[32,8,128]{2,1,0:T(8,128)}), f32[32,8,128]{2,1,0:T(8,128)S(1)}, u32[]{:S(2)}, u32[]{:S(2)}) async-start(f32[32,8,128]{2,1,0:T(8,128)} %get-tuple-element.59), calls=%async_computation.1 | async-start | bytes 262144 | tf_op jit(solution)/shard_map/all_to_all | solution.py:469
  35.7 0.7 collective-permute-start.4
  36.4 3.9 %collective-permute-start.5 = (f32[16,384]{1,0:T(8,128)}, f32[16,384]{1,0:T(8,128)S(1)}, u32[]{:S(2)}, u32[]{:S(2)}) collective-permute-start(f32[16,384]{1,0:T(8,128)} %get-tuple-element.56), channel_id=1, source_target_pairs={{0,4},{4,0},{8,12},{12,8},{16,20},{20,16},{24,28},{28,24},{1,5},{5... | collective-permute-start | bytes 73736 | tf_op jit(solution)/shard_map/ppermute | solution.py:89
  40.2 3.9 %collective-permute-start.6 = (f32[16,384]{1,0:T(8,128)}, f32[16,384]{1,0:T(8,128)S(1)}, u32[]{:S(2)}, u32[]{:S(2)}) collective-permute-start(f32[16,384]{1,0:T(8,128)} %get-tuple-element.57), channel_id=1, source_target_pairs={{1,2},{2,1},{5,6},{6,5},{9,10},{10,9},{13,14},{14,13},{17,18},{18,... | collective-permute-start | bytes 73736 | tf_op jit(solution)/shard_map/ppermute | solution.py:89
  44.1 0.1 collective-permute-start.7
  44.2 1.6 %collective-permute-done.6.refs_7_ = f32[16,384]{1,0:T(8,128)S(1)} collective-permute-done((f32[16,384]{1,0:T(8,128)}, f32[16,384]{1,0:T(8,128)S(1)}, u32[]{:S(2)}, u32[]{:S(2)}) %collective-permute-start.6) | collective-permute-done | bytes 24608 | tf_op jit(solution)/shard_map/ppermute | solution.py:89
  45.9 3.3 %first_direction.1 = (f32[4,16,384]{2,1,0:T(8,128)}, f32[4,16,384]{2,1,0:T(8,128)}, f32[4,16,384]{2,1,0:T(8,128)}, f32[32,8,128]{2,1,0:T(8,128)}, f32[16,384]{1,...) custom-call(f32[40,256]{1,0:T(8,128)} %get-tuple-element.51.refs_0_, ...), custom_call_target="tpu_custom_call" | custom-call | flops 46080000 | bytes 3981824 | tf_op jit(solution)/shard_map/first_direction/pallas_call | solution.py:456
  49.2 5.0 %all-to-all-start.2 = ((f32[32,8,128]{2,1,0:T(8,128)}), f32[32,8,128]{2,1,0:T(8,128)S(1)}, u32[]{:S(2)}, u32[]{:S(2)}) async-start(f32[32,8,128]{2,1,0:T(8,128)} %get-tuple-element.68), calls=%async_computation.2 | async-start | bytes 262144 | tf_op jit(solution)/shard_map/all_to_all | solution.py:469
  54.2 0.7 collective-permute-start.8
  54.8 3.9 %collective-permute-start.9 = (f32[16,384]{1,0:T(8,128)}, f32[16,384]{1,0:T(8,128)S(1)}, u32[]{:S(2)}, u32[]{:S(2)}) collective-permute-start(f32[16,384]{1,0:T(8,128)} %get-tuple-element.65), channel_id=1, source_target_pairs={{0,4},{4,0},{8,12},{12,8},{16,20},{20,16},{24,28},{28,24},{1,5},{5... | collective-permute-start | bytes 73736 | tf_op jit(solution)/shard_map/ppermute | solution.py:89
  58.7 3.9 %collective-permute-start.10 = (f32[16,384]{1,0:T(8,128)}, f32[16,384]{1,0:T(8,128)S(1)}, u32[]{:S(2)}, u32[]{:S(2)}) collective-permute-start(f32[16,384]{1,0:T(8,128)} %get-tuple-element.66), channel_id=1, source_target_pairs={{1,2},{2,1},{5,6},{6,5},{9,10},{10,9},{13,14},{14,13},{17,18},{18,... | collective-permute-start | bytes 73736 | tf_op jit(solution)/shard_map/ppermute | solution.py:89
  62.7 1.6 %collective-permute-done.10.refs_9_ = f32[16,384]{1,0:T(8,128)S(1)} collective-permute-done((f32[16,384]{1,0:T(8,128)}, f32[16,384]{1,0:T(8,128)S(1)}, u32[]{:S(2)}, u32[]{:S(2)}) %collective-permute-start.10) | collective-permute-done | bytes 24608 | tf_op jit(solution)/shard_map/ppermute | solution.py:89
  64.3 3.2 %second_direction.1 = (f32[4,16,384]{2,1,0:T(8,128)}, f32[4,16,384]{2,1,0:T(8,128)}, f32[4,16,384]{2,1,0:T(8,128)}, f32[4,16,384]{2,1,0:T(8,128)}, f32[4,16,384]...) custom-call(f32[40,256]{1,0:T(8,128)} %get-tuple-element.51.refs_0_,, ...), custom_call_target="tpu_custom_call" | custom-call | flops 46080000 | bytes 4379136 | tf_op jit(solution)/shard_map/second_direction/pallas_call | solution.py:456
  67.5 5.0 %all-to-all-start.3 = ((f32[32,8,128]{2,1,0:T(8,128)}), f32[32,8,128]{2,1,0:T(8,128)S(1)}, u32[]{:S(2)}, u32[]{:S(2)}) async-start(f32[32,8,128]{2,1,0:T(8,128)} %get-tuple-element.79), calls=%async_computation.3 | async-start | bytes 262144 | tf_op jit(solution)/shard_map/all_to_all | solution.py:469
  72.5 0.7 collective-permute-start.12
  73.1 3.9 %collective-permute-start.13 = (f32[16,384]{1,0:T(8,128)}, f32[16,384]{1,0:T(8,128)S(1)}, u32[]{:S(2)}, u32[]{:S(2)}) collective-permute-start(f32[16,384]{1,0:T(8,128)} %get-tuple-element.76), channel_id=1, source_target_pairs={{0,4},{4,0},{8,12},{12,8},{16,20},{20,16},{24,28},{28,24},{1,5},{5... | collective-permute-start | bytes 73736 | tf_op jit(solution)/shard_map/ppermute | solution.py:89
  77.0 3.9 %collective-permute-start.14 = (f32[16,384]{1,0:T(8,128)}, f32[16,384]{1,0:T(8,128)S(1)}, u32[]{:S(2)}, u32[]{:S(2)}) collective-permute-start(f32[16,384]{1,0:T(8,128)} %get-tuple-element.77), channel_id=1, source_target_pairs={{1,2},{2,1},{5,6},{6,5},{9,10},{10,9},{13,14},{14,13},{17,18},{18,... | collective-permute-start | bytes 73736 | tf_op jit(solution)/shard_map/ppermute | solution.py:89
  80.9 0.1 collective-permute-start.15
  81.0 1.6 %collective-permute-done.14.refs_10_ = f32[16,384]{1,0:T(8,128)S(1)} collective-permute-done((f32[16,384]{1,0:T(8,128)}, f32[16,384]{1,0:T(8,128)S(1)}, u32[]{:S(2)}, u32[]{:S(2)}) %collective-permute-start.14) | collective-permute-done | bytes 24608 | tf_op jit(solution)/shard_map/ppermute | solution.py:89
  82.6 1.9 %finish.1 = (f32[1,1,4,16,300]{4,3,2,1,0:T(8,128)}, f32[1,1,4,16,300]{4,3,2,1,0:T(8,128)}) custom-call(f32[8,128]{1,0:T(8,128)} %get-tuple-element.69.refs_0_, f32[4,16,384]{2,1,0:T(8,128)} %get-tuple-element.70.refs_1_, f32[8,384]{1,0:T(8,128)} %get-tuple-element.53.refs_3_.refs_2_, f32[4,16,384]{2,1,0:T(8,128)} %get-tuple-element.71.refs_3_, ...), custom_call_target="tpu_custom_call" | custom-call | bytes 989184 | tf_op jit(solution)/shard_map/finish/pallas_call | solution.py:456
  (16 shorter events, 0.1 us)
Async XLA Ops:
  1.5 10.6 %collective-permute-start = (f32[8,384]{1,0:T(8,128)S(1)}, f32[8,384]{1,0:T(8,128)S(1)}, u32[]{:S(2)}, u32[]{:S(2)}) collective-permute-start(f32[8,384]{1,0:T(8,128)S(1)} %get-tuple-element.43), channel_id=1, source_target_pairs={{4,8},{8,4},{12,16},{16,12},{20,24},{24,20},{5,9},{9,5},{13,17},{1... | collective-permute-start | bytes 36872 | tf_op jit(solution)/shard_map/ppermute | solution.py:89
  2.1 10.0 %collective-permute-start.1 = (f32[8,384]{1,0:T(8,128)S(1)}, f32[8,384]{1,0:T(8,128)S(1)}, u32[]{:S(2)}, u32[]{:S(2)}) collective-permute-start(f32[8,384]{1,0:T(8,128)S(1)} %get-tuple-element.44), channel_id=1, source_target_pairs={{0,4},{4,0},{8,12},{12,8},{16,20},{20,16},{24,28},{28,24},{1,5},{5... | collective-permute-start | bytes 36872 | tf_op jit(solution)/shard_map/ppermute | solution.py:89
  6.8 5.6 %collective-permute-start.2 = (f32[8,384]{1,0:T(8,128)S(1)}, f32[8,384]{1,0:T(8,128)S(1)}, u32[]{:S(2)}, u32[]{:S(2)}) collective-permute-start(f32[8,384]{1,0:T(8,128)S(1)} %get-tuple-element.45), channel_id=1, source_target_pairs={{1,2},{2,1},{5,6},{6,5},{9,10},{10,9},{13,14},{14,13},{17,18},{18,... | collective-permute-start | bytes 36872 | tf_op jit(solution)/shard_map/ppermute | solution.py:89
  11.0 1.4 %collective-permute-start.3 = (f32[8,384]{1,0:T(8,128)S(1)}, f32[8,384]{1,0:T(8,128)S(1)}, u32[]{:S(2)}, u32[]{:S(2)}) collective-permute-start(f32[8,384]{1,0:T(8,128)S(1)} %get-tuple-element.46), channel_id=1, source_target_pairs={{0,1},{1,0},{2,3},{3,2},{4,5},{5,4},{6,7},{7,6},{8,9},{9,8},{10,11... | collective-permute-start | bytes 36872 | tf_op jit(solution)/shard_map/ppermute | solution.py:89
  13.9 13.3 %all-to-all-start = ((f32[32,8,128]{2,1,0:T(8,128)}), f32[32,8,128]{2,1,0:T(8,128)S(1)}, u32[]{:S(2)}, u32[]{:S(2)}) async-start(f32[32,8,128]{2,1,0:T(8,128)} %get-tuple-element.49), calls=%async_computation | async-start | bytes 262144 | tf_op jit(solution)/shard_map/all_to_all | solution.py:469
  31.3 14.5 %all-to-all-start.1 = ((f32[32,8,128]{2,1,0:T(8,128)}), f32[32,8,128]{2,1,0:T(8,128)S(1)}, u32[]{:S(2)}, u32[]{:S(2)}) async-start(f32[32,8,128]{2,1,0:T(8,128)} %get-tuple-element.59), calls=%async_computation.1 | async-start | bytes 262144 | tf_op jit(solution)/shard_map/all_to_all | solution.py:469
  35.7 8.5 %collective-permute-start.4 = (f32[16,384]{1,0:T(8,128)}, f32[16,384]{1,0:T(8,128)S(1)}, u32[]{:S(2)}, u32[]{:S(2)}) collective-permute-start(f32[16,384]{1,0:T(8,128)} %get-tuple-element.55), channel_id=1, source_target_pairs={{4,8},{8,4},{12,16},{16,12},{20,24},{24,20},{5,9},{9,5},{13,17},{1... | collective-permute-start | bytes 73736 | tf_op jit(solution)/shard_map/ppermute | solution.py:89
  36.4 7.9 %collective-permute-start.5 = (f32[16,384]{1,0:T(8,128)}, f32[16,384]{1,0:T(8,128)S(1)}, u32[]{:S(2)}, u32[]{:S(2)}) collective-permute-start(f32[16,384]{1,0:T(8,128)} %get-tuple-element.56), channel_id=1, source_target_pairs={{0,4},{4,0},{8,12},{12,8},{16,20},{20,16},{24,28},{28,24},{1,5},{5... | collective-permute-start | bytes 73736 | tf_op jit(solution)/shard_map/ppermute | solution.py:89
  40.2 5.6 %collective-permute-start.6 = (f32[16,384]{1,0:T(8,128)}, f32[16,384]{1,0:T(8,128)S(1)}, u32[]{:S(2)}, u32[]{:S(2)}) collective-permute-start(f32[16,384]{1,0:T(8,128)} %get-tuple-element.57), channel_id=1, source_target_pairs={{1,2},{2,1},{5,6},{6,5},{9,10},{10,9},{13,14},{14,13},{17,18},{18,... | collective-permute-start | bytes 73736 | tf_op jit(solution)/shard_map/ppermute | solution.py:89
  44.1 1.7 %collective-permute-start.7 = (f32[16,384]{1,0:T(8,128)}, f32[16,384]{1,0:T(8,128)S(1)}, u32[]{:S(2)}, u32[]{:S(2)}) collective-permute-start(f32[16,384]{1,0:T(8,128)} %get-tuple-element.58), channel_id=1, source_target_pairs={{0,1},{1,0},{2,3},{3,2},{4,5},{5,4},{6,7},{7,6},{8,9},{9,8},{10,11... | collective-permute-start | bytes 73736 | tf_op jit(solution)/shard_map/ppermute | solution.py:89
  49.2 15.1 %all-to-all-start.2 = ((f32[32,8,128]{2,1,0:T(8,128)}), f32[32,8,128]{2,1,0:T(8,128)S(1)}, u32[]{:S(2)}, u32[]{:S(2)}) async-start(f32[32,8,128]{2,1,0:T(8,128)} %get-tuple-element.68), calls=%async_computation.2 | async-start | bytes 262144 | tf_op jit(solution)/shard_map/all_to_all | solution.py:469
  54.2 8.5 %collective-permute-start.8 = (f32[16,384]{1,0:T(8,128)}, f32[16,384]{1,0:T(8,128)S(1)}, u32[]{:S(2)}, u32[]{:S(2)}) collective-permute-start(f32[16,384]{1,0:T(8,128)} %get-tuple-element.64), channel_id=1, source_target_pairs={{4,8},{8,4},{12,16},{16,12},{20,24},{24,20},{5,9},{9,5},{13,17},{1... | collective-permute-start | bytes 73736 | tf_op jit(solution)/shard_map/ppermute | solution.py:89
  54.8 7.9 %collective-permute-start.9 = (f32[16,384]{1,0:T(8,128)}, f32[16,384]{1,0:T(8,128)S(1)}, u32[]{:S(2)}, u32[]{:S(2)}) collective-permute-start(f32[16,384]{1,0:T(8,128)} %get-tuple-element.65), channel_id=1, source_target_pairs={{0,4},{4,0},{8,12},{12,8},{16,20},{20,16},{24,28},{28,24},{1,5},{5... | collective-permute-start | bytes 73736 | tf_op jit(solution)/shard_map/ppermute | solution.py:89
  58.7 5.6 %collective-permute-start.10 = (f32[16,384]{1,0:T(8,128)}, f32[16,384]{1,0:T(8,128)S(1)}, u32[]{:S(2)}, u32[]{:S(2)}) collective-permute-start(f32[16,384]{1,0:T(8,128)} %get-tuple-element.66), channel_id=1, source_target_pairs={{1,2},{2,1},{5,6},{6,5},{9,10},{10,9},{13,14},{14,13},{17,18},{18,... | collective-permute-start | bytes 73736 | tf_op jit(solution)/shard_map/ppermute | solution.py:89
  62.6 1.7 %collective-permute-start.11 = (f32[16,384]{1,0:T(8,128)}, f32[16,384]{1,0:T(8,128)S(1)}, u32[]{:S(2)}, u32[]{:S(2)}) collective-permute-start(f32[16,384]{1,0:T(8,128)} %get-tuple-element.67), channel_id=1, source_target_pairs={{0,1},{1,0},{2,3},{3,2},{4,5},{5,4},{6,7},{7,6},{8,9},{9,8},{10,11... | collective-permute-start | bytes 73736 | tf_op jit(solution)/shard_map/ppermute | solution.py:89
  67.5 15.1 %all-to-all-start.3 = ((f32[32,8,128]{2,1,0:T(8,128)}), f32[32,8,128]{2,1,0:T(8,128)S(1)}, u32[]{:S(2)}, u32[]{:S(2)}) async-start(f32[32,8,128]{2,1,0:T(8,128)} %get-tuple-element.79), calls=%async_computation.3 | async-start | bytes 262144 | tf_op jit(solution)/shard_map/all_to_all | solution.py:469
  72.5 8.5 %collective-permute-start.12 = (f32[16,384]{1,0:T(8,128)}, f32[16,384]{1,0:T(8,128)S(1)}, u32[]{:S(2)}, u32[]{:S(2)}) collective-permute-start(f32[16,384]{1,0:T(8,128)} %get-tuple-element.75), channel_id=1, source_target_pairs={{4,8},{8,4},{12,16},{16,12},{20,24},{24,20},{5,9},{9,5},{13,17},{1... | collective-permute-start | bytes 73736 | tf_op jit(solution)/shard_map/ppermute | solution.py:89
  73.1 7.9 %collective-permute-start.13 = (f32[16,384]{1,0:T(8,128)}, f32[16,384]{1,0:T(8,128)S(1)}, u32[]{:S(2)}, u32[]{:S(2)}) collective-permute-start(f32[16,384]{1,0:T(8,128)} %get-tuple-element.76), channel_id=1, source_target_pairs={{0,4},{4,0},{8,12},{12,8},{16,20},{20,16},{24,28},{28,24},{1,5},{5... | collective-permute-start | bytes 73736 | tf_op jit(solution)/shard_map/ppermute | solution.py:89
  77.0 5.6 %collective-permute-start.14 = (f32[16,384]{1,0:T(8,128)}, f32[16,384]{1,0:T(8,128)S(1)}, u32[]{:S(2)}, u32[]{:S(2)}) collective-permute-start(f32[16,384]{1,0:T(8,128)} %get-tuple-element.77), channel_id=1, source_target_pairs={{1,2},{2,1},{5,6},{6,5},{9,10},{10,9},{13,14},{14,13},{17,18},{18,... | collective-permute-start | bytes 73736 | tf_op jit(solution)/shard_map/ppermute | solution.py:89
  80.9 1.7 %collective-permute-start.15 = (f32[16,384]{1,0:T(8,128)}, f32[16,384]{1,0:T(8,128)S(1)}, u32[]{:S(2)}, u32[]{:S(2)}) collective-permute-start(f32[16,384]{1,0:T(8,128)} %get-tuple-element.78), channel_id=1, source_target_pairs={{0,1},{1,0},{2,3},{3,2},{4,5},{5,4},{6,7},{7,6},{8,9},{9,8},{10,11... | collective-permute-start | bytes 73736 | tf_op jit(solution)/shard_map/ppermute | solution.py:89

commit v11 on v9

--- a/solution.py
+++ b/solution.py
@@ -508,19 +508,19 @@
     residual, direction, faces, coarse, *sent_faces = call(
         z, first_direction, [field, field, field, sent] + to_faces,
         [solve_rows, lift_rows, faces, masks, rows, *got, coarse, arranged],
-        [tile, packed], product_flops, near=2,
+        [tile, packed], product_flops, near=6,
     )
     coarse, got = gather(coarse), exchange(sent_faces)
     multipliers, residual, projected, image, faces, sums, coarse, *sent_faces = call(
         z, second_direction, [field, field, field, field, field, tile, sent] + to_faces,
         [solve_rows, lift_rows, faces, masks, residual, direction, multipliers, *got, coarse, arranged],
-        [packed], product_flops, near=2,
+        [packed], product_flops, near=6,
     )
     coarse, got = gather(coarse), exchange(sent_faces)
     whole = ((1, 1, 4, z.cases, z.face), F32)
     multipliers, residual = call(
         z, finish, [whole, whole],
-        [sums, faces, masks, residual, image, multipliers, projected, direction, *got, coarse], near=1,
+        [sums, faces, masks, residual, image, multipliers, projected, direction, *got, coarse], near=5,
     )
     return multipliers, residual
 

time: 84.5 us -> 82.4 us (0.975)
  local copies, waits for them, and re-layouts: 1.78 us -> 0 us
    unnamed x24 -> x0, local copies, waits for them, and re-layouts: 1.78 us -> none
where the time goes in v11:
time: 82.4 us; the launch traced here: 81 us
  starting transfers between devices  47.6 us (58%)
  Pallas kernels  22.6 us (27%)
  waiting for transfers between devices  9.96 us (12%)
  between operations  0.88 us (1%)
    ppermute x16, starting transfers between devices, exchange(): got.append(lax.ppermute(sent[i], axis, pairs))  27.8 us
    pallas_call x8, Pallas kernels, call(): pl.pallas_call(run, out_shape=[pltpu.HBM(a.shape, a.dtype) for a in shape...  22.6 us
    all_to_all x4, starting transfers between devices, gather(): return lax.all_to_all(values, AXES, 0, 0, tiled=True)  19.8 us
    ppermute x16, waiting for transfers between devices, exchange(): got.append(lax.ppermute(sent[i], axis, pairs))  9.79 us
  transfers between devices with their start and end apart: 20, of which 9 were waited for; matrix products, arithmetic and copies ran while one was open for 0% of the time, Pallas kernels for 9%

profile of v11, /device:TPU:5, one launch (start us, length us, event | category | flops | bytes accessed | tf_op | source)
XLA Modules:
  0.0 81.0 jit_solution(7164861965724820204)
XLA Ops:
  0.6 0.8 %prepare.1 = (f32[4,8,384]{2,1,0:T(8,128)S(1)}, f32[8,384]{1,0:T(8,128)S(1)}, f32[8,384]{1,0:T(8,128)S(1)}, f32[8,384]{1,0:T(8,128)S(1)}, f32[8,384]{1,0:T(8,128)S(1)}, /*index=5*/f32[8,384]{1,0:T(8,128)S(1)}) custom-call(f32[1,1,6,4,300]{4,3,2,1,0:T(4,128)} %bitcast.2, s32[1,1,4]{2,1,0:T(1,128)} %refs_1_.2), custom_call_target="tpu_custom_call" | custom-call | bytes 139408 | tf_op jit(solution)/shard_map/prepare/pallas_call | solution.py:456
  1.5 3.1 %collective-permute-start = (f32[8,384]{1,0:T(8,128)S(1)}, f32[8,384]{1,0:T(8,128)S(1)}, u32[]{:S(2)}, u32[]{:S(2)}) collective-permute-start(f32[8,384]{1,0:T(8,128)S(1)} %get-tuple-element.43), channel_id=1, source_target_pairs={{4,8},{8,4},{12,16},{16,12},{20,24},{24,20},{5,9},{9,5},{13,17},{1... | collective-permute-start | bytes 36872 | tf_op jit(solution)/shard_map/ppermute | solution.py:89
  4.6 4.0 %collective-permute-start.1 = (f32[8,384]{1,0:T(8,128)S(1)}, f32[8,384]{1,0:T(8,128)S(1)}, u32[]{:S(2)}, u32[]{:S(2)}) collective-permute-start(f32[8,384]{1,0:T(8,128)S(1)} %get-tuple-element.44), channel_id=1, source_target_pairs={{1,2},{2,1},{5,6},{6,5},{9,10},{10,9},{13,14},{14,13},{17,18},{18,... | collective-permute-start | bytes 36872 | tf_op jit(solution)/shard_map/ppermute | solution.py:89
  8.6 0.1 collective-permute-start.2
  8.7 0.1 collective-permute-start.3
  8.7 1.0 %invert.1.refs_2_ = f32[8,128]{1,0:T(8,128)S(1)} custom-call(f32[1,6,1,16]{3,2,1,0:T(1,128)} %bitcast.3, f32[4,8,384]{2,1,0:T(8,128)S(1)} %get-tuple-element.41.refs_1_.refs_0_, f32[8,384]{1,0:T(8,128)S(1)} %get-tuple-element.42.refs_2_.refs_1_), custom_call_target="tpu_custom_call" | custom-call | flops 46080000 | bytes 65920 | tf_op jit(solution)/shard_map/invert/pallas_call | solution.py:456
  9.8 0.2 collective-permute-done.1.refs_4_
  10.0 1.2 %collective-permute-done.2.refs_5_ = f32[8,384]{1,0:T(8,128)S(1)} collective-permute-done((f32[8,384]{1,0:T(8,128)S(1)}, f32[8,384]{1,0:T(8,128)S(1)}, u32[]{:S(2)}, u32[]{:S(2)}) %collective-permute-start.2) | collective-permute-done | bytes 12320 | tf_op jit(solution)/shard_map/ppermute | solution.py:89
  11.2 1.5 %couple.1 = (f32[32,8,128]{2,1,0:T(8,128)}, f32[8,384]{1,0:T(8,128)}, f32[4,16,384]{2,1,0:T(8,128)}) custom-call(f32[4,8,384]{2,1,0:T(8,128)S(1)} %get-tuple-element.41.refs_1_.refs_0_, f32[8,384]{1,0:T(8,128)S(1)} %get-tuple-element.42.refs_2_.refs_1_, f32[8,128]{1,0:T(8,128)S(1)} %invert.1.refs_2_, f32[8,384]{1,0:T(8,128)S(1)} %collective-permute-done.refs_3_, ...), custom_call_target="tpu_custom_call" | custom-call | bytes 356352 | tf_op jit(solution)/shard_map/couple/pallas_call | solution.py:456
  12.8 4.8 %all-to-all-start = ((f32[32,8,128]{2,1,0:T(8,128)}), f32[32,8,128]{2,1,0:T(8,128)S(1)}, u32[]{:S(2)}, u32[]{:S(2)}) async-start(f32[32,8,128]{2,1,0:T(8,128)} %get-tuple-element.49), calls=%async_computation | async-start | bytes 262144 | tf_op jit(solution)/shard_map/all_to_all | solution.py:469
  17.6 6.7 %arrange.1 = (f32[16,1200]{1,0:T(8,128)}, bf16[1200,1200]{1,0:T(8,128)(2,1)S(1)}) custom-call(s32[1,1,4,300]{3,2,1,0:T(4,128)} %refs_0_.1, bf16[1,1,1200,1200]{3,2,1,0:T(8,128)(2,1)} %refs_1_.3, f32[1,1,16,1200]{3,2,1,0:T(8,128)} %refs_2_.1), custom_call_target="tpu_custom_call" | custom-call | flops 2949120000 | bytes 5918400 | tf_op jit(solution)/shard_map/arrange/pallas_call | solution.py:456
  24.2 0.2 all-to-all-done.refs_2_
  24.4 4.1 %begin.1 = (f32[40,256]{1,0:T(8,128)}, f32[4,16,384]{2,1,0:T(8,128)}, f32[4,16,384]{2,1,0:T(8,128)}, f32[4,16,384]{2,1,0:T(8,128)}, f32[32,8,128]{2,1,0:T(8,128)...) custom-call(f32[4,16,384]{2,1,0:T(8,128)} %get-tuple-element.47.refs_0_.refs_1_, ...), custom_call_target="tpu_custom_call" | custom-call | flops 46080000 | bytes 3751424 | tf_op jit(solution)/shard_map/begin/pallas_call | solution.py:456
  28.5 5.7 %all-to-all-start.1 = ((f32[32,8,128]{2,1,0:T(8,128)}), f32[32,8,128]{2,1,0:T(8,128)S(1)}, u32[]{:S(2)}, u32[]{:S(2)}) async-start(f32[32,8,128]{2,1,0:T(8,128)} %get-tuple-element.59), calls=%async_computation.1 | async-start | bytes 262144 | tf_op jit(solution)/shard_map/all_to_all | solution.py:469
  34.2 3.1 %collective-permute-start.4 = (f32[16,384]{1,0:T(8,128)}, f32[16,384]{1,0:T(8,128)S(1)}, u32[]{:S(2)}, u32[]{:S(2)}) collective-permute-start(f32[16,384]{1,0:T(8,128)} %get-tuple-element.55), channel_id=1, source_target_pairs={{4,8},{8,4},{12,16},{16,12},{20,24},{24,20},{5,9},{9,5},{13,17},{1... | collective-permute-start | bytes 73736 | tf_op jit(solution)/shard_map/ppermute | solution.py:89
  37.3 3.6 %collective-permute-start.5 = (f32[16,384]{1,0:T(8,128)}, f32[16,384]{1,0:T(8,128)S(1)}, u32[]{:S(2)}, u32[]{:S(2)}) collective-permute-start(f32[16,384]{1,0:T(8,128)} %get-tuple-element.56), channel_id=1, source_target_pairs={{1,2},{2,1},{5,6},{6,5},{9,10},{10,9},{13,14},{14,13},{17,18},{18,... | collective-permute-start | bytes 73736 | tf_op jit(solution)/shard_map/ppermute | solution.py:89
  41.0 0.1 collective-permute-start.6
  41.1 1.6 %collective-permute-done.5.refs_6_ = f32[16,384]{1,0:T(8,128)S(1)} collective-permute-done((f32[16,384]{1,0:T(8,128)}, f32[16,384]{1,0:T(8,128)S(1)}, u32[]{:S(2)}, u32[]{:S(2)}) %collective-permute-start.5) | collective-permute-done | bytes 24608 | tf_op jit(solution)/shard_map/ppermute | solution.py:89
  42.7 1.2 %collective-permute-done.6.refs_7_ = f32[16,384]{1,0:T(8,128)S(1)} collective-permute-done((f32[16,384]{1,0:T(8,128)}, f32[16,384]{1,0:T(8,128)S(1)}, u32[]{:S(2)}, u32[]{:S(2)}) %collective-permute-start.6) | collective-permute-done | bytes 24608 | tf_op jit(solution)/shard_map/ppermute | solution.py:89
  43.9 3.3 %first_direction.1 = (f32[4,16,384]{2,1,0:T(8,128)}, f32[4,16,384]{2,1,0:T(8,128)}, f32[4,16,384]{2,1,0:T(8,128)}, f32[32,8,128]{2,1,0:T(8,128)}, f32[16,384]{1,...) custom-call(f32[40,256]{1,0:T(8,128)} %get-tuple-element.51.refs_0_, ...), custom_call_target="tpu_custom_call" | custom-call | flops 46080000 | bytes 3981824 | tf_op jit(solution)/shard_map/first_direction/pallas_call | solution.py:456
  47.2 4.6 %all-to-all-start.2 = ((f32[32,8,128]{2,1,0:T(8,128)}), f32[32,8,128]{2,1,0:T(8,128)S(1)}, u32[]{:S(2)}, u32[]{:S(2)}) async-start(f32[32,8,128]{2,1,0:T(8,128)} %get-tuple-element.68), calls=%async_computation.2 | async-start | bytes 262144 | tf_op jit(solution)/shard_map/all_to_all | solution.py:469
  51.9 3.1 %collective-permute-start.8 = (f32[16,384]{1,0:T(8,128)}, f32[16,384]{1,0:T(8,128)S(1)}, u32[]{:S(2)}, u32[]{:S(2)}) collective-permute-start(f32[16,384]{1,0:T(8,128)} %get-tuple-element.64), channel_id=1, source_target_pairs={{4,8},{8,4},{12,16},{16,12},{20,24},{24,20},{5,9},{9,5},{13,17},{1... | collective-permute-start | bytes 73736 | tf_op jit(solution)/shard_map/ppermute | solution.py:89
  55.0 3.6 %collective-permute-start.9 = (f32[16,384]{1,0:T(8,128)}, f32[16,384]{1,0:T(8,128)S(1)}, u32[]{:S(2)}, u32[]{:S(2)}) collective-permute-start(f32[16,384]{1,0:T(8,128)} %get-tuple-element.65), channel_id=1, source_target_pairs={{1,2},{2,1},{5,6},{6,5},{9,10},{10,9},{13,14},{14,13},{17,18},{18,... | collective-permute-start | bytes 73736 | tf_op jit(solution)/shard_map/ppermute | solution.py:89
  58.8 1.6 %collective-permute-done.9.refs_8_ = f32[16,384]{1,0:T(8,128)S(1)} collective-permute-done((f32[16,384]{1,0:T(8,128)}, f32[16,384]{1,0:T(8,128)S(1)}, u32[]{:S(2)}, u32[]{:S(2)}) %collective-permute-start.9) | collective-permute-done | bytes 24608 | tf_op jit(solution)/shard_map/ppermute | solution.py:89
  60.3 1.2 %collective-permute-done.10.refs_9_ = f32[16,384]{1,0:T(8,128)S(1)} collective-permute-done((f32[16,384]{1,0:T(8,128)}, f32[16,384]{1,0:T(8,128)S(1)}, u32[]{:S(2)}, u32[]{:S(2)}) %collective-permute-start.10) | collective-permute-done | bytes 24608 | tf_op jit(solution)/shard_map/ppermute | solution.py:89
  61.6 3.2 %second_direction.1 = (f32[4,16,384]{2,1,0:T(8,128)}, f32[4,16,384]{2,1,0:T(8,128)}, f32[4,16,384]{2,1,0:T(8,128)}, f32[4,16,384]{2,1,0:T(8,128)}, f32[4,16,384]...) custom-call(f32[40,256]{1,0:T(8,128)} %get-tuple-element.51.refs_0_,, ...), custom_call_target="tpu_custom_call" | custom-call | flops 46080000 | bytes 4379136 | tf_op jit(solution)/shard_map/second_direction/pallas_call | solution.py:456
  64.7 4.6 %all-to-all-start.3 = ((f32[32,8,128]{2,1,0:T(8,128)}), f32[32,8,128]{2,1,0:T(8,128)S(1)}, u32[]{:S(2)}, u32[]{:S(2)}) async-start(f32[32,8,128]{2,1,0:T(8,128)} %get-tuple-element.79), calls=%async_computation.3 | async-start | bytes 262144 | tf_op jit(solution)/shard_map/all_to_all | solution.py:469
  69.4 3.1 %collective-permute-start.12 = (f32[16,384]{1,0:T(8,128)}, f32[16,384]{1,0:T(8,128)S(1)}, u32[]{:S(2)}, u32[]{:S(2)}) collective-permute-start(f32[16,384]{1,0:T(8,128)} %get-tuple-element.75), channel_id=1, source_target_pairs={{4,8},{8,4},{12,16},{16,12},{20,24},{24,20},{5,9},{9,5},{13,17},{1... | collective-permute-start | bytes 73736 | tf_op jit(solution)/shard_map/ppermute | solution.py:89
  72.5 3.6 %collective-permute-start.13 = (f32[16,384]{1,0:T(8,128)}, f32[16,384]{1,0:T(8,128)S(1)}, u32[]{:S(2)}, u32[]{:S(2)}) collective-permute-start(f32[16,384]{1,0:T(8,128)} %get-tuple-element.76), channel_id=1, source_target_pairs={{1,2},{2,1},{5,6},{6,5},{9,10},{10,9},{13,14},{14,13},{17,18},{18,... | collective-permute-start | bytes 73736 | tf_op jit(solution)/shard_map/ppermute | solution.py:89
  76.3 1.6 %collective-permute-done.13.refs_9_ = f32[16,384]{1,0:T(8,128)S(1)} collective-permute-done((f32[16,384]{1,0:T(8,128)}, f32[16,384]{1,0:T(8,128)S(1)}, u32[]{:S(2)}, u32[]{:S(2)}) %collective-permute-start.13) | collective-permute-done | bytes 24608 | tf_op jit(solution)/shard_map/ppermute | solution.py:89
  77.9 1.2 %collective-permute-done.14.refs_10_ = f32[16,384]{1,0:T(8,128)S(1)} collective-permute-done((f32[16,384]{1,0:T(8,128)}, f32[16,384]{1,0:T(8,128)S(1)}, u32[]{:S(2)}, u32[]{:S(2)}) %collective-permute-start.14) | collective-permute-done | bytes 24608 | tf_op jit(solution)/shard_map/ppermute | solution.py:89
  79.1 1.9 %finish.1 = (f32[1,1,4,16,300]{4,3,2,1,0:T(8,128)}, f32[1,1,4,16,300]{4,3,2,1,0:T(8,128)}) custom-call(f32[8,128]{1,0:T(8,128)} %get-tuple-element.69.refs_0_, f32[4,16,384]{2,1,0:T(8,128)} %get-tuple-element.70.refs_1_, f32[8,384]{1,0:T(8,128)} %get-tuple-element.53.refs_3_.refs_2_, f32[4,16,384]{2,1,0:T(8,128)} %get-tuple-element.71.refs_3_, ...), custom_call_target="tpu_custom_call" | custom-call | bytes 989184 | tf_op jit(solution)/shard_map/finish/pallas_call | solution.py:456
  (16 shorter events, 0.4 us)
Async XLA Ops:
  1.5 8.3 %collective-permute-start = (f32[8,384]{1,0:T(8,128)S(1)}, f32[8,384]{1,0:T(8,128)S(1)}, u32[]{:S(2)}, u32[]{:S(2)}) collective-permute-start(f32[8,384]{1,0:T(8,128)S(1)} %get-tuple-element.43), channel_id=1, source_target_pairs={{4,8},{8,4},{12,16},{16,12},{20,24},{24,20},{5,9},{9,5},{13,17},{1... | collective-permute-start | bytes 36872 | tf_op jit(solution)/shard_map/ppermute | solution.py:89
  4.6 5.3 %collective-permute-start.1 = (f32[8,384]{1,0:T(8,128)S(1)}, f32[8,384]{1,0:T(8,128)S(1)}, u32[]{:S(2)}, u32[]{:S(2)}) collective-permute-start(f32[8,384]{1,0:T(8,128)S(1)} %get-tuple-element.44), channel_id=1, source_target_pairs={{1,2},{2,1},{5,6},{6,5},{9,10},{10,9},{13,14},{14,13},{17,18},{18,... | collective-permute-start | bytes 36872 | tf_op jit(solution)/shard_map/ppermute | solution.py:89
  8.6 2.6 %collective-permute-start.2 = (f32[8,384]{1,0:T(8,128)S(1)}, f32[8,384]{1,0:T(8,128)S(1)}, u32[]{:S(2)}, u32[]{:S(2)}) collective-permute-start(f32[8,384]{1,0:T(8,128)S(1)} %get-tuple-element.45), channel_id=1, source_target_pairs={{0,4},{4,0},{8,12},{12,8},{16,20},{20,16},{24,28},{28,24},{1,5},{5... | collective-permute-start | bytes 36872 | tf_op jit(solution)/shard_map/ppermute | solution.py:89
  8.7 2.5 %collective-permute-start.3 = (f32[8,384]{1,0:T(8,128)S(1)}, f32[8,384]{1,0:T(8,128)S(1)}, u32[]{:S(2)}, u32[]{:S(2)}) collective-permute-start(f32[8,384]{1,0:T(8,128)S(1)} %get-tuple-element.46), channel_id=1, source_target_pairs={{0,1},{1,0},{2,3},{3,2},{4,5},{5,4},{6,7},{7,6},{8,9},{9,8},{10,11... | collective-permute-start | bytes 36872 | tf_op jit(solution)/shard_map/ppermute | solution.py:89
  12.8 11.7 %all-to-all-start = ((f32[32,8,128]{2,1,0:T(8,128)}), f32[32,8,128]{2,1,0:T(8,128)S(1)}, u32[]{:S(2)}, u32[]{:S(2)}) async-start(f32[32,8,128]{2,1,0:T(8,128)} %get-tuple-element.49), calls=%async_computation | async-start | bytes 262144 | tf_op jit(solution)/shard_map/all_to_all | solution.py:469
  28.5 15.4 %all-to-all-start.1 = ((f32[32,8,128]{2,1,0:T(8,128)}), f32[32,8,128]{2,1,0:T(8,128)S(1)}, u32[]{:S(2)}, u32[]{:S(2)}) async-start(f32[32,8,128]{2,1,0:T(8,128)} %get-tuple-element.59), calls=%async_computation.1 | async-start | bytes 262144 | tf_op jit(solution)/shard_map/all_to_all | solution.py:469
  34.2 6.9 %collective-permute-start.4 = (f32[16,384]{1,0:T(8,128)}, f32[16,384]{1,0:T(8,128)S(1)}, u32[]{:S(2)}, u32[]{:S(2)}) collective-permute-start(f32[16,384]{1,0:T(8,128)} %get-tuple-element.55), channel_id=1, source_target_pairs={{4,8},{8,4},{12,16},{16,12},{20,24},{24,20},{5,9},{9,5},{13,17},{1... | collective-permute-start | bytes 73736 | tf_op jit(solution)/shard_map/ppermute | solution.py:89
  37.3 5.4 %collective-permute-start.5 = (f32[16,384]{1,0:T(8,128)}, f32[16,384]{1,0:T(8,128)S(1)}, u32[]{:S(2)}, u32[]{:S(2)}) collective-permute-start(f32[16,384]{1,0:T(8,128)} %get-tuple-element.56), channel_id=1, source_target_pairs={{1,2},{2,1},{5,6},{6,5},{9,10},{10,9},{13,14},{14,13},{17,18},{18,... | collective-permute-start | bytes 73736 | tf_op jit(solution)/shard_map/ppermute | solution.py:89
  41.0 3.0 %collective-permute-start.6 = (f32[16,384]{1,0:T(8,128)}, f32[16,384]{1,0:T(8,128)S(1)}, u32[]{:S(2)}, u32[]{:S(2)}) collective-permute-start(f32[16,384]{1,0:T(8,128)} %get-tuple-element.57), channel_id=1, source_target_pairs={{0,4},{4,0},{8,12},{12,8},{16,20},{20,16},{24,28},{28,24},{1,5},{5... | collective-permute-start | bytes 73736 | tf_op jit(solution)/shard_map/ppermute | solution.py:89
  41.0 2.9 %collective-permute-start.7 = (f32[16,384]{1,0:T(8,128)}, f32[16,384]{1,0:T(8,128)S(1)}, u32[]{:S(2)}, u32[]{:S(2)}) collective-permute-start(f32[16,384]{1,0:T(8,128)} %get-tuple-element.58), channel_id=1, source_target_pairs={{0,1},{1,0},{2,3},{3,2},{4,5},{5,4},{6,7},{7,6},{8,9},{9,8},{10,11... | collective-permute-start | bytes 73736 | tf_op jit(solution)/shard_map/ppermute | solution.py:89
  47.2 14.3 %all-to-all-start.2 = ((f32[32,8,128]{2,1,0:T(8,128)}), f32[32,8,128]{2,1,0:T(8,128)S(1)}, u32[]{:S(2)}, u32[]{:S(2)}) async-start(f32[32,8,128]{2,1,0:T(8,128)} %get-tuple-element.68), calls=%async_computation.2 | async-start | bytes 262144 | tf_op jit(solution)/shard_map/all_to_all | solution.py:469
  51.9 6.9 %collective-permute-start.8 = (f32[16,384]{1,0:T(8,128)}, f32[16,384]{1,0:T(8,128)S(1)}, u32[]{:S(2)}, u32[]{:S(2)}) collective-permute-start(f32[16,384]{1,0:T(8,128)} %get-tuple-element.64), channel_id=1, source_target_pairs={{4,8},{8,4},{12,16},{16,12},{20,24},{24,20},{5,9},{9,5},{13,17},{1... | collective-permute-start | bytes 73736 | tf_op jit(solution)/shard_map/ppermute | solution.py:89
  55.0 5.4 %collective-permute-start.9 = (f32[16,384]{1,0:T(8,128)}, f32[16,384]{1,0:T(8,128)S(1)}, u32[]{:S(2)}, u32[]{:S(2)}) collective-permute-start(f32[16,384]{1,0:T(8,128)} %get-tuple-element.65), channel_id=1, source_target_pairs={{1,2},{2,1},{5,6},{6,5},{9,10},{10,9},{13,14},{14,13},{17,18},{18,... | collective-permute-start | bytes 73736 | tf_op jit(solution)/shard_map/ppermute | solution.py:89
  58.6 3.0 %collective-permute-start.10 = (f32[16,384]{1,0:T(8,128)}, f32[16,384]{1,0:T(8,128)S(1)}, u32[]{:S(2)}, u32[]{:S(2)}) collective-permute-start(f32[16,384]{1,0:T(8,128)} %get-tuple-element.66), channel_id=1, source_target_pairs={{0,4},{4,0},{8,12},{12,8},{16,20},{20,16},{24,28},{28,24},{1,5},{5... | collective-permute-start | bytes 73736 | tf_op jit(solution)/shard_map/ppermute | solution.py:89
  58.7 2.9 %collective-permute-start.11 = (f32[16,384]{1,0:T(8,128)}, f32[16,384]{1,0:T(8,128)S(1)}, u32[]{:S(2)}, u32[]{:S(2)}) collective-permute-start(f32[16,384]{1,0:T(8,128)} %get-tuple-element.67), channel_id=1, source_target_pairs={{0,1},{1,0},{2,3},{3,2},{4,5},{5,4},{6,7},{7,6},{8,9},{9,8},{10,11... | collective-permute-start | bytes 73736 | tf_op jit(solution)/shard_map/ppermute | solution.py:89
  64.7 14.3 %all-to-all-start.3 = ((f32[32,8,128]{2,1,0:T(8,128)}), f32[32,8,128]{2,1,0:T(8,128)S(1)}, u32[]{:S(2)}, u32[]{:S(2)}) async-start(f32[32,8,128]{2,1,0:T(8,128)} %get-tuple-element.79), calls=%async_computation.3 | async-start | bytes 262144 | tf_op jit(solution)/shard_map/all_to_all | solution.py:469
  69.4 6.9 %collective-permute-start.12 = (f32[16,384]{1,0:T(8,128)}, f32[16,384]{1,0:T(8,128)S(1)}, u32[]{:S(2)}, u32[]{:S(2)}) collective-permute-start(f32[16,384]{1,0:T(8,128)} %get-tuple-element.75), channel_id=1, source_target_pairs={{4,8},{8,4},{12,16},{16,12},{20,24},{24,20},{5,9},{9,5},{13,17},{1... | collective-permute-start | bytes 73736 | tf_op jit(solution)/shard_map/ppermute | solution.py:89
  72.5 5.4 %collective-permute-start.13 = (f32[16,384]{1,0:T(8,128)}, f32[16,384]{1,0:T(8,128)S(1)}, u32[]{:S(2)}, u32[]{:S(2)}) collective-permute-start(f32[16,384]{1,0:T(8,128)} %get-tuple-element.76), channel_id=1, source_target_pairs={{1,2},{2,1},{5,6},{6,5},{9,10},{10,9},{13,14},{14,13},{17,18},{18,... | collective-permute-start | bytes 73736 | tf_op jit(solution)/shard_map/ppermute | solution.py:89
  76.1 3.0 %collective-permute-start.14 = (f32[16,384]{1,0:T(8,128)}, f32[16,384]{1,0:T(8,128)S(1)}, u32[]{:S(2)}, u32[]{:S(2)}) collective-permute-start(f32[16,384]{1,0:T(8,128)} %get-tuple-element.77), channel_id=1, source_target_pairs={{0,4},{4,0},{8,12},{12,8},{16,20},{20,16},{24,28},{28,24},{1,5},{5... | collective-permute-start | bytes 73736 | tf_op jit(solution)/shard_map/ppermute | solution.py:89
  76.2 2.9 %collective-permute-start.15 = (f32[16,384]{1,0:T(8,128)}, f32[16,384]{1,0:T(8,128)S(1)}, u32[]{:S(2)}, u32[]{:S(2)}) collective-permute-start(f32[16,384]{1,0:T(8,128)} %get-tuple-element.78), channel_id=1, source_target_pairs={{0,1},{1,0},{2,3},{3,2},{4,5},{5,4},{6,7},{7,6},{8,9},{9,8},{10,11... | collective-permute-start | bytes 73736 | tf_op jit(solution)/shard_map/ppermute | solution.py:89

commit v12 on v11

--- a/solution.py
+++ b/solution.py
@@ -264,8 +264,8 @@
 
 
 def begin(
-    z, lift_rows, primal, received, arranged,
-    solve_rows, rows, multipliers, faces, sent, to0, to1, to2, to3,
+    z, primal, lift_rows, received, arranged,
+    rows, multipliers, sent, to0, to1, to2, to3, solve_rows, faces,
     matrix, tile, packed,
 ):
     ix, iy = place()
@@ -297,18 +297,17 @@
     start = window_start(z, ix) * z.ny
     inverses = [received[pl.ds(start + spot, 1)][0][:, INVERSE_LANE : INVERSE_LANE + 8] for spot in near_spots]
     fields = []
-    for f in range(4):
-        both = lift_rows[f]
-        own, near = both[0:8] * SIGNS[f], both[8:16] * -SIGNS[f]
-        rows[f] = jnp.concatenate([dot(inverses[0], own), dot(inverses[1 + f], near)], axis=0)
+    own = dot(inverses[0], jnp.concatenate([lift_rows[f][0:8] * SIGNS[f] for f in range(4)], axis=1))
+    for f in range(4):
+        near = dot(inverses[1 + f], lift_rows[f][8:16] * -SIGNS[f])
+        rows[f] = jnp.concatenate([own[:, f * z.lanes : (f + 1) * z.lanes], near], axis=0)
         fields.append(lifted(z, amplitudes, lift_rows, f))
         multipliers[f] = fields[f]
-    for item in (solve_rows, rows, multipliers):
+    for item in (rows, multipliers):
         item.push()
     image = unpacked(z, primal[...] - apply(z, fields, arranged, packed), packed)
     for f in range(4):
         faces[f] = image[f]
-    faces.push()
     send_faces(z, image, (to0, to1, to2, to3))
     send_coarse(z, image, rows, [], sent, tile)
 
@@ -319,8 +318,8 @@
 
 
 def first_direction(
-    z, solve_rows, lift_rows, faces, masks, rows, got1, got3, got0, got2, received, arranged,
-    residual, direction, image, sent, to0, to1, to2, to3,
+    z, rows, solve_rows, lift_rows, faces, masks, got1, got3, got0, got2, received, arranged,
+    residual, direction, sent, to0, to1, to2, to3, image,
     tile, packed,
 ):
     amplitudes = coarse_amplitudes(z, received, solve_rows)
@@ -335,7 +334,6 @@
     found = unpacked(z, apply(z, moved, arranged, packed), packed)
     for f in range(4):
         image[f] = found[f]
-    image.push()
     gamma = sum(weights[f] * total(field[f] * moved[f]) for f in range(4))
     curvature = sum(SIGNS[f] * total(moved[f] * found[f]) for f in range(4))
     send_faces(z, found, (to0, to1, to2, to3))
@@ -343,9 +341,9 @@
 
 
 def second_direction(
-    z, solve_rows, lift_rows, faces, masks, residual, direction, multipliers,
+    z, residual, direction, multipliers, solve_rows, lift_rows, faces, masks,
     got1, got3, got0, got2, received, arranged,
-    next_multipliers, next_residual, projected, image, fresh, sums, sent, to0, to1, to2, to3,
+    next_multipliers, next_residual, projected, image, sums, sent, to0, to1, to2, to3, fresh,
     packed,
 ):
     amplitudes = coarse_amplitudes(z, received, solve_rows)
@@ -367,7 +365,6 @@
     found = unpacked(z, apply(z, moved, arranged, packed), packed)
     for f in range(4):
         fresh[f] = found[f]
-    fresh.push()
     send_faces(z, found, (to0, to1, to2, to3))
     gamma = sum(weights[f] * total(left[f] * moved[f]) for f in range(4))
     straight = sum(SIGNS[f] * total(moved[f] * found[f]) for f in range(4))
@@ -378,7 +375,7 @@
 
 
 def finish(
-    z, sums, faces, masks, residual, image, multipliers, projected, direction,
+    z, sums, residual, image, multipliers, projected, direction, faces, masks,
     got1, got3, got0, got2, received,
     out_multipliers, out_residual,
 ):
@@ -491,7 +488,7 @@
         [tile, ((8, z.cases), F32)], product_flops, near=2, kept=1,
     )
     blocks, masks, lift_rows = call(
-        z, couple, [sent, live_rows, pair_rows], [padded, masks, local_tile, *got], [tile], near=7,
+        z, couple, [sent, live_rows, pair_rows], [padded, masks, local_tile, *got], [tile], near=7, kept=2,
     )
     blocks = gather(blocks)
     packed = ((z.cases, z.padded), F32)
@@ -499,28 +496,28 @@
         z, arrange, [((z.cases, z.order), F32), ((z.order, z.order), BF16)], [maps, ops, primal],
         [((8, z.padded), jnp.int32), ((z.order, z.order), BF16)], 4 * z.order**2 * z.width, kept=1,
     )
-    solve_rows, rows, multipliers, faces, coarse, *sent_faces = call(
-        z, begin, [((40, z.rows), F32), pair_rows, field, field, sent] + to_faces,
-        [lift_rows, primal_packed, blocks, arranged],
-        [((z.rows, columns), F32), tile, packed], product_flops, near=2,
+    rows, multipliers, coarse, *sent_faces, solve_rows, faces = call(
+        z, begin, [pair_rows, field, sent] + to_faces + [((40, z.rows), F32), field],
+        [primal_packed, lift_rows, blocks, arranged],
+        [((z.rows, columns), F32), tile, packed], product_flops, near=3, kept=2,
     )
     coarse, got = gather(coarse), exchange(sent_faces)
-    residual, direction, faces, coarse, *sent_faces = call(
-        z, first_direction, [field, field, field, sent] + to_faces,
-        [solve_rows, lift_rows, faces, masks, rows, *got, coarse, arranged],
-        [tile, packed], product_flops, near=6,
+    residual, direction, coarse, *sent_faces, faces = call(
+        z, first_direction, [field, field, sent] + to_faces + [field],
+        [rows, solve_rows, lift_rows, faces, masks, *got, coarse, arranged],
+        [tile, packed], product_flops, near=10, kept=1,
     )
     coarse, got = gather(coarse), exchange(sent_faces)
-    multipliers, residual, projected, image, faces, sums, coarse, *sent_faces = call(
-        z, second_direction, [field, field, field, field, field, tile, sent] + to_faces,
-        [solve_rows, lift_rows, faces, masks, residual, direction, multipliers, *got, coarse, arranged],
-        [packed], product_flops, near=6,
+    multipliers, residual, projected, image, sums, coarse, *sent_faces, faces = call(
+        z, second_direction, [field, field, field, field, tile, sent] + to_faces + [field],
+        [residual, direction, multipliers, solve_rows, lift_rows, faces, masks, *got, coarse, arranged],
+        [packed], product_flops, near=10, kept=1,
     )
     coarse, got = gather(coarse), exchange(sent_faces)
     whole = ((1, 1, 4, z.cases, z.face), F32)
     multipliers, residual = call(
         z, finish, [whole, whole],
-        [sums, faces, masks, residual, image, multipliers, projected, direction, *got, coarse], near=5,
+        [sums, residual, image, multipliers, projected, direction, faces, masks, *got, coarse], near=7,
     )
     return multipliers, residual
 

time: 82.4 us -> 91.2 us (1.11)
  the two profiles are of different devices: /device:TPU:5 before, /device:TPU:0 now
where the time goes in v12:
time: 91.2 us; the launch traced here: 90 us
  starting transfers between devices  53.2 us (58%)
  Pallas kernels  22.6 us (25%)
  local copies, waits for them, and re-layouts  10.7 us (12%)
  waiting for transfers between devices  2.64 us (3%)
    ppermute x16, starting transfers between devices, exchange(): got.append(lax.ppermute(sent[i], axis, pairs))  34.9 us
    pallas_call x8, Pallas kernels, call(): pl.pallas_call(run, out_shape=[pltpu.HBM(a.shape, a.dtype) for a in shape...  22.6 us
    all_to_all x4, starting transfers between devices, gather(): return lax.all_to_all(values, AXES, 0, 0, tiled=True)  18.3 us
    unnamed x32, local copies, waits for them, and re-layouts  10.7 us
  transfers between devices with their start and end apart: 20, of which 2 were waited for; matrix products, arithmetic and copies ran while one was open for 0% of the time, Pallas kernels for 9%

profile of v12, /device:TPU:0, one launch (start us, length us, event | category | flops | bytes accessed | tf_op | source)
XLA Modules:
  0.0 90.0 jit_solution(1488067764141754820)
XLA Ops:
  0.6 0.8 prepare.1
  2.8 5.8 %collective-permute-start.2 = (f32[8,384]{1,0:T(8,128)S(1)}, f32[8,384]{1,0:T(8,128)S(1)}, u32[]{:S(2)}, u32[]{:S(2)}) collective-permute-start(f32[8,384]{1,0:T(8,128)S(1)} %get-tuple-element.46), channel_id=1, source_target_pairs={{0,4},{4,0},{8,12},{12,8},{16,20},{20,16},{24,28},{28,24},{1,5},{5... | collective-permute-start | bytes 36872 | tf_op jit(solution)/shard_map/ppermute | solution.py:89
  8.6 2.6 %collective-permute-start.3 = (f32[8,384]{1,0:T(8,128)S(1)}, f32[8,384]{1,0:T(8,128)S(1)}, u32[]{:S(2)}, u32[]{:S(2)}) collective-permute-start(f32[8,384]{1,0:T(8,128)S(1)} %get-tuple-element.47), channel_id=1, source_target_pairs={{0,1},{1,0},{2,3},{3,2},{4,5},{5,4},{6,7},{7,6},{8,9},{9,8},{10,11... | collective-permute-start | bytes 36872 | tf_op jit(solution)/shard_map/ppermute | solution.py:89
  11.2 1.0 %invert.1.refs_2_ = f32[8,128]{1,0:T(8,128)S(1)} custom-call(f32[1,6,1,16]{3,2,1,0:T(1,128)} %bitcast.3, f32[4,8,384]{2,1,0:T(8,128)S(1)} %get-tuple-element.42.refs_1_.refs_0_, f32[8,384]{1,0:T(8,128)S(1)} %get-tuple-element.43.refs_2_.refs_1_), custom_call_target="tpu_custom_call" | custom-call | flops 46080000 | bytes 65920 | tf_op jit(solution)/shard_map/invert/pallas_call | solution.py:453
  12.2 1.5 %couple.1 = (f32[32,8,128]{2,1,0:T(8,128)}, f32[8,384]{1,0:T(8,128)S(1)}, f32[4,16,384]{2,1,0:T(8,128)S(1)}) custom-call(f32[4,8,384]{2,1,0:T(8,128)S(1)} %get-tuple-element.42.refs_1_.refs_0_, f32[8,384]{1,0:T(8,128)S(1)} %get-tuple-element.43.refs_2_.refs_1_, f32[8,128]{1,0:T(8,128)S(1)} %invert.1.refs_2_, f32[8,384]{1,0:T(8,128)S(1)} %collective-permute-done.refs_3_, ...), custom_call_target="tpu_custom_call" | custom-call | bytes 356352 | tf_op jit(solution)/shard_map/couple/pallas_call | solution.py:453
  13.7 4.6 %all-to-all-start = ((f32[32,8,128]{2,1,0:T(8,128)}), f32[32,8,128]{2,1,0:T(8,128)S(1)}, u32[]{:S(2)}, u32[]{:S(2)}) async-start(f32[32,8,128]{2,1,0:T(8,128)} %get-tuple-element.49), calls=%async_computation | async-start | bytes 262144 | tf_op jit(solution)/shard_map/all_to_all | solution.py:466
  18.4 6.7 %arrange.1 = (f32[16,1200]{1,0:T(8,128)}, bf16[1200,1200]{1,0:T(8,128)(2,1)S(1)}) custom-call(s32[1,1,4,300]{3,2,1,0:T(4,128)} %refs_0_.1, bf16[1,1,1200,1200]{3,2,1,0:T(8,128)(2,1)} %refs_1_.2, f32[1,1,16,1200]{3,2,1,0:T(8,128)} %refs_2_.1), custom_call_target="tpu_custom_call" | custom-call | flops 2949120000 | bytes 5918400 | tf_op jit(solution)/shard_map/arrange/pallas_call | solution.py:453
  25.1 1.5 %all-to-all-done.refs_2_ = f32[32,8,128]{2,1,0:T(8,128)S(1)} async-done(((f32[32,8,128]{2,1,0:T(8,128)}), f32[32,8,128]{2,1,0:T(8,128)S(1)}, u32[]{:S(2)}, u32[]{:S(2)}) %all-to-all-start) | async-done | bytes 131104 | tf_op jit(solution)/shard_map/all_to_all | solution.py:466
  26.6 4.0 %begin.1 = (f32[4,16,384]{2,1,0:T(8,128)}, f32[4,16,384]{2,1,0:T(8,128)}, f32[32,8,128]{2,1,0:T(8,128)}, f32[16,384]{1,0:T(8,128)}, f32[16,384]{1,0:T(8,128)}, /...) custom-call(f32[16,1200]{1,0:T(8,128)} %get-tuple-element.41.refs_0_, ...), custom_call_target="tpu_custom_call" | custom-call | flops 46080000 | bytes 3751424 | tf_op jit(solution)/shard_map/begin/pallas_call | solution.py:453
  30.7 4.3 %all-to-all-start.1 = ((f32[32,8,128]{2,1,0:T(8,128)}), f32[32,8,128]{2,1,0:T(8,128)S(1)}, u32[]{:S(2)}, u32[]{:S(2)}) async-start(f32[32,8,128]{2,1,0:T(8,128)} %get-tuple-element.59), calls=%async_computation.1 | async-start | bytes 262144 | tf_op jit(solution)/shard_map/all_to_all | solution.py:466
  36.3 4.5 %collective-permute-start.6 = (f32[16,384]{1,0:T(8,128)}, f32[16,384]{1,0:T(8,128)S(1)}, u32[]{:S(2)}, u32[]{:S(2)}) collective-permute-start(f32[16,384]{1,0:T(8,128)} %get-tuple-element.57), channel_id=1, source_target_pairs={{0,4},{4,0},{8,12},{12,8},{16,20},{20,16},{24,28},{28,24},{1,5},{5... | collective-permute-start | bytes 73736 | tf_op jit(solution)/shard_map/ppermute | solution.py:89
  40.9 2.5 %collective-permute-start.7 = (f32[16,384]{1,0:T(8,128)}, f32[16,384]{1,0:T(8,128)S(1)}, u32[]{:S(2)}, u32[]{:S(2)}) collective-permute-start(f32[16,384]{1,0:T(8,128)} %get-tuple-element.58), channel_id=1, source_target_pairs={{0,1},{1,0},{2,3},{3,2},{4,5},{5,4},{6,7},{7,6},{8,9},{9,8},{10,11... | collective-permute-start | bytes 73736 | tf_op jit(solution)/shard_map/ppermute | solution.py:89
  45.8 0.7 copy-done.7
  46.6 0.7 copy-done.11
  47.3 0.7 copy-done.13
  48.0 0.7 copy-done.15
  48.8 3.5 %first_direction.1 = (f32[4,16,384]{2,1,0:T(8,128)}, f32[4,16,384]{2,1,0:T(8,128)}, f32[32,8,128]{2,1,0:T(8,128)}, f32[16,384]{1,0:T(8,128)}, f32[16,384]{1,0:T(...) custom-call(f32[4,16,384]{2,1,0:T(8,128)} %get-tuple-element.51.refs_0_, ...), custom_call_target="tpu_custom_call" | custom-call | flops 46080000 | bytes 3981824 | tf_op jit(solution)/shard_map/first_direction/pallas_call | solution.py:453
  52.3 4.7 %all-to-all-start.2 = ((f32[32,8,128]{2,1,0:T(8,128)}), f32[32,8,128]{2,1,0:T(8,128)S(1)}, u32[]{:S(2)}, u32[]{:S(2)}) async-start(f32[32,8,128]{2,1,0:T(8,128)} %get-tuple-element.68), calls=%async_computation.2 | async-start | bytes 262144 | tf_op jit(solution)/shard_map/all_to_all | solution.py:466
  57.0 0.7 collective-permute-start.8
  58.3 4.5 %collective-permute-start.10 = (f32[16,384]{1,0:T(8,128)}, f32[16,384]{1,0:T(8,128)S(1)}, u32[]{:S(2)}, u32[]{:S(2)}) collective-permute-start(f32[16,384]{1,0:T(8,128)} %get-tuple-element.66), channel_id=1, source_target_pairs={{0,4},{4,0},{8,12},{12,8},{16,20},{20,16},{24,28},{28,24},{1,5},{5... | collective-permute-start | bytes 73736 | tf_op jit(solution)/shard_map/ppermute | solution.py:89
  62.8 2.5 %collective-permute-start.11 = (f32[16,384]{1,0:T(8,128)}, f32[16,384]{1,0:T(8,128)S(1)}, u32[]{:S(2)}, u32[]{:S(2)}) collective-permute-start(f32[16,384]{1,0:T(8,128)} %get-tuple-element.67), channel_id=1, source_target_pairs={{0,1},{1,0},{2,3},{3,2},{4,5},{5,4},{6,7},{7,6},{8,9},{9,8},{10,11... | collective-permute-start | bytes 73736 | tf_op jit(solution)/shard_map/ppermute | solution.py:89
  67.8 0.7 copy-done.1
  68.6 0.7 copy-done.3
  69.3 0.7 copy-done.5
  70.1 0.7 copy-done.9
  70.8 3.2 %second_direction.1 = (f32[4,16,384]{2,1,0:T(8,128)}, f32[4,16,384]{2,1,0:T(8,128)}, f32[4,16,384]{2,1,0:T(8,128)}, f32[4,16,384]{2,1,0:T(8,128)}, f32[8,128]{1,...) custom-call(f32[4,16,384]{2,1,0:T(8,128)} %get-tuple-element.60.refs, ...), custom_call_target="tpu_custom_call" | custom-call | flops 46080000 | bytes 4379136 | tf_op jit(solution)/shard_map/second_direction/pallas_call | solution.py:453
  74.0 4.7 %all-to-all-start.3 = ((f32[32,8,128]{2,1,0:T(8,128)}), f32[32,8,128]{2,1,0:T(8,128)S(1)}, u32[]{:S(2)}, u32[]{:S(2)}) async-start(f32[32,8,128]{2,1,0:T(8,128)} %get-tuple-element.79), calls=%async_computation.3 | async-start | bytes 262144 | tf_op jit(solution)/shard_map/all_to_all | solution.py:466
  79.3 0.7 collective-permute-start.13
  80.0 4.5 %collective-permute-start.14 = (f32[16,384]{1,0:T(8,128)}, f32[16,384]{1,0:T(8,128)S(1)}, u32[]{:S(2)}, u32[]{:S(2)}) collective-permute-start(f32[16,384]{1,0:T(8,128)} %get-tuple-element.77), channel_id=1, source_target_pairs={{0,4},{4,0},{8,12},{12,8},{16,20},{20,16},{24,28},{28,24},{1,5},{5... | collective-permute-start | bytes 73736 | tf_op jit(solution)/shard_map/ppermute | solution.py:89
  84.6 2.5 %collective-permute-start.15 = (f32[16,384]{1,0:T(8,128)}, f32[16,384]{1,0:T(8,128)S(1)}, u32[]{:S(2)}, u32[]{:S(2)}) collective-permute-start(f32[16,384]{1,0:T(8,128)} %get-tuple-element.78), channel_id=1, source_target_pairs={{0,1},{1,0},{2,3},{3,2},{4,5},{5,4},{6,7},{7,6},{8,9},{9,8},{10,11... | collective-permute-start | bytes 73736 | tf_op jit(solution)/shard_map/ppermute | solution.py:89
  87.1 1.0 %collective-permute-done.15.refs_11_ = f32[16,384]{1,0:T(8,128)S(1)} collective-permute-done((f32[16,384]{1,0:T(8,128)}, f32[16,384]{1,0:T(8,128)S(1)}, u32[]{:S(2)}, u32[]{:S(2)}) %collective-permute-start.15) | collective-permute-done | bytes 24608 | tf_op jit(solution)/shard_map/ppermute | solution.py:89
  88.2 1.9 %finish.1 = (f32[1,1,4,16,300]{4,3,2,1,0:T(8,128)}, f32[1,1,4,16,300]{4,3,2,1,0:T(8,128)}) custom-call(f32[8,128]{1,0:T(8,128)} %get-tuple-element.69.refs_0_, f32[4,16,384]{2,1,0:T(8,128)} %get-tuple-element.70.refs_1_, f32[4,16,384]{2,1,0:T(8,128)} %get-tuple-element.71.refs_2_, f32[4,16,384]{2,1,0:T(8,128)} %get-tuple-element.72.refs_3_, ...), custom_call_target="tpu_custom_call" | custom-call | bytes 989184 | tf_op jit(solution)/shard_map/finish/pallas_call | solution.py:453
  (48 shorter events, 8.9 us)
Async XLA Ops:
  1.5 10.7 %collective-permute-start = (f32[8,384]{1,0:T(8,128)S(1)}, f32[8,384]{1,0:T(8,128)S(1)}, u32[]{:S(2)}, u32[]{:S(2)}) collective-permute-start(f32[8,384]{1,0:T(8,128)S(1)} %get-tuple-element.44), channel_id=1, source_target_pairs={{4,8},{8,4},{12,16},{16,12},{20,24},{24,20},{5,9},{9,5},{13,17},{1... | collective-permute-start | bytes 36872 | tf_op jit(solution)/shard_map/ppermute | solution.py:89
  2.1 10.1 %collective-permute-start.1 = (f32[8,384]{1,0:T(8,128)S(1)}, f32[8,384]{1,0:T(8,128)S(1)}, u32[]{:S(2)}, u32[]{:S(2)}) collective-permute-start(f32[8,384]{1,0:T(8,128)S(1)} %get-tuple-element.45), channel_id=1, source_target_pairs={{1,2},{2,1},{5,6},{6,5},{9,10},{10,9},{13,14},{14,13},{17,18},{18,... | collective-permute-start | bytes 36872 | tf_op jit(solution)/shard_map/ppermute | solution.py:89
  2.8 9.4 %collective-permute-start.2 = (f32[8,384]{1,0:T(8,128)S(1)}, f32[8,384]{1,0:T(8,128)S(1)}, u32[]{:S(2)}, u32[]{:S(2)}) collective-permute-start(f32[8,384]{1,0:T(8,128)S(1)} %get-tuple-element.46), channel_id=1, source_target_pairs={{0,4},{4,0},{8,12},{12,8},{16,20},{20,16},{24,28},{28,24},{1,5},{5... | collective-permute-start | bytes 36872 | tf_op jit(solution)/shard_map/ppermute | solution.py:89
  8.6 3.6 %collective-permute-start.3 = (f32[8,384]{1,0:T(8,128)S(1)}, f32[8,384]{1,0:T(8,128)S(1)}, u32[]{:S(2)}, u32[]{:S(2)}) collective-permute-start(f32[8,384]{1,0:T(8,128)S(1)} %get-tuple-element.47), channel_id=1, source_target_pairs={{0,1},{1,0},{2,3},{3,2},{4,5},{5,4},{6,7},{7,6},{8,9},{9,8},{10,11... | collective-permute-start | bytes 36872 | tf_op jit(solution)/shard_map/ppermute | solution.py:89
  13.7 12.9 %all-to-all-start = ((f32[32,8,128]{2,1,0:T(8,128)}), f32[32,8,128]{2,1,0:T(8,128)S(1)}, u32[]{:S(2)}, u32[]{:S(2)}) async-start(f32[32,8,128]{2,1,0:T(8,128)} %get-tuple-element.49), calls=%async_computation | async-start | bytes 262144 | tf_op jit(solution)/shard_map/all_to_all | solution.py:466
  30.7 15.2 %all-to-all-start.1 = ((f32[32,8,128]{2,1,0:T(8,128)}), f32[32,8,128]{2,1,0:T(8,128)S(1)}, u32[]{:S(2)}, u32[]{:S(2)}) async-start(f32[32,8,128]{2,1,0:T(8,128)} %get-tuple-element.59), calls=%async_computation.1 | async-start | bytes 262144 | tf_op jit(solution)/shard_map/all_to_all | solution.py:466
  35.0 8.4 %collective-permute-start.4 = (f32[16,384]{1,0:T(8,128)}, f32[16,384]{1,0:T(8,128)S(1)}, u32[]{:S(2)}, u32[]{:S(2)}) collective-permute-start(f32[16,384]{1,0:T(8,128)} %get-tuple-element.55), channel_id=1, source_target_pairs={{4,8},{8,4},{12,16},{16,12},{20,24},{24,20},{5,9},{9,5},{13,17},{1... | collective-permute-start | bytes 73736 | tf_op jit(solution)/shard_map/ppermute | solution.py:89
  35.6 8.4 %collective-permute-start.5 = (f32[16,384]{1,0:T(8,128)}, f32[16,384]{1,0:T(8,128)S(1)}, u32[]{:S(2)}, u32[]{:S(2)}) collective-permute-start(f32[16,384]{1,0:T(8,128)} %get-tuple-element.56), channel_id=1, source_target_pairs={{1,2},{2,1},{5,6},{6,5},{9,10},{10,9},{13,14},{14,13},{17,18},{18,... | collective-permute-start | bytes 73736 | tf_op jit(solution)/shard_map/ppermute | solution.py:89
  36.3 8.3 %collective-permute-start.6 = (f32[16,384]{1,0:T(8,128)}, f32[16,384]{1,0:T(8,128)S(1)}, u32[]{:S(2)}, u32[]{:S(2)}) collective-permute-start(f32[16,384]{1,0:T(8,128)} %get-tuple-element.57), channel_id=1, source_target_pairs={{0,4},{4,0},{8,12},{12,8},{16,20},{20,16},{24,28},{28,24},{1,5},{5... | collective-permute-start | bytes 73736 | tf_op jit(solution)/shard_map/ppermute | solution.py:89
  40.9 4.4 %collective-permute-start.7 = (f32[16,384]{1,0:T(8,128)}, f32[16,384]{1,0:T(8,128)S(1)}, u32[]{:S(2)}, u32[]{:S(2)}) collective-permute-start(f32[16,384]{1,0:T(8,128)} %get-tuple-element.58), channel_id=1, source_target_pairs={{0,1},{1,0},{2,3},{3,2},{4,5},{5,4},{6,7},{7,6},{8,9},{9,8},{10,11... | collective-permute-start | bytes 73736 | tf_op jit(solution)/shard_map/ppermute | solution.py:89
  44.6 0.6 copy-start.12
  45.8 0.7 copy-start.7
  46.6 0.7 copy-start.11
  47.3 0.7 copy-start.13
  48.0 0.7 copy-start.15
  52.3 15.6 %all-to-all-start.2 = ((f32[32,8,128]{2,1,0:T(8,128)}), f32[32,8,128]{2,1,0:T(8,128)S(1)}, u32[]{:S(2)}, u32[]{:S(2)}) async-start(f32[32,8,128]{2,1,0:T(8,128)} %get-tuple-element.68), calls=%async_computation.2 | async-start | bytes 262144 | tf_op jit(solution)/shard_map/all_to_all | solution.py:466
  57.0 8.4 %collective-permute-start.8 = (f32[16,384]{1,0:T(8,128)}, f32[16,384]{1,0:T(8,128)S(1)}, u32[]{:S(2)}, u32[]{:S(2)}) collective-permute-start(f32[16,384]{1,0:T(8,128)} %get-tuple-element.64), channel_id=1, source_target_pairs={{4,8},{8,4},{12,16},{16,12},{20,24},{24,20},{5,9},{9,5},{13,17},{1... | collective-permute-start | bytes 73736 | tf_op jit(solution)/shard_map/ppermute | solution.py:89
  57.6 8.4 %collective-permute-start.9 = (f32[16,384]{1,0:T(8,128)}, f32[16,384]{1,0:T(8,128)S(1)}, u32[]{:S(2)}, u32[]{:S(2)}) collective-permute-start(f32[16,384]{1,0:T(8,128)} %get-tuple-element.65), channel_id=1, source_target_pairs={{1,2},{2,1},{5,6},{6,5},{9,10},{10,9},{13,14},{14,13},{17,18},{18,... | collective-permute-start | bytes 73736 | tf_op jit(solution)/shard_map/ppermute | solution.py:89
  58.3 8.3 %collective-permute-start.10 = (f32[16,384]{1,0:T(8,128)}, f32[16,384]{1,0:T(8,128)S(1)}, u32[]{:S(2)}, u32[]{:S(2)}) collective-permute-start(f32[16,384]{1,0:T(8,128)} %get-tuple-element.66), channel_id=1, source_target_pairs={{0,4},{4,0},{8,12},{12,8},{16,20},{20,16},{24,28},{28,24},{1,5},{5... | collective-permute-start | bytes 73736 | tf_op jit(solution)/shard_map/ppermute | solution.py:89
  62.8 4.4 %collective-permute-start.11 = (f32[16,384]{1,0:T(8,128)}, f32[16,384]{1,0:T(8,128)S(1)}, u32[]{:S(2)}, u32[]{:S(2)}) collective-permute-start(f32[16,384]{1,0:T(8,128)} %get-tuple-element.67), channel_id=1, source_target_pairs={{0,1},{1,0},{2,3},{3,2},{4,5},{5,4},{6,7},{7,6},{8,9},{9,8},{10,11... | collective-permute-start | bytes 73736 | tf_op jit(solution)/shard_map/ppermute | solution.py:89
  65.4 0.6 copy-start
  66.6 0.6 copy-start.4
  67.2 0.6 copy-start.8
  67.8 0.7 copy-start.1
  68.6 0.7 copy-start.3
  69.3 0.7 copy-start.5
  70.1 0.7 copy-start.9
  74.0 14.2 %all-to-all-start.3 = ((f32[32,8,128]{2,1,0:T(8,128)}), f32[32,8,128]{2,1,0:T(8,128)S(1)}, u32[]{:S(2)}, u32[]{:S(2)}) async-start(f32[32,8,128]{2,1,0:T(8,128)} %get-tuple-element.79), calls=%async_computation.3 | async-start | bytes 262144 | tf_op jit(solution)/shard_map/all_to_all | solution.py:466
  78.7 8.4 %collective-permute-start.12 = (f32[16,384]{1,0:T(8,128)}, f32[16,384]{1,0:T(8,128)S(1)}, u32[]{:S(2)}, u32[]{:S(2)}) collective-permute-start(f32[16,384]{1,0:T(8,128)} %get-tuple-element.75), channel_id=1, source_target_pairs={{4,8},{8,4},{12,16},{16,12},{20,24},{24,20},{5,9},{9,5},{13,17},{1... | collective-permute-start | bytes 73736 | tf_op jit(solution)/shard_map/ppermute | solution.py:89
  79.3 7.8 %collective-permute-start.13 = (f32[16,384]{1,0:T(8,128)}, f32[16,384]{1,0:T(8,128)S(1)}, u32[]{:S(2)}, u32[]{:S(2)}) collective-permute-start(f32[16,384]{1,0:T(8,128)} %get-tuple-element.76), channel_id=1, source_target_pairs={{1,2},{2,1},{5,6},{6,5},{9,10},{10,9},{13,14},{14,13},{17,18},{18,... | collective-permute-start | bytes 73736 | tf_op jit(solution)/shard_map/ppermute | solution.py:89
  80.0 7.1 %collective-permute-start.14 = (f32[16,384]{1,0:T(8,128)}, f32[16,384]{1,0:T(8,128)S(1)}, u32[]{:S(2)}, u32[]{:S(2)}) collective-permute-start(f32[16,384]{1,0:T(8,128)} %get-tuple-element.77), channel_id=1, source_target_pairs={{0,4},{4,0},{8,12},{12,8},{16,20},{20,16},{24,28},{28,24},{1,5},{5... | collective-permute-start | bytes 73736 | tf_op jit(solution)/shard_map/ppermute | solution.py:89
  84.6 3.6 %collective-permute-start.15 = (f32[16,384]{1,0:T(8,128)}, f32[16,384]{1,0:T(8,128)S(1)}, u32[]{:S(2)}, u32[]{:S(2)}) collective-permute-start(f32[16,384]{1,0:T(8,128)} %get-tuple-element.78), channel_id=1, source_target_pairs={{0,1},{1,0},{2,3},{3,2},{4,5},{5,4},{6,7},{7,6},{8,9},{9,8},{10,11... | collective-permute-start | bytes 73736 | tf_op jit(solution)/shard_map/ppermute | solution.py:89
  (4 other events, 2.4 us)

commit v13 on v11

--- a/solution.py
+++ b/solution.py
@@ -18,7 +18,7 @@
 INVERSE_LANE = 48
 SCALAR_LANE = 96
 BLOCK = 256
-SWAPS = (1, 3, 0, 2)
+SWAPS = (3, 0, 1, 2)
 
 
 class Sizes:
@@ -170,7 +170,7 @@
     local_tile[:, INVERSE_LANE : INVERSE_LANE + 8] = inverse
 
 
-def couple(z, padded, masks, local_tile, got1, got3, got0, got2, sent, live_rows, lift_rows, tile):
+def couple(z, padded, masks, local_tile, got3, got0, got1, got2, sent, live_rows, lift_rows, tile):
     near = across_faces(z, (got0, got1, got2, got3))
     inverse = local_tile[:, INVERSE_LANE : INVERSE_LANE + 8]
     tile[...] = local_tile[...]
@@ -297,10 +297,10 @@
     start = window_start(z, ix) * z.ny
     inverses = [received[pl.ds(start + spot, 1)][0][:, INVERSE_LANE : INVERSE_LANE + 8] for spot in near_spots]
     fields = []
-    for f in range(4):
-        both = lift_rows[f]
-        own, near = both[0:8] * SIGNS[f], both[8:16] * -SIGNS[f]
-        rows[f] = jnp.concatenate([dot(inverses[0], own), dot(inverses[1 + f], near)], axis=0)
+    own = dot(inverses[0], jnp.concatenate([lift_rows[f][0:8] * SIGNS[f] for f in range(4)], axis=1))
+    for f in range(4):
+        near = dot(inverses[1 + f], lift_rows[f][8:16] * -SIGNS[f])
+        rows[f] = jnp.concatenate([own[:, f * z.lanes : (f + 1) * z.lanes], near], axis=0)
         fields.append(lifted(z, amplitudes, lift_rows, f))
         multipliers[f] = fields[f]
     for item in (solve_rows, rows, multipliers):
@@ -319,7 +319,7 @@
 
 
 def first_direction(
-    z, solve_rows, lift_rows, faces, masks, rows, got1, got3, got0, got2, received, arranged,
+    z, solve_rows, lift_rows, faces, masks, rows, got3, got0, got1, got2, received, arranged,
     residual, direction, image, sent, to0, to1, to2, to3,
     tile, packed,
 ):
@@ -344,7 +344,7 @@
 
 def second_direction(
     z, solve_rows, lift_rows, faces, masks, residual, direction, multipliers,
-    got1, got3, got0, got2, received, arranged,
+    got3, got0, got1, got2, received, arranged,
     next_multipliers, next_residual, projected, image, fresh, sums, sent, to0, to1, to2, to3,
     packed,
 ):
@@ -379,7 +379,7 @@
 
 def finish(
     z, sums, faces, masks, residual, image, multipliers, projected, direction,
-    got1, got3, got0, got2, received,
+    got3, got0, got1, got2, received,
     out_multipliers, out_residual,
 ):
     summed = jnp.sum(received[...], axis=0)

time: 82.4 us -> 85.6 us (1.039)
  starting transfers between devices: 47.6 us -> 55.5 us
  waiting for transfers between devices: 9.96 us -> 5.05 us
    ppermute x16, waiting for transfers between devices: 9.79 us -> 4.87 us  [exchange(): got.append(lax.ppermute(sent[i], axis, pairs))]
    all_to_all x4, starting transfers between devices: 19.8 us -> 24 us  [gather(): return lax.all_to_all(values, AXES, 0, 0, tiled=True)]
    ppermute x16, starting transfers between devices: 27.8 us -> 31.4 us  [exchange(): got.append(lax.ppermute(sent[i], axis, pairs))]
  transfers between devices with their start and end apart: 20 -> 20, of which waited for: 9 -> 5; matrix products, arithmetic and copies ran while one was open for 0% -> 0% of each run, Pallas kernels for 9% -> 9%
where the time goes in v13:
time: 85.6 us; the launch traced here: 84 us
  starting transfers between devices  55.5 us (65%)
  Pallas kernels  22.6 us (26%)
  waiting for transfers between devices  5.05 us (6%)
  between operations  0.88 us (1%)
    ppermute x16, starting transfers between devices, exchange(): got.append(lax.ppermute(sent[i], axis, pairs))  31.4 us
    all_to_all x4, starting transfers between devices, gather(): return lax.all_to_all(values, AXES, 0, 0, tiled=True)  24 us
    pallas_call x8, Pallas kernels, call(): pl.pallas_call(run, out_shape=[pltpu.HBM(a.shape, a.dtype) for a in shape...  22.6 us
    ppermute x16, waiting for transfers between devices, exchange(): got.append(lax.ppermute(sent[i], axis, pairs))  4.87 us
  transfers between devices with their start and end apart: 20, of which 5 were waited for; matrix products, arithmetic and copies ran while one was open for 0% of the time, Pallas kernels for 9%

profile of v13, /device:TPU:5, one launch (start us, length us, event | category | flops | bytes accessed | tf_op | source)
XLA Modules:
  0.0 84.0 jit_solution(13036538879319240047)
XLA Ops:
  0.6 0.8 prepare.1
  1.5 3.7 %collective-permute-start = (f32[8,384]{1,0:T(8,128)S(1)}, f32[8,384]{1,0:T(8,128)S(1)}, u32[]{:S(2)}, u32[]{:S(2)}) collective-permute-start(f32[8,384]{1,0:T(8,128)S(1)} %get-tuple-element.43), channel_id=1, source_target_pairs={{1,2},{2,1},{5,6},{6,5},{9,10},{10,9},{13,14},{14,13},{17,18},{18,... | collective-permute-start | bytes 36872 | tf_op jit(solution)/shard_map/ppermute | solution.py:89
  5.2 0.3 collective-permute-start.1
  5.4 4.1 %collective-permute-start.2 = (f32[8,384]{1,0:T(8,128)S(1)}, f32[8,384]{1,0:T(8,128)S(1)}, u32[]{:S(2)}, u32[]{:S(2)}) collective-permute-start(f32[8,384]{1,0:T(8,128)S(1)} %get-tuple-element.45), channel_id=1, source_target_pairs={{4,8},{8,4},{12,16},{16,12},{20,24},{24,20},{5,9},{9,5},{13,17},{1... | collective-permute-start | bytes 36872 | tf_op jit(solution)/shard_map/ppermute | solution.py:89
  9.6 0.1 collective-permute-start.3
  9.7 1.0 %invert.1.refs_2_ = f32[8,128]{1,0:T(8,128)S(1)} custom-call(f32[1,6,1,16]{3,2,1,0:T(1,128)} %bitcast.3, f32[4,8,384]{2,1,0:T(8,128)S(1)} %get-tuple-element.41.refs_1_.refs_0_, f32[8,384]{1,0:T(8,128)S(1)} %get-tuple-element.42.refs_2_.refs_1_), custom_call_target="tpu_custom_call" | custom-call | flops 46080000 | bytes 65920 | tf_op jit(solution)/shard_map/invert/pallas_call | solution.py:456
  10.8 0.1 collective-permute-done.3.refs_6_
  10.8 1.5 %couple.1 = (f32[32,8,128]{2,1,0:T(8,128)}, f32[8,384]{1,0:T(8,128)}, f32[4,16,384]{2,1,0:T(8,128)}) custom-call(f32[4,8,384]{2,1,0:T(8,128)S(1)} %get-tuple-element.41.refs_1_.refs_0_, f32[8,384]{1,0:T(8,128)S(1)} %get-tuple-element.42.refs_2_.refs_1_, f32[8,128]{1,0:T(8,128)S(1)} %invert.1.refs_2_, f32[8,384]{1,0:T(8,128)S(1)} %collective-permute-done.refs_3_, ...), custom_call_target="tpu_custom_call" | custom-call | bytes 356352 | tf_op jit(solution)/shard_map/couple/pallas_call | solution.py:456
  12.4 6.1 %all-to-all-start = ((f32[32,8,128]{2,1,0:T(8,128)}), f32[32,8,128]{2,1,0:T(8,128)S(1)}, u32[]{:S(2)}, u32[]{:S(2)}) async-start(f32[32,8,128]{2,1,0:T(8,128)} %get-tuple-element.49), calls=%async_computation | async-start | bytes 262144 | tf_op jit(solution)/shard_map/all_to_all | solution.py:469
  18.5 6.7 %arrange.1 = (f32[16,1200]{1,0:T(8,128)}, bf16[1200,1200]{1,0:T(8,128)(2,1)S(1)}) custom-call(s32[1,1,4,300]{3,2,1,0:T(4,128)} %refs_0_.1, bf16[1,1,1200,1200]{3,2,1,0:T(8,128)(2,1)} %refs_1_.3, f32[1,1,16,1200]{3,2,1,0:T(8,128)} %refs_2_.1), custom_call_target="tpu_custom_call" | custom-call | flops 2949120000 | bytes 5918400 | tf_op jit(solution)/shard_map/arrange/pallas_call | solution.py:456
  25.2 0.2 all-to-all-done.refs_2_
  25.3 4.1 %begin.1 = (f32[40,256]{1,0:T(8,128)}, f32[4,16,384]{2,1,0:T(8,128)}, f32[4,16,384]{2,1,0:T(8,128)}, f32[4,16,384]{2,1,0:T(8,128)}, f32[32,8,128]{2,1,0:T(8,128)...) custom-call(f32[4,16,384]{2,1,0:T(8,128)} %get-tuple-element.47.refs_0_.refs_1_, ...), custom_call_target="tpu_custom_call" | custom-call | flops 46080000 | bytes 3751424 | tf_op jit(solution)/shard_map/begin/pallas_call | solution.py:456
  29.5 5.7 %all-to-all-start.1 = ((f32[32,8,128]{2,1,0:T(8,128)}), f32[32,8,128]{2,1,0:T(8,128)S(1)}, u32[]{:S(2)}, u32[]{:S(2)}) async-start(f32[32,8,128]{2,1,0:T(8,128)} %get-tuple-element.59), calls=%async_computation.1 | async-start | bytes 262144 | tf_op jit(solution)/shard_map/all_to_all | solution.py:469
  35.1 3.3 %collective-permute-start.4 = (f32[16,384]{1,0:T(8,128)}, f32[16,384]{1,0:T(8,128)S(1)}, u32[]{:S(2)}, u32[]{:S(2)}) collective-permute-start(f32[16,384]{1,0:T(8,128)} %get-tuple-element.55), channel_id=1, source_target_pairs={{1,2},{2,1},{5,6},{6,5},{9,10},{10,9},{13,14},{14,13},{17,18},{18,... | collective-permute-start | bytes 73736 | tf_op jit(solution)/shard_map/ppermute | solution.py:89
  38.5 0.3 collective-permute-start.5
  38.8 4.0 %collective-permute-start.6 = (f32[16,384]{1,0:T(8,128)}, f32[16,384]{1,0:T(8,128)S(1)}, u32[]{:S(2)}, u32[]{:S(2)}) collective-permute-start(f32[16,384]{1,0:T(8,128)} %get-tuple-element.57), channel_id=1, source_target_pairs={{4,8},{8,4},{12,16},{16,12},{20,24},{24,20},{5,9},{9,5},{13,17},{1... | collective-permute-start | bytes 73736 | tf_op jit(solution)/shard_map/ppermute | solution.py:89
  42.8 0.1 collective-permute-start.7
  42.9 1.6 %collective-permute-done.6.refs_7_ = f32[16,384]{1,0:T(8,128)S(1)} collective-permute-done((f32[16,384]{1,0:T(8,128)}, f32[16,384]{1,0:T(8,128)S(1)}, u32[]{:S(2)}, u32[]{:S(2)}) %collective-permute-start.6) | collective-permute-done | bytes 24608 | tf_op jit(solution)/shard_map/ppermute | solution.py:89
  44.5 3.3 %first_direction.1 = (f32[4,16,384]{2,1,0:T(8,128)}, f32[4,16,384]{2,1,0:T(8,128)}, f32[4,16,384]{2,1,0:T(8,128)}, f32[32,8,128]{2,1,0:T(8,128)}, f32[16,384]{1,...) custom-call(f32[40,256]{1,0:T(8,128)} %get-tuple-element.51.refs_0_, ...), custom_call_target="tpu_custom_call" | custom-call | flops 46080000 | bytes 3981824 | tf_op jit(solution)/shard_map/first_direction/pallas_call | solution.py:456
  47.8 6.1 %all-to-all-start.2 = ((f32[32,8,128]{2,1,0:T(8,128)}), f32[32,8,128]{2,1,0:T(8,128)S(1)}, u32[]{:S(2)}, u32[]{:S(2)}) async-start(f32[32,8,128]{2,1,0:T(8,128)} %get-tuple-element.68), calls=%async_computation.2 | async-start | bytes 262144 | tf_op jit(solution)/shard_map/all_to_all | solution.py:469
  54.0 3.3 %collective-permute-start.8 = (f32[16,384]{1,0:T(8,128)}, f32[16,384]{1,0:T(8,128)S(1)}, u32[]{:S(2)}, u32[]{:S(2)}) collective-permute-start(f32[16,384]{1,0:T(8,128)} %get-tuple-element.64), channel_id=1, source_target_pairs={{1,2},{2,1},{5,6},{6,5},{9,10},{10,9},{13,14},{14,13},{17,18},{18,... | collective-permute-start | bytes 73736 | tf_op jit(solution)/shard_map/ppermute | solution.py:89
  57.3 0.3 collective-permute-start.9
  57.7 4.0 %collective-permute-start.10 = (f32[16,384]{1,0:T(8,128)}, f32[16,384]{1,0:T(8,128)S(1)}, u32[]{:S(2)}, u32[]{:S(2)}) collective-permute-start(f32[16,384]{1,0:T(8,128)} %get-tuple-element.66), channel_id=1, source_target_pairs={{4,8},{8,4},{12,16},{16,12},{20,24},{24,20},{5,9},{9,5},{13,17},{1... | collective-permute-start | bytes 73736 | tf_op jit(solution)/shard_map/ppermute | solution.py:89
  61.7 0.1 collective-permute-start.11
  61.8 1.6 %collective-permute-done.10.refs_9_ = f32[16,384]{1,0:T(8,128)S(1)} collective-permute-done((f32[16,384]{1,0:T(8,128)}, f32[16,384]{1,0:T(8,128)S(1)}, u32[]{:S(2)}, u32[]{:S(2)}) %collective-permute-start.10) | collective-permute-done | bytes 24608 | tf_op jit(solution)/shard_map/ppermute | solution.py:89
  63.4 3.2 %second_direction.1 = (f32[4,16,384]{2,1,0:T(8,128)}, f32[4,16,384]{2,1,0:T(8,128)}, f32[4,16,384]{2,1,0:T(8,128)}, f32[4,16,384]{2,1,0:T(8,128)}, f32[4,16,384]...) custom-call(f32[40,256]{1,0:T(8,128)} %get-tuple-element.51.refs_0_,, ...), custom_call_target="tpu_custom_call" | custom-call | flops 46080000 | bytes 4379136 | tf_op jit(solution)/shard_map/second_direction/pallas_call | solution.py:456
  66.5 6.1 %all-to-all-start.3 = ((f32[32,8,128]{2,1,0:T(8,128)}), f32[32,8,128]{2,1,0:T(8,128)S(1)}, u32[]{:S(2)}, u32[]{:S(2)}) async-start(f32[32,8,128]{2,1,0:T(8,128)} %get-tuple-element.79), calls=%async_computation.3 | async-start | bytes 262144 | tf_op jit(solution)/shard_map/all_to_all | solution.py:469
  72.7 3.3 %collective-permute-start.12 = (f32[16,384]{1,0:T(8,128)}, f32[16,384]{1,0:T(8,128)S(1)}, u32[]{:S(2)}, u32[]{:S(2)}) collective-permute-start(f32[16,384]{1,0:T(8,128)} %get-tuple-element.75), channel_id=1, source_target_pairs={{1,2},{2,1},{5,6},{6,5},{9,10},{10,9},{13,14},{14,13},{17,18},{18,... | collective-permute-start | bytes 73736 | tf_op jit(solution)/shard_map/ppermute | solution.py:89
  76.0 0.3 collective-permute-start.13
  76.4 4.0 %collective-permute-start.14 = (f32[16,384]{1,0:T(8,128)}, f32[16,384]{1,0:T(8,128)S(1)}, u32[]{:S(2)}, u32[]{:S(2)}) collective-permute-start(f32[16,384]{1,0:T(8,128)} %get-tuple-element.77), channel_id=1, source_target_pairs={{4,8},{8,4},{12,16},{16,12},{20,24},{24,20},{5,9},{9,5},{13,17},{1... | collective-permute-start | bytes 73736 | tf_op jit(solution)/shard_map/ppermute | solution.py:89
  80.5 1.6 %collective-permute-done.14.refs_10_ = f32[16,384]{1,0:T(8,128)S(1)} collective-permute-done((f32[16,384]{1,0:T(8,128)}, f32[16,384]{1,0:T(8,128)S(1)}, u32[]{:S(2)}, u32[]{:S(2)}) %collective-permute-start.14) | collective-permute-done | bytes 24608 | tf_op jit(solution)/shard_map/ppermute | solution.py:89
  82.0 1.9 %finish.1 = (f32[1,1,4,16,300]{4,3,2,1,0:T(8,128)}, f32[1,1,4,16,300]{4,3,2,1,0:T(8,128)}) custom-call(f32[8,128]{1,0:T(8,128)} %get-tuple-element.69.refs_0_, f32[4,16,384]{2,1,0:T(8,128)} %get-tuple-element.70.refs_1_, f32[8,384]{1,0:T(8,128)} %get-tuple-element.53.refs_3_.refs_2_, f32[4,16,384]{2,1,0:T(8,128)} %get-tuple-element.71.refs_3_, ...), custom_call_target="tpu_custom_call" | custom-call | bytes 989184 | tf_op jit(solution)/shard_map/finish/pallas_call | solution.py:456
  (16 shorter events, 0.1 us)
Async XLA Ops:
  1.5 9.2 %collective-permute-start = (f32[8,384]{1,0:T(8,128)S(1)}, f32[8,384]{1,0:T(8,128)S(1)}, u32[]{:S(2)}, u32[]{:S(2)}) collective-permute-start(f32[8,384]{1,0:T(8,128)S(1)} %get-tuple-element.43), channel_id=1, source_target_pairs={{1,2},{2,1},{5,6},{6,5},{9,10},{10,9},{13,14},{14,13},{17,18},{18,... | collective-permute-start | bytes 36872 | tf_op jit(solution)/shard_map/ppermute | solution.py:89
  5.2 5.6 %collective-permute-start.1 = (f32[8,384]{1,0:T(8,128)S(1)}, f32[8,384]{1,0:T(8,128)S(1)}, u32[]{:S(2)}, u32[]{:S(2)}) collective-permute-start(f32[8,384]{1,0:T(8,128)S(1)} %get-tuple-element.44), channel_id=1, source_target_pairs={{0,4},{4,0},{8,12},{12,8},{16,20},{20,16},{24,28},{28,24},{1,5},{5... | collective-permute-start | bytes 36872 | tf_op jit(solution)/shard_map/ppermute | solution.py:89
  5.4 5.3 %collective-permute-start.2 = (f32[8,384]{1,0:T(8,128)S(1)}, f32[8,384]{1,0:T(8,128)S(1)}, u32[]{:S(2)}, u32[]{:S(2)}) collective-permute-start(f32[8,384]{1,0:T(8,128)S(1)} %get-tuple-element.45), channel_id=1, source_target_pairs={{4,8},{8,4},{12,16},{16,12},{20,24},{24,20},{5,9},{9,5},{13,17},{1... | collective-permute-start | bytes 36872 | tf_op jit(solution)/shard_map/ppermute | solution.py:89
  9.6 1.2 %collective-permute-start.3 = (f32[8,384]{1,0:T(8,128)S(1)}, f32[8,384]{1,0:T(8,128)S(1)}, u32[]{:S(2)}, u32[]{:S(2)}) collective-permute-start(f32[8,384]{1,0:T(8,128)S(1)} %get-tuple-element.46), channel_id=1, source_target_pairs={{0,1},{1,0},{2,3},{3,2},{4,5},{5,4},{6,7},{7,6},{8,9},{9,8},{10,11... | collective-permute-start | bytes 36872 | tf_op jit(solution)/shard_map/ppermute | solution.py:89
  12.4 12.9 %all-to-all-start = ((f32[32,8,128]{2,1,0:T(8,128)}), f32[32,8,128]{2,1,0:T(8,128)S(1)}, u32[]{:S(2)}, u32[]{:S(2)}) async-start(f32[32,8,128]{2,1,0:T(8,128)} %get-tuple-element.49), calls=%async_computation | async-start | bytes 262144 | tf_op jit(solution)/shard_map/all_to_all | solution.py:469
  29.5 15.1 %all-to-all-start.1 = ((f32[32,8,128]{2,1,0:T(8,128)}), f32[32,8,128]{2,1,0:T(8,128)S(1)}, u32[]{:S(2)}, u32[]{:S(2)}) async-start(f32[32,8,128]{2,1,0:T(8,128)} %get-tuple-element.59), calls=%async_computation.1 | async-start | bytes 262144 | tf_op jit(solution)/shard_map/all_to_all | solution.py:469
  35.1 7.8 %collective-permute-start.4 = (f32[16,384]{1,0:T(8,128)}, f32[16,384]{1,0:T(8,128)S(1)}, u32[]{:S(2)}, u32[]{:S(2)}) collective-permute-start(f32[16,384]{1,0:T(8,128)} %get-tuple-element.55), channel_id=1, source_target_pairs={{1,2},{2,1},{5,6},{6,5},{9,10},{10,9},{13,14},{14,13},{17,18},{18,... | collective-permute-start | bytes 73736 | tf_op jit(solution)/shard_map/ppermute | solution.py:89
  38.5 4.4 %collective-permute-start.5 = (f32[16,384]{1,0:T(8,128)}, f32[16,384]{1,0:T(8,128)S(1)}, u32[]{:S(2)}, u32[]{:S(2)}) collective-permute-start(f32[16,384]{1,0:T(8,128)} %get-tuple-element.56), channel_id=1, source_target_pairs={{0,4},{4,0},{8,12},{12,8},{16,20},{20,16},{24,28},{28,24},{1,5},{5... | collective-permute-start | bytes 73736 | tf_op jit(solution)/shard_map/ppermute | solution.py:89
  38.8 5.7 %collective-permute-start.6 = (f32[16,384]{1,0:T(8,128)}, f32[16,384]{1,0:T(8,128)S(1)}, u32[]{:S(2)}, u32[]{:S(2)}) collective-permute-start(f32[16,384]{1,0:T(8,128)} %get-tuple-element.57), channel_id=1, source_target_pairs={{4,8},{8,4},{12,16},{16,12},{20,24},{24,20},{5,9},{9,5},{13,17},{1... | collective-permute-start | bytes 73736 | tf_op jit(solution)/shard_map/ppermute | solution.py:89
  42.8 1.7 %collective-permute-start.7 = (f32[16,384]{1,0:T(8,128)}, f32[16,384]{1,0:T(8,128)S(1)}, u32[]{:S(2)}, u32[]{:S(2)}) collective-permute-start(f32[16,384]{1,0:T(8,128)} %get-tuple-element.58), channel_id=1, source_target_pairs={{0,1},{1,0},{2,3},{3,2},{4,5},{5,4},{6,7},{7,6},{8,9},{9,8},{10,11... | collective-permute-start | bytes 73736 | tf_op jit(solution)/shard_map/ppermute | solution.py:89
  47.8 15.5 %all-to-all-start.2 = ((f32[32,8,128]{2,1,0:T(8,128)}), f32[32,8,128]{2,1,0:T(8,128)S(1)}, u32[]{:S(2)}, u32[]{:S(2)}) async-start(f32[32,8,128]{2,1,0:T(8,128)} %get-tuple-element.68), calls=%async_computation.2 | async-start | bytes 262144 | tf_op jit(solution)/shard_map/all_to_all | solution.py:469
  54.0 7.8 %collective-permute-start.8 = (f32[16,384]{1,0:T(8,128)}, f32[16,384]{1,0:T(8,128)S(1)}, u32[]{:S(2)}, u32[]{:S(2)}) collective-permute-start(f32[16,384]{1,0:T(8,128)} %get-tuple-element.64), channel_id=1, source_target_pairs={{1,2},{2,1},{5,6},{6,5},{9,10},{10,9},{13,14},{14,13},{17,18},{18,... | collective-permute-start | bytes 73736 | tf_op jit(solution)/shard_map/ppermute | solution.py:89
  57.3 4.4 %collective-permute-start.9 = (f32[16,384]{1,0:T(8,128)}, f32[16,384]{1,0:T(8,128)S(1)}, u32[]{:S(2)}, u32[]{:S(2)}) collective-permute-start(f32[16,384]{1,0:T(8,128)} %get-tuple-element.65), channel_id=1, source_target_pairs={{0,4},{4,0},{8,12},{12,8},{16,20},{20,16},{24,28},{28,24},{1,5},{5... | collective-permute-start | bytes 73736 | tf_op jit(solution)/shard_map/ppermute | solution.py:89
  57.7 5.7 %collective-permute-start.10 = (f32[16,384]{1,0:T(8,128)}, f32[16,384]{1,0:T(8,128)S(1)}, u32[]{:S(2)}, u32[]{:S(2)}) collective-permute-start(f32[16,384]{1,0:T(8,128)} %get-tuple-element.66), channel_id=1, source_target_pairs={{4,8},{8,4},{12,16},{16,12},{20,24},{24,20},{5,9},{9,5},{13,17},{1... | collective-permute-start | bytes 73736 | tf_op jit(solution)/shard_map/ppermute | solution.py:89
  61.7 1.7 %collective-permute-start.11 = (f32[16,384]{1,0:T(8,128)}, f32[16,384]{1,0:T(8,128)S(1)}, u32[]{:S(2)}, u32[]{:S(2)}) collective-permute-start(f32[16,384]{1,0:T(8,128)} %get-tuple-element.67), channel_id=1, source_target_pairs={{0,1},{1,0},{2,3},{3,2},{4,5},{5,4},{6,7},{7,6},{8,9},{9,8},{10,11... | collective-permute-start | bytes 73736 | tf_op jit(solution)/shard_map/ppermute | solution.py:89
  66.5 15.5 %all-to-all-start.3 = ((f32[32,8,128]{2,1,0:T(8,128)}), f32[32,8,128]{2,1,0:T(8,128)S(1)}, u32[]{:S(2)}, u32[]{:S(2)}) async-start(f32[32,8,128]{2,1,0:T(8,128)} %get-tuple-element.79), calls=%async_computation.3 | async-start | bytes 262144 | tf_op jit(solution)/shard_map/all_to_all | solution.py:469
  72.7 7.8 %collective-permute-start.12 = (f32[16,384]{1,0:T(8,128)}, f32[16,384]{1,0:T(8,128)S(1)}, u32[]{:S(2)}, u32[]{:S(2)}) collective-permute-start(f32[16,384]{1,0:T(8,128)} %get-tuple-element.75), channel_id=1, source_target_pairs={{1,2},{2,1},{5,6},{6,5},{9,10},{10,9},{13,14},{14,13},{17,18},{18,... | collective-permute-start | bytes 73736 | tf_op jit(solution)/shard_map/ppermute | solution.py:89
  76.0 4.4 %collective-permute-start.13 = (f32[16,384]{1,0:T(8,128)}, f32[16,384]{1,0:T(8,128)S(1)}, u32[]{:S(2)}, u32[]{:S(2)}) collective-permute-start(f32[16,384]{1,0:T(8,128)} %get-tuple-element.76), channel_id=1, source_target_pairs={{0,4},{4,0},{8,12},{12,8},{16,20},{20,16},{24,28},{28,24},{1,5},{5... | collective-permute-start | bytes 73736 | tf_op jit(solution)/shard_map/ppermute | solution.py:89
  76.4 5.7 %collective-permute-start.14 = (f32[16,384]{1,0:T(8,128)}, f32[16,384]{1,0:T(8,128)S(1)}, u32[]{:S(2)}, u32[]{:S(2)}) collective-permute-start(f32[16,384]{1,0:T(8,128)} %get-tuple-element.77), channel_id=1, source_target_pairs={{4,8},{8,4},{12,16},{16,12},{20,24},{24,20},{5,9},{9,5},{13,17},{1... | collective-permute-start | bytes 73736 | tf_op jit(solution)/shard_map/ppermute | solution.py:89
  80.4 1.7 %collective-permute-start.15 = (f32[16,384]{1,0:T(8,128)}, f32[16,384]{1,0:T(8,128)S(1)}, u32[]{:S(2)}, u32[]{:S(2)}) collective-permute-start(f32[16,384]{1,0:T(8,128)} %get-tuple-element.78), channel_id=1, source_target_pairs={{0,1},{1,0},{2,3},{3,2},{4,5},{5,4},{6,7},{7,6},{8,9},{9,8},{10,11... | collective-permute-start | bytes 73736 | tf_op jit(solution)/shard_map/ppermute | solution.py:89

commit v14 on v13

--- a/solution.py
+++ b/solution.py
@@ -18,7 +18,7 @@
 INVERSE_LANE = 48
 SCALAR_LANE = 96
 BLOCK = 256
-SWAPS = (3, 0, 1, 2)
+SWAPS = (3, 1, 0, 2)
 
 
 class Sizes:
@@ -170,7 +170,7 @@
     local_tile[:, INVERSE_LANE : INVERSE_LANE + 8] = inverse
 
 
-def couple(z, padded, masks, local_tile, got3, got0, got1, got2, sent, live_rows, lift_rows, tile):
+def couple(z, padded, masks, local_tile, got3, got1, got0, got2, sent, live_rows, lift_rows, tile):
     near = across_faces(z, (got0, got1, got2, got3))
     inverse = local_tile[:, INVERSE_LANE : INVERSE_LANE + 8]
     tile[...] = local_tile[...]
@@ -319,7 +319,7 @@
 
 
 def first_direction(
-    z, solve_rows, lift_rows, faces, masks, rows, got3, got0, got1, got2, received, arranged,
+    z, solve_rows, lift_rows, faces, masks, rows, got3, got1, got0, got2, received, arranged,
     residual, direction, image, sent, to0, to1, to2, to3,
     tile, packed,
 ):
@@ -344,7 +344,7 @@
 
 def second_direction(
     z, solve_rows, lift_rows, faces, masks, residual, direction, multipliers,
-    got3, got0, got1, got2, received, arranged,
+    got3, got1, got0, got2, received, arranged,
     next_multipliers, next_residual, projected, image, fresh, sums, sent, to0, to1, to2, to3,
     packed,
 ):
@@ -379,7 +379,7 @@
 
 def finish(
     z, sums, faces, masks, residual, image, multipliers, projected, direction,
-    got3, got0, got1, got2, received,
+    got3, got1, got0, got2, received,
     out_multipliers, out_residual,
 ):
     summed = jnp.sum(received[...], axis=0)

time: 85.6 us -> 82.7 us (0.966)
  starting transfers between devices: 55.5 us -> 47.9 us
  waiting for transfers between devices: 5.05 us -> 9.96 us
    ppermute x16, waiting for transfers between devices: 4.87 us -> 9.79 us  [exchange(): got.append(lax.ppermute(sent[i], axis, pairs))]
    ppermute x16, starting transfers between devices: 31.4 us -> 26.7 us  [exchange(): got.append(lax.ppermute(sent[i], axis, pairs))]
    all_to_all x4, starting transfers between devices: 24 us -> 21.2 us  [gather(): return lax.all_to_all(values, AXES, 0, 0, tiled=True)]
  transfers between devices with their start and end apart: 20 -> 20, of which waited for: 5 -> 9; matrix products, arithmetic and copies ran while one was open for 0% -> 0% of each run, Pallas kernels for 9% -> 9%
where the time goes in v14:
time: 82.7 us; the launch traced here: 81.3 us
  starting transfers between devices  47.9 us (58%)
  Pallas kernels  22.6 us (27%)
  waiting for transfers between devices  9.96 us (12%)
  between operations  0.88 us (1%)
    ppermute x16, starting transfers between devices, exchange(): got.append(lax.ppermute(sent[i], axis, pairs))  26.7 us
    pallas_call x8, Pallas kernels, call(): pl.pallas_call(run, out_shape=[pltpu.HBM(a.shape, a.dtype) for a in shape...  22.6 us
    all_to_all x4, starting transfers between devices, gather(): return lax.all_to_all(values, AXES, 0, 0, tiled=True)  21.2 us
    ppermute x16, waiting for transfers between devices, exchange(): got.append(lax.ppermute(sent[i], axis, pairs))  9.79 us
  transfers between devices with their start and end apart: 20, of which 9 were waited for; matrix products, arithmetic and copies ran while one was open for 0% of the time, Pallas kernels for 9%

profile of v14, /device:TPU:5, one launch (start us, length us, event | category | flops | bytes accessed | tf_op | source)
XLA Modules:
  0.0 81.3 jit_solution(8250700391433896361)
XLA Ops:
  0.6 0.8 %prepare.1 = (f32[4,8,384]{2,1,0:T(8,128)S(1)}, f32[8,384]{1,0:T(8,128)S(1)}, f32[8,384]{1,0:T(8,128)S(1)}, f32[8,384]{1,0:T(8,128)S(1)}, f32[8,384]{1,0:T(8,128)S(1)}, /*index=5*/f32[8,384]{1,0:T(8,128)S(1)}) custom-call(f32[1,1,6,4,300]{4,3,2,1,0:T(4,128)} %bitcast.2, s32[1,1,4]{2,1,0:T(1,128)} %refs_1_.2), custom_call_target="tpu_custom_call" | custom-call | bytes 139408 | tf_op jit(solution)/shard_map/prepare/pallas_call | solution.py:456
  1.5 3.7 %collective-permute-start = (f32[8,384]{1,0:T(8,128)S(1)}, f32[8,384]{1,0:T(8,128)S(1)}, u32[]{:S(2)}, u32[]{:S(2)}) collective-permute-start(f32[8,384]{1,0:T(8,128)S(1)} %get-tuple-element.43), channel_id=1, source_target_pairs={{1,2},{2,1},{5,6},{6,5},{9,10},{10,9},{13,14},{14,13},{17,18},{18,... | collective-permute-start | bytes 36872 | tf_op jit(solution)/shard_map/ppermute | solution.py:89
  5.2 3.1 %collective-permute-start.1 = (f32[8,384]{1,0:T(8,128)S(1)}, f32[8,384]{1,0:T(8,128)S(1)}, u32[]{:S(2)}, u32[]{:S(2)}) collective-permute-start(f32[8,384]{1,0:T(8,128)S(1)} %get-tuple-element.44), channel_id=1, source_target_pairs={{4,8},{8,4},{12,16},{16,12},{20,24},{24,20},{5,9},{9,5},{13,17},{1... | collective-permute-start | bytes 36872 | tf_op jit(solution)/shard_map/ppermute | solution.py:89
  8.3 0.1 collective-permute-start.2
  8.4 0.1 collective-permute-start.3
  8.5 1.0 %invert.1.refs_2_ = f32[8,128]{1,0:T(8,128)S(1)} custom-call(f32[1,6,1,16]{3,2,1,0:T(1,128)} %bitcast.3, f32[4,8,384]{2,1,0:T(8,128)S(1)} %get-tuple-element.41.refs_1_.refs_0_, f32[8,384]{1,0:T(8,128)S(1)} %get-tuple-element.42.refs_2_.refs_1_), custom_call_target="tpu_custom_call" | custom-call | flops 46080000 | bytes 65920 | tf_op jit(solution)/shard_map/invert/pallas_call | solution.py:456
  9.5 1.0 %collective-permute-done.1.refs_4_ = f32[8,384]{1,0:T(8,128)S(1)} collective-permute-done((f32[8,384]{1,0:T(8,128)S(1)}, f32[8,384]{1,0:T(8,128)S(1)}, u32[]{:S(2)}, u32[]{:S(2)}) %collective-permute-start.1) | collective-permute-done | bytes 12320 | tf_op jit(solution)/shard_map/ppermute | solution.py:89
  10.5 0.4 collective-permute-done.2.refs_5_
  10.9 1.5 %couple.1 = (f32[32,8,128]{2,1,0:T(8,128)}, f32[8,384]{1,0:T(8,128)}, f32[4,16,384]{2,1,0:T(8,128)}) custom-call(f32[4,8,384]{2,1,0:T(8,128)S(1)} %get-tuple-element.41.refs_1_.refs_0_, f32[8,384]{1,0:T(8,128)S(1)} %get-tuple-element.42.refs_2_.refs_1_, f32[8,128]{1,0:T(8,128)S(1)} %invert.1.refs_2_, f32[8,384]{1,0:T(8,128)S(1)} %collective-permute-done.refs_3_, ...), custom_call_target="tpu_custom_call" | custom-call | bytes 356352 | tf_op jit(solution)/shard_map/couple/pallas_call | solution.py:456
  12.5 5.1 %all-to-all-start = ((f32[32,8,128]{2,1,0:T(8,128)}), f32[32,8,128]{2,1,0:T(8,128)S(1)}, u32[]{:S(2)}, u32[]{:S(2)}) async-start(f32[32,8,128]{2,1,0:T(8,128)} %get-tuple-element.49), calls=%async_computation | async-start | bytes 262144 | tf_op jit(solution)/shard_map/all_to_all | solution.py:469
  17.6 6.7 %arrange.1 = (f32[16,1200]{1,0:T(8,128)}, bf16[1200,1200]{1,0:T(8,128)(2,1)S(1)}) custom-call(s32[1,1,4,300]{3,2,1,0:T(4,128)} %refs_0_.1, bf16[1,1,1200,1200]{3,2,1,0:T(8,128)(2,1)} %refs_1_.3, f32[1,1,16,1200]{3,2,1,0:T(8,128)} %refs_2_.1), custom_call_target="tpu_custom_call" | custom-call | flops 2949120000 | bytes 5918400 | tf_op jit(solution)/shard_map/arrange/pallas_call | solution.py:456
  24.2 0.2 all-to-all-done.refs_2_
  24.4 4.1 %begin.1 = (f32[40,256]{1,0:T(8,128)}, f32[4,16,384]{2,1,0:T(8,128)}, f32[4,16,384]{2,1,0:T(8,128)}, f32[4,16,384]{2,1,0:T(8,128)}, f32[32,8,128]{2,1,0:T(8,128)...) custom-call(f32[4,16,384]{2,1,0:T(8,128)} %get-tuple-element.47.refs_0_.refs_1_, ...), custom_call_target="tpu_custom_call" | custom-call | flops 46080000 | bytes 3751424 | tf_op jit(solution)/shard_map/begin/pallas_call | solution.py:456
  28.5 5.7 %all-to-all-start.1 = ((f32[32,8,128]{2,1,0:T(8,128)}), f32[32,8,128]{2,1,0:T(8,128)S(1)}, u32[]{:S(2)}, u32[]{:S(2)}) async-start(f32[32,8,128]{2,1,0:T(8,128)} %get-tuple-element.59), calls=%async_computation.1 | async-start | bytes 262144 | tf_op jit(solution)/shard_map/all_to_all | solution.py:469
  34.2 3.3 %collective-permute-start.4 = (f32[16,384]{1,0:T(8,128)}, f32[16,384]{1,0:T(8,128)S(1)}, u32[]{:S(2)}, u32[]{:S(2)}) collective-permute-start(f32[16,384]{1,0:T(8,128)} %get-tuple-element.55), channel_id=1, source_target_pairs={{1,2},{2,1},{5,6},{6,5},{9,10},{10,9},{13,14},{14,13},{17,18},{18,... | collective-permute-start | bytes 73736 | tf_op jit(solution)/shard_map/ppermute | solution.py:89
  37.6 3.1 %collective-permute-start.5 = (f32[16,384]{1,0:T(8,128)}, f32[16,384]{1,0:T(8,128)S(1)}, u32[]{:S(2)}, u32[]{:S(2)}) collective-permute-start(f32[16,384]{1,0:T(8,128)} %get-tuple-element.56), channel_id=1, source_target_pairs={{4,8},{8,4},{12,16},{16,12},{20,24},{24,20},{5,9},{9,5},{13,17},{1... | collective-permute-start | bytes 73736 | tf_op jit(solution)/shard_map/ppermute | solution.py:89
  40.8 2.4 %collective-permute-done.5.refs_6_ = f32[16,384]{1,0:T(8,128)S(1)} collective-permute-done((f32[16,384]{1,0:T(8,128)}, f32[16,384]{1,0:T(8,128)S(1)}, u32[]{:S(2)}, u32[]{:S(2)}) %collective-permute-start.5) | collective-permute-done | bytes 24608 | tf_op jit(solution)/shard_map/ppermute | solution.py:89
  43.3 0.4 collective-permute-done.6.refs_7_
  43.6 3.3 %first_direction.1 = (f32[4,16,384]{2,1,0:T(8,128)}, f32[4,16,384]{2,1,0:T(8,128)}, f32[4,16,384]{2,1,0:T(8,128)}, f32[32,8,128]{2,1,0:T(8,128)}, f32[16,384]{1,...) custom-call(f32[40,256]{1,0:T(8,128)} %get-tuple-element.51.refs_0_, ...), custom_call_target="tpu_custom_call" | custom-call | flops 46080000 | bytes 3981824 | tf_op jit(solution)/shard_map/first_direction/pallas_call | solution.py:456
  47.0 5.2 %all-to-all-start.2 = ((f32[32,8,128]{2,1,0:T(8,128)}), f32[32,8,128]{2,1,0:T(8,128)S(1)}, u32[]{:S(2)}, u32[]{:S(2)}) async-start(f32[32,8,128]{2,1,0:T(8,128)} %get-tuple-element.68), calls=%async_computation.2 | async-start | bytes 262144 | tf_op jit(solution)/shard_map/all_to_all | solution.py:469
  52.2 3.3 %collective-permute-start.8 = (f32[16,384]{1,0:T(8,128)}, f32[16,384]{1,0:T(8,128)S(1)}, u32[]{:S(2)}, u32[]{:S(2)}) collective-permute-start(f32[16,384]{1,0:T(8,128)} %get-tuple-element.64), channel_id=1, source_target_pairs={{1,2},{2,1},{5,6},{6,5},{9,10},{10,9},{13,14},{14,13},{17,18},{18,... | collective-permute-start | bytes 73736 | tf_op jit(solution)/shard_map/ppermute | solution.py:89
  55.5 3.1 %collective-permute-start.9 = (f32[16,384]{1,0:T(8,128)}, f32[16,384]{1,0:T(8,128)S(1)}, u32[]{:S(2)}, u32[]{:S(2)}) collective-permute-start(f32[16,384]{1,0:T(8,128)} %get-tuple-element.65), channel_id=1, source_target_pairs={{4,8},{8,4},{12,16},{16,12},{20,24},{24,20},{5,9},{9,5},{13,17},{1... | collective-permute-start | bytes 73736 | tf_op jit(solution)/shard_map/ppermute | solution.py:89
  58.6 0.1 collective-permute-start.10
  58.8 2.4 %collective-permute-done.9.refs_8_ = f32[16,384]{1,0:T(8,128)S(1)} collective-permute-done((f32[16,384]{1,0:T(8,128)}, f32[16,384]{1,0:T(8,128)S(1)}, u32[]{:S(2)}, u32[]{:S(2)}) %collective-permute-start.9) | collective-permute-done | bytes 24608 | tf_op jit(solution)/shard_map/ppermute | solution.py:89
  61.2 0.4 collective-permute-done.10.refs_9_
  61.6 3.2 %second_direction.1 = (f32[4,16,384]{2,1,0:T(8,128)}, f32[4,16,384]{2,1,0:T(8,128)}, f32[4,16,384]{2,1,0:T(8,128)}, f32[4,16,384]{2,1,0:T(8,128)}, f32[4,16,384]...) custom-call(f32[40,256]{1,0:T(8,128)} %get-tuple-element.51.refs_0_,, ...), custom_call_target="tpu_custom_call" | custom-call | flops 46080000 | bytes 4379136 | tf_op jit(solution)/shard_map/second_direction/pallas_call | solution.py:456
  64.7 5.2 %all-to-all-start.3 = ((f32[32,8,128]{2,1,0:T(8,128)}), f32[32,8,128]{2,1,0:T(8,128)S(1)}, u32[]{:S(2)}, u32[]{:S(2)}) async-start(f32[32,8,128]{2,1,0:T(8,128)} %get-tuple-element.79), calls=%async_computation.3 | async-start | bytes 262144 | tf_op jit(solution)/shard_map/all_to_all | solution.py:469
  70.0 3.3 %collective-permute-start.12 = (f32[16,384]{1,0:T(8,128)}, f32[16,384]{1,0:T(8,128)S(1)}, u32[]{:S(2)}, u32[]{:S(2)}) collective-permute-start(f32[16,384]{1,0:T(8,128)} %get-tuple-element.75), channel_id=1, source_target_pairs={{1,2},{2,1},{5,6},{6,5},{9,10},{10,9},{13,14},{14,13},{17,18},{18,... | collective-permute-start | bytes 73736 | tf_op jit(solution)/shard_map/ppermute | solution.py:89
  73.3 3.1 %collective-permute-start.13 = (f32[16,384]{1,0:T(8,128)}, f32[16,384]{1,0:T(8,128)S(1)}, u32[]{:S(2)}, u32[]{:S(2)}) collective-permute-start(f32[16,384]{1,0:T(8,128)} %get-tuple-element.76), channel_id=1, source_target_pairs={{4,8},{8,4},{12,16},{16,12},{20,24},{24,20},{5,9},{9,5},{13,17},{1... | collective-permute-start | bytes 73736 | tf_op jit(solution)/shard_map/ppermute | solution.py:89
  76.6 2.4 %collective-permute-done.13.refs_9_ = f32[16,384]{1,0:T(8,128)S(1)} collective-permute-done((f32[16,384]{1,0:T(8,128)}, f32[16,384]{1,0:T(8,128)S(1)}, u32[]{:S(2)}, u32[]{:S(2)}) %collective-permute-start.13) | collective-permute-done | bytes 24608 | tf_op jit(solution)/shard_map/ppermute | solution.py:89
  79.0 0.4 collective-permute-done.14.refs_10_
  79.4 1.9 %finish.1 = (f32[1,1,4,16,300]{4,3,2,1,0:T(8,128)}, f32[1,1,4,16,300]{4,3,2,1,0:T(8,128)}) custom-call(f32[8,128]{1,0:T(8,128)} %get-tuple-element.69.refs_0_, f32[4,16,384]{2,1,0:T(8,128)} %get-tuple-element.70.refs_1_, f32[8,384]{1,0:T(8,128)} %get-tuple-element.53.refs_3_.refs_2_, f32[4,16,384]{2,1,0:T(8,128)} %get-tuple-element.71.refs_3_, ...), custom_call_target="tpu_custom_call" | custom-call | bytes 989184 | tf_op jit(solution)/shard_map/finish/pallas_call | solution.py:456
  (16 shorter events, 0.4 us)
Async XLA Ops:
  1.5 8.0 %collective-permute-start = (f32[8,384]{1,0:T(8,128)S(1)}, f32[8,384]{1,0:T(8,128)S(1)}, u32[]{:S(2)}, u32[]{:S(2)}) collective-permute-start(f32[8,384]{1,0:T(8,128)S(1)} %get-tuple-element.43), channel_id=1, source_target_pairs={{1,2},{2,1},{5,6},{6,5},{9,10},{10,9},{13,14},{14,13},{17,18},{18,... | collective-permute-start | bytes 36872 | tf_op jit(solution)/shard_map/ppermute | solution.py:89
  5.2 5.3 %collective-permute-start.1 = (f32[8,384]{1,0:T(8,128)S(1)}, f32[8,384]{1,0:T(8,128)S(1)}, u32[]{:S(2)}, u32[]{:S(2)}) collective-permute-start(f32[8,384]{1,0:T(8,128)S(1)} %get-tuple-element.44), channel_id=1, source_target_pairs={{4,8},{8,4},{12,16},{16,12},{20,24},{24,20},{5,9},{9,5},{13,17},{1... | collective-permute-start | bytes 36872 | tf_op jit(solution)/shard_map/ppermute | solution.py:89
  8.3 2.6 %collective-permute-start.2 = (f32[8,384]{1,0:T(8,128)S(1)}, f32[8,384]{1,0:T(8,128)S(1)}, u32[]{:S(2)}, u32[]{:S(2)}) collective-permute-start(f32[8,384]{1,0:T(8,128)S(1)} %get-tuple-element.45), channel_id=1, source_target_pairs={{0,4},{4,0},{8,12},{12,8},{16,20},{20,16},{24,28},{28,24},{1,5},{5... | collective-permute-start | bytes 36872 | tf_op jit(solution)/shard_map/ppermute | solution.py:89
  8.4 2.5 %collective-permute-start.3 = (f32[8,384]{1,0:T(8,128)S(1)}, f32[8,384]{1,0:T(8,128)S(1)}, u32[]{:S(2)}, u32[]{:S(2)}) collective-permute-start(f32[8,384]{1,0:T(8,128)S(1)} %get-tuple-element.46), channel_id=1, source_target_pairs={{0,1},{1,0},{2,3},{3,2},{4,5},{5,4},{6,7},{7,6},{8,9},{9,8},{10,11... | collective-permute-start | bytes 36872 | tf_op jit(solution)/shard_map/ppermute | solution.py:89
  12.5 11.9 %all-to-all-start = ((f32[32,8,128]{2,1,0:T(8,128)}), f32[32,8,128]{2,1,0:T(8,128)S(1)}, u32[]{:S(2)}, u32[]{:S(2)}) async-start(f32[32,8,128]{2,1,0:T(8,128)} %get-tuple-element.49), calls=%async_computation | async-start | bytes 262144 | tf_op jit(solution)/shard_map/all_to_all | solution.py:469
  28.5 15.1 %all-to-all-start.1 = ((f32[32,8,128]{2,1,0:T(8,128)}), f32[32,8,128]{2,1,0:T(8,128)S(1)}, u32[]{:S(2)}, u32[]{:S(2)}) async-start(f32[32,8,128]{2,1,0:T(8,128)} %get-tuple-element.59), calls=%async_computation.1 | async-start | bytes 262144 | tf_op jit(solution)/shard_map/all_to_all | solution.py:469
  34.2 6.6 %collective-permute-start.4 = (f32[16,384]{1,0:T(8,128)}, f32[16,384]{1,0:T(8,128)S(1)}, u32[]{:S(2)}, u32[]{:S(2)}) collective-permute-start(f32[16,384]{1,0:T(8,128)} %get-tuple-element.55), channel_id=1, source_target_pairs={{1,2},{2,1},{5,6},{6,5},{9,10},{10,9},{13,14},{14,13},{17,18},{18,... | collective-permute-start | bytes 73736 | tf_op jit(solution)/shard_map/ppermute | solution.py:89
  37.6 5.7 %collective-permute-start.5 = (f32[16,384]{1,0:T(8,128)}, f32[16,384]{1,0:T(8,128)S(1)}, u32[]{:S(2)}, u32[]{:S(2)}) collective-permute-start(f32[16,384]{1,0:T(8,128)} %get-tuple-element.56), channel_id=1, source_target_pairs={{4,8},{8,4},{12,16},{16,12},{20,24},{24,20},{5,9},{9,5},{13,17},{1... | collective-permute-start | bytes 73736 | tf_op jit(solution)/shard_map/ppermute | solution.py:89
  40.7 3.0 %collective-permute-start.6 = (f32[16,384]{1,0:T(8,128)}, f32[16,384]{1,0:T(8,128)S(1)}, u32[]{:S(2)}, u32[]{:S(2)}) collective-permute-start(f32[16,384]{1,0:T(8,128)} %get-tuple-element.57), channel_id=1, source_target_pairs={{0,4},{4,0},{8,12},{12,8},{16,20},{20,16},{24,28},{28,24},{1,5},{5... | collective-permute-start | bytes 73736 | tf_op jit(solution)/shard_map/ppermute | solution.py:89
  40.8 2.9 %collective-permute-start.7 = (f32[16,384]{1,0:T(8,128)}, f32[16,384]{1,0:T(8,128)S(1)}, u32[]{:S(2)}, u32[]{:S(2)}) collective-permute-start(f32[16,384]{1,0:T(8,128)} %get-tuple-element.58), channel_id=1, source_target_pairs={{0,1},{1,0},{2,3},{3,2},{4,5},{5,4},{6,7},{7,6},{8,9},{9,8},{10,11... | collective-permute-start | bytes 73736 | tf_op jit(solution)/shard_map/ppermute | solution.py:89
  47.0 14.6 %all-to-all-start.2 = ((f32[32,8,128]{2,1,0:T(8,128)}), f32[32,8,128]{2,1,0:T(8,128)S(1)}, u32[]{:S(2)}, u32[]{:S(2)}) async-start(f32[32,8,128]{2,1,0:T(8,128)} %get-tuple-element.68), calls=%async_computation.2 | async-start | bytes 262144 | tf_op jit(solution)/shard_map/all_to_all | solution.py:469
  52.2 6.6 %collective-permute-start.8 = (f32[16,384]{1,0:T(8,128)}, f32[16,384]{1,0:T(8,128)S(1)}, u32[]{:S(2)}, u32[]{:S(2)}) collective-permute-start(f32[16,384]{1,0:T(8,128)} %get-tuple-element.64), channel_id=1, source_target_pairs={{1,2},{2,1},{5,6},{6,5},{9,10},{10,9},{13,14},{14,13},{17,18},{18,... | collective-permute-start | bytes 73736 | tf_op jit(solution)/shard_map/ppermute | solution.py:89
  55.5 5.7 %collective-permute-start.9 = (f32[16,384]{1,0:T(8,128)}, f32[16,384]{1,0:T(8,128)S(1)}, u32[]{:S(2)}, u32[]{:S(2)}) collective-permute-start(f32[16,384]{1,0:T(8,128)} %get-tuple-element.65), channel_id=1, source_target_pairs={{4,8},{8,4},{12,16},{16,12},{20,24},{24,20},{5,9},{9,5},{13,17},{1... | collective-permute-start | bytes 73736 | tf_op jit(solution)/shard_map/ppermute | solution.py:89
  58.6 3.0 %collective-permute-start.10 = (f32[16,384]{1,0:T(8,128)}, f32[16,384]{1,0:T(8,128)S(1)}, u32[]{:S(2)}, u32[]{:S(2)}) collective-permute-start(f32[16,384]{1,0:T(8,128)} %get-tuple-element.66), channel_id=1, source_target_pairs={{0,4},{4,0},{8,12},{12,8},{16,20},{20,16},{24,28},{28,24},{1,5},{5... | collective-permute-start | bytes 73736 | tf_op jit(solution)/shard_map/ppermute | solution.py:89
  58.7 2.9 %collective-permute-start.11 = (f32[16,384]{1,0:T(8,128)}, f32[16,384]{1,0:T(8,128)S(1)}, u32[]{:S(2)}, u32[]{:S(2)}) collective-permute-start(f32[16,384]{1,0:T(8,128)} %get-tuple-element.67), channel_id=1, source_target_pairs={{0,1},{1,0},{2,3},{3,2},{4,5},{5,4},{6,7},{7,6},{8,9},{9,8},{10,11... | collective-permute-start | bytes 73736 | tf_op jit(solution)/shard_map/ppermute | solution.py:89
  64.7 14.6 %all-to-all-start.3 = ((f32[32,8,128]{2,1,0:T(8,128)}), f32[32,8,128]{2,1,0:T(8,128)S(1)}, u32[]{:S(2)}, u32[]{:S(2)}) async-start(f32[32,8,128]{2,1,0:T(8,128)} %get-tuple-element.79), calls=%async_computation.3 | async-start | bytes 262144 | tf_op jit(solution)/shard_map/all_to_all | solution.py:469
  70.0 6.6 %collective-permute-start.12 = (f32[16,384]{1,0:T(8,128)}, f32[16,384]{1,0:T(8,128)S(1)}, u32[]{:S(2)}, u32[]{:S(2)}) collective-permute-start(f32[16,384]{1,0:T(8,128)} %get-tuple-element.75), channel_id=1, source_target_pairs={{1,2},{2,1},{5,6},{6,5},{9,10},{10,9},{13,14},{14,13},{17,18},{18,... | collective-permute-start | bytes 73736 | tf_op jit(solution)/shard_map/ppermute | solution.py:89
  73.3 5.7 %collective-permute-start.13 = (f32[16,384]{1,0:T(8,128)}, f32[16,384]{1,0:T(8,128)S(1)}, u32[]{:S(2)}, u32[]{:S(2)}) collective-permute-start(f32[16,384]{1,0:T(8,128)} %get-tuple-element.76), channel_id=1, source_target_pairs={{4,8},{8,4},{12,16},{16,12},{20,24},{24,20},{5,9},{9,5},{13,17},{1... | collective-permute-start | bytes 73736 | tf_op jit(solution)/shard_map/ppermute | solution.py:89
  76.4 3.0 %collective-permute-start.14 = (f32[16,384]{1,0:T(8,128)}, f32[16,384]{1,0:T(8,128)S(1)}, u32[]{:S(2)}, u32[]{:S(2)}) collective-permute-start(f32[16,384]{1,0:T(8,128)} %get-tuple-element.77), channel_id=1, source_target_pairs={{0,4},{4,0},{8,12},{12,8},{16,20},{20,16},{24,28},{28,24},{1,5},{5... | collective-permute-start | bytes 73736 | tf_op jit(solution)/shard_map/ppermute | solution.py:89
  76.5 2.9 %collective-permute-start.15 = (f32[16,384]{1,0:T(8,128)}, f32[16,384]{1,0:T(8,128)S(1)}, u32[]{:S(2)}, u32[]{:S(2)}) collective-permute-start(f32[16,384]{1,0:T(8,128)} %get-tuple-element.78), channel_id=1, source_target_pairs={{0,1},{1,0},{2,3},{3,2},{4,5},{5,4},{6,7},{7,6},{8,9},{9,8},{10,11... | collective-permute-start | bytes 73736 | tf_op jit(solution)/shard_map/ppermute | solution.py:89

commit v15 on v11

--- a/solution.py
+++ b/solution.py
@@ -297,10 +297,10 @@
     start = window_start(z, ix) * z.ny
     inverses = [received[pl.ds(start + spot, 1)][0][:, INVERSE_LANE : INVERSE_LANE + 8] for spot in near_spots]
     fields = []
-    for f in range(4):
-        both = lift_rows[f]
-        own, near = both[0:8] * SIGNS[f], both[8:16] * -SIGNS[f]
-        rows[f] = jnp.concatenate([dot(inverses[0], own), dot(inverses[1 + f], near)], axis=0)
+    own = dot(inverses[0], jnp.concatenate([lift_rows[f][0:8] * SIGNS[f] for f in range(4)], axis=1))
+    for f in range(4):
+        near = dot(inverses[1 + f], lift_rows[f][8:16] * -SIGNS[f])
+        rows[f] = jnp.concatenate([own[:, f * z.lanes : (f + 1) * z.lanes], near], axis=0)
         fields.append(lifted(z, amplitudes, lift_rows, f))
         multipliers[f] = fields[f]
     for item in (solve_rows, rows, multipliers):
@@ -336,8 +336,8 @@
     for f in range(4):
         image[f] = found[f]
     image.push()
-    gamma = sum(weights[f] * total(field[f] * moved[f]) for f in range(4))
-    curvature = sum(SIGNS[f] * total(moved[f] * found[f]) for f in range(4))
+    gamma = total(sum(weights[f] * (field[f] * moved[f]) for f in range(4)))
+    curvature = total(sum(SIGNS[f] * (moved[f] * found[f]) for f in range(4)))
     send_faces(z, found, (to0, to1, to2, to3))
     send_coarse(z, found, rows, [gamma, curvature], sent, tile)
 
@@ -369,11 +369,11 @@
         fresh[f] = found[f]
     fresh.push()
     send_faces(z, found, (to0, to1, to2, to3))
-    gamma = sum(weights[f] * total(left[f] * moved[f]) for f in range(4))
-    straight = sum(SIGNS[f] * total(moved[f] * found[f]) for f in range(4))
-    crossed = sum(
-        weights[f] * total(moved[f] * field[f]) + SIGNS[f] * total(direction[f] * found[f]) for f in range(4)
-    )
+    gamma = total(sum(weights[f] * (left[f] * moved[f]) for f in range(4)))
+    straight = total(sum(SIGNS[f] * (moved[f] * found[f]) for f in range(4)))
+    crossed = total(sum(
+        weights[f] * (moved[f] * field[f]) + SIGNS[f] * (direction[f] * found[f]) for f in range(4)
+    ))
     send_tile(jnp.zeros((8, 128), F32), [gamma, straight, crossed], sent)
 
 

time: 82.4 us -> 82.4 us (level)
  no operation moved by 1% of the time
where the time goes in v15:
time: 82.4 us; the launch traced here: 81 us
  starting transfers between devices  47.6 us (58%)
  Pallas kernels  22.6 us (27%)
  waiting for transfers between devices  9.96 us (12%)
  between operations  0.88 us (1%)
    ppermute x16, starting transfers between devices, exchange(): got.append(lax.ppermute(sent[i], axis, pairs))  27.8 us
    pallas_call x8, Pallas kernels, call(): pl.pallas_call(run, out_shape=[pltpu.HBM(a.shape, a.dtype) for a in shape...  22.6 us
    all_to_all x4, starting transfers between devices, gather(): return lax.all_to_all(values, AXES, 0, 0, tiled=True)  19.8 us
    ppermute x16, waiting for transfers between devices, exchange(): got.append(lax.ppermute(sent[i], axis, pairs))  9.79 us
  transfers between devices with their start and end apart: 20, of which 9 were waited for; matrix products, arithmetic and copies ran while one was open for 0% of the time, Pallas kernels for 9%

profile of v15, /device:TPU:5, one launch (start us, length us, event | category | flops | bytes accessed | tf_op | source)
XLA Modules:
  0.0 81.0 jit_solution(13921619808900354758)
XLA Ops:
  0.6 0.8 %prepare.1 = (f32[4,8,384]{2,1,0:T(8,128)S(1)}, f32[8,384]{1,0:T(8,128)S(1)}, f32[8,384]{1,0:T(8,128)S(1)}, f32[8,384]{1,0:T(8,128)S(1)}, f32[8,384]{1,0:T(8,128)S(1)}, /*index=5*/f32[8,384]{1,0:T(8,128)S(1)}) custom-call(f32[1,1,6,4,300]{4,3,2,1,0:T(4,128)} %bitcast.2, s32[1,1,4]{2,1,0:T(1,128)} %refs_1_.2), custom_call_target="tpu_custom_call" | custom-call | bytes 139408 | tf_op jit(solution)/shard_map/prepare/pallas_call | solution.py:456
  1.5 3.1 %collective-permute-start = (f32[8,384]{1,0:T(8,128)S(1)}, f32[8,384]{1,0:T(8,128)S(1)}, u32[]{:S(2)}, u32[]{:S(2)}) collective-permute-start(f32[8,384]{1,0:T(8,128)S(1)} %get-tuple-element.43), channel_id=1, source_target_pairs={{4,8},{8,4},{12,16},{16,12},{20,24},{24,20},{5,9},{9,5},{13,17},{1... | collective-permute-start | bytes 36872 | tf_op jit(solution)/shard_map/ppermute | solution.py:89
  4.6 4.0 %collective-permute-start.1 = (f32[8,384]{1,0:T(8,128)S(1)}, f32[8,384]{1,0:T(8,128)S(1)}, u32[]{:S(2)}, u32[]{:S(2)}) collective-permute-start(f32[8,384]{1,0:T(8,128)S(1)} %get-tuple-element.44), channel_id=1, source_target_pairs={{1,2},{2,1},{5,6},{6,5},{9,10},{10,9},{13,14},{14,13},{17,18},{18,... | collective-permute-start | bytes 36872 | tf_op jit(solution)/shard_map/ppermute | solution.py:89
  8.6 0.1 collective-permute-start.2
  8.7 0.1 collective-permute-start.3
  8.7 1.0 %invert.1.refs_2_ = f32[8,128]{1,0:T(8,128)S(1)} custom-call(f32[1,6,1,16]{3,2,1,0:T(1,128)} %bitcast.3, f32[4,8,384]{2,1,0:T(8,128)S(1)} %get-tuple-element.41.refs_1_.refs_0_, f32[8,384]{1,0:T(8,128)S(1)} %get-tuple-element.42.refs_2_.refs_1_), custom_call_target="tpu_custom_call" | custom-call | flops 46080000 | bytes 65920 | tf_op jit(solution)/shard_map/invert/pallas_call | solution.py:456
  9.8 0.2 collective-permute-done.1.refs_4_
  10.0 1.2 %collective-permute-done.2.refs_5_ = f32[8,384]{1,0:T(8,128)S(1)} collective-permute-done((f32[8,384]{1,0:T(8,128)S(1)}, f32[8,384]{1,0:T(8,128)S(1)}, u32[]{:S(2)}, u32[]{:S(2)}) %collective-permute-start.2) | collective-permute-done | bytes 12320 | tf_op jit(solution)/shard_map/ppermute | solution.py:89
  11.2 1.5 %couple.1 = (f32[32,8,128]{2,1,0:T(8,128)}, f32[8,384]{1,0:T(8,128)}, f32[4,16,384]{2,1,0:T(8,128)}) custom-call(f32[4,8,384]{2,1,0:T(8,128)S(1)} %get-tuple-element.41.refs_1_.refs_0_, f32[8,384]{1,0:T(8,128)S(1)} %get-tuple-element.42.refs_2_.refs_1_, f32[8,128]{1,0:T(8,128)S(1)} %invert.1.refs_2_, f32[8,384]{1,0:T(8,128)S(1)} %collective-permute-done.refs_3_, ...), custom_call_target="tpu_custom_call" | custom-call | bytes 356352 | tf_op jit(solution)/shard_map/couple/pallas_call | solution.py:456
  12.8 4.8 %all-to-all-start = ((f32[32,8,128]{2,1,0:T(8,128)}), f32[32,8,128]{2,1,0:T(8,128)S(1)}, u32[]{:S(2)}, u32[]{:S(2)}) async-start(f32[32,8,128]{2,1,0:T(8,128)} %get-tuple-element.49), calls=%async_computation | async-start | bytes 262144 | tf_op jit(solution)/shard_map/all_to_all | solution.py:469
  17.6 6.7 %arrange.1 = (f32[16,1200]{1,0:T(8,128)}, bf16[1200,1200]{1,0:T(8,128)(2,1)S(1)}) custom-call(s32[1,1,4,300]{3,2,1,0:T(4,128)} %refs_0_.1, bf16[1,1,1200,1200]{3,2,1,0:T(8,128)(2,1)} %refs_1_.3, f32[1,1,16,1200]{3,2,1,0:T(8,128)} %refs_2_.1), custom_call_target="tpu_custom_call" | custom-call | flops 2949120000 | bytes 5918400 | tf_op jit(solution)/shard_map/arrange/pallas_call | solution.py:456
  24.2 0.2 all-to-all-done.refs_2_
  24.4 4.1 %begin.1 = (f32[40,256]{1,0:T(8,128)}, f32[4,16,384]{2,1,0:T(8,128)}, f32[4,16,384]{2,1,0:T(8,128)}, f32[4,16,384]{2,1,0:T(8,128)}, f32[32,8,128]{2,1,0:T(8,128)...) custom-call(f32[4,16,384]{2,1,0:T(8,128)} %get-tuple-element.47.refs_0_.refs_1_, ...), custom_call_target="tpu_custom_call" | custom-call | flops 46080000 | bytes 3751424 | tf_op jit(solution)/shard_map/begin/pallas_call | solution.py:456
  28.5 5.7 %all-to-all-start.1 = ((f32[32,8,128]{2,1,0:T(8,128)}), f32[32,8,128]{2,1,0:T(8,128)S(1)}, u32[]{:S(2)}, u32[]{:S(2)}) async-start(f32[32,8,128]{2,1,0:T(8,128)} %get-tuple-element.59), calls=%async_computation.1 | async-start | bytes 262144 | tf_op jit(solution)/shard_map/all_to_all | solution.py:469
  34.2 3.1 %collective-permute-start.4 = (f32[16,384]{1,0:T(8,128)}, f32[16,384]{1,0:T(8,128)S(1)}, u32[]{:S(2)}, u32[]{:S(2)}) collective-permute-start(f32[16,384]{1,0:T(8,128)} %get-tuple-element.55), channel_id=1, source_target_pairs={{4,8},{8,4},{12,16},{16,12},{20,24},{24,20},{5,9},{9,5},{13,17},{1... | collective-permute-start | bytes 73736 | tf_op jit(solution)/shard_map/ppermute | solution.py:89
  37.3 3.6 %collective-permute-start.5 = (f32[16,384]{1,0:T(8,128)}, f32[16,384]{1,0:T(8,128)S(1)}, u32[]{:S(2)}, u32[]{:S(2)}) collective-permute-start(f32[16,384]{1,0:T(8,128)} %get-tuple-element.56), channel_id=1, source_target_pairs={{1,2},{2,1},{5,6},{6,5},{9,10},{10,9},{13,14},{14,13},{17,18},{18,... | collective-permute-start | bytes 73736 | tf_op jit(solution)/shard_map/ppermute | solution.py:89
  41.1 1.6 %collective-permute-done.5.refs_6_ = f32[16,384]{1,0:T(8,128)S(1)} collective-permute-done((f32[16,384]{1,0:T(8,128)}, f32[16,384]{1,0:T(8,128)S(1)}, u32[]{:S(2)}, u32[]{:S(2)}) %collective-permute-start.5) | collective-permute-done | bytes 24608 | tf_op jit(solution)/shard_map/ppermute | solution.py:89
  42.7 1.2 %collective-permute-done.6.refs_7_ = f32[16,384]{1,0:T(8,128)S(1)} collective-permute-done((f32[16,384]{1,0:T(8,128)}, f32[16,384]{1,0:T(8,128)S(1)}, u32[]{:S(2)}, u32[]{:S(2)}) %collective-permute-start.6) | collective-permute-done | bytes 24608 | tf_op jit(solution)/shard_map/ppermute | solution.py:89
  43.9 3.3 %first_direction.1 = (f32[4,16,384]{2,1,0:T(8,128)}, f32[4,16,384]{2,1,0:T(8,128)}, f32[4,16,384]{2,1,0:T(8,128)}, f32[32,8,128]{2,1,0:T(8,128)}, f32[16,384]{1,...) custom-call(f32[40,256]{1,0:T(8,128)} %get-tuple-element.51.refs_0_, ...), custom_call_target="tpu_custom_call" | custom-call | flops 46080000 | bytes 3981824 | tf_op jit(solution)/shard_map/first_direction/pallas_call | solution.py:456
  47.2 4.6 %all-to-all-start.2 = ((f32[32,8,128]{2,1,0:T(8,128)}), f32[32,8,128]{2,1,0:T(8,128)S(1)}, u32[]{:S(2)}, u32[]{:S(2)}) async-start(f32[32,8,128]{2,1,0:T(8,128)} %get-tuple-element.68), calls=%async_computation.2 | async-start | bytes 262144 | tf_op jit(solution)/shard_map/all_to_all | solution.py:469
  51.9 3.1 %collective-permute-start.8 = (f32[16,384]{1,0:T(8,128)}, f32[16,384]{1,0:T(8,128)S(1)}, u32[]{:S(2)}, u32[]{:S(2)}) collective-permute-start(f32[16,384]{1,0:T(8,128)} %get-tuple-element.64), channel_id=1, source_target_pairs={{4,8},{8,4},{12,16},{16,12},{20,24},{24,20},{5,9},{9,5},{13,17},{1... | collective-permute-start | bytes 73736 | tf_op jit(solution)/shard_map/ppermute | solution.py:89
  55.0 3.6 %collective-permute-start.9 = (f32[16,384]{1,0:T(8,128)}, f32[16,384]{1,0:T(8,128)S(1)}, u32[]{:S(2)}, u32[]{:S(2)}) collective-permute-start(f32[16,384]{1,0:T(8,128)} %get-tuple-element.65), channel_id=1, source_target_pairs={{1,2},{2,1},{5,6},{6,5},{9,10},{10,9},{13,14},{14,13},{17,18},{18,... | collective-permute-start | bytes 73736 | tf_op jit(solution)/shard_map/ppermute | solution.py:89
  58.8 1.6 %collective-permute-done.9.refs_8_ = f32[16,384]{1,0:T(8,128)S(1)} collective-permute-done((f32[16,384]{1,0:T(8,128)}, f32[16,384]{1,0:T(8,128)S(1)}, u32[]{:S(2)}, u32[]{:S(2)}) %collective-permute-start.9) | collective-permute-done | bytes 24608 | tf_op jit(solution)/shard_map/ppermute | solution.py:89
  60.4 1.2 %collective-permute-done.10.refs_9_ = f32[16,384]{1,0:T(8,128)S(1)} collective-permute-done((f32[16,384]{1,0:T(8,128)}, f32[16,384]{1,0:T(8,128)S(1)}, u32[]{:S(2)}, u32[]{:S(2)}) %collective-permute-start.10) | collective-permute-done | bytes 24608 | tf_op jit(solution)/shard_map/ppermute | solution.py:89
  61.6 3.1 %second_direction.1 = (f32[4,16,384]{2,1,0:T(8,128)}, f32[4,16,384]{2,1,0:T(8,128)}, f32[4,16,384]{2,1,0:T(8,128)}, f32[4,16,384]{2,1,0:T(8,128)}, f32[4,16,384]...) custom-call(f32[40,256]{1,0:T(8,128)} %get-tuple-element.51.refs_0_,, ...), custom_call_target="tpu_custom_call" | custom-call | flops 46080000 | bytes 4379136 | tf_op jit(solution)/shard_map/second_direction/pallas_call | solution.py:456
  64.7 4.6 %all-to-all-start.3 = ((f32[32,8,128]{2,1,0:T(8,128)}), f32[32,8,128]{2,1,0:T(8,128)S(1)}, u32[]{:S(2)}, u32[]{:S(2)}) async-start(f32[32,8,128]{2,1,0:T(8,128)} %get-tuple-element.79), calls=%async_computation.3 | async-start | bytes 262144 | tf_op jit(solution)/shard_map/all_to_all | solution.py:469
  69.4 3.1 %collective-permute-start.12 = (f32[16,384]{1,0:T(8,128)}, f32[16,384]{1,0:T(8,128)S(1)}, u32[]{:S(2)}, u32[]{:S(2)}) collective-permute-start(f32[16,384]{1,0:T(8,128)} %get-tuple-element.75), channel_id=1, source_target_pairs={{4,8},{8,4},{12,16},{16,12},{20,24},{24,20},{5,9},{9,5},{13,17},{1... | collective-permute-start | bytes 73736 | tf_op jit(solution)/shard_map/ppermute | solution.py:89
  72.5 3.6 %collective-permute-start.13 = (f32[16,384]{1,0:T(8,128)}, f32[16,384]{1,0:T(8,128)S(1)}, u32[]{:S(2)}, u32[]{:S(2)}) collective-permute-start(f32[16,384]{1,0:T(8,128)} %get-tuple-element.76), channel_id=1, source_target_pairs={{1,2},{2,1},{5,6},{6,5},{9,10},{10,9},{13,14},{14,13},{17,18},{18,... | collective-permute-start | bytes 73736 | tf_op jit(solution)/shard_map/ppermute | solution.py:89
  76.1 0.1 collective-permute-start.14
  76.3 1.6 %collective-permute-done.13.refs_9_ = f32[16,384]{1,0:T(8,128)S(1)} collective-permute-done((f32[16,384]{1,0:T(8,128)}, f32[16,384]{1,0:T(8,128)S(1)}, u32[]{:S(2)}, u32[]{:S(2)}) %collective-permute-start.13) | collective-permute-done | bytes 24608 | tf_op jit(solution)/shard_map/ppermute | solution.py:89
  77.8 1.2 %collective-permute-done.14.refs_10_ = f32[16,384]{1,0:T(8,128)S(1)} collective-permute-done((f32[16,384]{1,0:T(8,128)}, f32[16,384]{1,0:T(8,128)S(1)}, u32[]{:S(2)}, u32[]{:S(2)}) %collective-permute-start.14) | collective-permute-done | bytes 24608 | tf_op jit(solution)/shard_map/ppermute | solution.py:89
  79.1 1.9 %finish.1 = (f32[1,1,4,16,300]{4,3,2,1,0:T(8,128)}, f32[1,1,4,16,300]{4,3,2,1,0:T(8,128)}) custom-call(f32[8,128]{1,0:T(8,128)} %get-tuple-element.69.refs_0_, f32[4,16,384]{2,1,0:T(8,128)} %get-tuple-element.70.refs_1_, f32[8,384]{1,0:T(8,128)} %get-tuple-element.53.refs_3_.refs_2_, f32[4,16,384]{2,1,0:T(8,128)} %get-tuple-element.71.refs_3_, ...), custom_call_target="tpu_custom_call" | custom-call | bytes 989184 | tf_op jit(solution)/shard_map/finish/pallas_call | solution.py:456
  (16 shorter events, 0.4 us)
Async XLA Ops:
  1.5 8.3 %collective-permute-start = (f32[8,384]{1,0:T(8,128)S(1)}, f32[8,384]{1,0:T(8,128)S(1)}, u32[]{:S(2)}, u32[]{:S(2)}) collective-permute-start(f32[8,384]{1,0:T(8,128)S(1)} %get-tuple-element.43), channel_id=1, source_target_pairs={{4,8},{8,4},{12,16},{16,12},{20,24},{24,20},{5,9},{9,5},{13,17},{1... | collective-permute-start | bytes 36872 | tf_op jit(solution)/shard_map/ppermute | solution.py:89
  4.6 5.3 %collective-permute-start.1 = (f32[8,384]{1,0:T(8,128)S(1)}, f32[8,384]{1,0:T(8,128)S(1)}, u32[]{:S(2)}, u32[]{:S(2)}) collective-permute-start(f32[8,384]{1,0:T(8,128)S(1)} %get-tuple-element.44), channel_id=1, source_target_pairs={{1,2},{2,1},{5,6},{6,5},{9,10},{10,9},{13,14},{14,13},{17,18},{18,... | collective-permute-start | bytes 36872 | tf_op jit(solution)/shard_map/ppermute | solution.py:89
  8.6 2.6 %collective-permute-start.2 = (f32[8,384]{1,0:T(8,128)S(1)}, f32[8,384]{1,0:T(8,128)S(1)}, u32[]{:S(2)}, u32[]{:S(2)}) collective-permute-start(f32[8,384]{1,0:T(8,128)S(1)} %get-tuple-element.45), channel_id=1, source_target_pairs={{0,4},{4,0},{8,12},{12,8},{16,20},{20,16},{24,28},{28,24},{1,5},{5... | collective-permute-start | bytes 36872 | tf_op jit(solution)/shard_map/ppermute | solution.py:89
  8.7 2.5 %collective-permute-start.3 = (f32[8,384]{1,0:T(8,128)S(1)}, f32[8,384]{1,0:T(8,128)S(1)}, u32[]{:S(2)}, u32[]{:S(2)}) collective-permute-start(f32[8,384]{1,0:T(8,128)S(1)} %get-tuple-element.46), channel_id=1, source_target_pairs={{0,1},{1,0},{2,3},{3,2},{4,5},{5,4},{6,7},{7,6},{8,9},{9,8},{10,11... | collective-permute-start | bytes 36872 | tf_op jit(solution)/shard_map/ppermute | solution.py:89
  12.8 11.7 %all-to-all-start = ((f32[32,8,128]{2,1,0:T(8,128)}), f32[32,8,128]{2,1,0:T(8,128)S(1)}, u32[]{:S(2)}, u32[]{:S(2)}) async-start(f32[32,8,128]{2,1,0:T(8,128)} %get-tuple-element.49), calls=%async_computation | async-start | bytes 262144 | tf_op jit(solution)/shard_map/all_to_all | solution.py:469
  28.5 15.4 %all-to-all-start.1 = ((f32[32,8,128]{2,1,0:T(8,128)}), f32[32,8,128]{2,1,0:T(8,128)S(1)}, u32[]{:S(2)}, u32[]{:S(2)}) async-start(f32[32,8,128]{2,1,0:T(8,128)} %get-tuple-element.59), calls=%async_computation.1 | async-start | bytes 262144 | tf_op jit(solution)/shard_map/all_to_all | solution.py:469
  34.2 6.9 %collective-permute-start.4 = (f32[16,384]{1,0:T(8,128)}, f32[16,384]{1,0:T(8,128)S(1)}, u32[]{:S(2)}, u32[]{:S(2)}) collective-permute-start(f32[16,384]{1,0:T(8,128)} %get-tuple-element.55), channel_id=1, source_target_pairs={{4,8},{8,4},{12,16},{16,12},{20,24},{24,20},{5,9},{9,5},{13,17},{1... | collective-permute-start | bytes 73736 | tf_op jit(solution)/shard_map/ppermute | solution.py:89
  37.3 5.4 %collective-permute-start.5 = (f32[16,384]{1,0:T(8,128)}, f32[16,384]{1,0:T(8,128)S(1)}, u32[]{:S(2)}, u32[]{:S(2)}) collective-permute-start(f32[16,384]{1,0:T(8,128)} %get-tuple-element.56), channel_id=1, source_target_pairs={{1,2},{2,1},{5,6},{6,5},{9,10},{10,9},{13,14},{14,13},{17,18},{18,... | collective-permute-start | bytes 73736 | tf_op jit(solution)/shard_map/ppermute | solution.py:89
  41.0 3.0 %collective-permute-start.6 = (f32[16,384]{1,0:T(8,128)}, f32[16,384]{1,0:T(8,128)S(1)}, u32[]{:S(2)}, u32[]{:S(2)}) collective-permute-start(f32[16,384]{1,0:T(8,128)} %get-tuple-element.57), channel_id=1, source_target_pairs={{0,4},{4,0},{8,12},{12,8},{16,20},{20,16},{24,28},{28,24},{1,5},{5... | collective-permute-start | bytes 73736 | tf_op jit(solution)/shard_map/ppermute | solution.py:89
  41.0 2.9 %collective-permute-start.7 = (f32[16,384]{1,0:T(8,128)}, f32[16,384]{1,0:T(8,128)S(1)}, u32[]{:S(2)}, u32[]{:S(2)}) collective-permute-start(f32[16,384]{1,0:T(8,128)} %get-tuple-element.58), channel_id=1, source_target_pairs={{0,1},{1,0},{2,3},{3,2},{4,5},{5,4},{6,7},{7,6},{8,9},{9,8},{10,11... | collective-permute-start | bytes 73736 | tf_op jit(solution)/shard_map/ppermute | solution.py:89
  47.2 14.3 %all-to-all-start.2 = ((f32[32,8,128]{2,1,0:T(8,128)}), f32[32,8,128]{2,1,0:T(8,128)S(1)}, u32[]{:S(2)}, u32[]{:S(2)}) async-start(f32[32,8,128]{2,1,0:T(8,128)} %get-tuple-element.68), calls=%async_computation.2 | async-start | bytes 262144 | tf_op jit(solution)/shard_map/all_to_all | solution.py:469
  51.9 6.9 %collective-permute-start.8 = (f32[16,384]{1,0:T(8,128)}, f32[16,384]{1,0:T(8,128)S(1)}, u32[]{:S(2)}, u32[]{:S(2)}) collective-permute-start(f32[16,384]{1,0:T(8,128)} %get-tuple-element.64), channel_id=1, source_target_pairs={{4,8},{8,4},{12,16},{16,12},{20,24},{24,20},{5,9},{9,5},{13,17},{1... | collective-permute-start | bytes 73736 | tf_op jit(solution)/shard_map/ppermute | solution.py:89
  55.0 5.4 %collective-permute-start.9 = (f32[16,384]{1,0:T(8,128)}, f32[16,384]{1,0:T(8,128)S(1)}, u32[]{:S(2)}, u32[]{:S(2)}) collective-permute-start(f32[16,384]{1,0:T(8,128)} %get-tuple-element.65), channel_id=1, source_target_pairs={{1,2},{2,1},{5,6},{6,5},{9,10},{10,9},{13,14},{14,13},{17,18},{18,... | collective-permute-start | bytes 73736 | tf_op jit(solution)/shard_map/ppermute | solution.py:89
  58.6 3.0 %collective-permute-start.10 = (f32[16,384]{1,0:T(8,128)}, f32[16,384]{1,0:T(8,128)S(1)}, u32[]{:S(2)}, u32[]{:S(2)}) collective-permute-start(f32[16,384]{1,0:T(8,128)} %get-tuple-element.66), channel_id=1, source_target_pairs={{0,4},{4,0},{8,12},{12,8},{16,20},{20,16},{24,28},{28,24},{1,5},{5... | collective-permute-start | bytes 73736 | tf_op jit(solution)/shard_map/ppermute | solution.py:89
  58.7 2.9 %collective-permute-start.11 = (f32[16,384]{1,0:T(8,128)}, f32[16,384]{1,0:T(8,128)S(1)}, u32[]{:S(2)}, u32[]{:S(2)}) collective-permute-start(f32[16,384]{1,0:T(8,128)} %get-tuple-element.67), channel_id=1, source_target_pairs={{0,1},{1,0},{2,3},{3,2},{4,5},{5,4},{6,7},{7,6},{8,9},{9,8},{10,11... | collective-permute-start | bytes 73736 | tf_op jit(solution)/shard_map/ppermute | solution.py:89
  64.7 14.3 %all-to-all-start.3 = ((f32[32,8,128]{2,1,0:T(8,128)}), f32[32,8,128]{2,1,0:T(8,128)S(1)}, u32[]{:S(2)}, u32[]{:S(2)}) async-start(f32[32,8,128]{2,1,0:T(8,128)} %get-tuple-element.79), calls=%async_computation.3 | async-start | bytes 262144 | tf_op jit(solution)/shard_map/all_to_all | solution.py:469
  69.4 6.9 %collective-permute-start.12 = (f32[16,384]{1,0:T(8,128)}, f32[16,384]{1,0:T(8,128)S(1)}, u32[]{:S(2)}, u32[]{:S(2)}) collective-permute-start(f32[16,384]{1,0:T(8,128)} %get-tuple-element.75), channel_id=1, source_target_pairs={{4,8},{8,4},{12,16},{16,12},{20,24},{24,20},{5,9},{9,5},{13,17},{1... | collective-permute-start | bytes 73736 | tf_op jit(solution)/shard_map/ppermute | solution.py:89
  72.5 5.4 %collective-permute-start.13 = (f32[16,384]{1,0:T(8,128)}, f32[16,384]{1,0:T(8,128)S(1)}, u32[]{:S(2)}, u32[]{:S(2)}) collective-permute-start(f32[16,384]{1,0:T(8,128)} %get-tuple-element.76), channel_id=1, source_target_pairs={{1,2},{2,1},{5,6},{6,5},{9,10},{10,9},{13,14},{14,13},{17,18},{18,... | collective-permute-start | bytes 73736 | tf_op jit(solution)/shard_map/ppermute | solution.py:89
  76.1 3.0 %collective-permute-start.14 = (f32[16,384]{1,0:T(8,128)}, f32[16,384]{1,0:T(8,128)S(1)}, u32[]{:S(2)}, u32[]{:S(2)}) collective-permute-start(f32[16,384]{1,0:T(8,128)} %get-tuple-element.77), channel_id=1, source_target_pairs={{0,4},{4,0},{8,12},{12,8},{16,20},{20,16},{24,28},{28,24},{1,5},{5... | collective-permute-start | bytes 73736 | tf_op jit(solution)/shard_map/ppermute | solution.py:89
  76.2 2.9 %collective-permute-start.15 = (f32[16,384]{1,0:T(8,128)}, f32[16,384]{1,0:T(8,128)S(1)}, u32[]{:S(2)}, u32[]{:S(2)}) collective-permute-start(f32[16,384]{1,0:T(8,128)} %get-tuple-element.78), channel_id=1, source_target_pairs={{0,1},{1,0},{2,3},{3,2},{4,5},{5,4},{6,7},{7,6},{8,9},{9,8},{10,11... | collective-permute-start | bytes 73736 | tf_op jit(solution)/shard_map/ppermute | solution.py:89
